TPU v7x, 32 devices: a whole 2x2x4 slice. The times are simulated.
32 devices in a mesh: row: 8 (over z, x), space: 4 (over y, core).
Axes of the slice: x: 2, y: 2, z: 4, core: 2. Of those that a mesh axis runs over, the one named last changes fastest.
Arguments:
- features: bfloat16 [512, 128], P(('row', 'space')), may hold values from -6 to 6
- positions: float32 [3, 512], P(None, ('row', 'space')), may hold values from -0.5 to 38, as said below
- species: int32 [512], P(('row', 'space')), may hold values from 0 to 3
- ghost_list: int32 [8, 16, 32], P('row', 'space'), may hold values from 0 to 15
- edge_recv: int32 [16384], P(('row', 'space')), may hold values from 0 to 16, as said below
- edge_send: int32 [16384], P(('row', 'space')), may hold values from 0 to 143
- edge_vec: float32 [3, 16384], P(None, ('row', 'space')), may hold values from -5.8 to 5.8, as said below
- w_msg: bfloat16 [128, 256], replicated, may hold values from -0.5 to 0.5
- w_rad1: float32 [8, 128], replicated, may hold values from -2 to 2
- w_rad2: bfloat16 [128, 256], replicated, may hold values from -0.5 to 0.5
- w_up: bfloat16 [256, 128], replicated, may hold values from -0.375 to 0.375
- w_out: float32 [128], replicated, may hold values from -0.5 to 0.5
- hardness: float32 [4], replicated, may hold values from 2 to 4
- width: float32 [4], replicated, may hold values from 0.8 to 1.6
- chi_shift: float32 [4], replicated, may hold values from -1 to 1
- field: float32 [1], replicated, may hold values from 0.01 to 0.03
Outputs:
- new_features: bfloat16 [512, 128], P(('row', 'space'))
- charges: float32 [512], P(('row', 'space'))
- forces: float32 [3, 512], P(None, ('row', 'space'))
- virial: float32 [6, 512], P(None, ('row', 'space'))
Inputs may be any that keep to these rules, and one draw needn't show every extreme that they name: `edge_recv`: in every domain the edges are ordered by receiver; the slots in use fill the first whole blocks of 128 rows, a quarter of the blocks or more, and the other slots hold 16; some domain uses all its slots. `positions`: every two atoms are 1.5 or more apart. `edge_vec`: each edge's length lies between 1.2 and 5.8.
All inputs are finite; a program needn't handle non-finite values.
Results may differ from a plain program's by a relative error of at most 0.0045.
Values may be sent and summed in bfloat16 or wider, within the bound.
No kernel may reach another device: no remote copies, remote signals or barrier semaphores. Data moves between devices by JAX's collectives and lax.ppermute only.
A program may use at most 64 MiB of HBM per device.

v0:
```python
import math

import jax
import jax.numpy as jnp
from jax import lax
from jax.sharding import PartitionSpec as P

ITERS = 2


cutoff = 6.0
message_scale = 0.125
two_over_root_pi = 2.0 / math.sqrt(math.pi)
inverse_root_pi = 1.0 / math.sqrt(math.pi)
pair_limit = 262144


def lookup(species, table):
    result = jnp.zeros(species.shape, jnp.float32)
    for kind in range(table.shape[0]):
        result = result + jnp.where(species == kind, table[kind], 0.0)
    return result


def pair_block(target, target_labels, source, source_labels, source_charge, forces):
    delta = target[:3, :, None] - source[:3, None, :]
    squared = jnp.sum(delta * delta, axis=0)
    same = target_labels[:, None] == source_labels[None, :]
    squared = jnp.where(same, 1.0, squared)
    inverse = lax.rsqrt(squared)
    radius = squared * inverse
    spread = target[3][:, None] * target[3][:, None] + source[3][None, :] * source[3][None, :]
    scale = lax.rsqrt(2.0 * spread)
    scaled = radius * scale
    smear = lax.erf(scaled)
    if forces:
        slope = (
            two_over_root_pi * scale * jnp.exp(-scaled * scaled) * inverse
            - smear * inverse * inverse
        )
        weight = jnp.where(same, 0.0, source_charge[None, :] * slope * inverse)
        first = jnp.sum(weight[None] * delta, axis=2)
        pairs = ((0, 0), (1, 1), (2, 2), (0, 1), (0, 2), (1, 2))
        second = jnp.stack(
            [jnp.sum(weight * delta[left] * delta[right], axis=1) for left, right in pairs]
        )
        return jnp.concatenate([first, second], axis=0)
    kernel = jnp.where(same, 0.0, smear * inverse)
    return jnp.sum(kernel * source_charge[None, :], axis=1)


def pair_sums(target, target_labels, source, source_labels, source_charge, forces):
    count = target.shape[1]
    extent = source.shape[1]
    block = extent
    while block * count > pair_limit and block % 2 == 0:
        block = block // 2
    turns = extent // block
    source_blocks = source.reshape(4, turns, block).transpose(1, 0, 2)
    label_blocks = source_labels.reshape(turns, block)
    charge_blocks = source_charge.reshape(turns, block)
    start_value = jnp.zeros((9, count) if forces else (count,), jnp.float32)

    def accumulate(carry, item):
        return (carry + pair_block(target, target_labels, item[0], item[1], item[2], forces), None)

    total, _ = lax.scan(accumulate, start_value, (source_blocks, label_blocks, charge_blocks))
    return total


def edge_terms(receive, sender_rows, vectors, projected, w_rad1, w_rad2, atoms):
    length = jnp.sqrt(jnp.sum(vectors * vectors, axis=0))
    unit = vectors / length
    order = jnp.arange(1, w_rad1.shape[0] + 1, dtype=jnp.int32).astype(jnp.float32)[:, None]
    ratio = length / cutoff
    envelope = (1.0 - ratio * ratio) * (1.0 - ratio * ratio)
    basis = jnp.sin(order * math.pi * ratio) / ratio * envelope
    mixed = lax.dot_general(
        basis, w_rad1, (((0,), (0,)), ((), ())), precision=lax.Precision.HIGHEST
    )
    radial = jax.nn.silu(mixed).astype(jnp.bfloat16)
    filters = jnp.dot(radial, w_rad2, preferred_element_type=jnp.float32)
    picked = jnp.take(projected, sender_rows, axis=0).astype(jnp.float32) * filters
    chans = w_rad1.shape[1]
    scalar = picked[:, :chans]
    carried = picked[:, chans:]
    joined = [
        scalar,
        unit[0][:, None] * carried,
        unit[1][:, None] * carried,
        unit[2][:, None] * carried,
    ]
    message = jnp.concatenate(joined, axis=1).astype(jnp.bfloat16)
    onehot = (jnp.arange(atoms, dtype=jnp.int32)[:, None] == receive[None, :]).astype(jnp.bfloat16)
    return jnp.dot(onehot, message, preferred_element_type=jnp.float32)


def shards(
    features,
    positions,
    species,
    ghost_list,
    edge_recv,
    edge_send,
    edge_vec,
    w_msg,
    w_rad1,
    w_rad2,
    w_up,
    w_out,
    hardness,
    width,
    chi_shift,
    field,
):
    atoms = features.shape[0]
    chans = features.shape[1]
    lanes = lax.axis_size("space")
    row_at = lax.axis_index("row")
    space_at = lax.axis_index("space")
    lists = ghost_list[0]
    outgoing = jnp.take(features, lists.reshape(-1), axis=0).reshape(lanes, lists.shape[1], chans)
    ghost_rows = jnp.einsum(
        "dkc,cf->dkf",
        lax.all_to_all(outgoing, "space", split_axis=0, concat_axis=0, tiled=True),
        w_msg,
        preferred_element_type=jnp.float32,
    ).astype(jnp.bfloat16)
    own_rows = jnp.dot(features, w_msg, preferred_element_type=jnp.float32).astype(jnp.bfloat16)
    projected = jnp.concatenate([own_rows, ghost_rows.reshape(-1, 2 * chans)], axis=0)
    summed = edge_terms(edge_recv, edge_send, edge_vec, projected, w_rad1, w_rad2, atoms)
    summed = summed * message_scale
    vector_part = summed[:, chans:].reshape(atoms, 3, chans)
    invariant = jnp.concatenate(
        [summed[:, :chans], jnp.sum(vector_part * vector_part, axis=1)], axis=1
    ).astype(jnp.bfloat16)
    hidden = jax.nn.silu(jnp.dot(invariant, w_up, preferred_element_type=jnp.float32))
    new_features = (features.astype(jnp.float32) + hidden).astype(jnp.bfloat16)
    chi = jnp.dot(hidden, w_out, precision=lax.Precision.HIGHEST) + lookup(species, chi_shift)
    sigma = lookup(species, width)
    diag = lookup(species, hardness) + inverse_root_pi / sigma
    placed = jnp.concatenate([positions, sigma[None, :]], axis=0)
    own_labels = (row_at * lanes + space_at) * atoms + jnp.arange(atoms, dtype=jnp.int32)
    everyone = lax.all_gather(placed, ("row", "space"), axis=1, tiled=True)
    all_labels = jnp.arange(everyone.shape[1], dtype=jnp.int32)

    def spread_out(vector):
        return lax.all_gather(vector, ("row", "space"), axis=0, tiled=True)

    rhs = field[0] * positions[2] - chi
    charges = jnp.zeros_like(rhs)
    residual = rhs

    def squares(current):
        return lax.psum(jnp.sum(current * current), ("row", "space"))

    direction = residual
    norm_now = squares(residual)
    for step in range(ITERS):
        image = diag * direction + pair_sums(
            placed, own_labels, everyone, all_labels, spread_out(direction), False
        )
        alpha = norm_now / lax.psum(jnp.sum(direction * image), ("row", "space"))
        charges = charges + alpha * direction
        residual = residual - alpha * image
        fresh = squares(residual)
        direction = residual + fresh / norm_now * direction
        norm_now = fresh
    sums = pair_sums(placed, own_labels, everyone, all_labels, spread_out(charges), True)
    pull = -charges[None, :] * sums[:3]
    forces = jnp.concatenate([pull[:2], pull[2:] + (charges * field[0])[None, :]], axis=0)
    virial = 0.5 * charges[None, :] * sums[3:]
    return (new_features, charges, forces, virial)


def solution(mesh):
    return jax.shard_map(
        shards,
        mesh=mesh,
        in_specs=(
            P(("row", "space"), None),
            P(None, ("row", "space")),
            P(("row", "space")),
            P("row", "space", None),
            P(("row", "space")),
            P(("row", "space")),
            P(None, ("row", "space")),
            P(),
            P(),
            P(),
            P(),
            P(),
            P(),
            P(),
            P(),
            P(),
        ),
        out_specs=(
            P(("row", "space"), None),
            P(("row", "space")),
            P(None, ("row", "space")),
            P(None, ("row", "space")),
        ),
        check_vma=False,
    )
```

profile of v0, /device:TPU:0, one launch (start us, length us, event | category | flops | bytes accessed | tf_op | source)
XLA Modules:
  0.0 320.6 jit_solution(11400748328552827323)
XLA Ops:
  0.7 0.8 reshape_squeeze.6
  1.5 0.7 copy-done.1
  2.2 0.7 gather_fusion
  2.9 0.7 broadcast_select_fusion
  3.6 4.4 %all-to-all-start = ((bf16[4,32,128]{2,1,0:T(8,128)(2,1)}), bf16[4,32,128]{2,1,0:T(8,128)(2,1)S(1)}, u32[]{:S(2)}, u32[]{:S(2)}) async-start(bf16[4,32,128]{2,1,0:T(8,128)(2,1)} %broadcast_select_fusion), calls=%async_computation | async-start | bytes 65536 | tf_op jit(solution)/shard_map/all_to_all | solution.py:125
  8.0 0.6 copy-done.4
  8.7 0.1 convolution_convert_fusion.1
  8.9 0.6 copy-done.8
  9.5 0.6 fusion.45
  10.1 0.6 fusion.44
  10.8 0.7 copy-done.12
  11.4 2.5 fusion.40
  13.9 0.7 copy-done.5
  14.6 42.9 %all-gather = f32[32,16,4]{1,2,0:T(4,128)S(1)} all-gather(f32[1,16,4]{1,2,0:T(4,128)S(1)} %maximum_bitcast_fusion), channel_id=1, replica_groups=mesh['row'=8,'space'=4] {'row','space'}, dimensions={0}, use_global_device_ids=true | all-gather | bytes 8448 | tf_op jit(solution)/shard_map/all_gather | solution.py:144
  57.5 0.1 reshape.216
  57.7 0.6 copy-done.10
  58.4 0.7 fusion.43
  59.0 0.7 copy-done.14
  59.7 0.7 multiply_convert_fusion.3
  61.1 0.1 convolution_convert_fusion
  61.3 2.0 gather_fusion.1
  63.3 0.1 copy.25
  63.4 0.3 convolution_multiply_fusion
  63.8 0.7 copy-done.15
  64.5 0.2 convolution_multiply_fusion.1
  64.8 0.8 copy-done.3
  65.6 0.7 add_convert_fusion
  66.3 0.7 copy-done.16
  67.0 2.7 fusion.1
  69.7 0.2 dynamic-update-slice
  69.9 36.9 %all-reduce = f32[512]{0:T(512)S(1)} all-reduce(f32[512]{0:T(512)S(1)} %dynamic-update-slice), channel_id=1, replica_groups=mesh['row'=8,'space'=4] {'row','space'}, use_global_device_ids=true, to_apply=%add | all-reduce | flops 512 | bytes 4096
  106.7 0.2 multiply_reduce_fusion.8
  106.9 3.1 multiply_reduce_fusion.12
  110.0 41.4 %all-reduce.3 = (f32[]{:T(128)}, f32[]{:T(128)}) all-reduce(f32[]{:T(128)} %get-tuple-element.67, f32[]{:T(128)} %get-tuple-element.66), channel_id=1, replica_groups=mesh['row'=8,'space'=4] {'row','space'}, use_global_device_ids=true, to_apply=%region_3.4 | all-reduce | flops 2 | bytes 16 | tf_op jit(solution)/shard_map/psum | solution.py:155
  152.8 0.6 multiply_reduce_fusion.11
  153.4 40.0 %psum.30 = f32[]{:T(128)} all-reduce(f32[]{:T(128)} %get-tuple-element.83), channel_id=1, replica_groups=mesh['row'=8,'space'=4] {'row','space'}, use_global_device_ids=true, to_apply=%region_9.10 | all-reduce | flops 1 | bytes 8 | tf_op jit(solution)/shard_map/psum | solution.py:155
  194.7 0.1 fusion.39
  194.8 40.6 %all-reduce.1 = f32[512]{0:T(512)S(1)} all-reduce(f32[512]{0:T(512)S(1)} %get-tuple-element.81), channel_id=1, replica_groups=mesh['row'=8,'space'=4] {'row','space'}, use_global_device_ids=true, to_apply=%add.1 | all-reduce | flops 512 | bytes 4096
  235.4 0.2 multiply_reduce_fusion.7
  235.6 0.6 multiply_reduce_fusion.10
  236.2 39.7 %psum.31 = f32[]{:T(128)} all-reduce(f32[]{:T(128)} %multiply_reduce_fusion.10), channel_id=1, replica_groups=mesh['row'=8,'space'=4] {'row','space'}, use_global_device_ids=true, to_apply=%region_12.13 | all-reduce | flops 1 | bytes 8 | tf_op jit(solution)/shard_map/psum | solution.py:163
  277.3 0.2 dynamic-update-slice.2
  277.6 40.7 %all-reduce.2 = f32[512]{0:T(512)S(1)} all-reduce(f32[512]{0:T(512)S(1)} %dynamic-update-slice.2), channel_id=1, replica_groups=mesh['row'=8,'space'=4] {'row','space'}, use_global_device_ids=true, to_apply=%add.2 | all-reduce | flops 512 | bytes 4096
  318.2 0.3 multiply_reduce_fusion.2
  318.5 0.2 multiply_reduce_fusion
  318.7 0.6 copy-done.11
  319.3 0.6 broadcast_multiply_fusion
  320.0 0.6 pad_maximum_fusion.1
  (57 shorter events, 0.5 us)
Async XLA Ops:
  0.6 62.8 %copy-start = (bf16[128,256]{1,0:T(8,128)(2,1)S(1)}, bf16[128,256]{1,0:T(8,128)(2,1)}, u32[]{:S(2)}) copy-start(bf16[128,256]{1,0:T(8,128)(2,1)} %param.25) | copy-start | bytes 196612
  0.6 0.8 copy-start.6
  1.5 0.7 copy-start.1
  2.9 5.8 %copy-start.2 = (bf16[128,256]{1,0:T(8,128)(2,1)S(1)}, bf16[128,256]{1,0:T(8,128)(2,1)}, u32[]{:S(2)}) copy-start(bf16[128,256]{1,0:T(8,128)(2,1)} %param.23) | copy-start | bytes 196612
  3.6 4.4 %copy-start.7 = (s32[512]{0:T(512)S(1)}, s32[512]{0:T(512)}, u32[]{:S(2)}) copy-start(s32[512]{0:T(512)} %param.21) | copy-start | bytes 6148
  3.6 57.5 %all-to-all-start = ((bf16[4,32,128]{2,1,0:T(8,128)(2,1)}), bf16[4,32,128]{2,1,0:T(8,128)(2,1)S(1)}, u32[]{:S(2)}, u32[]{:S(2)}) async-start(bf16[4,32,128]{2,1,0:T(8,128)(2,1)} %broadcast_select_fusion), calls=%async_computation | async-start | bytes 65536 | tf_op jit(solution)/shard_map/all_to_all | solution.py:125
  8.0 0.7 copy-start.4
  8.8 0.7 copy-start.8
  8.9 1.3 copy-start.9
  10.8 0.7 copy-start.12
  13.9 0.7 copy-start.5
  57.7 0.7 copy-start.10
  59.0 0.7 copy-start.14
  63.8 0.7 copy-start.15
  64.7 0.9 copy-start.3
  66.3 0.7 copy-start.16
  277.3 41.4 %copy-start.13 = (f32[16]{0:T(128)}, f32[16]{0:T(128)S(1)}, u32[]{:S(2)}) copy-start(f32[16]{0:T(128)S(1)} %get-tuple-element.71) | copy-start | bytes 196
  318.7 0.6 copy-start.11
  319.3 0.7 slice-start
where the time goes:
time: 322 us; the launch traced here: 321 us
  blocking collectives  282 us (88%)
  local copies, waits for them, and re-layouts  13.6 us (4%)
  other arithmetic  9.94 us (3%)
  between operations  5.64 us (2%)
  matrix products  4.94 us (2%)
  starting transfers between devices  4.37 us (1%)
    unnamed x3, blocking collectives  118 us
    psum x2, blocking collectives, squares(): return lax.psum(jnp.sum(current * current), ('row', 'space'))  81.4 us
    all_gather x1, blocking collectives, shards(): everyone = lax.all_gather(placed, ('row', 'space'), axis=1, tiled=True)  42.9 us
    psum x1, blocking collectives, shards(): alpha = norm_now / lax.psum(jnp.sum(direction * image), ('row', 'space'))  39.7 us
    unnamed x40, local copies, waits for them, and re-layouts  7.86 us
  transfers between devices with their start and end apart: 1, of which 0 were waited for; matrix products, arithmetic and copies ran while one was open for 2% of the time, Pallas kernels for 0%

commit v1 on v0

v1 whole, which is shorter than its diff:
```python
import math

import jax
import jax.numpy as jnp
from jax import lax
from jax.sharding import PartitionSpec as P

ITERS = 2


cutoff = 6.0
message_scale = 0.125
two_over_root_pi = 2.0 / math.sqrt(math.pi)
inverse_root_pi = 1.0 / math.sqrt(math.pi)
replicate_limit = 1024
everywhere = ("row", "space")


def lookup(species, table):
    result = jnp.zeros(species.shape, jnp.float32)
    for kind in range(table.shape[0]):
        result = result + jnp.where(species == kind, table[kind], 0.0)
    return result


def pair_terms(target, target_labels, source, source_labels):
    delta = target[:3, :, None] - source[:3, None, :]
    squared = jnp.sum(delta * delta, axis=0)
    same = target_labels[:, None] == source_labels[None, :]
    squared = jnp.where(same, 1.0, squared)
    inverse = lax.rsqrt(squared)
    radius = squared * inverse
    spread = target[3][:, None] * target[3][:, None] + source[3][None, :] * source[3][None, :]
    scale = lax.rsqrt(2.0 * spread)
    scaled = radius * scale
    smear = lax.erf(scaled)
    return delta, same, inverse, scale, scaled, smear


def coulomb(target, target_labels, source, source_labels):
    _, same, inverse, _, _, smear = pair_terms(target, target_labels, source, source_labels)
    return jnp.where(same, 0.0, smear * inverse)


def pair_forces(target, target_labels, source, source_labels, source_charge):
    delta, same, inverse, scale, scaled, smear = pair_terms(
        target, target_labels, source, source_labels
    )
    slope = (
        two_over_root_pi * scale * jnp.exp(-scaled * scaled) * inverse - smear * inverse * inverse
    )
    weight = jnp.where(same, 0.0, source_charge[None, :] * slope * inverse)
    first = jnp.sum(weight[None] * delta, axis=2)
    pairs = ((0, 0), (1, 1), (2, 2), (0, 1), (0, 2), (1, 2))
    second = jnp.stack(
        [jnp.sum(weight * delta[left] * delta[right], axis=1) for left, right in pairs]
    )
    return jnp.concatenate([first, second], axis=0)


def edge_terms(receive, sender_rows, vectors, projected, w_rad1, w_rad2, atoms):
    length = jnp.sqrt(jnp.sum(vectors * vectors, axis=0))
    unit = vectors / length
    order = jnp.arange(1, w_rad1.shape[0] + 1, dtype=jnp.int32).astype(jnp.float32)[:, None]
    ratio = length / cutoff
    envelope = (1.0 - ratio * ratio) * (1.0 - ratio * ratio)
    basis = jnp.sin(order * math.pi * ratio) / ratio * envelope
    mixed = lax.dot_general(
        basis, w_rad1, (((0,), (0,)), ((), ())), precision=lax.Precision.HIGHEST
    )
    radial = jax.nn.silu(mixed).astype(jnp.bfloat16)
    filters = jnp.dot(radial, w_rad2, preferred_element_type=jnp.float32)
    picked = jnp.take(projected, sender_rows, axis=0).astype(jnp.float32) * filters
    chans = w_rad1.shape[1]
    scalar = picked[:, :chans]
    carried = picked[:, chans:]
    joined = [
        scalar,
        unit[0][:, None] * carried,
        unit[1][:, None] * carried,
        unit[2][:, None] * carried,
    ]
    message = jnp.concatenate(joined, axis=1).astype(jnp.bfloat16)
    onehot = (jnp.arange(atoms, dtype=jnp.int32)[:, None] == receive[None, :]).astype(jnp.bfloat16)
    return jnp.dot(onehot, message, preferred_element_type=jnp.float32)


def gathered(block, devices):
    copies = jnp.broadcast_to(block[None], (devices,) + block.shape)
    return lax.all_to_all(copies, everywhere, split_axis=0, concat_axis=0, tiled=True)


def shards(
    features,
    positions,
    species,
    ghost_list,
    edge_recv,
    edge_send,
    edge_vec,
    w_msg,
    w_rad1,
    w_rad2,
    w_up,
    w_out,
    hardness,
    width,
    chi_shift,
    field,
):
    atoms = features.shape[0]
    chans = features.shape[1]
    lanes = lax.axis_size("space")
    devices = lanes * lax.axis_size("row")
    everybody = devices * atoms
    me = lax.axis_index("row") * lanes + lax.axis_index("space")
    sigma = lookup(species, width)
    diag = lookup(species, hardness) + inverse_root_pi / sigma
    placed = jnp.concatenate([positions, sigma[None, :], diag[None, :]], axis=0)
    everyone = gathered(placed, devices).transpose(1, 0, 2).reshape(5, everybody)
    lists = ghost_list[0]
    outgoing = jnp.take(features, lists.reshape(-1), axis=0).reshape(lanes, lists.shape[1], chans)
    ghost_rows = jnp.einsum(
        "dkc,cf->dkf",
        lax.all_to_all(outgoing, "space", split_axis=0, concat_axis=0, tiled=True),
        w_msg,
        preferred_element_type=jnp.float32,
    ).astype(jnp.bfloat16)
    own_rows = jnp.dot(features, w_msg, preferred_element_type=jnp.float32).astype(jnp.bfloat16)
    projected = jnp.concatenate([own_rows, ghost_rows.reshape(-1, 2 * chans)], axis=0)
    summed = edge_terms(edge_recv, edge_send, edge_vec, projected, w_rad1, w_rad2, atoms)
    summed = summed * message_scale
    vector_part = summed[:, chans:].reshape(atoms, 3, chans)
    invariant = jnp.concatenate(
        [summed[:, :chans], jnp.sum(vector_part * vector_part, axis=1)], axis=1
    ).astype(jnp.bfloat16)
    hidden = jax.nn.silu(jnp.dot(invariant, w_up, preferred_element_type=jnp.float32))
    new_features = (features.astype(jnp.float32) + hidden).astype(jnp.bfloat16)
    chi = jnp.dot(hidden, w_out, precision=lax.Precision.HIGHEST) + lookup(species, chi_shift)
    own_labels = me * atoms + jnp.arange(atoms, dtype=jnp.int32)
    all_labels = jnp.arange(everybody, dtype=jnp.int32)
    rhs = field[0] * positions[2] - chi

    if everybody <= replicate_limit:
        kernel = coulomb(everyone, all_labels, everyone, all_labels)
        residual = gathered(rhs, devices).reshape(everybody)
        all_charges = conjugate(
            residual, lambda v: everyone[4] * v + jnp.sum(kernel * v[None, :], axis=1), jnp.sum
        )
        charges = lax.dynamic_slice(all_charges, (me * atoms,), (atoms,))
    else:
        kernel = coulomb(placed, own_labels, everyone, all_labels)

        def spread(vector):
            return gathered(vector, devices).reshape(everybody)

        charges = conjugate(
            rhs,
            lambda v: diag * v + jnp.sum(kernel * spread(v)[None, :], axis=1),
            lambda v: lax.psum(jnp.sum(v), everywhere),
        )
        all_charges = spread(charges)
    sums = pair_forces(placed, own_labels, everyone, all_labels, all_charges)
    pull = -charges[None, :] * sums[:3]
    forces = jnp.concatenate([pull[:2], pull[2:] + (charges * field[0])[None, :]], axis=0)
    virial = 0.5 * charges[None, :] * sums[3:]
    return (new_features, charges, forces, virial)


def conjugate(rhs, apply, total):
    charges = jnp.zeros_like(rhs)
    residual = rhs
    direction = rhs
    norm_now = total(residual * residual)
    for step in range(ITERS):
        image = apply(direction)
        alpha = norm_now / total(direction * image)
        charges = charges + alpha * direction
        if step + 1 < ITERS:
            residual = residual - alpha * image
            fresh = total(residual * residual)
            direction = residual + fresh / norm_now * direction
            norm_now = fresh
    return charges


def solution(mesh):
    return jax.shard_map(
        shards,
        mesh=mesh,
        in_specs=(
            P(("row", "space"), None),
            P(None, ("row", "space")),
            P(("row", "space")),
            P("row", "space", None),
            P(("row", "space")),
            P(("row", "space")),
            P(None, ("row", "space")),
            P(),
            P(),
            P(),
            P(),
            P(),
            P(),
            P(),
            P(),
            P(),
        ),
        out_specs=(
            P(("row", "space"), None),
            P(("row", "space")),
            P(None, ("row", "space")),
            P(None, ("row", "space")),
        ),
        check_vma=False,
    )
```

time: 322 us -> 67.1 us (0.21)
  blocking collectives: 282 us -> 0 us
  starting transfers between devices: 4.37 us -> 15.5 us
  waiting for transfers between devices: 0.01 us -> 10.3 us
  other arithmetic: 9.94 us -> 16.9 us
    psum x3 -> x0, blocking collectives: 121 us -> none  [the longest x2 81.4 us: squares(): return lax.psum(jnp.sum(current * current), ('row', 'space'))]
    unnamed x3 -> x0, blocking collectives: 118 us -> none
    all_gather x1 -> x0, blocking collectives: 42.9 us -> none  [shards(): everyone = lax.all_gather(placed, ('row', 'space'), axis=1, tiled=True)]
    all_to_all x0 -> x2, starting transfers between devices: none -> 12.2 us  [gathered(): lax.all_to_all(copies, everywhere, split_axis=0, concat_axis=0, tiled=True)]
    unnamed x40 -> x18, local copies, waits for them, and re-layouts: 7.86 us -> 0.54 us
    all_to_all x0 -> x2, waiting for transfers between devices: none -> 6.62 us  [gathered(): lax.all_to_all(copies, everywhere, split_axis=0, concat_axis=0, tiled=True)]
    all_to_all x1, waiting for transfers between devices: 0.01 us -> 3.67 us  [shards(): lax.all_to_all(outgoing, 'space', split_axis=0, concat_axis=0, tiled=True)]
  transfers between devices with their start and end apart: 1 -> 3, of which waited for: 0 -> 2; matrix products, arithmetic and copies ran while one was open for 2% -> 16% of each run, Pallas kernels for 0% -> 0%
where the time goes in v1:
time: 67.1 us; the launch traced here: 66.2 us
  other arithmetic  16.9 us (25%)
  starting transfers between devices  15.5 us (23%)
  local copies, waits for them, and re-layouts  11.4 us (17%)
  waiting for transfers between devices  10.3 us (15%)
  matrix products  6.53 us (10%)
  between operations  5.63 us (8%)
    all_to_all x2, starting transfers between devices, gathered(): lax.all_to_all(copies, everywhere, split_axis=0, concat_axis=0, tiled=True)  12.2 us
    all_to_all x2, waiting for transfers between devices, gathered(): lax.all_to_all(copies, everywhere, split_axis=0, concat_axis=0, tiled=True)  6.62 us
    slice x3, local copies, waits for them, and re-layouts, lookup(): result = result + jnp.where(species == kind, table[kind], 0.0)  4.26 us
    all_to_all x1, waiting for transfers between devices, shards(): lax.all_to_all(outgoing, 'space', split_axis=0, concat_axis=0, tiled=True)  3.67 us
    all_to_all x1, starting transfers between devices, shards(): lax.all_to_all(outgoing, 'space', split_axis=0, concat_axis=0, tiled=True)  3.27 us
    mul x1, other arithmetic, pair_terms(): target[3][:, None] * target[3][:, None]  3.25 us
    broadcast_in_dim x1, other arithmetic, shards(): placed = jnp.concatenate([positions, sigma[None, :], diag[None, :]], axis=0)  3.17 us
    dot_general x1, matrix products, shards(): jnp.dot(hidden, w_out, precision=lax.Precision.HIGHEST)  2.7 us
  transfers between devices with their start and end apart: 3, of which 2 were waited for; matrix products, arithmetic and copies ran while one was open for 16% of the time, Pallas kernels for 0%

profile of v1, /device:TPU:0, one launch (start us, length us, event | category | flops | bytes accessed | tf_op | source)
XLA Modules:
  0.0 66.2 jit_solution(4699821257842051537)
XLA Ops:
  0.6 1.4 %fusion.50 = (f32[1]{0:T(128)}, f32[1]{0:T(128)}, f32[1]{0:T(128)}, f32[1]{0:T(128)}) fusion(f32[4]{0:T(128)} %param.29), kind=kLoop, calls=%fused_computation.124 | loop fusion | bytes 32 | tf_op jit(solution)/shard_map/slice | solution.py:22
  2.0 1.5 %fusion.49 = (f32[1]{0:T(128)}, f32[1]{0:T(128)}, f32[1]{0:T(128)}, f32[1]{0:T(128)}) fusion(f32[4]{0:T(128)} %param.28), kind=kLoop, calls=%fused_computation.123 | loop fusion | bytes 32 | tf_op jit(solution)/shard_map/slice | solution.py:22
  3.5 3.2 %fusion.44 = (f32[16]{0:T(128)S(1)}, f32[16]{0:T(128)S(1)}) fusion(f32[]{:T(128)} %bitcast.20, s32[16]{0:T(128)} %param.18, f32[]{:T(128)} %bitcast.19, f32[]{:T(128)} %bitcast.18, f32[]{:T(128)} %bitcast.17), kind=kLoop, calls=%fused_computation.119 | loop fusion | flops 192 | bytes 208 | tf_op jit(solution)/shard_map/mul | solution.py:33
  6.7 3.2 %fusion.40 = f32[1,16]{1,0:T(1,128)S(1)} fusion(f32[16]{0:T(128)S(1)} %get-tuple-element.16, f32[]{:T(128)} %bitcast.25, f32[]{:T(128)} %bitcast.24, f32[]{:T(128)} %bitcast.23, f32[]{:T(128)} %bitcast.22, s32[16]{0:T(128)} %param.18), kind=kLoop, calls=%fused_computation.111 | loop fusion | flops 208 | bytes 208 | tf_op jit(solution)/shard_map/broadcast_in_dim | solution.py:119
  9.9 0.7 %pad_maximum_fusion.1 = f32[5,16]{1,0:T(8,128)S(1)} fusion(f32[1,16]{1,0:T(1,128)S(1)} %fusion.40, f32[1,16]{1,0:T(1,128)S(1)} %bitcast.121, f32[3,16]{1,0:T(4,128)} %param.17), kind=kLoop, calls=%fused_computation.92 | loop fusion | flops 160 | bytes 640 | tf_op jit(solution)/shard_map/concatenate | solution.py:119
  10.6 0.6 broadcast_in_dim.150
  11.3 7.3 %all-to-all-start.2 = ((f32[32,5,16]{2,1,0:T(8,128)}), f32[32,5,16]{2,1,0:T(8,128)S(1)}, u32[]{:S(2)}, u32[]{:S(2)}) async-start(f32[32,5,16]{2,1,0:T(8,128)} %broadcast_in_dim.150), calls=%async_computation.2 | async-start | bytes 262144 | tf_op jit(solution)/shard_map/all_to_all | solution.py:90
  18.6 0.8 %reshape_squeeze.6 = s32[128,1]{0,1:T(1,128)S(1)} reshape(s32[1,4,32]{2,1,0:T(4,128)} %param.19) | data formatting | bytes 1024 | tf_op jit(solution)/shard_map/reshape;squeeze | solution.py:122
  19.3 0.7 %compare_and_fusion = pred[4,32]{1,0:T(4,128)(4,1)S(1)} fusion(s32[1,4,32]{2,1,0:T(4,128)} %param.19), kind=kLoop, calls=%fused_computation.100 | loop fusion | flops 768 | bytes 640 | tf_op jit(solution)/shard_map/jit(_take)/and | solution.py:122
  20.0 0.7 %compare_select_fusion.1 = s32[512]{0:T(512)S(1)} fusion(s32[512]{0:T(512)} %param.21), kind=kLoop, calls=%fused_computation.89 | loop fusion | flops 1536 | bytes 4096 | tf_op jit(solution)/shard_map/jit(_take)/jit(_where)/select_n | solution.py:73
  20.7 0.7 %compare_and_fusion.1 = pred[512]{0:T(512)(128)(4,1)S(1)} fusion(s32[512]{0:T(512)} %param.21), kind=kLoop, calls=%fused_computation.101 | loop fusion | flops 3072 | bytes 2560 | tf_op jit(solution)/shard_map/jit(_take)/and | solution.py:73
  21.4 0.7 %multiply_reduce_fusion.13 = f32[512]{0:T(512)S(1)} fusion(f32[3,512]{1,0:T(4,128)} %param.22), kind=kLoop, calls=%fused_computation.86 | loop fusion | flops 2560 | bytes 8192 | tf_op jit(solution)/shard_map/reduce_sum | solution.py:62
  22.2 1.3 %gather_fusion = bf16[128,128]{1,0:T(8,128)(2,1)S(1)} fusion(bf16[16,128]{1,0:T(8,128)(2,1)} %param.16, s32[1024]{0:T(1024)S(1)} %pad_clamp_fusion.1), kind=kCustom, calls=%fused_computation | custom fusion | bytes 66048 | tf_op jit(solution)/shard_map/jit(_take)/gather | solution.py:122
  23.5 1.0 %convolution_convert_fusion.1 = bf16[16,256]{1,0:T(8,128)(2,1)S(1)} fusion(bf16[16,128]{1,0:T(8,128)(2,1)} %param.16, bf16[128,256]{1,0:T(8,128)(2,1)} %param.23), kind=kOutput, calls=%fused_computation.8 | convolution fusion | flops 1052672 | bytes 77824 | tf_op jit(solution)/shard_map/dot_general | solution.py:129
  24.6 0.7 %broadcast_divide_fusion = f32[3,512]{1,0:T(4,128)S(1)} fusion(f32[3,512]{1,0:T(4,128)} %param.22, f32[512]{0:T(512)S(1)} %get-tuple-element.29), kind=kLoop, calls=%fused_computation.93 | loop fusion | flops 1536 | bytes 14336 | tf_op jit(solution)/shard_map/div | solution.py:63
  25.3 1.4 %fusion.51 = (f32[1]{0:T(128)}, f32[1]{0:T(128)}, f32[1]{0:T(128)}, f32[1]{0:T(128)}) fusion(f32[4]{0:T(128)} %param.30), kind=kLoop, calls=%fused_computation.125 | loop fusion | bytes 32 | tf_op jit(solution)/shard_map/slice | solution.py:22
  26.7 0.7 %broadcast_select_fusion = bf16[4,32,128]{2,1,0:T(8,128)(2,1)} fusion(bf16[4,32,128]{2,1,0:T(8,128)(2,1)S(1)} %bitcast.117, pred[4,32]{1,0:T(4,128)(4,1)S(1)} %compare_and_fusion), kind=kLoop, calls=%fused_computation.58 | loop fusion | flops 16384 | bytes 65664 | tf_op jit(solution)/shard_map/jit(_take)/select_n | solution.py:122
  27.4 1.4 %multiply_convert_fusion.3 = bf16[512,128]{1,0:T(8,128)(2,1)S(1)} fusion(f32[8,128]{1,0:T(8,128)} %param.24, f32[512]{0:T(512)S(1)} %get-tuple-element.31, f32[512]{0:T(512)S(1)} %get-tuple-element.30, f32[8]{0:T(128)S(1)} %convert_multiply_fusion), kind=kOutput, calls=%fused_computation.28 | convolution fusion | flops 6631424 | bytes 139296 | tf_op jit(solution)/shard_map/dot_general | solution.py:68
  29.5 3.3 %all-to-all-start = ((bf16[4,32,128]{2,1,0:T(8,128)(2,1)}), bf16[4,32,128]{2,1,0:T(8,128)(2,1)S(1)}, u32[]{:S(2)}, u32[]{:S(2)}) async-start(bf16[4,32,128]{2,1,0:T(8,128)(2,1)} %broadcast_select_fusion), calls=%async_computation | async-start | bytes 65536 | tf_op jit(solution)/shard_map/all_to_all | solution.py:125
  32.8 0.1 sub.62
  32.9 0.1 multiply_reduce_fusion.4
  33.0 3.7 %all-to-all-done = bf16[4,32,128]{2,1,0:T(8,128)(2,1)S(1)} async-done(((bf16[4,32,128]{2,1,0:T(8,128)(2,1)}), bf16[4,32,128]{2,1,0:T(8,128)(2,1)S(1)}, u32[]{:S(2)}, u32[]{:S(2)}) %all-to-all-start) | async-done | bytes 32800 | tf_op jit(solution)/shard_map/all_to_all | solution.py:125
  36.7 0.1 convolution_convert_fusion
  36.8 2.0 %gather_fusion.1 = bf16[512,256]{1,0:T(8,128)(2,1)S(1)} fusion(bf16[144,256]{1,0:T(8,128)(2,1)S(1)} %pad_maximum_fusion, s32[1024]{0:T(1024)S(1)} %pad_clamp_fusion), kind=kCustom, calls=%fused_computation.1 | custom fusion | bytes 526336 | tf_op jit(solution)/shard_map/jit(_take)/gather | solution.py:73
  38.8 0.1 copy.24
  39.0 0.3 convolution_multiply_fusion
  39.4 0.3 copy-done.7
  39.6 0.2 convolution_multiply_fusion.1
  40.0 0.2 copy-done.3
  40.2 0.7 %add_convert_fusion = (bf16[16,128]{1,0:T(8,128)(2,1)}, f32[16,128]{1,0:T(8,128)S(1)}) fusion(bf16[16,128]{1,0:T(8,128)(2,1)S(1)} %copy-done.1, bf16[256,128]{1,0:T(8,128)(2,1)S(1)} %copy-done.3, bf16[16,128]{1,0:T(8,128)(2,1)S(1)} %reduce_sum.158, bf16[16,128]{1,0:T(8,128)(2,1)S(1)} %slice.189), kind=kOutput, calls=%fused_computation.82 | convolution fusion | flops 1079296 | bytes 90112 | tf_op jit(solution)/shard_map/dot_general | solution.py:137
  40.9 2.7 %fusion.1 = f32[16]{0:T(128)S(1)} fusion(f32[16,128]{1,0:T(8,128)S(1)} %get-tuple-element.45, f32[128]{0:T(128)S(1)} %copy-done.8, f32[3,16]{1,0:T(4,128)S(1)} %copy-done.4, f32[]{:T(128)} %bitcast.15, f32[]{:T(128)} %bitcast.14, f32[]{:T(128)} %bitcast.13, f32[]{:T(128)} %bitcast.12, f32[]{:T(128)} %bitcast.106, s32[16]{0:T(128)S(1)} %copy-done.5), kind=kOutput, calls=%fused_computation.11 | convolution fusion | flops 24800 | bytes 8916 | tf_op jit(solution)/shard_map/dot_general | solution.py:139
  43.6 0.6 broadcast_in_dim.139
  44.2 4.9 %all-to-all-start.1 = ((f32[32,1,16]{2,1,0:T(1,128)}), f32[32,1,16]{2,1,0:T(1,128)S(1)}, u32[]{:S(2)}, u32[]{:S(2)}) async-start(f32[32,1,16]{2,1,0:T(1,128)} %broadcast_in_dim.139), calls=%async_computation.1 | async-start | bytes 32768 | tf_op jit(solution)/shard_map/all_to_all | solution.py:90
  49.2 0.4 multiply_reduce_fusion
  49.7 6.6 %all-to-all-done.1 = f32[32,1,16]{2,1,0:T(1,128)S(1)} async-done(((f32[32,1,16]{2,1,0:T(1,128)}), f32[32,1,16]{2,1,0:T(1,128)S(1)}, u32[]{:S(2)}, u32[]{:S(2)}) %all-to-all-start.1) | async-done | bytes 2080 | tf_op jit(solution)/shard_map/all_to_all | solution.py:90
  56.3 0.5 broadcast.234
  56.8 0.7 %reduce.7 = f32[32,16]{1,0:T(8,128)S(1)} reduce(f32[32,1,16]{2,1,0:T(1,128)S(1)} %all-to-all-done.1, f32[]{:T(128)} %broadcast.234), dimensions={1}, to_apply=%all_to_all.13.reduce_sub_computation.3 | reduce | bytes 4100 | tf_op jit(solution)/shard_map/all_to_all | solution.py:90
  57.6 0.6 multiply_reduce_fusion.2
  58.2 0.1 reduce_sum.162
  58.3 0.6 multiply_reduce_fusion.11
  60.3 0.6 multiply_reduce_fusion.10
  62.2 0.2 multiply_reduce_fusion.1
  62.5 0.6 fusion.23
  64.4 0.1 broadcast_multiply_fusion.3
  64.5 0.3 multiply_reduce_fusion.5
  64.8 0.2 multiply_reduce_fusion.3
  65.0 0.6 pad_maximum_fusion.2
  65.6 0.6 broadcast_multiply_fusion
  (45 shorter events, 0.7 us)
Async XLA Ops:
  0.6 38.3 %copy-start = (bf16[128,256]{1,0:T(8,128)(2,1)S(1)}, bf16[128,256]{1,0:T(8,128)(2,1)}, u32[]{:S(2)}) copy-start(bf16[128,256]{1,0:T(8,128)(2,1)} %param.25) | copy-start | bytes 196612
  11.3 18.2 %all-to-all-start.2 = ((f32[32,5,16]{2,1,0:T(8,128)}), f32[32,5,16]{2,1,0:T(8,128)S(1)}, u32[]{:S(2)}, u32[]{:S(2)}) async-start(f32[32,5,16]{2,1,0:T(8,128)} %broadcast_in_dim.150), calls=%async_computation.2 | async-start | bytes 262144 | tf_op jit(solution)/shard_map/all_to_all | solution.py:90
  22.2 10.7 %copy-start.4 = (f32[3,16]{1,0:T(4,128)S(1)}, f32[3,16]{1,0:T(4,128)}, u32[]{:S(2)}) copy-start(f32[3,16]{1,0:T(4,128)} %param.17) | copy-start | bytes 580
  23.5 13.2 %copy-start.2 = (bf16[128,256]{1,0:T(8,128)(2,1)S(1)}, bf16[128,256]{1,0:T(8,128)(2,1)}, u32[]{:S(2)}) copy-start(bf16[128,256]{1,0:T(8,128)(2,1)} %param.23) | copy-start | bytes 196612
  29.5 7.2 %all-to-all-start = ((bf16[4,32,128]{2,1,0:T(8,128)(2,1)}), bf16[4,32,128]{2,1,0:T(8,128)(2,1)S(1)}, u32[]{:S(2)}, u32[]{:S(2)}) async-start(bf16[4,32,128]{2,1,0:T(8,128)(2,1)} %broadcast_select_fusion), calls=%async_computation | async-start | bytes 65536 | tf_op jit(solution)/shard_map/all_to_all | solution.py:125
  38.9 0.7 %copy-start.7 = (s32[512]{0:T(512)S(1)}, s32[512]{0:T(512)}, u32[]{:S(2)}) copy-start(s32[512]{0:T(512)} %param.20) | copy-start | bytes 6148
  39.3 0.7 %copy-start.1 = (bf16[16,128]{1,0:T(8,128)(2,1)S(1)}, bf16[16,128]{1,0:T(8,128)(2,1)}, u32[]{:S(2)}) copy-start(bf16[16,128]{1,0:T(8,128)(2,1)} %param.16) | copy-start | bytes 12292
  39.3 0.8 %copy-start.3 = (bf16[256,128]{1,0:T(8,128)(2,1)S(1)}, bf16[256,128]{1,0:T(8,128)(2,1)}, u32[]{:S(2)}) copy-start(bf16[256,128]{1,0:T(8,128)(2,1)} %param.26) | copy-start | bytes 196612
  39.3 1.6 %copy-start.5 = (s32[16]{0:T(128)S(1)}, s32[16]{0:T(128)}, u32[]{:S(2)}) copy-start(s32[16]{0:T(128)} %param.18) | copy-start | bytes 196
  39.4 1.6 %copy-start.8 = (f32[128]{0:T(128)S(1)}, f32[128]{0:T(128)}, u32[]{:S(2)}) copy-start(f32[128]{0:T(128)} %param.27) | copy-start | bytes 1540
  44.2 12.1 %all-to-all-start.1 = ((f32[32,1,16]{2,1,0:T(1,128)}), f32[32,1,16]{2,1,0:T(1,128)S(1)}, u32[]{:S(2)}, u32[]{:S(2)}) async-start(f32[32,1,16]{2,1,0:T(1,128)} %broadcast_in_dim.139), calls=%async_computation.1 | async-start | bytes 32768 | tf_op jit(solution)/shard_map/all_to_all | solution.py:90
  64.5 1.7 %copy-start.6 = (f32[16]{0:T(128)}, f32[16]{0:T(128)S(1)}, u32[]{:S(2)}) copy-start(f32[16]{0:T(128)S(1)} %get-tuple-element.13) | copy-start | bytes 196

commit v2 on v1

--- a/solution.py
+++ b/solution.py
@@ -85,9 +85,19 @@
     return jnp.dot(onehot, message, preferred_element_type=jnp.float32)
 
 
-def gathered(block, devices):
-    copies = jnp.broadcast_to(block[None], (devices,) + block.shape)
-    return lax.all_to_all(copies, everywhere, split_axis=0, concat_axis=0, tiled=True)
+def exchanged(block, axis, step):
+    size = lax.axis_size(axis)
+    return lax.ppermute(block, axis, [(place, place ^ step) for place in range(size)])
+
+
+def gathered(block, axes):
+    held = block[None]
+    for axis in axes:
+        size = lax.axis_size(axis)
+        if size & (size - 1):
+            raise ValueError("size")
+        held = jnp.concatenate([held] + [exchanged(held, axis, step) for step in range(1, size)])
+    return held
 
 
 def shards(
@@ -113,21 +123,35 @@
     lanes = lax.axis_size("space")
     devices = lanes * lax.axis_size("row")
     everybody = devices * atoms
-    me = lax.axis_index("row") * lanes + lax.axis_index("space")
+    direct = (everywhere,) if devices <= 32 else ("space", "row")
     sigma = lookup(species, width)
     diag = lookup(species, hardness) + inverse_root_pi / sigma
     placed = jnp.concatenate([positions, sigma[None, :], diag[None, :]], axis=0)
-    everyone = gathered(placed, devices).transpose(1, 0, 2).reshape(5, everybody)
+    everyone = gathered(placed, direct).transpose(1, 0, 2).reshape(5, everybody)
     lists = ghost_list[0]
     outgoing = jnp.take(features, lists.reshape(-1), axis=0).reshape(lanes, lists.shape[1], chans)
+    if lanes <= 4:
+        space = lax.axis_index("space")
+        parts = [lax.dynamic_index_in_dim(outgoing, space, 0, False)]
+        for step in range(1, lanes):
+            part = lax.dynamic_index_in_dim(outgoing, space ^ step, 0, False)
+            parts.append(exchanged(part, "space", step))
+        incoming = jnp.stack(parts)
+    else:
+        incoming = lax.all_to_all(outgoing, "space", split_axis=0, concat_axis=0, tiled=True)
     ghost_rows = jnp.einsum(
         "dkc,cf->dkf",
-        lax.all_to_all(outgoing, "space", split_axis=0, concat_axis=0, tiled=True),
+        incoming,
         w_msg,
         preferred_element_type=jnp.float32,
     ).astype(jnp.bfloat16)
     own_rows = jnp.dot(features, w_msg, preferred_element_type=jnp.float32).astype(jnp.bfloat16)
     projected = jnp.concatenate([own_rows, ghost_rows.reshape(-1, 2 * chans)], axis=0)
+    if lanes <= 4:
+        slots = edge_send - atoms
+        width_of = lists.shape[1]
+        moved = (slots // width_of ^ space) * width_of + slots % width_of + atoms
+        edge_send = jnp.where(edge_send < atoms, edge_send, moved)
     summed = edge_terms(edge_recv, edge_send, edge_vec, projected, w_rad1, w_rad2, atoms)
     summed = summed * message_scale
     vector_part = summed[:, chans:].reshape(atoms, 3, chans)
@@ -137,22 +161,22 @@
     hidden = jax.nn.silu(jnp.dot(invariant, w_up, preferred_element_type=jnp.float32))
     new_features = (features.astype(jnp.float32) + hidden).astype(jnp.bfloat16)
     chi = jnp.dot(hidden, w_out, precision=lax.Precision.HIGHEST) + lookup(species, chi_shift)
-    own_labels = me * atoms + jnp.arange(atoms, dtype=jnp.int32)
+    own_labels = jnp.arange(atoms, dtype=jnp.int32)
     all_labels = jnp.arange(everybody, dtype=jnp.int32)
     rhs = field[0] * positions[2] - chi
 
     if everybody <= replicate_limit:
         kernel = coulomb(everyone, all_labels, everyone, all_labels)
-        residual = gathered(rhs, devices).reshape(everybody)
+        residual = gathered(rhs, ("space", "row")).reshape(everybody)
         all_charges = conjugate(
             residual, lambda v: everyone[4] * v + jnp.sum(kernel * v[None, :], axis=1), jnp.sum
         )
-        charges = lax.dynamic_slice(all_charges, (me * atoms,), (atoms,))
+        charges = all_charges[:atoms]
     else:
         kernel = coulomb(placed, own_labels, everyone, all_labels)
 
         def spread(vector):
-            return gathered(vector, devices).reshape(everybody)
+            return gathered(vector, ("space", "row")).reshape(everybody)
 
         charges = conjugate(
             rhs,

time: 67.1 us -> 118 us (1.76)
  starting transfers between devices: 15.5 us -> 67.1 us
  local copies, waits for them, and re-layouts: 11.4 us -> 13.5 us
  other arithmetic: 16.9 us -> 15.5 us
  waiting for transfers between devices: 10.3 us -> 9.08 us
    ppermute x0 -> x44, starting transfers between devices: none -> 67.1 us  [exchanged(): lax.ppermute(block, axis, [(place, place ^ step) for place in range(size)])]
    all_to_all x3 -> x0, starting transfers between devices: 15.5 us -> none  [the longest x2 12.2 us: gathered(): lax.all_to_all(copies, everywhere, split_axis=0, concat_axis=0, tiled=True)]
    all_to_all x3 -> x0, waiting for transfers between devices: 10.3 us -> none  [the longest x2 6.62 us: gathered(): lax.all_to_all(copies, everywhere, split_axis=0, concat_axis=0, tiled=True)]
    ppermute x0 -> x44, waiting for transfers between devices: none -> 9.08 us  [exchanged(): lax.ppermute(block, axis, [(place, place ^ step) for place in range(size)])]
    ppermute x0 -> x31, local copies, waits for them, and re-layouts: none -> 3.29 us  [exchanged(): lax.ppermute(block, axis, [(place, place ^ step) for place in range(size)])]
  transfers between devices with their start and end apart: 3 -> 44, of which waited for: 2 -> 4; matrix products, arithmetic and copies ran while one was open for 16% -> 12% of each run, Pallas kernels for 0% -> 0%
where the time goes in v2:
time: 118 us; the launch traced here: 117 us
  starting transfers between devices  67.1 us (57%)
  other arithmetic  15.5 us (13%)
  local copies, waits for them, and re-layouts  13.5 us (11%)
  waiting for transfers between devices  9.08 us (8%)
  matrix products  6.4 us (5%)
  between operations  5.79 us (5%)
    ppermute x44, starting transfers between devices, exchanged(): lax.ppermute(block, axis, [(place, place ^ step) for place in range(size)])  67.1 us
    ppermute x44, waiting for transfers between devices, exchanged(): lax.ppermute(block, axis, [(place, place ^ step) for place in range(size)])  9.08 us
    slice x3, local copies, waits for them, and re-layouts, lookup(): result = result + jnp.where(species == kind, table[kind], 0.0)  4.26 us
    ppermute x31, local copies, waits for them, and re-layouts, exchanged(): lax.ppermute(block, axis, [(place, place ^ step) for place in range(size)])  3.29 us
    mul x1, other arithmetic, pair_terms(): target[3][:, None] * target[3][:, None]  3.25 us
    broadcast_in_dim x1, other arithmetic, shards(): placed = jnp.concatenate([positions, sigma[None, :], diag[None, :]], axis=0)  3.14 us
    dot_general x1, matrix products, shards(): jnp.dot(hidden, w_out, precision=lax.Precision.HIGHEST)  2.61 us
  transfers between devices with their start and end apart: 44, of which 4 were waited for; matrix products, arithmetic and copies ran while one was open for 12% of the time, Pallas kernels for 0%

profile of v2, /device:TPU:0, one launch (start us, length us, event | category | flops | bytes accessed | tf_op | source)
XLA Modules:
  0.0 117.4 jit_solution(11423218582898575464)
XLA Ops:
  0.6 1.4 %fusion.61 = (f32[1]{0:T(128)}, f32[1]{0:T(128)}, f32[1]{0:T(128)}, f32[1]{0:T(128)}) fusion(f32[4]{0:T(128)} %param.29), kind=kLoop, calls=%fused_computation.145 | loop fusion | bytes 32 | tf_op jit(solution)/shard_map/slice | solution.py:22
  2.0 1.5 %fusion.60 = (f32[1]{0:T(128)}, f32[1]{0:T(128)}, f32[1]{0:T(128)}, f32[1]{0:T(128)}) fusion(f32[4]{0:T(128)} %param.28), kind=kLoop, calls=%fused_computation.144 | loop fusion | bytes 32 | tf_op jit(solution)/shard_map/slice | solution.py:22
  3.5 3.2 %fusion.55 = (f32[16]{0:T(128)S(1)}, f32[16]{0:T(128)S(1)}) fusion(f32[]{:T(128)} %bitcast.26, s32[16]{0:T(128)} %param.18, f32[]{:T(128)} %bitcast.25, f32[]{:T(128)} %bitcast.24, f32[]{:T(128)} %bitcast.23), kind=kLoop, calls=%fused_computation.140 | loop fusion | flops 192 | bytes 208 | tf_op jit(solution)/shard_map/mul | solution.py:33
  6.8 3.1 %fusion.50 = f32[1,16]{1,0:T(1,128)S(1)} fusion(f32[16]{0:T(128)S(1)} %get-tuple-element.14, f32[]{:T(128)} %bitcast.31, f32[]{:T(128)} %bitcast.30, f32[]{:T(128)} %bitcast.29, f32[]{:T(128)} %bitcast.28, s32[16]{0:T(128)} %param.18), kind=kLoop, calls=%fused_computation.131 | loop fusion | flops 208 | bytes 208 | tf_op jit(solution)/shard_map/broadcast_in_dim | solution.py:129
  9.9 0.7 maximum_bitcast_fusion
  11.0 2.6 %collective-permute-start.14 = (f32[1,5,16]{2,1,0:T(8,128)S(1)}, f32[1,5,16]{2,1,0:T(8,128)S(1)}, u32[]{:S(2)}, u32[]{:S(2)}) collective-permute-start(f32[1,5,16]{2,1,0:T(8,128)S(1)} %maximum_bitcast_fusion), channel_id=1, source_target_pairs={{0,2},{1,3},{2,0},{3,1},{4,6},{5,7},{6,4},{7,5},{8,10},{9,11},{10,... | collective-permute-start | bytes 968 | tf_op jit(solution)/shard_map/ppermute | solution.py:90
  13.7 1.7 %collective-permute-start.16 = (f32[1,5,16]{2,1,0:T(8,128)S(1)}, f32[1,5,16]{2,1,0:T(8,128)S(1)}, u32[]{:S(2)}, u32[]{:S(2)}) collective-permute-start(f32[1,5,16]{2,1,0:T(8,128)S(1)} %maximum_bitcast_fusion), channel_id=1, source_target_pairs={{0,4},{1,5},{2,6},{3,7},{4,0},{5,1},{6,2},{7,3},{8,12},{9,13},{10,... | collective-permute-start | bytes 968 | tf_op jit(solution)/shard_map/ppermute | solution.py:90
  15.4 0.8 reshape_squeeze.6
  16.2 0.7 compare_and_fusion
  16.9 0.7 multiply_reduce_fusion.11
  17.6 1.3 %gather_fusion = bf16[128,128]{1,0:T(8,128)(2,1)S(1)} fusion(bf16[16,128]{1,0:T(8,128)(2,1)} %param.16, s32[1024]{0:T(1024)S(1)} %pad_clamp_fusion.1), kind=kCustom, calls=%fused_computation | custom fusion | bytes 66048 | tf_op jit(solution)/shard_map/jit(_take)/gather | solution.py:132
  19.0 1.0 convolution_convert_fusion.1
  19.9 0.7 compare_and_fusion.1
  20.7 0.7 broadcast_divide_fusion
  21.4 1.4 %fusion.62 = (f32[1]{0:T(128)}, f32[1]{0:T(128)}, f32[1]{0:T(128)}, f32[1]{0:T(128)}) fusion(f32[4]{0:T(128)} %param.30), kind=kLoop, calls=%fused_computation.146 | loop fusion | bytes 32 | tf_op jit(solution)/shard_map/slice | solution.py:22
  22.9 1.4 %multiply_convert_fusion.3 = bf16[512,128]{1,0:T(8,128)(2,1)S(1)} fusion(f32[8,128]{1,0:T(8,128)} %param.24, f32[512]{0:T(512)S(1)} %get-tuple-element.35, f32[512]{0:T(512)S(1)} %get-tuple-element.34, f32[8]{0:T(128)S(1)} %convert_multiply_fusion), kind=kOutput, calls=%fused_computation.29 | convolution fusion | flops 6631424 | bytes 139296 | tf_op jit(solution)/shard_map/dot_general | solution.py:68
  25.1 2.7 %collective-permute-start.18 = (f32[1,5,16]{2,1,0:T(8,128)S(1)}, f32[1,5,16]{2,1,0:T(8,128)S(1)}, u32[]{:S(2)}, u32[]{:S(2)}) collective-permute-start(f32[1,5,16]{2,1,0:T(8,128)S(1)} %maximum_bitcast_fusion), channel_id=1, source_target_pairs={{0,6},{1,7},{2,4},{3,5},{4,2},{5,3},{6,0},{7,1},{8,14},{9,15},{10,... | collective-permute-start | bytes 968 | tf_op jit(solution)/shard_map/ppermute | solution.py:90
  28.1 1.8 %collective-permute-start.20 = (f32[1,5,16]{2,1,0:T(8,128)S(1)}, f32[1,5,16]{2,1,0:T(8,128)S(1)}, u32[]{:S(2)}, u32[]{:S(2)}) collective-permute-start(f32[1,5,16]{2,1,0:T(8,128)S(1)} %maximum_bitcast_fusion), channel_id=1, source_target_pairs={{0,8},{1,9},{2,10},{3,11},{4,12},{5,13},{6,14},{7,15},{8,0},{9,1},... | collective-permute-start | bytes 968 | tf_op jit(solution)/shard_map/ppermute | solution.py:90
  30.3 2.7 %collective-permute-start.22 = (f32[1,5,16]{2,1,0:T(8,128)S(1)}, f32[1,5,16]{2,1,0:T(8,128)S(1)}, u32[]{:S(2)}, u32[]{:S(2)}) collective-permute-start(f32[1,5,16]{2,1,0:T(8,128)S(1)} %maximum_bitcast_fusion), channel_id=1, source_target_pairs={{0,10},{1,11},{2,8},{3,9},{4,14},{5,15},{6,12},{7,13},{8,2},{9,3},... | collective-permute-start | bytes 968 | tf_op jit(solution)/shard_map/ppermute | solution.py:90
  33.3 2.7 %collective-permute-start.24 = (f32[1,5,16]{2,1,0:T(8,128)S(1)}, f32[1,5,16]{2,1,0:T(8,128)S(1)}, u32[]{:S(2)}, u32[]{:S(2)}) collective-permute-start(f32[1,5,16]{2,1,0:T(8,128)S(1)} %maximum_bitcast_fusion), channel_id=1, source_target_pairs={{0,12},{1,13},{2,14},{3,15},{4,8},{5,9},{6,10},{7,11},{8,4},{9,5},... | collective-permute-start | bytes 968 | tf_op jit(solution)/shard_map/ppermute | solution.py:90
  36.3 3.6 %collective-permute-start.26 = (f32[1,5,16]{2,1,0:T(8,128)S(1)}, f32[1,5,16]{2,1,0:T(8,128)S(1)}, u32[]{:S(2)}, u32[]{:S(2)}) collective-permute-start(f32[1,5,16]{2,1,0:T(8,128)S(1)} %maximum_bitcast_fusion), channel_id=1, source_target_pairs={{0,14},{1,15},{2,12},{3,13},{4,10},{5,11},{6,8},{7,9},{8,6},{9,7},... | collective-permute-start | bytes 968 | tf_op jit(solution)/shard_map/ppermute | solution.py:90
  40.2 2.7 %collective-permute-start.28 = (f32[1,5,16]{2,1,0:T(8,128)S(1)}, f32[1,5,16]{2,1,0:T(8,128)S(1)}, u32[]{:S(2)}, u32[]{:S(2)}) collective-permute-start(f32[1,5,16]{2,1,0:T(8,128)S(1)} %maximum_bitcast_fusion), channel_id=1, source_target_pairs={{0,16},{1,17},{2,18},{3,19},{4,20},{5,21},{6,22},{7,23},{8,24},{9,... | collective-permute-start | bytes 968 | tf_op jit(solution)/shard_map/ppermute | solution.py:90
  43.2 3.6 %collective-permute-start.30 = (f32[1,5,16]{2,1,0:T(8,128)S(1)}, f32[1,5,16]{2,1,0:T(8,128)S(1)}, u32[]{:S(2)}, u32[]{:S(2)}) collective-permute-start(f32[1,5,16]{2,1,0:T(8,128)S(1)} %maximum_bitcast_fusion), channel_id=1, source_target_pairs={{0,18},{1,19},{2,16},{3,17},{4,22},{5,23},{6,20},{7,21},{8,26},{9,... | collective-permute-start | bytes 968 | tf_op jit(solution)/shard_map/ppermute | solution.py:90
  47.1 3.6 %collective-permute-start.32 = (f32[1,5,16]{2,1,0:T(8,128)S(1)}, f32[1,5,16]{2,1,0:T(8,128)S(1)}, u32[]{:S(2)}, u32[]{:S(2)}) collective-permute-start(f32[1,5,16]{2,1,0:T(8,128)S(1)} %maximum_bitcast_fusion), channel_id=1, source_target_pairs={{0,20},{1,21},{2,22},{3,23},{4,16},{5,17},{6,18},{7,19},{8,28},{9,... | collective-permute-start | bytes 968 | tf_op jit(solution)/shard_map/ppermute | solution.py:90
  51.0 4.5 %collective-permute-start.34 = (f32[1,5,16]{2,1,0:T(8,128)S(1)}, f32[1,5,16]{2,1,0:T(8,128)S(1)}, u32[]{:S(2)}, u32[]{:S(2)}) collective-permute-start(f32[1,5,16]{2,1,0:T(8,128)S(1)} %maximum_bitcast_fusion), channel_id=1, source_target_pairs={{0,22},{1,23},{2,20},{3,21},{4,18},{5,19},{6,16},{7,17},{8,30},{9,... | collective-permute-start | bytes 968 | tf_op jit(solution)/shard_map/ppermute | solution.py:90
  55.8 3.6 %collective-permute-start.36 = (f32[1,5,16]{2,1,0:T(8,128)S(1)}, f32[1,5,16]{2,1,0:T(8,128)S(1)}, u32[]{:S(2)}, u32[]{:S(2)}) collective-permute-start(f32[1,5,16]{2,1,0:T(8,128)S(1)} %maximum_bitcast_fusion), channel_id=1, source_target_pairs={{0,24},{1,25},{2,26},{3,27},{4,28},{5,29},{6,30},{7,31},{8,16},{9,... | collective-permute-start | bytes 968 | tf_op jit(solution)/shard_map/ppermute | solution.py:90
  59.8 4.5 %collective-permute-start.38 = (f32[1,5,16]{2,1,0:T(8,128)S(1)}, f32[1,5,16]{2,1,0:T(8,128)S(1)}, u32[]{:S(2)}, u32[]{:S(2)}) collective-permute-start(f32[1,5,16]{2,1,0:T(8,128)S(1)} %maximum_bitcast_fusion), channel_id=1, source_target_pairs={{0,26},{1,27},{2,24},{3,25},{4,30},{5,31},{6,28},{7,29},{8,18},{9,... | collective-permute-start | bytes 968 | tf_op jit(solution)/shard_map/ppermute | solution.py:90
  64.6 4.5 %collective-permute-start.40 = (f32[1,5,16]{2,1,0:T(8,128)S(1)}, f32[1,5,16]{2,1,0:T(8,128)S(1)}, u32[]{:S(2)}, u32[]{:S(2)}) collective-permute-start(f32[1,5,16]{2,1,0:T(8,128)S(1)} %maximum_bitcast_fusion), channel_id=1, source_target_pairs={{0,28},{1,29},{2,30},{3,31},{4,24},{5,25},{6,26},{7,27},{8,20},{9,... | collective-permute-start | bytes 968 | tf_op jit(solution)/shard_map/ppermute | solution.py:90
  69.4 5.4 %collective-permute-start.42 = (f32[1,5,16]{2,1,0:T(8,128)S(1)}, f32[1,5,16]{2,1,0:T(8,128)S(1)}, u32[]{:S(2)}, u32[]{:S(2)}) collective-permute-start(f32[1,5,16]{2,1,0:T(8,128)S(1)} %maximum_bitcast_fusion), channel_id=1, source_target_pairs={{0,30},{1,31},{2,28},{3,29},{4,26},{5,27},{6,24},{7,25},{8,22},{9,... | collective-permute-start | bytes 968 | tf_op jit(solution)/shard_map/ppermute | solution.py:90
  75.1 1.5 %collective-permute-start.2 = (bf16[32,128]{1,0:T(8,128)(2,1)S(1)}, bf16[32,128]{1,0:T(8,128)(2,1)S(1)}, u32[]{:S(2)}, u32[]{:S(2)}) collective-permute-start(bf16[32,128]{1,0:T(8,128)(2,1)S(1)} %get-tuple-element.25), channel_id=1, source_target_pairs={{0,3},{1,2},{2,1},{3,0},{4,7},{5,6},{6,5},{7,4},{8,11},{9,10},{10,... | collective-permute-start | bytes 24584 | tf_op jit(solution)/shard_map/ppermute | solution.py:90
  77.7 3.9 %collective-permute-done.43 = f32[1,5,16]{2,1,0:T(8,128)S(1)} collective-permute-done((f32[1,5,16]{2,1,0:T(8,128)S(1)}, f32[1,5,16]{2,1,0:T(8,128)S(1)}, u32[]{:S(2)}, u32[]{:S(2)}) %collective-permute-start.43) | collective-permute-done | bytes 352 | tf_op jit(solution)/shard_map/ppermute | solution.py:90
  83.1 2.0 %gather_fusion.1 = bf16[512,256]{1,0:T(8,128)(2,1)S(1)} fusion(bf16[144,256]{1,0:T(8,128)(2,1)S(1)} %pad_maximum_fusion, s32[1024]{0:T(1024)S(1)} %pad_clamp_fusion), kind=kCustom, calls=%fused_computation.1 | custom fusion | bytes 526336 | tf_op jit(solution)/shard_map/jit(_take)/gather | solution.py:73
  86.4 0.7 add_convert_fusion
  87.2 2.6 %fusion.2 = f32[1,16]{1,0:T(1,128)S(1)} fusion(f32[16,128]{1,0:T(8,128)S(1)} %get-tuple-element.49, f32[128]{0:T(128)S(1)} %copy-done.8, f32[3,16]{1,0:T(4,128)S(1)} %copy-done.4, f32[]{:T(128)} %bitcast.21, f32[]{:T(128)} %bitcast.20, f32[]{:T(128)} %bitcast.19, f32[]{:T(128)} %bitcast.18, f32[]{:T(128)} %bitcast.100, s32[16]{0:T(128)S(1)} %copy-done.5), kind=kOutput, calls=%fused_computation.12 | convolution fusion | flops 24800 | bytes 8916 | tf_op jit(solution)/shard_map/dot_general | solution.py:163
  90.5 1.2 %collective-permute-start.5 = (f32[1,16]{1,0:T(1,128)S(1)}, f32[1,16]{1,0:T(1,128)S(1)}, u32[]{:S(2)}, u32[]{:S(2)}) collective-permute-start(f32[1,16]{1,0:T(1,128)S(1)} %fusion.2), channel_id=1, source_target_pairs={{0,3},{1,2},{2,1},{3,0},{4,7},{5,6},{6,5},{7,4},{8,11},{9,10},{10,... | collective-permute-start | bytes 200 | tf_op jit(solution)/shard_map/ppermute | solution.py:90
  91.7 1.8 %collective-permute-done.4 = f32[1,16]{1,0:T(1,128)S(1)} collective-permute-done((f32[1,16]{1,0:T(1,128)S(1)}, f32[1,16]{1,0:T(1,128)S(1)}, u32[]{:S(2)}, u32[]{:S(2)}) %collective-permute-start.4) | collective-permute-done | bytes 96 | tf_op jit(solution)/shard_map/ppermute | solution.py:90
  93.5 0.6 collective-permute-start.6
  94.2 2.9 %collective-permute-start.8 = (f32[4,16]{1,0:T(4,128)S(1)}, f32[4,16]{1,0:T(4,128)S(1)}, u32[]{:S(2)}, u32[]{:S(2)}) collective-permute-start(f32[4,16]{1,0:T(4,128)S(1)} %pad_maximum_fusion.1), channel_id=1, source_target_pairs={{0,12},{4,8},{8,4},{12,0},{16,28},{20,24},{24,20},{28,16},{1,13},{... | collective-permute-start | bytes 776 | tf_op jit(solution)/shard_map/ppermute | solution.py:90
  97.2 2.9 %collective-permute-start.10 = (f32[4,16]{1,0:T(4,128)S(1)}, f32[4,16]{1,0:T(4,128)S(1)}, u32[]{:S(2)}, u32[]{:S(2)}) collective-permute-start(f32[4,16]{1,0:T(4,128)S(1)} %pad_maximum_fusion.1), channel_id=1, source_target_pairs={{0,20},{4,16},{8,28},{12,24},{16,4},{20,0},{24,12},{28,8},{1,21},{... | collective-permute-start | bytes 776 | tf_op jit(solution)/shard_map/ppermute | solution.py:90
  100.1 1.8 %collective-permute-start.11 = (f32[4,16]{1,0:T(4,128)S(1)}, f32[4,16]{1,0:T(4,128)S(1)}, u32[]{:S(2)}, u32[]{:S(2)}) collective-permute-start(f32[4,16]{1,0:T(4,128)S(1)} %pad_maximum_fusion.1), channel_id=1, source_target_pairs={{0,24},{4,28},{8,16},{12,20},{16,8},{20,12},{24,0},{28,4},{1,25},{... | collective-permute-start | bytes 776 | tf_op jit(solution)/shard_map/ppermute | solution.py:90
  101.9 2.9 %collective-permute-start.12 = (f32[4,16]{1,0:T(4,128)S(1)}, f32[4,16]{1,0:T(4,128)S(1)}, u32[]{:S(2)}, u32[]{:S(2)}) collective-permute-start(f32[4,16]{1,0:T(4,128)S(1)} %pad_maximum_fusion.1), channel_id=1, source_target_pairs={{0,28},{4,24},{8,20},{12,16},{16,12},{20,8},{24,4},{28,0},{1,29},{... | collective-permute-start | bytes 776 | tf_op jit(solution)/shard_map/ppermute | solution.py:90
  105.5 2.7 %collective-permute-done.12 = f32[4,16]{1,0:T(4,128)S(1)} collective-permute-done((f32[4,16]{1,0:T(4,128)S(1)}, f32[4,16]{1,0:T(4,128)S(1)}, u32[]{:S(2)}, u32[]{:S(2)}) %collective-permute-start.12) | collective-permute-done | bytes 288 | tf_op jit(solution)/shard_map/ppermute | solution.py:90
  108.4 0.6 multiply_reduce_fusion.10
  109.0 0.6 multiply_reduce_fusion.2
  109.6 0.6 multiply_reduce_fusion.14
  111.6 0.6 multiply_reduce_fusion.13
  113.7 0.6 multiply_reduce_fusion.12
  116.8 0.6 broadcast_multiply_fusion
  (158 shorter events, 11.4 us)
Async XLA Ops:
  0.6 84.6 %copy-start = (bf16[128,256]{1,0:T(8,128)(2,1)S(1)}, bf16[128,256]{1,0:T(8,128)(2,1)}, u32[]{:S(2)}) copy-start(bf16[128,256]{1,0:T(8,128)(2,1)} %param.25) | copy-start | bytes 196612
  10.6 14.5 %collective-permute-start.13 = (f32[1,5,16]{2,1,0:T(8,128)S(1)}, f32[1,5,16]{2,1,0:T(8,128)S(1)}, u32[]{:S(2)}, u32[]{:S(2)}) collective-permute-start(f32[1,5,16]{2,1,0:T(8,128)S(1)} %maximum_bitcast_fusion), channel_id=1, source_target_pairs={{0,1},{1,0},{2,3},{3,2},{4,5},{5,4},{6,7},{7,6},{8,9},{9,8},{10,11... | collective-permute-start | bytes 968 | tf_op jit(solution)/shard_map/ppermute | solution.py:90
  11.0 16.9 %collective-permute-start.14 = (f32[1,5,16]{2,1,0:T(8,128)S(1)}, f32[1,5,16]{2,1,0:T(8,128)S(1)}, u32[]{:S(2)}, u32[]{:S(2)}) collective-permute-start(f32[1,5,16]{2,1,0:T(8,128)S(1)} %maximum_bitcast_fusion), channel_id=1, source_target_pairs={{0,2},{1,3},{2,0},{3,1},{4,6},{5,7},{6,4},{7,5},{8,10},{9,11},{10,... | collective-permute-start | bytes 968 | tf_op jit(solution)/shard_map/ppermute | solution.py:90
  13.6 14.5 %collective-permute-start.15 = (f32[1,5,16]{2,1,0:T(8,128)S(1)}, f32[1,5,16]{2,1,0:T(8,128)S(1)}, u32[]{:S(2)}, u32[]{:S(2)}) collective-permute-start(f32[1,5,16]{2,1,0:T(8,128)S(1)} %maximum_bitcast_fusion), channel_id=1, source_target_pairs={{0,3},{1,2},{2,1},{3,0},{4,7},{5,6},{6,5},{7,4},{8,11},{9,10},{10,... | collective-permute-start | bytes 968 | tf_op jit(solution)/shard_map/ppermute | solution.py:90
  13.7 16.4 %collective-permute-start.16 = (f32[1,5,16]{2,1,0:T(8,128)S(1)}, f32[1,5,16]{2,1,0:T(8,128)S(1)}, u32[]{:S(2)}, u32[]{:S(2)}) collective-permute-start(f32[1,5,16]{2,1,0:T(8,128)S(1)} %maximum_bitcast_fusion), channel_id=1, source_target_pairs={{0,4},{1,5},{2,6},{3,7},{4,0},{5,1},{6,2},{7,3},{8,12},{9,13},{10,... | collective-permute-start | bytes 968 | tf_op jit(solution)/shard_map/ppermute | solution.py:90
  15.4 14.9 %collective-permute-start.17 = (f32[1,5,16]{2,1,0:T(8,128)S(1)}, f32[1,5,16]{2,1,0:T(8,128)S(1)}, u32[]{:S(2)}, u32[]{:S(2)}) collective-permute-start(f32[1,5,16]{2,1,0:T(8,128)S(1)} %maximum_bitcast_fusion), channel_id=1, source_target_pairs={{0,5},{1,4},{2,7},{3,6},{4,1},{5,0},{6,3},{7,2},{8,13},{9,12},{10,... | collective-permute-start | bytes 968 | tf_op jit(solution)/shard_map/ppermute | solution.py:90
  25.1 8.0 %collective-permute-start.18 = (f32[1,5,16]{2,1,0:T(8,128)S(1)}, f32[1,5,16]{2,1,0:T(8,128)S(1)}, u32[]{:S(2)}, u32[]{:S(2)}) collective-permute-start(f32[1,5,16]{2,1,0:T(8,128)S(1)} %maximum_bitcast_fusion), channel_id=1, source_target_pairs={{0,6},{1,7},{2,4},{3,5},{4,2},{5,3},{6,0},{7,1},{8,14},{9,15},{10,... | collective-permute-start | bytes 968 | tf_op jit(solution)/shard_map/ppermute | solution.py:90
  27.9 5.4 %collective-permute-start.19 = (f32[1,5,16]{2,1,0:T(8,128)S(1)}, f32[1,5,16]{2,1,0:T(8,128)S(1)}, u32[]{:S(2)}, u32[]{:S(2)}) collective-permute-start(f32[1,5,16]{2,1,0:T(8,128)S(1)} %maximum_bitcast_fusion), channel_id=1, source_target_pairs={{0,7},{1,6},{2,5},{3,4},{4,3},{5,2},{6,1},{7,0},{8,15},{9,14},{10,... | collective-permute-start | bytes 968 | tf_op jit(solution)/shard_map/ppermute | solution.py:90
  28.1 7.9 %collective-permute-start.20 = (f32[1,5,16]{2,1,0:T(8,128)S(1)}, f32[1,5,16]{2,1,0:T(8,128)S(1)}, u32[]{:S(2)}, u32[]{:S(2)}) collective-permute-start(f32[1,5,16]{2,1,0:T(8,128)S(1)} %maximum_bitcast_fusion), channel_id=1, source_target_pairs={{0,8},{1,9},{2,10},{3,11},{4,12},{5,13},{6,14},{7,15},{8,0},{9,1},... | collective-permute-start | bytes 968 | tf_op jit(solution)/shard_map/ppermute | solution.py:90
  30.1 6.2 %collective-permute-start.21 = (f32[1,5,16]{2,1,0:T(8,128)S(1)}, f32[1,5,16]{2,1,0:T(8,128)S(1)}, u32[]{:S(2)}, u32[]{:S(2)}) collective-permute-start(f32[1,5,16]{2,1,0:T(8,128)S(1)} %maximum_bitcast_fusion), channel_id=1, source_target_pairs={{0,9},{1,8},{2,11},{3,10},{4,13},{5,12},{6,15},{7,14},{8,1},{9,0},... | collective-permute-start | bytes 968 | tf_op jit(solution)/shard_map/ppermute | solution.py:90
  30.3 9.7 %collective-permute-start.22 = (f32[1,5,16]{2,1,0:T(8,128)S(1)}, f32[1,5,16]{2,1,0:T(8,128)S(1)}, u32[]{:S(2)}, u32[]{:S(2)}) collective-permute-start(f32[1,5,16]{2,1,0:T(8,128)S(1)} %maximum_bitcast_fusion), channel_id=1, source_target_pairs={{0,10},{1,11},{2,8},{3,9},{4,14},{5,15},{6,12},{7,13},{8,2},{9,3},... | collective-permute-start | bytes 968 | tf_op jit(solution)/shard_map/ppermute | solution.py:90
  33.1 7.1 %collective-permute-start.23 = (f32[1,5,16]{2,1,0:T(8,128)S(1)}, f32[1,5,16]{2,1,0:T(8,128)S(1)}, u32[]{:S(2)}, u32[]{:S(2)}) collective-permute-start(f32[1,5,16]{2,1,0:T(8,128)S(1)} %maximum_bitcast_fusion), channel_id=1, source_target_pairs={{0,11},{1,10},{2,9},{3,8},{4,15},{5,14},{6,13},{7,12},{8,3},{9,2},... | collective-permute-start | bytes 968 | tf_op jit(solution)/shard_map/ppermute | solution.py:90
  33.3 9.7 %collective-permute-start.24 = (f32[1,5,16]{2,1,0:T(8,128)S(1)}, f32[1,5,16]{2,1,0:T(8,128)S(1)}, u32[]{:S(2)}, u32[]{:S(2)}) collective-permute-start(f32[1,5,16]{2,1,0:T(8,128)S(1)} %maximum_bitcast_fusion), channel_id=1, source_target_pairs={{0,12},{1,13},{2,14},{3,15},{4,8},{5,9},{6,10},{7,11},{8,4},{9,5},... | collective-permute-start | bytes 968 | tf_op jit(solution)/shard_map/ppermute | solution.py:90
  36.1 7.1 %collective-permute-start.25 = (f32[1,5,16]{2,1,0:T(8,128)S(1)}, f32[1,5,16]{2,1,0:T(8,128)S(1)}, u32[]{:S(2)}, u32[]{:S(2)}) collective-permute-start(f32[1,5,16]{2,1,0:T(8,128)S(1)} %maximum_bitcast_fusion), channel_id=1, source_target_pairs={{0,13},{1,12},{2,15},{3,14},{4,9},{5,8},{6,11},{7,10},{8,5},{9,4},... | collective-permute-start | bytes 968 | tf_op jit(solution)/shard_map/ppermute | solution.py:90
  36.3 10.7 %collective-permute-start.26 = (f32[1,5,16]{2,1,0:T(8,128)S(1)}, f32[1,5,16]{2,1,0:T(8,128)S(1)}, u32[]{:S(2)}, u32[]{:S(2)}) collective-permute-start(f32[1,5,16]{2,1,0:T(8,128)S(1)} %maximum_bitcast_fusion), channel_id=1, source_target_pairs={{0,14},{1,15},{2,12},{3,13},{4,10},{5,11},{6,8},{7,9},{8,6},{9,7},... | collective-permute-start | bytes 968 | tf_op jit(solution)/shard_map/ppermute | solution.py:90
  40.0 7.2 %collective-permute-start.27 = (f32[1,5,16]{2,1,0:T(8,128)S(1)}, f32[1,5,16]{2,1,0:T(8,128)S(1)}, u32[]{:S(2)}, u32[]{:S(2)}) collective-permute-start(f32[1,5,16]{2,1,0:T(8,128)S(1)} %maximum_bitcast_fusion), channel_id=1, source_target_pairs={{0,15},{1,14},{2,13},{3,12},{4,11},{5,10},{6,9},{7,8},{8,7},{9,6},... | collective-permute-start | bytes 968 | tf_op jit(solution)/shard_map/ppermute | solution.py:90
  40.2 10.6 %collective-permute-start.28 = (f32[1,5,16]{2,1,0:T(8,128)S(1)}, f32[1,5,16]{2,1,0:T(8,128)S(1)}, u32[]{:S(2)}, u32[]{:S(2)}) collective-permute-start(f32[1,5,16]{2,1,0:T(8,128)S(1)} %maximum_bitcast_fusion), channel_id=1, source_target_pairs={{0,16},{1,17},{2,18},{3,19},{4,20},{5,21},{6,22},{7,23},{8,24},{9,... | collective-permute-start | bytes 968 | tf_op jit(solution)/shard_map/ppermute | solution.py:90
  43.0 8.0 %collective-permute-start.29 = (f32[1,5,16]{2,1,0:T(8,128)S(1)}, f32[1,5,16]{2,1,0:T(8,128)S(1)}, u32[]{:S(2)}, u32[]{:S(2)}) collective-permute-start(f32[1,5,16]{2,1,0:T(8,128)S(1)} %maximum_bitcast_fusion), channel_id=1, source_target_pairs={{0,17},{1,16},{2,19},{3,18},{4,21},{5,20},{6,23},{7,22},{8,25},{9,... | collective-permute-start | bytes 968 | tf_op jit(solution)/shard_map/ppermute | solution.py:90
  43.2 12.4 %collective-permute-start.30 = (f32[1,5,16]{2,1,0:T(8,128)S(1)}, f32[1,5,16]{2,1,0:T(8,128)S(1)}, u32[]{:S(2)}, u32[]{:S(2)}) collective-permute-start(f32[1,5,16]{2,1,0:T(8,128)S(1)} %maximum_bitcast_fusion), channel_id=1, source_target_pairs={{0,18},{1,19},{2,16},{3,17},{4,22},{5,23},{6,20},{7,21},{8,26},{9,... | collective-permute-start | bytes 968 | tf_op jit(solution)/shard_map/ppermute | solution.py:90
  46.9 8.9 %collective-permute-start.31 = (f32[1,5,16]{2,1,0:T(8,128)S(1)}, f32[1,5,16]{2,1,0:T(8,128)S(1)}, u32[]{:S(2)}, u32[]{:S(2)}) collective-permute-start(f32[1,5,16]{2,1,0:T(8,128)S(1)} %maximum_bitcast_fusion), channel_id=1, source_target_pairs={{0,19},{1,18},{2,17},{3,16},{4,23},{5,22},{6,21},{7,20},{8,27},{9,... | collective-permute-start | bytes 968 | tf_op jit(solution)/shard_map/ppermute | solution.py:90
  47.1 12.4 %collective-permute-start.32 = (f32[1,5,16]{2,1,0:T(8,128)S(1)}, f32[1,5,16]{2,1,0:T(8,128)S(1)}, u32[]{:S(2)}, u32[]{:S(2)}) collective-permute-start(f32[1,5,16]{2,1,0:T(8,128)S(1)} %maximum_bitcast_fusion), channel_id=1, source_target_pairs={{0,20},{1,21},{2,22},{3,23},{4,16},{5,17},{6,18},{7,19},{8,28},{9,... | collective-permute-start | bytes 968 | tf_op jit(solution)/shard_map/ppermute | solution.py:90
  50.8 8.9 %collective-permute-start.33 = (f32[1,5,16]{2,1,0:T(8,128)S(1)}, f32[1,5,16]{2,1,0:T(8,128)S(1)}, u32[]{:S(2)}, u32[]{:S(2)}) collective-permute-start(f32[1,5,16]{2,1,0:T(8,128)S(1)} %maximum_bitcast_fusion), channel_id=1, source_target_pairs={{0,21},{1,20},{2,23},{3,22},{4,17},{5,16},{6,19},{7,18},{8,29},{9,... | collective-permute-start | bytes 968 | tf_op jit(solution)/shard_map/ppermute | solution.py:90
  51.0 13.4 %collective-permute-start.34 = (f32[1,5,16]{2,1,0:T(8,128)S(1)}, f32[1,5,16]{2,1,0:T(8,128)S(1)}, u32[]{:S(2)}, u32[]{:S(2)}) collective-permute-start(f32[1,5,16]{2,1,0:T(8,128)S(1)} %maximum_bitcast_fusion), channel_id=1, source_target_pairs={{0,22},{1,23},{2,20},{3,21},{4,18},{5,19},{6,16},{7,17},{8,30},{9,... | collective-permute-start | bytes 968 | tf_op jit(solution)/shard_map/ppermute | solution.py:90
  55.6 9.0 %collective-permute-start.35 = (f32[1,5,16]{2,1,0:T(8,128)S(1)}, f32[1,5,16]{2,1,0:T(8,128)S(1)}, u32[]{:S(2)}, u32[]{:S(2)}) collective-permute-start(f32[1,5,16]{2,1,0:T(8,128)S(1)} %maximum_bitcast_fusion), channel_id=1, source_target_pairs={{0,23},{1,22},{2,21},{3,20},{4,19},{5,18},{6,17},{7,16},{8,31},{9,... | collective-permute-start | bytes 968 | tf_op jit(solution)/shard_map/ppermute | solution.py:90
  55.8 13.3 %collective-permute-start.36 = (f32[1,5,16]{2,1,0:T(8,128)S(1)}, f32[1,5,16]{2,1,0:T(8,128)S(1)}, u32[]{:S(2)}, u32[]{:S(2)}) collective-permute-start(f32[1,5,16]{2,1,0:T(8,128)S(1)} %maximum_bitcast_fusion), channel_id=1, source_target_pairs={{0,24},{1,25},{2,26},{3,27},{4,28},{5,29},{6,30},{7,31},{8,16},{9,... | collective-permute-start | bytes 968 | tf_op jit(solution)/shard_map/ppermute | solution.py:90
  59.6 22.7 %copy-start.4 = (f32[3,16]{1,0:T(4,128)S(1)}, f32[3,16]{1,0:T(4,128)}, u32[]{:S(2)}) copy-start(f32[3,16]{1,0:T(4,128)} %param.17) | copy-start | bytes 580
  59.6 9.8 %collective-permute-start.37 = (f32[1,5,16]{2,1,0:T(8,128)S(1)}, f32[1,5,16]{2,1,0:T(8,128)S(1)}, u32[]{:S(2)}, u32[]{:S(2)}) collective-permute-start(f32[1,5,16]{2,1,0:T(8,128)S(1)} %maximum_bitcast_fusion), channel_id=1, source_target_pairs={{0,25},{1,24},{2,27},{3,26},{4,29},{5,28},{6,31},{7,30},{8,17},{9,... | collective-permute-start | bytes 968 | tf_op jit(solution)/shard_map/ppermute | solution.py:90
  59.8 15.1 %collective-permute-start.38 = (f32[1,5,16]{2,1,0:T(8,128)S(1)}, f32[1,5,16]{2,1,0:T(8,128)S(1)}, u32[]{:S(2)}, u32[]{:S(2)}) collective-permute-start(f32[1,5,16]{2,1,0:T(8,128)S(1)} %maximum_bitcast_fusion), channel_id=1, source_target_pairs={{0,26},{1,27},{2,24},{3,25},{4,30},{5,31},{6,28},{7,29},{8,18},{9,... | collective-permute-start | bytes 968 | tf_op jit(solution)/shard_map/ppermute | solution.py:90
  64.4 10.7 %collective-permute-start.39 = (f32[1,5,16]{2,1,0:T(8,128)S(1)}, f32[1,5,16]{2,1,0:T(8,128)S(1)}, u32[]{:S(2)}, u32[]{:S(2)}) collective-permute-start(f32[1,5,16]{2,1,0:T(8,128)S(1)} %maximum_bitcast_fusion), channel_id=1, source_target_pairs={{0,27},{1,26},{2,25},{3,24},{4,31},{5,30},{6,29},{7,28},{8,19},{9,... | collective-permute-start | bytes 968 | tf_op jit(solution)/shard_map/ppermute | solution.py:90
  64.6 12.1 %collective-permute-start.40 = (f32[1,5,16]{2,1,0:T(8,128)S(1)}, f32[1,5,16]{2,1,0:T(8,128)S(1)}, u32[]{:S(2)}, u32[]{:S(2)}) collective-permute-start(f32[1,5,16]{2,1,0:T(8,128)S(1)} %maximum_bitcast_fusion), channel_id=1, source_target_pairs={{0,28},{1,29},{2,30},{3,31},{4,24},{5,25},{6,26},{7,27},{8,20},{9,... | collective-permute-start | bytes 968 | tf_op jit(solution)/shard_map/ppermute | solution.py:90
  69.2 8.2 %collective-permute-start.41 = (f32[1,5,16]{2,1,0:T(8,128)S(1)}, f32[1,5,16]{2,1,0:T(8,128)S(1)}, u32[]{:S(2)}, u32[]{:S(2)}) collective-permute-start(f32[1,5,16]{2,1,0:T(8,128)S(1)} %maximum_bitcast_fusion), channel_id=1, source_target_pairs={{0,29},{1,28},{2,31},{3,30},{4,25},{5,24},{6,27},{7,26},{8,21},{9,... | collective-permute-start | bytes 968 | tf_op jit(solution)/shard_map/ppermute | solution.py:90
  69.4 8.2 %collective-permute-start.42 = (f32[1,5,16]{2,1,0:T(8,128)S(1)}, f32[1,5,16]{2,1,0:T(8,128)S(1)}, u32[]{:S(2)}, u32[]{:S(2)}) collective-permute-start(f32[1,5,16]{2,1,0:T(8,128)S(1)} %maximum_bitcast_fusion), channel_id=1, source_target_pairs={{0,30},{1,31},{2,28},{3,29},{4,26},{5,27},{6,24},{7,25},{8,22},{9,... | collective-permute-start | bytes 968 | tf_op jit(solution)/shard_map/ppermute | solution.py:90
  74.9 6.7 %collective-permute-start.43 = (f32[1,5,16]{2,1,0:T(8,128)S(1)}, f32[1,5,16]{2,1,0:T(8,128)S(1)}, u32[]{:S(2)}, u32[]{:S(2)}) collective-permute-start(f32[1,5,16]{2,1,0:T(8,128)S(1)} %maximum_bitcast_fusion), channel_id=1, source_target_pairs={{0,31},{1,30},{2,29},{3,28},{4,27},{5,26},{6,25},{7,24},{8,23},{9,... | collective-permute-start | bytes 968 | tf_op jit(solution)/shard_map/ppermute | solution.py:90
  75.1 7.8 %collective-permute-start.2 = (bf16[32,128]{1,0:T(8,128)(2,1)S(1)}, bf16[32,128]{1,0:T(8,128)(2,1)S(1)}, u32[]{:S(2)}, u32[]{:S(2)}) collective-permute-start(bf16[32,128]{1,0:T(8,128)(2,1)S(1)} %get-tuple-element.25), channel_id=1, source_target_pairs={{0,3},{1,2},{2,1},{3,0},{4,7},{5,6},{6,5},{7,4},{8,11},{9,10},{10,... | collective-permute-start | bytes 24584 | tf_op jit(solution)/shard_map/ppermute | solution.py:90
  76.7 6.2 %collective-permute-start.1 = (bf16[32,128]{1,0:T(8,128)(2,1)S(1)}, bf16[32,128]{1,0:T(8,128)(2,1)S(1)}, u32[]{:S(2)}, u32[]{:S(2)}) collective-permute-start(bf16[32,128]{1,0:T(8,128)(2,1)S(1)} %get-tuple-element.26), channel_id=1, source_target_pairs={{0,2},{1,3},{2,0},{3,1},{4,6},{5,7},{6,4},{7,5},{8,10},{9,11},{10,... | collective-permute-start | bytes 24584 | tf_op jit(solution)/shard_map/ppermute | solution.py:90
  77.4 5.5 %collective-permute-start = (bf16[32,128]{1,0:T(8,128)(2,1)S(1)}, bf16[32,128]{1,0:T(8,128)(2,1)S(1)}, u32[]{:S(2)}, u32[]{:S(2)}) collective-permute-start(bf16[32,128]{1,0:T(8,128)(2,1)S(1)} %get-tuple-element.27), channel_id=1, source_target_pairs={{0,1},{1,0},{2,3},{3,2},{4,5},{5,4},{6,7},{7,6},{8,9},{9,8},{10,11... | collective-permute-start | bytes 24584 | tf_op jit(solution)/shard_map/ppermute | solution.py:90
  85.6 1.6 %copy-start.5 = (s32[16]{0:T(128)S(1)}, s32[16]{0:T(128)}, u32[]{:S(2)}) copy-start(s32[16]{0:T(128)} %param.18) | copy-start | bytes 196
  89.8 1.9 %collective-permute-start.3 = (f32[1,16]{1,0:T(1,128)S(1)}, f32[1,16]{1,0:T(1,128)S(1)}, u32[]{:S(2)}, u32[]{:S(2)}) collective-permute-start(f32[1,16]{1,0:T(1,128)S(1)} %fusion.2), channel_id=1, source_target_pairs={{0,1},{1,0},{2,3},{3,2},{4,5},{5,4},{6,7},{7,6},{8,9},{9,8},{10,11... | collective-permute-start | bytes 200 | tf_op jit(solution)/shard_map/ppermute | solution.py:90
  90.0 3.5 %collective-permute-start.4 = (f32[1,16]{1,0:T(1,128)S(1)}, f32[1,16]{1,0:T(1,128)S(1)}, u32[]{:S(2)}, u32[]{:S(2)}) collective-permute-start(f32[1,16]{1,0:T(1,128)S(1)} %fusion.2), channel_id=1, source_target_pairs={{0,2},{1,3},{2,0},{3,1},{4,6},{5,7},{6,4},{7,5},{8,10},{9,11},{10,... | collective-permute-start | bytes 200 | tf_op jit(solution)/shard_map/ppermute | solution.py:90
  90.5 3.0 %collective-permute-start.5 = (f32[1,16]{1,0:T(1,128)S(1)}, f32[1,16]{1,0:T(1,128)S(1)}, u32[]{:S(2)}, u32[]{:S(2)}) collective-permute-start(f32[1,16]{1,0:T(1,128)S(1)} %fusion.2), channel_id=1, source_target_pairs={{0,3},{1,2},{2,1},{3,0},{4,7},{5,6},{6,5},{7,4},{8,11},{9,10},{10,... | collective-permute-start | bytes 200 | tf_op jit(solution)/shard_map/ppermute | solution.py:90
  93.5 6.5 %collective-permute-start.6 = (f32[4,16]{1,0:T(4,128)S(1)}, f32[4,16]{1,0:T(4,128)S(1)}, u32[]{:S(2)}, u32[]{:S(2)}) collective-permute-start(f32[4,16]{1,0:T(4,128)S(1)} %pad_maximum_fusion.1), channel_id=1, source_target_pairs={{0,4},{4,0},{8,12},{12,8},{16,20},{20,16},{24,28},{28,24},{1,5},{5... | collective-permute-start | bytes 776 | tf_op jit(solution)/shard_map/ppermute | solution.py:90
  94.2 7.7 %collective-permute-start.7 = (f32[4,16]{1,0:T(4,128)S(1)}, f32[4,16]{1,0:T(4,128)S(1)}, u32[]{:S(2)}, u32[]{:S(2)}) collective-permute-start(f32[4,16]{1,0:T(4,128)S(1)} %pad_maximum_fusion.1), channel_id=1, source_target_pairs={{0,8},{4,12},{8,0},{12,4},{16,24},{20,28},{24,16},{28,20},{1,9},{5... | collective-permute-start | bytes 776 | tf_op jit(solution)/shard_map/ppermute | solution.py:90
  94.2 10.7 %collective-permute-start.8 = (f32[4,16]{1,0:T(4,128)S(1)}, f32[4,16]{1,0:T(4,128)S(1)}, u32[]{:S(2)}, u32[]{:S(2)}) collective-permute-start(f32[4,16]{1,0:T(4,128)S(1)} %pad_maximum_fusion.1), channel_id=1, source_target_pairs={{0,12},{4,8},{8,4},{12,0},{16,28},{20,24},{24,20},{28,16},{1,13},{... | collective-permute-start | bytes 776 | tf_op jit(solution)/shard_map/ppermute | solution.py:90
  97.2 7.7 %collective-permute-start.9 = (f32[4,16]{1,0:T(4,128)S(1)}, f32[4,16]{1,0:T(4,128)S(1)}, u32[]{:S(2)}, u32[]{:S(2)}) collective-permute-start(f32[4,16]{1,0:T(4,128)S(1)} %pad_maximum_fusion.1), channel_id=1, source_target_pairs={{0,16},{4,20},{8,24},{12,28},{16,0},{20,4},{24,8},{28,12},{1,17},{... | collective-permute-start | bytes 776 | tf_op jit(solution)/shard_map/ppermute | solution.py:90
  97.2 7.7 %collective-permute-start.10 = (f32[4,16]{1,0:T(4,128)S(1)}, f32[4,16]{1,0:T(4,128)S(1)}, u32[]{:S(2)}, u32[]{:S(2)}) collective-permute-start(f32[4,16]{1,0:T(4,128)S(1)} %pad_maximum_fusion.1), channel_id=1, source_target_pairs={{0,20},{4,16},{8,28},{12,24},{16,4},{20,0},{24,12},{28,8},{1,21},{... | collective-permute-start | bytes 776 | tf_op jit(solution)/shard_map/ppermute | solution.py:90
  100.1 5.4 %collective-permute-start.11 = (f32[4,16]{1,0:T(4,128)S(1)}, f32[4,16]{1,0:T(4,128)S(1)}, u32[]{:S(2)}, u32[]{:S(2)}) collective-permute-start(f32[4,16]{1,0:T(4,128)S(1)} %pad_maximum_fusion.1), channel_id=1, source_target_pairs={{0,24},{4,28},{8,16},{12,20},{16,8},{20,12},{24,0},{28,4},{1,25},{... | collective-permute-start | bytes 776 | tf_op jit(solution)/shard_map/ppermute | solution.py:90
  101.9 6.3 %collective-permute-start.12 = (f32[4,16]{1,0:T(4,128)S(1)}, f32[4,16]{1,0:T(4,128)S(1)}, u32[]{:S(2)}, u32[]{:S(2)}) collective-permute-start(f32[4,16]{1,0:T(4,128)S(1)} %pad_maximum_fusion.1), channel_id=1, source_target_pairs={{0,28},{4,24},{8,20},{12,16},{16,12},{20,8},{24,4},{28,0},{1,29},{... | collective-permute-start | bytes 776 | tf_op jit(solution)/shard_map/ppermute | solution.py:90
  115.6 1.7 %copy-start.6 = (f32[16]{0:T(128)}, f32[16]{0:T(128)S(1)}, u32[]{:S(2)}) copy-start(f32[16]{0:T(128)S(1)} %get-tuple-element.11) | copy-start | bytes 196
  (5 other events, 4.7 us)

commit v3 on v1

--- a/solution.py
+++ b/solution.py
@@ -3,6 +3,8 @@
 import jax
 import jax.numpy as jnp
 from jax import lax
+from jax.experimental import pallas as pl
+from jax.experimental.pallas import tpu as pltpu
 from jax.sharding import PartitionSpec as P
 
 ITERS = 2
@@ -184,9 +186,318 @@
     return charges
 
 
+def split3(value):
+    first = value.astype(jnp.bfloat16).astype(jnp.float32)
+    rest = value - first
+    second = rest.astype(jnp.bfloat16).astype(jnp.float32)
+    third = (rest - second).astype(jnp.bfloat16).astype(jnp.float32)
+    return first, second, third
+
+
+def over_first(left, right):
+    return lax.dot_general(
+        left, right, (((0,), (0,)), ((), ())), preferred_element_type=jnp.float32
+    )
+
+
+def over_last(left, right, precision=None):
+    return lax.dot_general(
+        left,
+        right,
+        (((1,), (1,)), ((), ())),
+        precision=precision,
+        preferred_element_type=jnp.float32,
+    )
+
+
+def silu(value):
+    return value / (1.0 + jnp.exp(-value))
+
+
+sine_series = [(-1.0) ** k * math.pi ** (2 * k + 1) / math.factorial(2 * k + 1) for k in range(7)]
+
+
+def edge_kernel(vec_ref, recv_ref, first_ref, second_ref, filter_ref, combine_ref):
+    atoms = combine_ref.shape[0] // 7
+    edges = vec_ref.shape[1]
+    orders = first_ref.shape[0]
+    vec = vec_ref[...]
+    east, north, up = vec[0:1], vec[1:2], vec[2:3]
+    squared = east * east + north * north + up * up
+    inverse = lax.rsqrt(squared)
+    ratio = squared * inverse * (1.0 / cutoff)
+    envelope = (1.0 - ratio * ratio) * (1.0 - ratio * ratio) * (cutoff * inverse)
+    order = lax.broadcasted_iota(jnp.int32, (orders, edges), 0).astype(jnp.float32) + 1.0
+    turns = order * ratio
+    whole = jnp.floor(turns + 0.5)
+    part = turns - whole
+    sign = 1.0 - 2.0 * (whole - 2.0 * jnp.floor(whole * 0.5))
+    series = jnp.full_like(part, sine_series[-1])
+    for coefficient in sine_series[-2::-1]:
+        series = series * (part * part) + coefficient
+    basis = series * part * (sign * envelope)
+    b1, b2, b3 = split3(basis)
+    w1, w2, w3 = split3(first_ref[...])
+    mixed = over_first(
+        jnp.concatenate([w1, w1, w2, w2, w1, w3], axis=0).astype(jnp.bfloat16),
+        jnp.concatenate([b1, b2, b1, b2, b3, b1], axis=0).astype(jnp.bfloat16),
+    )
+    radial = silu(mixed).astype(jnp.bfloat16)
+    filter_ref[...] = over_first(second_ref[...], radial)
+    local = lax.broadcasted_iota(jnp.int32, (atoms, edges), 0)
+    hit = local == recv_ref[...]
+    rows = [jnp.where(hit, 1.0, 0.0)]
+    low = []
+    for component in (east, north, up):
+        unit = component * inverse
+        high = unit.astype(jnp.bfloat16).astype(jnp.float32)
+        rows.append(jnp.where(hit, high, 0.0))
+        low.append(jnp.where(hit, unit - high, 0.0))
+    combine_ref[...] = jnp.concatenate(rows + low, axis=0).astype(jnp.bfloat16)
+
+
+def node_kernel(
+    space_ref,
+    own_ref,
+    near_ref,
+    side_ref,
+    far_ref,
+    send_ref,
+    filter_ref,
+    combine_ref,
+    project_ref,
+    update_ref,
+    out_ref,
+    species_ref,
+    hardness_ref,
+    width_ref,
+    shift_ref,
+    field_ref,
+    positions_ref,
+    features_ref,
+    block_ref,
+):
+    atoms = positions_ref.shape[1]
+    edges = send_ref.shape[1]
+    chans = features_ref.shape[1]
+    space = space_ref[0]
+    packed = [ref[...].astype(jnp.float32) for ref in (own_ref, near_ref, side_ref, far_ref)]
+    lanes = len(packed)
+    slots = chans // lanes
+    group = jnp.concatenate([value[:atoms] for value in packed], axis=0).astype(jnp.bfloat16)
+    picks = jnp.zeros((8, chans), jnp.float32)
+    line = lax.broadcasted_iota(jnp.int32, (packed[0].shape[0] - atoms, chans), 0)
+    for place, value in enumerate(packed):
+        mine = jnp.sum(jnp.where(line == space, value[atoms:], 0.0), axis=0, keepdims=True)
+        mine = jnp.broadcast_to(mine, (8, chans))
+        picks = picks + (pltpu.roll(mine, place * slots, 1) if place else mine)
+    slot_owner = lax.broadcasted_iota(jnp.int32, (1, chans), 1) // slots * atoms
+    chosen = slot_owner + picks[0:1].astype(jnp.int32)
+    members = lanes * atoms
+    fill = jnp.where(
+        lax.broadcasted_iota(jnp.int32, (members, chans), 0) == chosen, 1.0, 0.0
+    ).astype(jnp.bfloat16)
+    send = send_ref[...]
+    own = send < atoms
+    slot = jnp.where(own, -1, (send - atoms) ^ (space * slots))
+    from_slot = jnp.where(
+        lax.broadcasted_iota(jnp.int32, (chans, edges), 0) == slot, 1.0, 0.0
+    ).astype(jnp.bfloat16)
+    from_own = jnp.where(
+        lax.broadcasted_iota(jnp.int32, (members, edges), 0) == jnp.where(own, send, -1), 1.0, 0.0
+    )
+    sender = jnp.dot(fill, from_slot, preferred_element_type=jnp.float32) + from_own
+    projected = jnp.dot(group, project_ref[...], preferred_element_type=jnp.float32)
+    picked = over_first(projected.astype(jnp.bfloat16), sender.astype(jnp.bfloat16))
+    message = (picked * filter_ref[...]).astype(jnp.bfloat16)
+    summed = over_last(combine_ref[...], message) * message_scale
+    square = jnp.zeros((atoms, chans), jnp.float32)
+    for component in range(1, 4):
+        high = summed[component * atoms : (component + 1) * atoms, chans:]
+        low = summed[(component + 3) * atoms : (component + 4) * atoms, chans:]
+        square = square + (high + low) * (high + low)
+    invariant = jnp.concatenate([summed[:atoms, :chans], square], axis=1).astype(jnp.bfloat16)
+    hidden = silu(jnp.dot(invariant, update_ref[...], preferred_element_type=jnp.float32))
+    features_ref[...] = (packed[0][:atoms] + hidden).astype(jnp.bfloat16)
+    readout = jnp.broadcast_to(out_ref[...], (8, chans))
+    chi = over_last(readout, hidden, lax.Precision.HIGHEST)[0:1]
+    species = species_ref[...]
+
+    def table(ref):
+        result = jnp.zeros(species.shape, jnp.float32)
+        for kind in range(ref.shape[1]):
+            result = result + jnp.where(species == kind, ref[:, kind : kind + 1], 0.0)
+        return result
+
+    chi = chi + table(shift_ref)
+    sigma = table(width_ref)
+    diag = table(hardness_ref) + inverse_root_pi / sigma
+    positions = positions_ref[...]
+    rhs = field_ref[...] * positions[2:3] - chi
+    blank = jnp.zeros((2, atoms), jnp.float32)
+    block_ref[...] = jnp.concatenate([positions, sigma, diag, rhs, blank], axis=0)
+
+
+def smeared(scaled):
+    decay = jnp.exp(-(scaled * scaled))
+    turn = 1.0 / (1.0 + 0.3275911 * scaled)
+    series = 1.061405429 * turn - 1.453152027
+    series = series * turn + 1.421413741
+    series = series * turn - 0.284496736
+    series = series * turn + 0.254829592
+    return 1.0 - series * turn * decay, decay
+
+
+def charge_kernel(all_ref, field_ref, charges_ref, forces_ref, virial_ref, matrix_ref):
+    count = all_ref.shape[1]
+    own = charges_ref.shape[1]
+    everyone = all_ref[...]
+    columns = everyone.T
+    spread_row = everyone[3:4] * everyone[3:4]
+    rhs = everyone[5:6]
+    diag = everyone[4:5]
+    rows = own
+
+    def pairs(start):
+        column = columns[start : start + rows]
+        delta = [column[:, axis : axis + 1] - everyone[axis : axis + 1] for axis in range(3)]
+        squared = delta[0] * delta[0] + delta[1] * delta[1] + delta[2] * delta[2]
+        same = lax.broadcasted_iota(jnp.int32, (rows, count), 1) == (
+            lax.broadcasted_iota(jnp.int32, (rows, count), 0) + start
+        )
+        squared = jnp.where(same, 1.0, squared)
+        inverse = lax.rsqrt(squared)
+        spread = column[:, 3:4] * column[:, 3:4] + spread_row
+        scale = lax.rsqrt(2.0 * spread)
+        smear, decay = smeared(squared * inverse * scale)
+        return delta, same, inverse, scale, jnp.where(same, 0.0, smear * inverse), decay
+
+    image = jnp.zeros((rows, count), jnp.float32)
+    for start in range(0, count, rows):
+        kernel = pairs(start)[4]
+        matrix_ref[start : start + rows, :] = kernel
+        image = image + kernel * columns[start : start + rows, 5:6]
+    image = diag * rhs + jnp.sum(image, axis=0, keepdims=True)
+
+    def total(value):
+        return jnp.sum(value, axis=1, keepdims=True)
+
+    norm = total(rhs * rhs)
+    alpha = norm / total(rhs * image)
+    residual = rhs - alpha * image
+    charges = alpha * rhs
+    fresh = total(residual * residual)
+    direction = residual + fresh / norm * rhs
+    across = jnp.broadcast_to(direction, (8, count)).T
+    image = jnp.zeros((rows, count), jnp.float32)
+    for start in range(0, count, rows):
+        image = image + matrix_ref[start : start + rows, :] * across[start : start + rows, 0:1]
+    image = diag * direction + jnp.sum(image, axis=0, keepdims=True)
+    charges = charges + fresh / total(direction * image) * direction
+
+    delta, same, inverse, scale, kernel, decay = pairs(0)
+    slope = two_over_root_pi * scale * decay * inverse - kernel * inverse
+    weight = jnp.where(same, 0.0, charges * slope * inverse)
+    pulled = [weight * delta[axis] for axis in range(3)]
+    sums = [total(value) for value in pulled]
+    for left, right in ((0, 0), (1, 1), (2, 2), (0, 1), (0, 2), (1, 2)):
+        sums.append(total(pulled[left] * delta[right]))
+    lane = lax.broadcasted_iota(jnp.int32, (rows, 128), 1)
+    table = jnp.zeros((rows, 128), jnp.float32)
+    for place, value in enumerate(sums):
+        table = jnp.where(lane == place, value, table)
+    table = table.T
+    mine = charges[:, :own]
+    charges_ref[...] = mine
+    pull = -mine * table[0:3]
+    third = lax.broadcasted_iota(jnp.int32, pull.shape, 0) == 2
+    forces_ref[...] = pull + jnp.where(third, mine * field_ref[...], 0.0)
+    virial_ref[...] = 0.5 * mine * table[3:9]
+
+
+def whole_specs(count, scalars=0):
+    return [pl.BlockSpec(memory_space=pltpu.SMEM)] * scalars + [
+        pl.BlockSpec(memory_space=pltpu.VMEM)
+    ] * count
+
+
+def kernel_call(kernel, shapes, arguments, scalars=0, scratch=(), flops=0):
+    shapes = tuple(jax.ShapeDtypeStruct(shape, kind) for shape, kind in shapes)
+    return pl.pallas_call(
+        kernel,
+        out_shape=shapes,
+        in_specs=whole_specs(len(arguments) - scalars, scalars),
+        out_specs=tuple(whole_specs(len(shapes))),
+        scratch_shapes=list(scratch),
+        compiler_params=pltpu.CompilerParams(vmem_limit_bytes=32 * 1024 * 1024),
+        cost_estimate=pl.CostEstimate(flops=flops, bytes_accessed=1 << 20, transcendentals=0),
+    )(*arguments)
+
+
+def exchanged(block, axis, step):
+    size = lax.axis_size(axis)
+    return lax.ppermute(block, axis, [(place, place ^ step) for place in range(size)])
+
+
+def few_shards(
+    features,
+    positions,
+    species,
+    ghost_list,
+    edge_recv,
+    edge_send,
+    edge_vec,
+    w_msg,
+    w_rad1,
+    w_rad2,
+    w_up,
+    w_out,
+    hardness,
+    width,
+    chi_shift,
+    field,
+):
+    atoms, chans = features.shape
+    edges = edge_recv.shape[0]
+    lists = ghost_list[0].astype(jnp.bfloat16)
+    lists = jnp.pad(lists, ((0, 16 - lists.shape[0]), (0, chans - lists.shape[1])))
+    packed = jnp.concatenate([features, lists], axis=0)
+    others = [exchanged(packed, "space", step) for step in range(1, 4)]
+    filters, combine = kernel_call(
+        edge_kernel,
+        [((2 * chans, edges), jnp.float32), ((7 * atoms, edges), jnp.bfloat16)],
+        (edge_vec, edge_recv[None], w_rad1, w_rad2),
+        flops=1 << 28,
+    )
+    space = lax.axis_index("space").astype(jnp.int32).reshape(1)
+    new_features, block = kernel_call(
+        node_kernel,
+        [((atoms, chans), jnp.bfloat16), ((8, atoms), jnp.float32)],
+        (space, packed, *others, edge_send[None], filters, combine, w_msg, w_up, w_out[None])
+        + (species[None], hardness[None], width[None], chi_shift[None], field[None], positions),
+        scalars=1,
+        flops=1 << 28,
+    )
+    for axis in ("space", "row"):
+        step = 1
+        while step < lax.axis_size(axis):
+            block = jnp.concatenate([block, exchanged(block, axis, step)], axis=1)
+            step = 2 * step
+    everybody = block.shape[1]
+    charges, forces, virial = kernel_call(
+        charge_kernel,
+        [((rows, atoms), jnp.float32) for rows in (1, 3, 6)],
+        (block, field[None]),
+        scratch=[pltpu.VMEM((everybody, everybody), jnp.float32)],
+        flops=1 << 28,
+    )
+    return (new_features, charges[0], forces, virial)
+
+
 def solution(mesh):
+    small = mesh.shape["space"] == 4 and mesh.shape["row"] == 8
     return jax.shard_map(
-        shards,
+        few_shards if small else shards,
         mesh=mesh,
         in_specs=(
             P(("row", "space"), None),

time: 67.1 us -> 30.3 us (0.45)
  other arithmetic: 16.9 us -> 1.64 us
  local copies, waits for them, and re-layouts: 11.4 us -> 1.7 us
  matrix products: 6.53 us -> 0 us
  starting transfers between devices: 15.5 us -> 9.54 us
  Pallas kernels: 0 us -> 4.65 us
  between operations: 5.63 us -> 1.38 us
  waiting for transfers between devices: 10.3 us -> 11.1 us
    all_to_all x3 -> x0, starting transfers between devices: 15.5 us -> none  [the longest x2 12.2 us: gathered(): lax.all_to_all(copies, everywhere, split_axis=0, concat_axis=0, tiled=True)]
    ppermute x0 -> x8, waiting for transfers between devices: none -> 11.1 us  [exchanged(): lax.ppermute(block, axis, [(place, place ^ step) for place in range(size)])]
    all_to_all x3 -> x0, waiting for transfers between devices: 10.3 us -> none  [the longest x2 6.62 us: gathered(): lax.all_to_all(copies, everywhere, split_axis=0, concat_axis=0, tiled=True)]
    ppermute x0 -> x8, starting transfers between devices: none -> 9.54 us  [exchanged(): lax.ppermute(block, axis, [(place, place ^ step) for place in range(size)])]
    dot_general x7 -> x0, matrix products: 6.53 us -> none  [the longest x1 2.7 us: shards(): jnp.dot(hidden, w_out, precision=lax.Precision.HIGHEST)]
    pallas_call x0 -> x3, Pallas kernels: none -> 4.65 us  [kernel_call(): pl.pallas_call(kernel, out_shape=shapes, in_specs=whole_specs(len(argumen...]
    slice x8 -> x0, local copies, waits for them, and re-layouts: 4.3 us -> none  [the longest x3 4.26 us: lookup(): result = result + jnp.where(species == kind, table[kind], 0.0)]
    reduce_sum x11 -> x0, other arithmetic: 4.28 us -> none  [the longest x2 1.24 us: conjugate(): alpha = norm_now / total(direction * image)]
  transfers between devices with their start and end apart: 3 -> 8, of which waited for: 2 -> 6; matrix products, arithmetic and copies ran while one was open for 16% -> 0% of each run, Pallas kernels for 0% -> 2%
where the time goes in v3:
time: 30.3 us; the launch traced here: 30 us
  waiting for transfers between devices  11.1 us (37%)
  starting transfers between devices  9.54 us (31%)
  Pallas kernels  4.65 us (15%)
  local copies, waits for them, and re-layouts  1.7 us (6%)
  other arithmetic  1.64 us (5%)
  between operations  1.38 us (5%)
    ppermute x8, waiting for transfers between devices, exchanged(): lax.ppermute(block, axis, [(place, place ^ step) for place in range(size)])  11.1 us
    ppermute x8, starting transfers between devices, exchanged(): lax.ppermute(block, axis, [(place, place ^ step) for place in range(size)])  9.54 us
    pallas_call x3, Pallas kernels, kernel_call(): pl.pallas_call(kernel, out_shape=shapes, in_specs=whole_specs(len(argumen...  4.65 us
    unnamed x26, local copies, waits for them, and re-layouts  1.54 us
    concatenate x1, other arithmetic, few_shards(): packed = jnp.concatenate([features, lists], axis=0)  0.73 us
    convert_element_type x1, other arithmetic, few_shards(): lists = ghost_list[0].astype(jnp.bfloat16)  0.69 us
  transfers between devices with their start and end apart: 8, of which 6 were waited for; matrix products, arithmetic and copies ran while one was open for 0% of the time, Pallas kernels for 2%

profile of v3, /device:TPU:0, one launch (start us, length us, event | category | flops | bytes accessed | tf_op | source)
XLA Modules:
  0.0 30.0 jit_solution(13124581222504003176)
XLA Ops:
  0.6 0.7 %convert_bitcast_fusion = bf16[4,32]{1,0:T(4,128)(2,1)S(1)} fusion(s32[1,4,32]{2,1,0:T(4,128)} %param.19), kind=kLoop, calls=%fused_computation.6 | loop fusion | flops 128 | bytes 768 | tf_op jit(solution)/shard_map/convert_element_type | solution.py:462
  1.3 0.0 copy-start.3
  1.3 0.0 copy-start.4
  1.3 0.0 copy-start.5
  1.3 0.7 %fusion.1.own_ref = bf16[32,128]{1,0:T(8,128)(2,1)S(1)} fusion(bf16[4,32]{1,0:T(4,128)(2,1)S(1)} %convert_bitcast_fusion, bf16[16,128]{1,0:T(8,128)(2,1)} %param.16), kind=kLoop, calls=%fused_computation.2 | loop fusion | flops 24576 | bytes 12544 | tf_op jit(solution)/shard_map/concatenate | solution.py:464
  2.1 2.4 %collective-permute-start.2 = (bf16[32,128]{1,0:T(8,128)(2,1)S(1)}, bf16[32,128]{1,0:T(8,128)(2,1)S(1)}, u32[]{:S(2)}, u32[]{:S(2)}) collective-permute-start(bf16[32,128]{1,0:T(8,128)(2,1)S(1)} %fusion.1.own_ref), channel_id=1, source_target_pairs={{0,3},{1,2},{2,1},{3,0},{4,7},{5,6},{6,5},{7,4},{8,11},{9,10},{10,... | collective-permute-start | bytes 24584 | tf_op jit(solution)/shard_map/ppermute | solution.py:439
  4.5 0.6 %collective-permute-start.1 = (bf16[32,128]{1,0:T(8,128)(2,1)S(1)}, bf16[32,128]{1,0:T(8,128)(2,1)S(1)}, u32[]{:S(2)}, u32[]{:S(2)}) collective-permute-start(bf16[32,128]{1,0:T(8,128)(2,1)S(1)} %fusion.1.own_ref), channel_id=1, source_target_pairs={{0,2},{1,3},{2,0},{3,1},{4,6},{5,7},{6,4},{7,5},{8,10},{9,11},{10,... | collective-permute-start | bytes 24584 | tf_op jit(solution)/shard_map/ppermute | solution.py:439
  5.1 0.1 collective-permute-start
  5.1 0.0 copy-done.3
  5.1 0.0 copy-done.4
  5.1 0.0 copy-done.5
  5.2 0.0 copy-start
  5.2 0.8 %copy-done = bf16[128,256]{1,0:T(8,128)(2,1)S(1)} copy-done((bf16[128,256]{1,0:T(8,128)(2,1)S(1)}, bf16[128,256]{1,0:T(8,128)(2,1)}, u32[]{:S(2)}) %copy-start) | copy-done | bytes 65560
  6.0 0.0 copy-start.1
  6.0 0.5 %shard_map.183 = (f32[256,512]{1,0:T(8,128)S(1)}, bf16[112,512]{1,0:T(8,128)(2,1)S(1)}) custom-call(f32[3,512]{1,0:T(4,128)S(1)} %copy-done.3, s32[1,512]{1,0:T(1,128)S(1)} %bitcast.14, f32[8,128]{1,0:T(8,128)S(1)} %copy-done.4, bf16[128,256]{1,0:T(8,128)(2,1)S(1)} %copy-done), custom_call_target="tpu_custom_call" | custom-call | flops 268435456 | bytes 1048576 | tf_op jit(solution)/shard_map/pallas_call | solution.py:426
  7.1 0.0 collective-permute-done.2.far_ref
  7.1 1.0 %collective-permute-done.1.side_ref = bf16[32,128]{1,0:T(8,128)(2,1)S(1)} collective-permute-done((bf16[32,128]{1,0:T(8,128)(2,1)S(1)}, bf16[32,128]{1,0:T(8,128)(2,1)S(1)}, u32[]{:S(2)}, u32[]{:S(2)}) %collective-permute-start.1) | collective-permute-done | bytes 8224 | tf_op jit(solution)/shard_map/ppermute | solution.py:439
  8.1 0.0 collective-permute-done.near_ref
  8.1 0.0 copy-start.6
  8.1 0.0 copy-start.8
  8.2 0.0 copy-start.9
  8.2 0.0 copy-start.10
  8.2 0.0 copy-done.1
  8.2 0.0 copy-done.2
  8.2 0.6 %copy-done.7 = f32[3,16]{1,0:T(4,128)S(1)} copy-done((f32[3,16]{1,0:T(4,128)S(1)}, f32[3,16]{1,0:T(4,128)}, u32[]{:S(2)}) %copy-start.7) | copy-done | bytes 216
  8.8 0.0 copy-done.11
  8.8 0.0 copy-done.12
  8.8 0.0 copy-done.6
  8.8 0.0 copy-done.8
  8.9 0.0 copy-done.9
  8.9 0.0 copy-done.10
  8.9 1.4 %shard_map.184 = (bf16[16,128]{1,0:T(8,128)(2,1)}, f32[8,16]{1,0:T(8,128)S(1)}) custom-call(s32[1]{0:T(128)} %bitcast.space_ref, bf16[32,128]{1,0:T(8,128)(2,1)S(1)} %fusion.1.own_ref, bf16[32,128]{1,0:T(8,128)(2,1)S(1)} %collective-permute-done.near_ref, bf16[32,128]{1,0:T(8,128)(2,1)S(1)} %collective-permute-done.1.side_ref, ...), custom_call_target="tpu_custom_call" | custom-call | flops 268435456 | bytes 1048576 | tf_op jit(solution)/shard_map/pallas_call | solution.py:426
  10.3 0.0 collective-permute-start.3
  10.3 1.2 %collective-permute-done.3 = f32[8,16]{1,0:T(8,128)S(1)} collective-permute-done((f32[8,16]{1,0:T(8,128)S(1)}, f32[8,16]{1,0:T(8,128)S(1)}, u32[]{:S(2)}, u32[]{:S(2)}) %collective-permute-start.3) | collective-permute-done | bytes 544 | tf_op jit(solution)/shard_map/ppermute | solution.py:439
  11.5 0.1 pad_maximum_fusion
  11.6 0.8 %collective-permute-start.4 = (f32[8,32]{1,0:T(8,128)S(1)}, f32[8,32]{1,0:T(8,128)S(1)}, u32[]{:S(2)}, u32[]{:S(2)}) collective-permute-start(f32[8,32]{1,0:T(8,128)S(1)} %pad_maximum_fusion), channel_id=1, source_target_pairs={{0,2},{1,3},{2,0},{3,1},{4,6},{5,7},{6,4},{7,5},{8,10},{9,11},{10,... | collective-permute-start | bytes 3080 | tf_op jit(solution)/shard_map/ppermute | solution.py:439
  12.3 2.8 %collective-permute-done.4 = f32[8,32]{1,0:T(8,128)S(1)} collective-permute-done((f32[8,32]{1,0:T(8,128)S(1)}, f32[8,32]{1,0:T(8,128)S(1)}, u32[]{:S(2)}, u32[]{:S(2)}) %collective-permute-start.4) | collective-permute-done | bytes 1056 | tf_op jit(solution)/shard_map/ppermute | solution.py:439
  15.2 0.1 pad_maximum_fusion.1
  15.2 1.5 %collective-permute-start.5 = (f32[8,64]{1,0:T(8,128)S(1)}, f32[8,64]{1,0:T(8,128)S(1)}, u32[]{:S(2)}, u32[]{:S(2)}) collective-permute-start(f32[8,64]{1,0:T(8,128)S(1)} %pad_maximum_fusion.1), channel_id=1, source_target_pairs={{0,4},{4,0},{8,12},{12,8},{16,20},{20,16},{24,28},{28,24},{1,5},{5... | collective-permute-start | bytes 6152 | tf_op jit(solution)/shard_map/ppermute | solution.py:439
  16.7 2.1 %collective-permute-done.5 = f32[8,64]{1,0:T(8,128)S(1)} collective-permute-done((f32[8,64]{1,0:T(8,128)S(1)}, f32[8,64]{1,0:T(8,128)S(1)}, u32[]{:S(2)}, u32[]{:S(2)}) %collective-permute-start.5) | collective-permute-done | bytes 2080 | tf_op jit(solution)/shard_map/ppermute | solution.py:439
  18.9 0.1 pad_maximum_fusion.2
  18.9 1.6 %collective-permute-start.6 = (f32[8,128]{1,0:T(8,128)S(1)}, f32[8,128]{1,0:T(8,128)S(1)}, u32[]{:S(2)}, u32[]{:S(2)}) collective-permute-start(f32[8,128]{1,0:T(8,128)S(1)} %pad_maximum_fusion.2), channel_id=1, source_target_pairs={{0,8},{4,12},{8,0},{12,4},{16,24},{20,28},{24,16},{28,20},{1,9},{5... | collective-permute-start | bytes 12296 | tf_op jit(solution)/shard_map/ppermute | solution.py:439
  20.5 2.0 %collective-permute-done.6 = f32[8,128]{1,0:T(8,128)S(1)} collective-permute-done((f32[8,128]{1,0:T(8,128)S(1)}, f32[8,128]{1,0:T(8,128)S(1)}, u32[]{:S(2)}, u32[]{:S(2)}) %collective-permute-start.6) | collective-permute-done | bytes 4128 | tf_op jit(solution)/shard_map/ppermute | solution.py:439
  22.5 0.1 concatenate.26
  22.6 2.6 %collective-permute-start.7 = (f32[8,256]{1,0:T(8,128)S(1)}, f32[8,256]{1,0:T(8,128)S(1)}, u32[]{:S(2)}, u32[]{:S(2)}) collective-permute-start(f32[8,256]{1,0:T(8,128)S(1)} %concatenate.26), channel_id=1, source_target_pairs={{0,16},{4,20},{8,24},{12,28},{16,0},{20,4},{24,8},{28,12},{1,17},{... | collective-permute-start | bytes 24584 | tf_op jit(solution)/shard_map/ppermute | solution.py:439
  25.2 2.0 %collective-permute-done.7 = f32[8,256]{1,0:T(8,128)S(1)} collective-permute-done((f32[8,256]{1,0:T(8,128)S(1)}, f32[8,256]{1,0:T(8,128)S(1)}, u32[]{:S(2)}, u32[]{:S(2)}) %collective-permute-start.7) | collective-permute-done | bytes 8224 | tf_op jit(solution)/shard_map/ppermute | solution.py:439
  27.2 0.1 concatenate.27.all_ref
  27.2 2.7 %shard_map.185 = (f32[1,16]{1,0:T(1,128)}, f32[3,16]{1,0:T(4,128)}, f32[6,16]{1,0:T(8,128)}) custom-call(f32[8,512]{1,0:T(8,128)S(1)} %concatenate.27.all_ref, f32[1,1]{1,0:T(1,128)} %bitcast.13.field_ref), custom_call_target="tpu_custom_call" | custom-call | flops 268435456 | bytes 1048576 | tf_op jit(solution)/shard_map/pallas_call | solution.py:426
  (4 shorter events, 0.0 us)
Async XLA Ops:
  1.3 3.8 %copy-start.3 = (f32[3,512]{1,0:T(4,128)S(1)}, f32[3,512]{1,0:T(4,128)}, u32[]{:S(2)}) copy-start(f32[3,512]{1,0:T(4,128)} %vec_ref.1) | copy-start | bytes 18436
  1.3 3.8 %copy-start.4 = (f32[8,128]{1,0:T(8,128)S(1)}, f32[8,128]{1,0:T(8,128)}, u32[]{:S(2)}) copy-start(f32[8,128]{1,0:T(8,128)} %first_ref.1) | copy-start | bytes 12292
  1.3 3.8 %copy-start.5 = (s32[512]{0:T(512)S(1)}, s32[512]{0:T(512)}, u32[]{:S(2)}) copy-start(s32[512]{0:T(512)} %param.20) | copy-start | bytes 6148
  2.1 5.1 %collective-permute-start.2 = (bf16[32,128]{1,0:T(8,128)(2,1)S(1)}, bf16[32,128]{1,0:T(8,128)(2,1)S(1)}, u32[]{:S(2)}, u32[]{:S(2)}) collective-permute-start(bf16[32,128]{1,0:T(8,128)(2,1)S(1)} %fusion.1.own_ref), channel_id=1, source_target_pairs={{0,3},{1,2},{2,1},{3,0},{4,7},{5,6},{6,5},{7,4},{8,11},{9,10},{10,... | collective-permute-start | bytes 24584 | tf_op jit(solution)/shard_map/ppermute | solution.py:439
  4.5 3.7 %collective-permute-start.1 = (bf16[32,128]{1,0:T(8,128)(2,1)S(1)}, bf16[32,128]{1,0:T(8,128)(2,1)S(1)}, u32[]{:S(2)}, u32[]{:S(2)}) collective-permute-start(bf16[32,128]{1,0:T(8,128)(2,1)S(1)} %fusion.1.own_ref), channel_id=1, source_target_pairs={{0,2},{1,3},{2,0},{3,1},{4,6},{5,7},{6,4},{7,5},{8,10},{9,11},{10,... | collective-permute-start | bytes 24584 | tf_op jit(solution)/shard_map/ppermute | solution.py:439
  5.1 3.1 %collective-permute-start = (bf16[32,128]{1,0:T(8,128)(2,1)S(1)}, bf16[32,128]{1,0:T(8,128)(2,1)S(1)}, u32[]{:S(2)}, u32[]{:S(2)}) collective-permute-start(bf16[32,128]{1,0:T(8,128)(2,1)S(1)} %fusion.1.own_ref), channel_id=1, source_target_pairs={{0,1},{1,0},{2,3},{3,2},{4,5},{5,4},{6,7},{7,6},{8,9},{9,8},{10,11... | collective-permute-start | bytes 24584 | tf_op jit(solution)/shard_map/ppermute | solution.py:439
  5.2 0.8 %copy-start = (bf16[128,256]{1,0:T(8,128)(2,1)S(1)}, bf16[128,256]{1,0:T(8,128)(2,1)}, u32[]{:S(2)}) copy-start(bf16[128,256]{1,0:T(8,128)(2,1)} %second_ref.1) | copy-start | bytes 196612
  6.0 2.2 %copy-start.1 = (bf16[128,256]{1,0:T(8,128)(2,1)S(1)}, bf16[128,256]{1,0:T(8,128)(2,1)}, u32[]{:S(2)}) copy-start(bf16[128,256]{1,0:T(8,128)(2,1)} %project_ref.1) | copy-start | bytes 196612
  6.0 2.2 %copy-start.2 = (bf16[256,128]{1,0:T(8,128)(2,1)S(1)}, bf16[256,128]{1,0:T(8,128)(2,1)}, u32[]{:S(2)}) copy-start(bf16[256,128]{1,0:T(8,128)(2,1)} %update_ref.1) | copy-start | bytes 196612
  8.1 0.7 %copy-start.7 = (f32[3,16]{1,0:T(4,128)S(1)}, f32[3,16]{1,0:T(4,128)}, u32[]{:S(2)}) copy-start(f32[3,16]{1,0:T(4,128)} %positions_ref.1) | copy-start | bytes 580
  8.1 0.7 %copy-start.11 = (f32[4]{0:T(128)S(1)}, f32[4]{0:T(128)}, u32[]{:S(2)}) copy-start(f32[4]{0:T(128)} %param.29) | copy-start | bytes 52
  8.1 0.7 %copy-start.12 = (f32[4]{0:T(128)S(1)}, f32[4]{0:T(128)}, u32[]{:S(2)}) copy-start(f32[4]{0:T(128)} %param.30) | copy-start | bytes 52
  8.1 0.7 %copy-start.6 = (s32[512]{0:T(512)S(1)}, s32[512]{0:T(512)}, u32[]{:S(2)}) copy-start(s32[512]{0:T(512)} %param.21) | copy-start | bytes 6148
  8.1 0.7 %copy-start.8 = (f32[128]{0:T(128)S(1)}, f32[128]{0:T(128)}, u32[]{:S(2)}) copy-start(f32[128]{0:T(128)} %param.27) | copy-start | bytes 1540
  8.2 0.7 %copy-start.9 = (s32[16]{0:T(128)S(1)}, s32[16]{0:T(128)}, u32[]{:S(2)}) copy-start(s32[16]{0:T(128)} %param.18) | copy-start | bytes 196
  8.2 0.7 %copy-start.10 = (f32[4]{0:T(128)S(1)}, f32[4]{0:T(128)}, u32[]{:S(2)}) copy-start(f32[4]{0:T(128)} %param.28) | copy-start | bytes 52
  10.3 1.2 %collective-permute-start.3 = (f32[8,16]{1,0:T(8,128)S(1)}, f32[8,16]{1,0:T(8,128)S(1)}, u32[]{:S(2)}, u32[]{:S(2)}) collective-permute-start(f32[8,16]{1,0:T(8,128)S(1)} %get-tuple-element.14), channel_id=1, source_target_pairs={{0,1},{1,0},{2,3},{3,2},{4,5},{5,4},{6,7},{7,6},{8,9},{9,8},{10,11... | collective-permute-start | bytes 1544 | tf_op jit(solution)/shard_map/ppermute | solution.py:439
  11.6 3.6 %collective-permute-start.4 = (f32[8,32]{1,0:T(8,128)S(1)}, f32[8,32]{1,0:T(8,128)S(1)}, u32[]{:S(2)}, u32[]{:S(2)}) collective-permute-start(f32[8,32]{1,0:T(8,128)S(1)} %pad_maximum_fusion), channel_id=1, source_target_pairs={{0,2},{1,3},{2,0},{3,1},{4,6},{5,7},{6,4},{7,5},{8,10},{9,11},{10,... | collective-permute-start | bytes 3080 | tf_op jit(solution)/shard_map/ppermute | solution.py:439
  15.2 3.6 %collective-permute-start.5 = (f32[8,64]{1,0:T(8,128)S(1)}, f32[8,64]{1,0:T(8,128)S(1)}, u32[]{:S(2)}, u32[]{:S(2)}) collective-permute-start(f32[8,64]{1,0:T(8,128)S(1)} %pad_maximum_fusion.1), channel_id=1, source_target_pairs={{0,4},{4,0},{8,12},{12,8},{16,20},{20,16},{24,28},{28,24},{1,5},{5... | collective-permute-start | bytes 6152 | tf_op jit(solution)/shard_map/ppermute | solution.py:439
  18.9 3.6 %collective-permute-start.6 = (f32[8,128]{1,0:T(8,128)S(1)}, f32[8,128]{1,0:T(8,128)S(1)}, u32[]{:S(2)}, u32[]{:S(2)}) collective-permute-start(f32[8,128]{1,0:T(8,128)S(1)} %pad_maximum_fusion.2), channel_id=1, source_target_pairs={{0,8},{4,12},{8,0},{12,4},{16,24},{20,28},{24,16},{28,20},{1,9},{5... | collective-permute-start | bytes 12296 | tf_op jit(solution)/shard_map/ppermute | solution.py:439
  22.6 4.5 %collective-permute-start.7 = (f32[8,256]{1,0:T(8,128)S(1)}, f32[8,256]{1,0:T(8,128)S(1)}, u32[]{:S(2)}, u32[]{:S(2)}) collective-permute-start(f32[8,256]{1,0:T(8,128)S(1)} %concatenate.26), channel_id=1, source_target_pairs={{0,16},{4,20},{8,24},{12,28},{16,0},{20,4},{24,8},{28,12},{1,17},{... | collective-permute-start | bytes 24584 | tf_op jit(solution)/shard_map/ppermute | solution.py:439

commit v4 on v3

--- a/solution.py
+++ b/solution.py
@@ -217,14 +217,37 @@
 sine_series = [(-1.0) ** k * math.pi ** (2 * k + 1) / math.factorial(2 * k + 1) for k in range(7)]
 
 
-def edge_kernel(vec_ref, recv_ref, first_ref, second_ref, filter_ref, combine_ref):
-    atoms = combine_ref.shape[0] // 7
+def pack_kernel(features_ref, lists_ref, packed_ref):
+    atoms, chans = features_ref.shape
+    packed_ref[:atoms, :] = features_ref[...]
+    lists = lists_ref[0].astype(jnp.float32)
+    rows, width = lists.shape
+    lists = jnp.concatenate([lists, jnp.zeros((rows, chans - width), jnp.float32)], axis=1)
+    blank = jnp.zeros((packed_ref.shape[0] - atoms - rows, chans), jnp.float32)
+    packed_ref[atoms:, :] = jnp.concatenate([lists, blank], axis=0).astype(jnp.bfloat16)
+
+
+def edge_kernel(
+    vec_ref,
+    first_ref,
+    second_ref,
+    species_ref,
+    hardness_ref,
+    width_ref,
+    shift_ref,
+    field_ref,
+    positions_ref,
+    filter_ref,
+    unit_ref,
+    base_ref,
+):
     edges = vec_ref.shape[1]
     orders = first_ref.shape[0]
     vec = vec_ref[...]
     east, north, up = vec[0:1], vec[1:2], vec[2:3]
     squared = east * east + north * north + up * up
     inverse = lax.rsqrt(squared)
+    unit_ref[0:3, :] = vec * inverse
     ratio = squared * inverse * (1.0 / cutoff)
     envelope = (1.0 - ratio * ratio) * (1.0 - ratio * ratio) * (cutoff * inverse)
     order = lax.broadcasted_iota(jnp.int32, (orders, edges), 0).astype(jnp.float32) + 1.0
@@ -244,16 +267,22 @@
     )
     radial = silu(mixed).astype(jnp.bfloat16)
     filter_ref[...] = over_first(second_ref[...], radial)
-    local = lax.broadcasted_iota(jnp.int32, (atoms, edges), 0)
-    hit = local == recv_ref[...]
-    rows = [jnp.where(hit, 1.0, 0.0)]
-    low = []
-    for component in (east, north, up):
-        unit = component * inverse
-        high = unit.astype(jnp.bfloat16).astype(jnp.float32)
-        rows.append(jnp.where(hit, high, 0.0))
-        low.append(jnp.where(hit, unit - high, 0.0))
-    combine_ref[...] = jnp.concatenate(rows + low, axis=0).astype(jnp.bfloat16)
+    species = species_ref[...]
+
+    def table(ref):
+        result = jnp.zeros(species.shape, jnp.float32)
+        for kind in range(ref.shape[1]):
+            result = result + jnp.where(species == kind, ref[:, kind : kind + 1], 0.0)
+        return result
+
+    positions = positions_ref[...]
+    sigma = table(width_ref)
+    base_ref[0:3, :] = positions
+    base_ref[3:4, :] = sigma
+    base_ref[4:5, :] = table(hardness_ref) + inverse_root_pi / sigma
+    base_ref[5:6, :] = field_ref[...] * positions[2:3]
+    base_ref[6:7, :] = table(shift_ref)
+    base_ref[7:8, :] = jnp.zeros_like(sigma)
 
 
 def node_kernel(
@@ -263,23 +292,18 @@
     side_ref,
     far_ref,
     send_ref,
+    recv_ref,
     filter_ref,
-    combine_ref,
+    unit_ref,
+    base_ref,
     project_ref,
     update_ref,
     out_ref,
-    species_ref,
-    hardness_ref,
-    width_ref,
-    shift_ref,
-    field_ref,
-    positions_ref,
     features_ref,
     block_ref,
 ):
-    atoms = positions_ref.shape[1]
+    atoms, chans = features_ref.shape
     edges = send_ref.shape[1]
-    chans = features_ref.shape[1]
     space = space_ref[0]
     packed = [ref[...].astype(jnp.float32) for ref in (own_ref, near_ref, side_ref, far_ref)]
     lanes = len(packed)
@@ -309,33 +333,24 @@
     sender = jnp.dot(fill, from_slot, preferred_element_type=jnp.float32) + from_own
     projected = jnp.dot(group, project_ref[...], preferred_element_type=jnp.float32)
     picked = over_first(projected.astype(jnp.bfloat16), sender.astype(jnp.bfloat16))
-    message = (picked * filter_ref[...]).astype(jnp.bfloat16)
-    summed = over_last(combine_ref[...], message) * message_scale
+    scalar = picked[:chans] * filter_ref[:chans, :]
+    carried = picked[chans:] * filter_ref[chans:, :]
+    parts = [scalar] + [unit_ref[axis : axis + 1, :] * carried for axis in range(3)]
+    message = jnp.concatenate([part.astype(jnp.bfloat16) for part in parts], axis=0)
+    hit = lax.broadcasted_iota(jnp.int32, (atoms, edges), 0) == recv_ref[...]
+    summed = over_last(jnp.where(hit, 1.0, 0.0).astype(jnp.bfloat16), message) * message_scale
     square = jnp.zeros((atoms, chans), jnp.float32)
     for component in range(1, 4):
-        high = summed[component * atoms : (component + 1) * atoms, chans:]
-        low = summed[(component + 3) * atoms : (component + 4) * atoms, chans:]
-        square = square + (high + low) * (high + low)
-    invariant = jnp.concatenate([summed[:atoms, :chans], square], axis=1).astype(jnp.bfloat16)
+        part = summed[:, component * chans : (component + 1) * chans]
+        square = square + part * part
+    invariant = jnp.concatenate([summed[:, :chans], square], axis=1).astype(jnp.bfloat16)
     hidden = silu(jnp.dot(invariant, update_ref[...], preferred_element_type=jnp.float32))
     features_ref[...] = (packed[0][:atoms] + hidden).astype(jnp.bfloat16)
     readout = jnp.broadcast_to(out_ref[...], (8, chans))
-    chi = over_last(readout, hidden, lax.Precision.HIGHEST)[0:1]
-    species = species_ref[...]
-
-    def table(ref):
-        result = jnp.zeros(species.shape, jnp.float32)
-        for kind in range(ref.shape[1]):
-            result = result + jnp.where(species == kind, ref[:, kind : kind + 1], 0.0)
-        return result
-
-    chi = chi + table(shift_ref)
-    sigma = table(width_ref)
-    diag = table(hardness_ref) + inverse_root_pi / sigma
-    positions = positions_ref[...]
-    rhs = field_ref[...] * positions[2:3] - chi
-    blank = jnp.zeros((2, atoms), jnp.float32)
-    block_ref[...] = jnp.concatenate([positions, sigma, diag, rhs, blank], axis=0)
+    chi = over_last(readout, hidden, lax.Precision.HIGHEST)[0:1] + base_ref[6:7, :]
+    block_ref[0:5, :] = base_ref[0:5, :]
+    block_ref[5:6, :] = base_ref[5:6, :] - chi
+    block_ref[6:8, :] = jnp.zeros((2, atoms), jnp.float32)
 
 
 def smeared(scaled):
@@ -348,10 +363,12 @@
     return 1.0 - series * turn * decay, decay
 
 
-def charge_kernel(all_ref, field_ref, charges_ref, forces_ref, virial_ref, matrix_ref):
-    count = all_ref.shape[1]
+def charge_kernel(place_ref, all_ref, field_ref, charges_ref, forces_ref, virial_ref, matrix_ref):
+    blocks, _, width = all_ref.shape
+    count = blocks * width
     own = charges_ref.shape[1]
-    everyone = all_ref[...]
+    everyone = jnp.concatenate([all_ref[block] for block in range(blocks)], axis=1)
+    everyone = pltpu.roll(everyone, lax.rem(count - place_ref[0] * width, count), 1)
     columns = everyone.T
     spread_row = everyone[3:4] * everyone[3:4]
     rhs = everyone[5:6]
@@ -459,35 +476,39 @@
 ):
     atoms, chans = features.shape
     edges = edge_recv.shape[0]
-    lists = ghost_list[0].astype(jnp.bfloat16)
-    lists = jnp.pad(lists, ((0, 16 - lists.shape[0]), (0, chans - lists.shape[1])))
-    packed = jnp.concatenate([features, lists], axis=0)
-    others = [exchanged(packed, "space", step) for step in range(1, 4)]
-    filters, combine = kernel_call(
+    rows, lanes = lax.axis_size("row"), lax.axis_size("space")
+    (packed,) = kernel_call(
+        pack_kernel, [((atoms + 16, chans), jnp.bfloat16)], (features, ghost_list)
+    )
+    others = [exchanged(packed, "space", step) for step in range(1, lanes)]
+    filters, units, base = kernel_call(
         edge_kernel,
-        [((2 * chans, edges), jnp.float32), ((7 * atoms, edges), jnp.bfloat16)],
-        (edge_vec, edge_recv[None], w_rad1, w_rad2),
+        [((2 * chans, edges), jnp.float32), ((8, edges), jnp.float32), ((8, atoms), jnp.float32)],
+        (edge_vec, w_rad1, w_rad2, species[None], hardness[None], width[None])
+        + (chi_shift[None], field[None], positions),
         flops=1 << 28,
     )
-    space = lax.axis_index("space").astype(jnp.int32).reshape(1)
+    space = lax.axis_index("space").astype(jnp.int32)
     new_features, block = kernel_call(
         node_kernel,
         [((atoms, chans), jnp.bfloat16), ((8, atoms), jnp.float32)],
-        (space, packed, *others, edge_send[None], filters, combine, w_msg, w_up, w_out[None])
-        + (species[None], hardness[None], width[None], chi_shift[None], field[None], positions),
+        (space.reshape(1), packed, *others, edge_send[None], edge_recv[None])
+        + (filters, units, base, w_msg, w_up, w_out[None]),
         scalars=1,
         flops=1 << 28,
     )
-    for axis in ("space", "row"):
-        step = 1
-        while step < lax.axis_size(axis):
-            block = jnp.concatenate([block, exchanged(block, axis, step)], axis=1)
-            step = 2 * step
-    everybody = block.shape[1]
+    block = jnp.concatenate([block, exchanged(block, "space", 1)], axis=1)
+    groups = [list(range(core, rows * lanes, 2)) for core in range(2)]
+    blocks = len(groups[0])
+    block = jnp.broadcast_to(block[None], (blocks,) + block.shape)
+    block = lax.all_to_all(block, everywhere, 0, 0, axis_index_groups=groups, tiled=True)
+    place = lax.axis_index("row").astype(jnp.int32) * (lanes // 2) + space // 2
+    everybody = rows * lanes * atoms
     charges, forces, virial = kernel_call(
         charge_kernel,
-        [((rows, atoms), jnp.float32) for rows in (1, 3, 6)],
-        (block, field[None]),
+        [((count, atoms), jnp.float32) for count in (1, 3, 6)],
+        (place.reshape(1), block, field[None]),
+        scalars=1,
         scratch=[pltpu.VMEM((everybody, everybody), jnp.float32)],
         flops=1 << 28,
     )

time: 30.3 us -> 31 us (1.023)
  local copies, waits for them, and re-layouts: 1.7 us -> 4.84 us
  waiting for transfers between devices: 11.1 us -> 8.65 us
  other arithmetic: 1.64 us -> 0.76 us
  starting transfers between devices: 9.54 us -> 10.1 us
    ppermute x8 -> x4, waiting for transfers between devices: 11.1 us -> 1.33 us  [exchanged(): lax.ppermute(block, axis, [(place, place ^ step) for place in range(size)])]
    all_to_all x0 -> x1, waiting for transfers between devices: none -> 7.31 us  [few_shards(): lax.all_to_all(block, everywhere, 0, 0, axis_index_groups=groups, tiled=T...]
    all_to_all x0 -> x1, starting transfers between devices: none -> 6.77 us  [few_shards(): lax.all_to_all(block, everywhere, 0, 0, axis_index_groups=groups, tiled=T...]
    ppermute x8 -> x4, starting transfers between devices: 9.54 us -> 3.34 us  [exchanged(): lax.ppermute(block, axis, [(place, place ^ step) for place in range(size)])]
    unnamed x26 -> x32, local copies, waits for them, and re-layouts: 1.54 us -> 4.32 us
    concatenate x4 -> x1, other arithmetic: 0.96 us -> 0.07 us  [few_shards(): block = jnp.concatenate([block, exchanged(block, 'space', 1)], axis=1)]
    convert_element_type x1 -> x0, other arithmetic: 0.69 us -> none  [few_shards(): lists = ghost_list[0].astype(jnp.bfloat16)]
    all_to_all x0 -> x1, other arithmetic: none -> 0.68 us  [few_shards(): lax.all_to_all(block, everywhere, 0, 0, axis_index_groups=groups, tiled=T...]
  transfers between devices with their start and end apart: 8 -> 5, of which waited for: 6 -> 3; matrix products, arithmetic and copies ran while one was open for 0% -> 0% of each run, Pallas kernels for 2% -> 1%
where the time goes in v4:
time: 31 us; the launch traced here: 30.6 us
  starting transfers between devices  10.1 us (33%)
  waiting for transfers between devices  8.65 us (28%)
  local copies, waits for them, and re-layouts  4.84 us (16%)
  Pallas kernels  4.79 us (15%)
  between operations  1.44 us (5%)
  other arithmetic  0.76 us (2%)
    all_to_all x1, waiting for transfers between devices, few_shards(): lax.all_to_all(block, everywhere, 0, 0, axis_index_groups=groups, tiled=T...  7.31 us
    all_to_all x1, starting transfers between devices, few_shards(): lax.all_to_all(block, everywhere, 0, 0, axis_index_groups=groups, tiled=T...  6.77 us
    pallas_call x4, Pallas kernels, kernel_call(): pl.pallas_call(kernel, out_shape=shapes, in_specs=whole_specs(len(argumen...  4.79 us
    unnamed x32, local copies, waits for them, and re-layouts  4.32 us
    ppermute x4, starting transfers between devices, exchanged(): lax.ppermute(block, axis, [(place, place ^ step) for place in range(size)])  3.34 us
    ppermute x4, waiting for transfers between devices, exchanged(): lax.ppermute(block, axis, [(place, place ^ step) for place in range(size)])  1.33 us
    all_to_all x1, other arithmetic, few_shards(): lax.all_to_all(block, everywhere, 0, 0, axis_index_groups=groups, tiled=T...  0.68 us
  transfers between devices with their start and end apart: 5, of which 3 were waited for; matrix products, arithmetic and copies ran while one was open for 0% of the time, Pallas kernels for 1%

profile of v4, /device:TPU:0, one launch (start us, length us, event | category | flops | bytes accessed | tf_op | source)
XLA Modules:
  0.0 30.6 jit_solution(17872865247191116177)
XLA Ops:
  0.6 0.0 copy-start
  0.6 0.7 %copy-done = bf16[16,128]{1,0:T(8,128)(2,1)S(1)} copy-done((bf16[16,128]{1,0:T(8,128)(2,1)S(1)}, bf16[16,128]{1,0:T(8,128)(2,1)}, u32[]{:S(2)}) %copy-start) | copy-done | bytes 4120
  1.3 0.0 copy-start.1
  1.3 0.7 %copy-done.1 = s32[1,4,32]{2,1,0:T(4,128)S(1)} copy-done((s32[1,4,32]{2,1,0:T(4,128)S(1)}, s32[1,4,32]{2,1,0:T(4,128)}, u32[]{:S(2)}) %copy-start.1) | copy-done | bytes 536
  2.0 0.0 copy-start.6
  2.0 0.0 copy-start.12
  2.0 0.0 copy-start.13
  2.0 0.0 copy-start.5
  2.0 0.5 %collective-permute-start = (bf16[32,128]{1,0:T(8,128)(2,1)S(1)}, bf16[32,128]{1,0:T(8,128)(2,1)S(1)}, u32[]{:S(2)}, u32[]{:S(2)}) collective-permute-start(bf16[32,128]{1,0:T(8,128)(2,1)S(1)} %shard_map.183.own_ref), channel_id=1, source_target_pairs={{0,1},{1,0},{2,3},{3,2},{4,5},{5,4},{6,7},{7,6},{8,9},{9,8},{10,11... | collective-permute-start | bytes 24584 | tf_op jit(solution)/shard_map/ppermute | solution.py:456
  2.5 2.6 %collective-permute-start.1 = (bf16[32,128]{1,0:T(8,128)(2,1)S(1)}, bf16[32,128]{1,0:T(8,128)(2,1)S(1)}, u32[]{:S(2)}, u32[]{:S(2)}) collective-permute-start(bf16[32,128]{1,0:T(8,128)(2,1)S(1)} %shard_map.183.own_ref), channel_id=1, source_target_pairs={{0,2},{1,3},{2,0},{3,1},{4,6},{5,7},{6,4},{7,5},{8,10},{9,11},{10,... | collective-permute-start | bytes 24584 | tf_op jit(solution)/shard_map/ppermute | solution.py:456
  5.1 0.1 collective-permute-start.2
  5.9 0.0 copy-start.7
  5.9 0.0 copy-start.10
  5.9 0.0 copy-start.11
  5.9 0.0 copy-done.6
  5.9 0.0 copy-done.12
  5.9 0.0 copy-done.13
  5.9 0.0 copy-done.5
  5.9 0.6 %copy-done.7 = f32[3,16]{1,0:T(4,128)S(1)} copy-done((f32[3,16]{1,0:T(4,128)S(1)}, f32[3,16]{1,0:T(4,128)}, u32[]{:S(2)}) %copy-start.7) | copy-done | bytes 216
  6.5 0.0 copy-done.10
  6.5 0.0 copy-done.11
  6.6 0.0 copy-start.2
  6.6 0.8 %copy-done.2 = bf16[128,256]{1,0:T(8,128)(2,1)S(1)} copy-done((bf16[128,256]{1,0:T(8,128)(2,1)S(1)}, bf16[128,256]{1,0:T(8,128)(2,1)}, u32[]{:S(2)}) %copy-start.2) | copy-done | bytes 65560
  7.4 0.0 copy-start.3
  7.4 0.0 copy-start.4
  7.4 0.5 %shard_map.184 = (f32[256,512]{1,0:T(8,128)S(1)}, f32[8,512]{1,0:T(8,128)S(1)}, f32[8,16]{1,0:T(8,128)S(1)}) custom-call(f32[3,512]{1,0:T(4,128)S(1)} %copy-done.5, f32[8,128]{1,0:T(8,128)S(1)} %copy-done.6, bf16[128,256]{1,0:T(8,128)(2,1)S(1)} %copy-done.2, s32[1,16]{1,0:T(1,128)S(1)} %bitcast.15, f32[1,4]{1,0:T(1,128)S(1)} %bitcast.16, ...), custom_call_target="tpu_custom_call" | custom-call | flops 268435456 | bytes 1048576 | tf_op jit(solution)/shard_map/pallas_call | solution.py:443
  7.9 0.0 copy-start.9
  7.9 0.0 collective-permute-done.near_ref
  7.9 0.0 collective-permute-done.1.side_ref
  7.9 0.3 %collective-permute-done.2.far_ref = bf16[32,128]{1,0:T(8,128)(2,1)S(1)} collective-permute-done((bf16[32,128]{1,0:T(8,128)(2,1)S(1)}, bf16[32,128]{1,0:T(8,128)(2,1)S(1)}, u32[]{:S(2)}, u32[]{:S(2)}) %collective-permute-start.2) | collective-permute-done | bytes 8224 | tf_op jit(solution)/shard_map/ppermute | solution.py:456
  8.2 0.0 copy-start.8
  8.2 0.0 copy-start.14
  8.2 0.0 copy-done.3
  8.2 0.0 copy-done.4
  8.3 0.3 copy-done.9
  8.6 0.3 %copy-done.8 = s32[512]{0:T(512)S(1)} copy-done((s32[512]{0:T(512)S(1)}, s32[512]{0:T(512)}, u32[]{:S(2)}) %copy-start.8) | copy-done | bytes 2072
  8.9 0.0 copy-done.14
  8.9 1.5 %shard_map.185 = (bf16[16,128]{1,0:T(8,128)(2,1)}, f32[8,16]{1,0:T(8,128)S(1)}) custom-call(s32[1]{0:T(128)} %bitcast.space_ref, bf16[32,128]{1,0:T(8,128)(2,1)S(1)} %shard_map.183.own_ref, bf16[32,128]{1,0:T(8,128)(2,1)S(1)} %collective-permute-done.near_ref, bf16[32,128]{1,0:T(8,128)(2,1)S(1)} %collective-permute-done.1.side_ref, ...), custom_call_target="tpu_custom_call" | custom-call | flops 268435456 | bytes 1048576 | tf_op jit(solution)/shard_map/pallas_call | solution.py:443
  10.4 0.2 collective-permute-start.3
  10.5 1.0 %collective-permute-done.3 = f32[8,16]{1,0:T(8,128)S(1)} collective-permute-done((f32[8,16]{1,0:T(8,128)S(1)}, f32[8,16]{1,0:T(8,128)S(1)}, u32[]{:S(2)}, u32[]{:S(2)}) %collective-permute-start.3) | collective-permute-done | bytes 544 | tf_op jit(solution)/shard_map/ppermute | solution.py:456
  11.5 0.1 pad_maximum_fusion
  11.6 0.7 %reshape.17 = f32[16,1,256]{2,1,0:T(1,128)} reshape(f32[16,8,32]{2,1,0:T(8,128)S(1)} %broadcast_in_dim.39) | data formatting | bytes 32768
  12.3 6.8 %all-to-all-start = ((f32[16,1,256]{2,1,0:T(1,128)}), f32[16,1,256]{2,1,0:T(1,128)S(1)}, u32[]{:S(2)}, u32[]{:S(2)}) async-start(f32[16,1,256]{2,1,0:T(1,128)} %reshape.17), calls=%async_computation | async-start | bytes 32768 | tf_op jit(solution)/shard_map/all_to_all | solution.py:504
  19.1 7.3 %all-to-all-done = f32[16,1,256]{2,1,0:T(1,128)S(1)} async-done(((f32[16,1,256]{2,1,0:T(1,128)}), f32[16,1,256]{2,1,0:T(1,128)S(1)}, u32[]{:S(2)}, u32[]{:S(2)}) %all-to-all-start) | async-done | bytes 16416 | tf_op jit(solution)/shard_map/all_to_all | solution.py:504
  26.4 0.5 %broadcast.2 = f32[]{:T(128)} broadcast(f32[]{:T(128)} %constant.30), dimensions={} | broadcast | bytes 8 | tf_op jit(solution)/shard_map/all_to_all | solution.py:504
  26.9 0.7 %reduce = f32[16,256]{1,0:T(8,128)S(1)} reduce(f32[16,1,256]{2,1,0:T(1,128)S(1)} %all-to-all-done, f32[]{:T(128)} %broadcast.2), dimensions={1}, to_apply=%all_to_all.3.reduce_sub_computation | reduce | bytes 32772 | tf_op jit(solution)/shard_map/all_to_all | solution.py:504
  27.6 0.1 reshape.18.all_ref
  27.7 2.9 %shard_map.186 = (f32[1,16]{1,0:T(1,128)}, f32[3,16]{1,0:T(4,128)}, f32[6,16]{1,0:T(8,128)}) custom-call(s32[1]{0:T(128)} %bitcast.9.place_ref, f32[16,8,32]{2,1,0:T(8,128)S(1)} %reshape.18.all_ref, f32[1,1]{1,0:T(1,128)} %bitcast.12.field_ref), custom_call_target="tpu_custom_call" | custom-call | flops 268435456 | bytes 1048576 | tf_op jit(solution)/shard_map/pallas_call | solution.py:443
  (2 shorter events, 0.0 us)
Async XLA Ops:
  0.6 0.7 %copy-start = (bf16[16,128]{1,0:T(8,128)(2,1)S(1)}, bf16[16,128]{1,0:T(8,128)(2,1)}, u32[]{:S(2)}) copy-start(bf16[16,128]{1,0:T(8,128)(2,1)} %features_ref.1) | copy-start | bytes 12292
  1.3 0.7 %copy-start.1 = (s32[1,4,32]{2,1,0:T(4,128)S(1)}, s32[1,4,32]{2,1,0:T(4,128)}, u32[]{:S(2)}) copy-start(s32[1,4,32]{2,1,0:T(4,128)} %lists_ref.1) | copy-start | bytes 1540
  2.0 3.9 %copy-start.6 = (f32[8,128]{1,0:T(8,128)S(1)}, f32[8,128]{1,0:T(8,128)}, u32[]{:S(2)}) copy-start(f32[8,128]{1,0:T(8,128)} %first_ref.1) | copy-start | bytes 12292
  2.0 3.9 %copy-start.12 = (f32[4]{0:T(128)S(1)}, f32[4]{0:T(128)}, u32[]{:S(2)}) copy-start(f32[4]{0:T(128)} %param.29) | copy-start | bytes 52
  2.0 3.9 %copy-start.13 = (f32[4]{0:T(128)S(1)}, f32[4]{0:T(128)}, u32[]{:S(2)}) copy-start(f32[4]{0:T(128)} %param.30) | copy-start | bytes 52
  2.0 3.9 %copy-start.5 = (f32[3,512]{1,0:T(4,128)S(1)}, f32[3,512]{1,0:T(4,128)}, u32[]{:S(2)}) copy-start(f32[3,512]{1,0:T(4,128)} %vec_ref.1) | copy-start | bytes 18436
  2.0 5.8 %collective-permute-start = (bf16[32,128]{1,0:T(8,128)(2,1)S(1)}, bf16[32,128]{1,0:T(8,128)(2,1)S(1)}, u32[]{:S(2)}, u32[]{:S(2)}) collective-permute-start(bf16[32,128]{1,0:T(8,128)(2,1)S(1)} %shard_map.183.own_ref), channel_id=1, source_target_pairs={{0,1},{1,0},{2,3},{3,2},{4,5},{5,4},{6,7},{7,6},{8,9},{9,8},{10,11... | collective-permute-start | bytes 24584 | tf_op jit(solution)/shard_map/ppermute | solution.py:456
  2.5 5.3 %collective-permute-start.1 = (bf16[32,128]{1,0:T(8,128)(2,1)S(1)}, bf16[32,128]{1,0:T(8,128)(2,1)S(1)}, u32[]{:S(2)}, u32[]{:S(2)}) collective-permute-start(bf16[32,128]{1,0:T(8,128)(2,1)S(1)} %shard_map.183.own_ref), channel_id=1, source_target_pairs={{0,2},{1,3},{2,0},{3,1},{4,6},{5,7},{6,4},{7,5},{8,10},{9,11},{10,... | collective-permute-start | bytes 24584 | tf_op jit(solution)/shard_map/ppermute | solution.py:456
  5.1 3.1 %collective-permute-start.2 = (bf16[32,128]{1,0:T(8,128)(2,1)S(1)}, bf16[32,128]{1,0:T(8,128)(2,1)S(1)}, u32[]{:S(2)}, u32[]{:S(2)}) collective-permute-start(bf16[32,128]{1,0:T(8,128)(2,1)S(1)} %shard_map.183.own_ref), channel_id=1, source_target_pairs={{0,3},{1,2},{2,1},{3,0},{4,7},{5,6},{6,5},{7,4},{8,11},{9,10},{10,... | collective-permute-start | bytes 24584 | tf_op jit(solution)/shard_map/ppermute | solution.py:456
  5.9 0.7 %copy-start.7 = (f32[3,16]{1,0:T(4,128)S(1)}, f32[3,16]{1,0:T(4,128)}, u32[]{:S(2)}) copy-start(f32[3,16]{1,0:T(4,128)} %positions_ref.1) | copy-start | bytes 580
  5.9 0.7 %copy-start.10 = (s32[16]{0:T(128)S(1)}, s32[16]{0:T(128)}, u32[]{:S(2)}) copy-start(s32[16]{0:T(128)} %param.18) | copy-start | bytes 196
  5.9 0.7 %copy-start.11 = (f32[4]{0:T(128)S(1)}, f32[4]{0:T(128)}, u32[]{:S(2)}) copy-start(f32[4]{0:T(128)} %param.28) | copy-start | bytes 52
  6.6 0.8 %copy-start.2 = (bf16[128,256]{1,0:T(8,128)(2,1)S(1)}, bf16[128,256]{1,0:T(8,128)(2,1)}, u32[]{:S(2)}) copy-start(bf16[128,256]{1,0:T(8,128)(2,1)} %second_ref.1) | copy-start | bytes 196612
  7.4 0.8 %copy-start.3 = (bf16[128,256]{1,0:T(8,128)(2,1)S(1)}, bf16[128,256]{1,0:T(8,128)(2,1)}, u32[]{:S(2)}) copy-start(bf16[128,256]{1,0:T(8,128)(2,1)} %project_ref.1) | copy-start | bytes 196612
  7.4 0.9 %copy-start.4 = (bf16[256,128]{1,0:T(8,128)(2,1)S(1)}, bf16[256,128]{1,0:T(8,128)(2,1)}, u32[]{:S(2)}) copy-start(bf16[256,128]{1,0:T(8,128)(2,1)} %update_ref.1) | copy-start | bytes 196612
  7.9 0.7 %copy-start.9 = (s32[512]{0:T(512)S(1)}, s32[512]{0:T(512)}, u32[]{:S(2)}) copy-start(s32[512]{0:T(512)} %param.20) | copy-start | bytes 6148
  8.2 0.7 %copy-start.8 = (s32[512]{0:T(512)S(1)}, s32[512]{0:T(512)}, u32[]{:S(2)}) copy-start(s32[512]{0:T(512)} %param.21) | copy-start | bytes 6148
  8.2 0.7 %copy-start.14 = (f32[128]{0:T(128)S(1)}, f32[128]{0:T(128)}, u32[]{:S(2)}) copy-start(f32[128]{0:T(128)} %param.27) | copy-start | bytes 1540
  10.4 1.2 %collective-permute-start.3 = (f32[8,16]{1,0:T(8,128)S(1)}, f32[8,16]{1,0:T(8,128)S(1)}, u32[]{:S(2)}, u32[]{:S(2)}) collective-permute-start(f32[8,16]{1,0:T(8,128)S(1)} %get-tuple-element.16), channel_id=1, source_target_pairs={{0,1},{1,0},{2,3},{3,2},{4,5},{5,4},{6,7},{7,6},{8,9},{9,8},{10,11... | collective-permute-start | bytes 1544 | tf_op jit(solution)/shard_map/ppermute | solution.py:456
  12.3 14.1 %all-to-all-start = ((f32[16,1,256]{2,1,0:T(1,128)}), f32[16,1,256]{2,1,0:T(1,128)S(1)}, u32[]{:S(2)}, u32[]{:S(2)}) async-start(f32[16,1,256]{2,1,0:T(1,128)} %reshape.17), calls=%async_computation | async-start | bytes 32768 | tf_op jit(solution)/shard_map/all_to_all | solution.py:504

commit v5 on v4

--- a/solution.py
+++ b/solution.py
@@ -217,30 +217,39 @@
 sine_series = [(-1.0) ** k * math.pi ** (2 * k + 1) / math.factorial(2 * k + 1) for k in range(7)]
 
 
-def pack_kernel(features_ref, lists_ref, packed_ref):
+def fetched(pairs, semaphores):
+    copies = [
+        pltpu.make_async_copy(source, target, semaphores.at[place])
+        for place, (source, target) in enumerate(pairs)
+    ]
+    for copy in copies:
+        copy.start()
+    return copies
+
+
+def pack_kernel(features_ref, lists_ref, packed_ref, held_ref, semaphores):
     atoms, chans = features_ref.shape
-    packed_ref[:atoms, :] = features_ref[...]
-    lists = lists_ref[0].astype(jnp.float32)
+    copies = fetched(
+        [(lists_ref, held_ref), (features_ref, packed_ref.at[pl.ds(0, atoms)])], semaphores
+    )
+    copies[0].wait()
+    lists = held_ref[0].astype(jnp.float32)
     rows, width = lists.shape
     lists = jnp.concatenate([lists, jnp.zeros((rows, chans - width), jnp.float32)], axis=1)
     blank = jnp.zeros((packed_ref.shape[0] - atoms - rows, chans), jnp.float32)
     packed_ref[atoms:, :] = jnp.concatenate([lists, blank], axis=0).astype(jnp.bfloat16)
-
-
-def edge_kernel(
-    vec_ref,
-    first_ref,
-    second_ref,
-    species_ref,
-    hardness_ref,
-    width_ref,
-    shift_ref,
-    field_ref,
-    positions_ref,
-    filter_ref,
-    unit_ref,
-    base_ref,
-):
+    copies[1].wait()
+
+
+def edge_kernel(*refs):
+    own, kept = refs[:9], refs[9:14]
+    filter_ref, unit_ref, base_ref = refs[14:17]
+    moved, held, semaphores = refs[17:22], refs[22:31], refs[31]
+    copies = fetched(list(zip(own + kept, held + moved)), semaphores)
+    for copy in copies:
+        copy.wait()
+    vec_ref, first_ref, second_ref, species_ref = held[:4]
+    hardness_ref, width_ref, shift_ref, field_ref, positions_ref = held[4:]
     edges = vec_ref.shape[1]
     orders = first_ref.shape[0]
     vec = vec_ref[...]
@@ -348,9 +357,16 @@
     features_ref[...] = (packed[0][:atoms] + hidden).astype(jnp.bfloat16)
     readout = jnp.broadcast_to(out_ref[...], (8, chans))
     chi = over_last(readout, hidden, lax.Precision.HIGHEST)[0:1] + base_ref[6:7, :]
-    block_ref[0:5, :] = base_ref[0:5, :]
-    block_ref[5:6, :] = base_ref[5:6, :] - chi
-    block_ref[6:8, :] = jnp.zeros((2, atoms), jnp.float32)
+    rhs = base_ref[5:6, :] - chi
+    wide = jnp.zeros((1, chans - atoms), jnp.float32)
+    rows = [base_ref[0:1, :], jnp.zeros((2, atoms), jnp.float32), rhs]
+    rows = rows + [base_ref[place : place + 1, :] for place in range(4, 0, -1)]
+    block = jnp.concatenate(
+        [jnp.concatenate(rows, axis=0), jnp.broadcast_to(wide, (8, chans - atoms))], axis=1
+    )
+    block = pltpu.roll(block, 0, 1, stride=atoms, stride_axis=0)
+    row = jnp.sum(block, axis=0, keepdims=True)
+    block_ref[...] = jnp.broadcast_to(row[None], block_ref.shape)
 
 
 def smeared(scaled):
@@ -364,11 +380,22 @@
 
 
 def charge_kernel(place_ref, all_ref, field_ref, charges_ref, forces_ref, virial_ref, matrix_ref):
-    blocks, _, width = all_ref.shape
-    count = blocks * width
+    blocks, _, lanes = all_ref.shape
     own = charges_ref.shape[1]
-    everyone = jnp.concatenate([all_ref[block] for block in range(blocks)], axis=1)
-    everyone = pltpu.roll(everyone, lax.rem(count - place_ref[0] * width, count), 1)
+    count = blocks * own
+    fit = lanes // own
+    segment = lax.broadcasted_iota(jnp.int32, (8, lanes), 1) // own
+    tiles = []
+    for first in range(0, blocks, fit):
+        tile = jnp.zeros((8, lanes), jnp.float32)
+        for place in range(fit):
+            row = jnp.broadcast_to(all_ref[first + place], (8, lanes))
+            row = pltpu.roll(row, 0, 1, stride=own, stride_axis=0)
+            row = pltpu.roll(row, place * own, 1) if place else row
+            tile = jnp.where(segment == place, row, tile)
+        tiles.append(tile)
+    everyone = jnp.concatenate(tiles, axis=1)
+    everyone = pltpu.roll(everyone, lax.rem(count - place_ref[0] * own, count), 1)
     columns = everyone.T
     spread_row = everyone[3:4] * everyone[3:4]
     rhs = everyone[5:6]
@@ -432,23 +459,23 @@
     virial_ref[...] = 0.5 * mine * table[3:9]
 
 
-def whole_specs(count, scalars=0):
-    return [pl.BlockSpec(memory_space=pltpu.SMEM)] * scalars + [
-        pl.BlockSpec(memory_space=pltpu.VMEM)
-    ] * count
-
-
-def kernel_call(kernel, shapes, arguments, scalars=0, scratch=(), flops=0):
+def kernel_call(kernel, shapes, arguments, scalars=0, far=0, scratch=(), flops=0):
     shapes = tuple(jax.ShapeDtypeStruct(shape, kind) for shape, kind in shapes)
+    spaces = [pltpu.SMEM] * scalars + [pltpu.HBM] * far
+    spaces = spaces + [pltpu.VMEM] * (len(arguments) - len(spaces))
     return pl.pallas_call(
         kernel,
         out_shape=shapes,
-        in_specs=whole_specs(len(arguments) - scalars, scalars),
-        out_specs=tuple(whole_specs(len(shapes))),
+        in_specs=[pl.BlockSpec(memory_space=space) for space in spaces],
+        out_specs=tuple(pl.BlockSpec(memory_space=pltpu.VMEM) for _ in shapes),
         scratch_shapes=list(scratch),
         compiler_params=pltpu.CompilerParams(vmem_limit_bytes=32 * 1024 * 1024),
         cost_estimate=pl.CostEstimate(flops=flops, bytes_accessed=1 << 20, transcendentals=0),
     )(*arguments)
+
+
+def shape_of(value):
+    return (value.shape, value.dtype)
 
 
 def exchanged(block, axis, step):
@@ -478,31 +505,39 @@
     edges = edge_recv.shape[0]
     rows, lanes = lax.axis_size("row"), lax.axis_size("space")
     (packed,) = kernel_call(
-        pack_kernel, [((atoms + 16, chans), jnp.bfloat16)], (features, ghost_list)
+        pack_kernel,
+        [((atoms + 16, chans), jnp.bfloat16)],
+        (features, ghost_list),
+        far=2,
+        scratch=[pltpu.VMEM(*shape_of(ghost_list)), pltpu.SemaphoreType.DMA((2,))],
     )
     others = [exchanged(packed, "space", step) for step in range(1, lanes)]
-    filters, units, base = kernel_call(
+    own = (edge_vec, w_rad1, w_rad2, species[None], hardness[None], width[None])
+    own = own + (chi_shift[None], field[None], positions)
+    kept = (edge_send[None], edge_recv[None], w_msg, w_up, w_out[None])
+    filters, units, base, *kept = kernel_call(
         edge_kernel,
-        [((2 * chans, edges), jnp.float32), ((8, edges), jnp.float32), ((8, atoms), jnp.float32)],
-        (edge_vec, w_rad1, w_rad2, species[None], hardness[None], width[None])
-        + (chi_shift[None], field[None], positions),
+        [((2 * chans, edges), jnp.float32), ((8, edges), jnp.float32), ((8, atoms), jnp.float32)]
+        + [shape_of(value) for value in kept],
+        own + kept,
+        far=len(own + kept),
+        scratch=[pltpu.VMEM(*shape_of(value)) for value in own]
+        + [pltpu.SemaphoreType.DMA((len(own + kept),))],
         flops=1 << 28,
     )
+    send, receive, project, update, readout = kept
     space = lax.axis_index("space").astype(jnp.int32)
+    devices = rows * lanes
     new_features, block = kernel_call(
         node_kernel,
-        [((atoms, chans), jnp.bfloat16), ((8, atoms), jnp.float32)],
-        (space.reshape(1), packed, *others, edge_send[None], edge_recv[None])
-        + (filters, units, base, w_msg, w_up, w_out[None]),
+        [((atoms, chans), jnp.bfloat16), ((devices, 1, chans), jnp.float32)],
+        (space.reshape(1), packed, *others, send, receive)
+        + (filters, units, base, project, update, readout),
         scalars=1,
         flops=1 << 28,
     )
-    block = jnp.concatenate([block, exchanged(block, "space", 1)], axis=1)
-    groups = [list(range(core, rows * lanes, 2)) for core in range(2)]
-    blocks = len(groups[0])
-    block = jnp.broadcast_to(block[None], (blocks,) + block.shape)
-    block = lax.all_to_all(block, everywhere, 0, 0, axis_index_groups=groups, tiled=True)
-    place = lax.axis_index("row").astype(jnp.int32) * (lanes // 2) + space // 2
+    block = lax.all_to_all(block, everywhere, 0, 0, tiled=True)
+    place = lax.axis_index("row").astype(jnp.int32) * lanes + space
     everybody = rows * lanes * atoms
     charges, forces, virial = kernel_call(
         charge_kernel,

time: 31 us -> 28.3 us (0.913)
  waiting for transfers between devices: 8.65 us -> 7.15 us
  starting transfers between devices: 10.1 us -> 9.23 us
  other arithmetic: 0.76 us -> 0 us
  Pallas kernels: 4.79 us -> 5.54 us
    ppermute x4 -> x3, waiting for transfers between devices: 1.33 us -> 0.01 us  [exchanged(): lax.ppermute(block, axis, [(place, place ^ step) for place in range(size)])]
    pallas_call x4, Pallas kernels: 4.79 us -> 5.54 us  [kernel_call(): pl.pallas_call(kernel, out_shape=shapes, in_specs=[pl.BlockSpec(memory_sp...]
    all_to_all x1, starting transfers between devices: 6.77 us -> 6.08 us  [few_shards(): block = lax.all_to_all(block, everywhere, 0, 0, tiled=True)]
    all_to_all x1 -> x0, other arithmetic: 0.68 us -> none  [few_shards(): lax.all_to_all(block, everywhere, 0, 0, axis_index_groups=groups, tiled=T...]
    all_to_all x1 -> x0, local copies, waits for them, and re-layouts: 0.51 us -> none  [few_shards(): lax.all_to_all(block, everywhere, 0, 0, axis_index_groups=groups, tiled=T...]
    unnamed x32 -> x30, local copies, waits for them, and re-layouts: 4.32 us -> 4.53 us
    ppermute x4 -> x3, starting transfers between devices: 3.34 us -> 3.15 us  [exchanged(): lax.ppermute(block, axis, [(place, place ^ step) for place in range(size)])]
  transfers between devices with their start and end apart: 5 -> 4, of which waited for: 3 -> 1; matrix products, arithmetic and copies ran while one was open for 0% -> 0% of each run, Pallas kernels for 1% -> 3%
where the time goes in v5:
time: 28.3 us; the launch traced here: 27.9 us
  starting transfers between devices  9.23 us (33%)
  waiting for transfers between devices  7.15 us (25%)
  Pallas kernels  5.54 us (20%)
  local copies, waits for them, and re-layouts  4.53 us (16%)
  between operations  1.46 us (5%)
    all_to_all x1, waiting for transfers between devices, few_shards(): block = lax.all_to_all(block, everywhere, 0, 0, tiled=True)  7.14 us
    all_to_all x1, starting transfers between devices, few_shards(): block = lax.all_to_all(block, everywhere, 0, 0, tiled=True)  6.08 us
    pallas_call x4, Pallas kernels, kernel_call(): pl.pallas_call(kernel, out_shape=shapes, in_specs=[pl.BlockSpec(memory_sp...  5.54 us
    unnamed x30, local copies, waits for them, and re-layouts  4.53 us
    ppermute x3, starting transfers between devices, exchanged(): lax.ppermute(block, axis, [(place, place ^ step) for place in range(size)])  3.15 us
  transfers between devices with their start and end apart: 4, of which 1 were waited for; matrix products, arithmetic and copies ran while one was open for 0% of the time, Pallas kernels for 3%

profile of v5, /device:TPU:0, one launch (start us, length us, event | category | flops | bytes accessed | tf_op | source)
XLA Modules:
  0.0 27.9 jit_solution(14311298866759766037)
XLA Ops:
  0.6 0.0 copy-start
  0.6 0.7 %copy-done = bf16[16,128]{1,0:T(8,128)(2,1)S(1)} copy-done((bf16[16,128]{1,0:T(8,128)(2,1)S(1)}, bf16[16,128]{1,0:T(8,128)(2,1)}, u32[]{:S(2)}) %copy-start) | copy-done | bytes 4120
  1.3 0.0 copy-start.1
  1.3 0.7 %copy-done.1 = s32[1,4,32]{2,1,0:T(4,128)S(1)} copy-done((s32[1,4,32]{2,1,0:T(4,128)S(1)}, s32[1,4,32]{2,1,0:T(4,128)}, u32[]{:S(2)}) %copy-start.1) | copy-done | bytes 536
  2.0 0.0 copy-start.9
  2.0 0.0 copy-start.12
  2.0 0.0 copy-start.13
  2.0 0.0 copy-start.14
  2.1 2.5 %collective-permute-start.2 = (bf16[32,128]{1,0:T(8,128)(2,1)S(1)}, bf16[32,128]{1,0:T(8,128)(2,1)S(1)}, u32[]{:S(2)}, u32[]{:S(2)}) collective-permute-start(bf16[32,128]{1,0:T(8,128)(2,1)S(1)} %shard_map.183.own_ref), channel_id=1, source_target_pairs={{0,3},{1,2},{2,1},{3,0},{4,7},{5,6},{6,5},{7,4},{8,11},{9,10},{10,... | collective-permute-start | bytes 24584 | tf_op jit(solution)/shard_map/ppermute | solution.py:483
  4.5 0.6 %collective-permute-start.1 = (bf16[32,128]{1,0:T(8,128)(2,1)S(1)}, bf16[32,128]{1,0:T(8,128)(2,1)S(1)}, u32[]{:S(2)}, u32[]{:S(2)}) collective-permute-start(bf16[32,128]{1,0:T(8,128)(2,1)S(1)} %shard_map.183.own_ref), channel_id=1, source_target_pairs={{0,2},{1,3},{2,0},{3,1},{4,6},{5,7},{6,4},{7,5},{8,10},{9,11},{10,... | collective-permute-start | bytes 24584 | tf_op jit(solution)/shard_map/ppermute | solution.py:483
  5.2 0.0 collective-permute-start
  5.2 0.0 copy-start.8
  5.9 0.0 copy-start.5
  5.9 0.0 copy-start.6
  5.9 0.0 copy-start.7
  5.9 0.0 copy-start.10
  5.9 0.0 copy-start.11
  5.9 0.0 copy-done.9
  5.9 0.0 copy-done.12
  6.0 0.0 copy-done.13
  6.0 0.0 copy-done.14
  6.0 0.0 copy-done.8
  6.0 0.6 %copy-done.5 = f32[3,512]{1,0:T(4,128)S(1)} copy-done((f32[3,512]{1,0:T(4,128)S(1)}, f32[3,512]{1,0:T(4,128)}, u32[]{:S(2)}) %copy-start.5) | copy-done | bytes 6168
  6.6 0.0 copy-done.6
  6.6 0.0 copy-done.7
  6.6 0.0 copy-done.10
  6.6 0.0 copy-done.11
  6.6 0.0 copy-start.2
  6.6 0.8 %copy-done.2 = bf16[128,256]{1,0:T(8,128)(2,1)S(1)} copy-done((bf16[128,256]{1,0:T(8,128)(2,1)S(1)}, bf16[128,256]{1,0:T(8,128)(2,1)}, u32[]{:S(2)}) %copy-start.2) | copy-done | bytes 65560
  7.4 0.0 copy-start.3
  7.4 0.8 %copy-done.3 = bf16[128,256]{1,0:T(8,128)(2,1)S(1)} copy-done((bf16[128,256]{1,0:T(8,128)(2,1)S(1)}, bf16[128,256]{1,0:T(8,128)(2,1)}, u32[]{:S(2)}) %copy-start.3) | copy-done | bytes 65560
  8.3 0.0 copy-start.4
  8.3 0.8 %copy-done.4 = bf16[256,128]{1,0:T(8,128)(2,1)S(1)} copy-done((bf16[256,128]{1,0:T(8,128)(2,1)S(1)}, bf16[256,128]{1,0:T(8,128)(2,1)}, u32[]{:S(2)}) %copy-start.4) | copy-done | bytes 65560
  9.1 0.9 %shard_map.184 = (f32[256,512]{1,0:T(8,128)S(1)}, f32[8,512]{1,0:T(8,128)S(1)}, f32[8,16]{1,0:T(8,128)S(1)}, s32[1,512]{1,0:T(1,128)S(1)}, s32[1,512]{1,0:T(1,12...) custom-call(f32[3,512]{1,0:T(4,128)S(1)} %copy-done.5, ...), custom_call_target="tpu_custom_call" | custom-call | flops 268435456 | bytes 1048576 | tf_op jit(solution)/shard_map/pallas_call | solution.py:466
  10.0 0.0 collective-permute-done.2.far_ref
  10.0 0.0 collective-permute-done.1.side_ref
  10.0 0.0 collective-permute-done.near_ref
  10.0 1.7 %shard_map.185 = (bf16[16,128]{1,0:T(8,128)(2,1)}, f32[32,1,128]{2,1,0:T(1,128)}) custom-call(s32[1]{0:T(128)} %bitcast.space_ref, bf16[32,128]{1,0:T(8,128)(2,1)S(1)} %shard_map.183.own_ref, bf16[32,128]{1,0:T(8,128)(2,1)S(1)} %collective-permute-done.near_ref, bf16[32,128]{1,0:T(8,128)(2,1)S(1)} %collective-permute-done.1.side_ref, ...), custom_call_target="tpu_custom_call" | custom-call | flops 268435456 | bytes 1048576 | tf_op jit(solution)/shard_map/pallas_call | solution.py:466
  11.7 6.1 %all-to-all-start = ((f32[32,1,128]{2,1,0:T(1,128)}), f32[32,1,128]{2,1,0:T(1,128)S(1)}, u32[]{:S(2)}, u32[]{:S(2)}) async-start(f32[32,1,128]{2,1,0:T(1,128)} %get-tuple-element.26), calls=%async_computation | async-start | bytes 32768 | tf_op jit(solution)/shard_map/all_to_all | solution.py:539
  17.8 7.1 %all-to-all-done.all_ref = f32[32,1,128]{2,1,0:T(1,128)S(1)} async-done(((f32[32,1,128]{2,1,0:T(1,128)}), f32[32,1,128]{2,1,0:T(1,128)S(1)}, u32[]{:S(2)}, u32[]{:S(2)}) %all-to-all-start) | async-done | bytes 16416 | tf_op jit(solution)/shard_map/all_to_all | solution.py:539
  24.9 3.0 %shard_map.186 = (f32[1,16]{1,0:T(1,128)}, f32[3,16]{1,0:T(4,128)}, f32[6,16]{1,0:T(8,128)}) custom-call(s32[1]{0:T(128)} %bitcast.9.place_ref, f32[32,1,128]{2,1,0:T(1,128)S(1)} %all-to-all-done.all_ref, f32[1,1]{1,0:T(1,128)} %bitcast.12.field_ref), custom_call_target="tpu_custom_call" | custom-call | flops 268435456 | bytes 1048576 | tf_op jit(solution)/shard_map/pallas_call | solution.py:466
  (1 shorter events, 0.0 us)
Async XLA Ops:
  0.6 0.7 %copy-start = (bf16[16,128]{1,0:T(8,128)(2,1)S(1)}, bf16[16,128]{1,0:T(8,128)(2,1)}, u32[]{:S(2)}) copy-start(bf16[16,128]{1,0:T(8,128)(2,1)} %features_ref.1) | copy-start | bytes 12292
  1.3 0.7 %copy-start.1 = (s32[1,4,32]{2,1,0:T(4,128)S(1)}, s32[1,4,32]{2,1,0:T(4,128)}, u32[]{:S(2)}) copy-start(s32[1,4,32]{2,1,0:T(4,128)} %lists_ref.1) | copy-start | bytes 1540
  2.0 3.9 %copy-start.9 = (s32[512]{0:T(512)S(1)}, s32[512]{0:T(512)}, u32[]{:S(2)}) copy-start(s32[512]{0:T(512)} %param.20) | copy-start | bytes 6148
  2.0 3.9 %copy-start.12 = (f32[4]{0:T(128)S(1)}, f32[4]{0:T(128)}, u32[]{:S(2)}) copy-start(f32[4]{0:T(128)} %param.29) | copy-start | bytes 52
  2.0 4.0 %copy-start.13 = (f32[4]{0:T(128)S(1)}, f32[4]{0:T(128)}, u32[]{:S(2)}) copy-start(f32[4]{0:T(128)} %param.30) | copy-start | bytes 52
  2.0 4.0 %copy-start.14 = (f32[128]{0:T(128)S(1)}, f32[128]{0:T(128)}, u32[]{:S(2)}) copy-start(f32[128]{0:T(128)} %param.27) | copy-start | bytes 1540
  2.1 7.9 %collective-permute-start.2 = (bf16[32,128]{1,0:T(8,128)(2,1)S(1)}, bf16[32,128]{1,0:T(8,128)(2,1)S(1)}, u32[]{:S(2)}, u32[]{:S(2)}) collective-permute-start(bf16[32,128]{1,0:T(8,128)(2,1)S(1)} %shard_map.183.own_ref), channel_id=1, source_target_pairs={{0,3},{1,2},{2,1},{3,0},{4,7},{5,6},{6,5},{7,4},{8,11},{9,10},{10,... | collective-permute-start | bytes 24584 | tf_op jit(solution)/shard_map/ppermute | solution.py:483
  4.5 5.5 %collective-permute-start.1 = (bf16[32,128]{1,0:T(8,128)(2,1)S(1)}, bf16[32,128]{1,0:T(8,128)(2,1)S(1)}, u32[]{:S(2)}, u32[]{:S(2)}) collective-permute-start(bf16[32,128]{1,0:T(8,128)(2,1)S(1)} %shard_map.183.own_ref), channel_id=1, source_target_pairs={{0,2},{1,3},{2,0},{3,1},{4,6},{5,7},{6,4},{7,5},{8,10},{9,11},{10,... | collective-permute-start | bytes 24584 | tf_op jit(solution)/shard_map/ppermute | solution.py:483
  5.2 4.9 %collective-permute-start = (bf16[32,128]{1,0:T(8,128)(2,1)S(1)}, bf16[32,128]{1,0:T(8,128)(2,1)S(1)}, u32[]{:S(2)}, u32[]{:S(2)}) collective-permute-start(bf16[32,128]{1,0:T(8,128)(2,1)S(1)} %shard_map.183.own_ref), channel_id=1, source_target_pairs={{0,1},{1,0},{2,3},{3,2},{4,5},{5,4},{6,7},{7,6},{8,9},{9,8},{10,11... | collective-permute-start | bytes 24584 | tf_op jit(solution)/shard_map/ppermute | solution.py:483
  5.2 0.8 %copy-start.8 = (s32[512]{0:T(512)S(1)}, s32[512]{0:T(512)}, u32[]{:S(2)}) copy-start(s32[512]{0:T(512)} %param.21) | copy-start | bytes 6148
  5.9 0.7 %copy-start.5 = (f32[3,512]{1,0:T(4,128)S(1)}, f32[3,512]{1,0:T(4,128)}, u32[]{:S(2)}) copy-start(f32[3,512]{1,0:T(4,128)} %refs_0_.1) | copy-start | bytes 18436
  5.9 0.7 %copy-start.6 = (f32[8,128]{1,0:T(8,128)S(1)}, f32[8,128]{1,0:T(8,128)}, u32[]{:S(2)}) copy-start(f32[8,128]{1,0:T(8,128)} %refs_1_.1) | copy-start | bytes 12292
  5.9 0.7 %copy-start.7 = (f32[3,16]{1,0:T(4,128)S(1)}, f32[3,16]{1,0:T(4,128)}, u32[]{:S(2)}) copy-start(f32[3,16]{1,0:T(4,128)} %refs_8_.1) | copy-start | bytes 580
  5.9 0.7 %copy-start.10 = (s32[16]{0:T(128)S(1)}, s32[16]{0:T(128)}, u32[]{:S(2)}) copy-start(s32[16]{0:T(128)} %param.18) | copy-start | bytes 196
  5.9 0.7 %copy-start.11 = (f32[4]{0:T(128)S(1)}, f32[4]{0:T(128)}, u32[]{:S(2)}) copy-start(f32[4]{0:T(128)} %param.28) | copy-start | bytes 52
  6.6 0.8 %copy-start.2 = (bf16[128,256]{1,0:T(8,128)(2,1)S(1)}, bf16[128,256]{1,0:T(8,128)(2,1)}, u32[]{:S(2)}) copy-start(bf16[128,256]{1,0:T(8,128)(2,1)} %refs_2_.1) | copy-start | bytes 196612
  7.4 0.8 %copy-start.3 = (bf16[128,256]{1,0:T(8,128)(2,1)S(1)}, bf16[128,256]{1,0:T(8,128)(2,1)}, u32[]{:S(2)}) copy-start(bf16[128,256]{1,0:T(8,128)(2,1)} %refs_11_.1) | copy-start | bytes 196612
  8.3 0.8 %copy-start.4 = (bf16[256,128]{1,0:T(8,128)(2,1)S(1)}, bf16[256,128]{1,0:T(8,128)(2,1)}, u32[]{:S(2)}) copy-start(bf16[256,128]{1,0:T(8,128)(2,1)} %refs_12_.1) | copy-start | bytes 196612
  11.7 13.2 %all-to-all-start = ((f32[32,1,128]{2,1,0:T(1,128)}), f32[32,1,128]{2,1,0:T(1,128)S(1)}, u32[]{:S(2)}, u32[]{:S(2)}) async-start(f32[32,1,128]{2,1,0:T(1,128)} %get-tuple-element.26), calls=%async_computation | async-start | bytes 32768 | tf_op jit(solution)/shard_map/all_to_all | solution.py:539

commit v6 on v5

--- a/solution.py
+++ b/solution.py
@@ -241,15 +241,15 @@
     copies[1].wait()
 
 
-def edge_kernel(*refs):
-    own, kept = refs[:9], refs[9:14]
-    filter_ref, unit_ref, base_ref = refs[14:17]
-    moved, held, semaphores = refs[17:22], refs[22:31], refs[31]
+def edge_kernel(field_ref, *refs):
+    own, kept = refs[:8], refs[8:13]
+    filter_ref, unit_ref, base_ref = refs[13:16]
+    moved, held, semaphores = refs[16:21], refs[21:29], refs[29]
     copies = fetched(list(zip(own + kept, held + moved)), semaphores)
     for copy in copies:
         copy.wait()
     vec_ref, first_ref, second_ref, species_ref = held[:4]
-    hardness_ref, width_ref, shift_ref, field_ref, positions_ref = held[4:]
+    hardness_ref, width_ref, shift_ref, positions_ref = held[4:]
     edges = vec_ref.shape[1]
     orders = first_ref.shape[0]
     vec = vec_ref[...]
@@ -289,7 +289,7 @@
     base_ref[0:3, :] = positions
     base_ref[3:4, :] = sigma
     base_ref[4:5, :] = table(hardness_ref) + inverse_root_pi / sigma
-    base_ref[5:6, :] = field_ref[...] * positions[2:3]
+    base_ref[5:6, :] = field_ref[0] * positions[2:3]
     base_ref[6:7, :] = table(shift_ref)
     base_ref[7:8, :] = jnp.zeros_like(sigma)
 
@@ -379,7 +379,7 @@
     return 1.0 - series * turn * decay, decay
 
 
-def charge_kernel(place_ref, all_ref, field_ref, charges_ref, forces_ref, virial_ref, matrix_ref):
+def charge_kernel(place_ref, field_ref, all_ref, charges_ref, forces_ref, virial_ref, matrix_ref):
     blocks, _, lanes = all_ref.shape
     own = charges_ref.shape[1]
     count = blocks * own
@@ -455,7 +455,7 @@
     charges_ref[...] = mine
     pull = -mine * table[0:3]
     third = lax.broadcasted_iota(jnp.int32, pull.shape, 0) == 2
-    forces_ref[...] = pull + jnp.where(third, mine * field_ref[...], 0.0)
+    forces_ref[...] = pull + jnp.where(third, mine * field_ref[0], 0.0)
     virial_ref[...] = 0.5 * mine * table[3:9]
 
 
@@ -463,6 +463,10 @@
     shapes = tuple(jax.ShapeDtypeStruct(shape, kind) for shape, kind in shapes)
     spaces = [pltpu.SMEM] * scalars + [pltpu.HBM] * far
     spaces = spaces + [pltpu.VMEM] * (len(arguments) - len(spaces))
+    arguments = [
+        pltpu.with_memory_space_constraint(value, space) if space is pltpu.HBM else value
+        for value, space in zip(arguments, spaces)
+    ]
     return pl.pallas_call(
         kernel,
         out_shape=shapes,
@@ -513,13 +517,14 @@
     )
     others = [exchanged(packed, "space", step) for step in range(1, lanes)]
     own = (edge_vec, w_rad1, w_rad2, species[None], hardness[None], width[None])
-    own = own + (chi_shift[None], field[None], positions)
+    own = own + (chi_shift[None], positions)
     kept = (edge_send[None], edge_recv[None], w_msg, w_up, w_out[None])
     filters, units, base, *kept = kernel_call(
         edge_kernel,
         [((2 * chans, edges), jnp.float32), ((8, edges), jnp.float32), ((8, atoms), jnp.float32)]
         + [shape_of(value) for value in kept],
-        own + kept,
+        (field,) + own + kept,
+        scalars=1,
         far=len(own + kept),
         scratch=[pltpu.VMEM(*shape_of(value)) for value in own]
         + [pltpu.SemaphoreType.DMA((len(own + kept),))],
@@ -542,8 +547,8 @@
     charges, forces, virial = kernel_call(
         charge_kernel,
         [((count, atoms), jnp.float32) for count in (1, 3, 6)],
-        (place.reshape(1), block, field[None]),
-        scalars=1,
+        (place.reshape(1), field, block),
+        scalars=2,
         scratch=[pltpu.VMEM((everybody, everybody), jnp.float32)],
         flops=1 << 28,
     )

time: 28.3 us -> 25 us (0.88)
  local copies, waits for them, and re-layouts: 4.53 us -> 0 us
  Pallas kernels: 5.54 us -> 6.97 us
  waiting for transfers between devices: 7.15 us -> 7.84 us
  starting transfers between devices: 9.23 us -> 8.56 us
    unnamed x30 -> x0, local copies, waits for them, and re-layouts: 4.53 us -> none
    pallas_call x4, Pallas kernels: 5.54 us -> 6.97 us  [kernel_call(): pl.pallas_call(kernel, out_shape=shapes, in_specs=[pl.BlockSpec(memory_sp...]
    ppermute x3, waiting for transfers between devices: 0.01 us -> 0.69 us  [exchanged(): lax.ppermute(block, axis, [(place, place ^ step) for place in range(size)])]
    all_to_all x1, starting transfers between devices: 6.08 us -> 5.41 us  [few_shards(): block = lax.all_to_all(block, everywhere, 0, 0, tiled=True)]
  transfers between devices with their start and end apart: 4 -> 4, of which waited for: 1 -> 2; matrix products, arithmetic and copies ran while one was open for 0% -> 0% of each run, Pallas kernels for 3% -> 7%
where the time goes in v6:
time: 25 us; the launch traced here: 24.7 us
  starting transfers between devices  8.56 us (34%)
  waiting for transfers between devices  7.84 us (31%)
  Pallas kernels  6.97 us (28%)
  between operations  1.33 us (5%)
    all_to_all x1, waiting for transfers between devices, few_shards(): block = lax.all_to_all(block, everywhere, 0, 0, tiled=True)  7.14 us
    pallas_call x4, Pallas kernels, kernel_call(): pl.pallas_call(kernel, out_shape=shapes, in_specs=[pl.BlockSpec(memory_sp...  6.97 us
    all_to_all x1, starting transfers between devices, few_shards(): block = lax.all_to_all(block, everywhere, 0, 0, tiled=True)  5.41 us
    ppermute x3, starting transfers between devices, exchanged(): lax.ppermute(block, axis, [(place, place ^ step) for place in range(size)])  3.15 us
    ppermute x3, waiting for transfers between devices, exchanged(): lax.ppermute(block, axis, [(place, place ^ step) for place in range(size)])  0.69 us
  transfers between devices with their start and end apart: 4, of which 2 were waited for; matrix products, arithmetic and copies ran while one was open for 0% of the time, Pallas kernels for 7%

profile of v6, /device:TPU:0, one launch (start us, length us, event | category | flops | bytes accessed | tf_op | source)
XLA Modules:
  0.0 24.7 jit_solution(12875539807262262947)
XLA Ops:
  0.6 0.7 %shard_map.183.own_ref = bf16[32,128]{1,0:T(8,128)(2,1)S(1)} custom-call(bf16[16,128]{1,0:T(8,128)(2,1)} %features_ref.1, s32[1,4,32]{2,1,0:T(4,128)} %lists_ref.1), custom_call_target="tpu_custom_call" | custom-call | bytes 1048576 | tf_op jit(solution)/shard_map/pallas_call | solution.py:470
  1.4 2.5 %collective-permute-start.2 = (bf16[32,128]{1,0:T(8,128)(2,1)S(1)}, bf16[32,128]{1,0:T(8,128)(2,1)S(1)}, u32[]{:S(2)}, u32[]{:S(2)}) collective-permute-start(bf16[32,128]{1,0:T(8,128)(2,1)S(1)} %shard_map.183.own_ref), channel_id=1, source_target_pairs={{0,3},{1,2},{2,1},{3,0},{4,7},{5,6},{6,5},{7,4},{8,11},{9,10},{10,... | collective-permute-start | bytes 24584 | tf_op jit(solution)/shard_map/ppermute | solution.py:487
  3.8 0.6 %collective-permute-start.1 = (bf16[32,128]{1,0:T(8,128)(2,1)S(1)}, bf16[32,128]{1,0:T(8,128)(2,1)S(1)}, u32[]{:S(2)}, u32[]{:S(2)}) collective-permute-start(bf16[32,128]{1,0:T(8,128)(2,1)S(1)} %shard_map.183.own_ref), channel_id=1, source_target_pairs={{0,2},{1,3},{2,0},{3,1},{4,6},{5,7},{6,4},{7,5},{8,10},{9,11},{10,... | collective-permute-start | bytes 24584 | tf_op jit(solution)/shard_map/ppermute | solution.py:487
  4.5 0.0 collective-permute-start
  5.2 1.6 %shard_map.184 = (f32[256,512]{1,0:T(8,128)S(1)}, f32[8,512]{1,0:T(8,128)S(1)}, f32[8,16]{1,0:T(8,128)S(1)}, s32[1,512]{1,0:T(1,128)S(1)}, s32[1,512]{1,0:T(1,12...) custom-call(f32[1]{0:T(128)S(6)} %copy.20.field_ref, f32[3,512]{1,0:T(4,128)} %refs_0_.1, ...), custom_call_target="tpu_custom_call" | custom-call | flops 268435456 | bytes 1048576 | tf_op jit(solution)/shard_map/pallas_call | solution.py:470
  6.8 0.0 collective-permute-done.2.far_ref
  6.8 0.7 %collective-permute-done.1.side_ref = bf16[32,128]{1,0:T(8,128)(2,1)S(1)} collective-permute-done((bf16[32,128]{1,0:T(8,128)(2,1)S(1)}, bf16[32,128]{1,0:T(8,128)(2,1)S(1)}, u32[]{:S(2)}, u32[]{:S(2)}) %collective-permute-start.1) | collective-permute-done | bytes 8224 | tf_op jit(solution)/shard_map/ppermute | solution.py:487
  7.5 0.0 collective-permute-done.near_ref
  7.5 1.7 %shard_map.185 = (bf16[16,128]{1,0:T(8,128)(2,1)}, f32[32,1,128]{2,1,0:T(1,128)}) custom-call(s32[1]{0:T(128)} %bitcast.space_ref, bf16[32,128]{1,0:T(8,128)(2,1)S(1)} %shard_map.183.own_ref, bf16[32,128]{1,0:T(8,128)(2,1)S(1)} %collective-permute-done.near_ref, bf16[32,128]{1,0:T(8,128)(2,1)S(1)} %collective-permute-done.1.side_ref, ...), custom_call_target="tpu_custom_call" | custom-call | flops 268435456 | bytes 1048576 | tf_op jit(solution)/shard_map/pallas_call | solution.py:470
  9.2 5.4 %all-to-all-start = ((f32[32,1,128]{2,1,0:T(1,128)}), f32[32,1,128]{2,1,0:T(1,128)S(1)}, u32[]{:S(2)}, u32[]{:S(2)}) async-start(f32[32,1,128]{2,1,0:T(1,128)} %get-tuple-element.26), calls=%async_computation | async-start | bytes 32768 | tf_op jit(solution)/shard_map/all_to_all | solution.py:544
  14.6 7.1 %all-to-all-done.all_ref = f32[32,1,128]{2,1,0:T(1,128)S(1)} async-done(((f32[32,1,128]{2,1,0:T(1,128)}), f32[32,1,128]{2,1,0:T(1,128)S(1)}, u32[]{:S(2)}, u32[]{:S(2)}) %all-to-all-start) | async-done | bytes 16416 | tf_op jit(solution)/shard_map/all_to_all | solution.py:544
  21.7 3.0 %shard_map.186 = (f32[1,16]{1,0:T(1,128)}, f32[3,16]{1,0:T(4,128)}, f32[6,16]{1,0:T(8,128)}) custom-call(s32[1]{0:T(128)} %bitcast.8.place_ref, f32[1]{0:T(128)S(6)} %copy.20.field_ref, f32[32,1,128]{2,1,0:T(1,128)S(1)} %all-to-all-done.all_ref), custom_call_target="tpu_custom_call" | custom-call | flops 268435456 | bytes 1048576 | tf_op jit(solution)/shard_map/pallas_call | solution.py:470
Async XLA Ops:
  1.4 5.4 %collective-permute-start.2 = (bf16[32,128]{1,0:T(8,128)(2,1)S(1)}, bf16[32,128]{1,0:T(8,128)(2,1)S(1)}, u32[]{:S(2)}, u32[]{:S(2)}) collective-permute-start(bf16[32,128]{1,0:T(8,128)(2,1)S(1)} %shard_map.183.own_ref), channel_id=1, source_target_pairs={{0,3},{1,2},{2,1},{3,0},{4,7},{5,6},{6,5},{7,4},{8,11},{9,10},{10,... | collective-permute-start | bytes 24584 | tf_op jit(solution)/shard_map/ppermute | solution.py:487
  3.8 3.7 %collective-permute-start.1 = (bf16[32,128]{1,0:T(8,128)(2,1)S(1)}, bf16[32,128]{1,0:T(8,128)(2,1)S(1)}, u32[]{:S(2)}, u32[]{:S(2)}) collective-permute-start(bf16[32,128]{1,0:T(8,128)(2,1)S(1)} %shard_map.183.own_ref), channel_id=1, source_target_pairs={{0,2},{1,3},{2,0},{3,1},{4,6},{5,7},{6,4},{7,5},{8,10},{9,11},{10,... | collective-permute-start | bytes 24584 | tf_op jit(solution)/shard_map/ppermute | solution.py:487
  4.5 3.0 %collective-permute-start = (bf16[32,128]{1,0:T(8,128)(2,1)S(1)}, bf16[32,128]{1,0:T(8,128)(2,1)S(1)}, u32[]{:S(2)}, u32[]{:S(2)}) collective-permute-start(bf16[32,128]{1,0:T(8,128)(2,1)S(1)} %shard_map.183.own_ref), channel_id=1, source_target_pairs={{0,1},{1,0},{2,3},{3,2},{4,5},{5,4},{6,7},{7,6},{8,9},{9,8},{10,11... | collective-permute-start | bytes 24584 | tf_op jit(solution)/shard_map/ppermute | solution.py:487
  9.2 12.6 %all-to-all-start = ((f32[32,1,128]{2,1,0:T(1,128)}), f32[32,1,128]{2,1,0:T(1,128)S(1)}, u32[]{:S(2)}, u32[]{:S(2)}) async-start(f32[32,1,128]{2,1,0:T(1,128)} %get-tuple-element.26), calls=%async_computation | async-start | bytes 32768 | tf_op jit(solution)/shard_map/all_to_all | solution.py:544

commit v7 on v6

--- a/solution.py
+++ b/solution.py
@@ -214,6 +214,10 @@
     return value / (1.0 + jnp.exp(-value))
 
 
+def silu_half(value):
+    return (0.5 * value) * (1.0 + jnp.tanh(0.5 * value))
+
+
 sine_series = [(-1.0) ** k * math.pi ** (2 * k + 1) / math.factorial(2 * k + 1) for k in range(7)]
 
 
@@ -227,29 +231,48 @@
     return copies
 
 
-def pack_kernel(features_ref, lists_ref, packed_ref, held_ref, semaphores):
+rhs_segment = 3
+
+
+def pack_kernel(*refs):
+    count = (len(refs) - 3) // 2
+    features_ref, lists_ref, packed_ref = refs[0], refs[1], refs[count + 1]
+    held_ref, semaphores = refs[-2:]
     atoms, chans = features_ref.shape
-    copies = fetched(
-        [(lists_ref, held_ref), (features_ref, packed_ref.at[pl.ds(0, atoms)])], semaphores
-    )
+    pairs = [(lists_ref, held_ref), (features_ref, packed_ref.at[pl.ds(0, atoms)])]
+    copies = fetched(pairs + list(zip(refs[2 : count + 1], refs[count + 2 : -2])), semaphores)
     copies[0].wait()
     lists = held_ref[0].astype(jnp.float32)
     rows, width = lists.shape
     lists = jnp.concatenate([lists, jnp.zeros((rows, chans - width), jnp.float32)], axis=1)
     blank = jnp.zeros((packed_ref.shape[0] - atoms - rows, chans), jnp.float32)
     packed_ref[atoms:, :] = jnp.concatenate([lists, blank], axis=0).astype(jnp.bfloat16)
-    copies[1].wait()
-
-
-def edge_kernel(field_ref, *refs):
-    own, kept = refs[:8], refs[8:13]
-    filter_ref, unit_ref, base_ref = refs[13:16]
-    moved, held, semaphores = refs[16:21], refs[21:29], refs[29]
-    copies = fetched(list(zip(own + kept, held + moved)), semaphores)
-    for copy in copies:
+    for copy in copies[1:]:
         copy.wait()
-    vec_ref, first_ref, second_ref, species_ref = held[:4]
-    hardness_ref, width_ref, shift_ref, positions_ref = held[4:]
+
+
+def edge_kernel(
+    field_ref,
+    space_ref,
+    vec_ref,
+    first_ref,
+    second_ref,
+    species_ref,
+    hardness_ref,
+    width_ref,
+    shift_ref,
+    positions_ref,
+    send_ref,
+    recv_ref,
+    project_ref,
+    filter_ref,
+    unit_ref,
+    row_ref,
+    slot_ref,
+    local_ref,
+    hit_ref,
+    turned_ref,
+):
     edges = vec_ref.shape[1]
     orders = first_ref.shape[0]
     vec = vec_ref[...]
@@ -274,7 +297,7 @@
         jnp.concatenate([w1, w1, w2, w2, w1, w3], axis=0).astype(jnp.bfloat16),
         jnp.concatenate([b1, b2, b1, b2, b3, b1], axis=0).astype(jnp.bfloat16),
     )
-    radial = silu(mixed).astype(jnp.bfloat16)
+    radial = silu_half(mixed).astype(jnp.bfloat16)
     filter_ref[...] = over_first(second_ref[...], radial)
     species = species_ref[...]
 
@@ -286,12 +309,32 @@
 
     positions = positions_ref[...]
     sigma = table(width_ref)
-    base_ref[0:3, :] = positions
-    base_ref[3:4, :] = sigma
-    base_ref[4:5, :] = table(hardness_ref) + inverse_root_pi / sigma
-    base_ref[5:6, :] = field_ref[0] * positions[2:3]
-    base_ref[6:7, :] = table(shift_ref)
-    base_ref[7:8, :] = jnp.zeros_like(sigma)
+    atoms = species.shape[1]
+    chans = row_ref.shape[1]
+    diag = table(hardness_ref) + inverse_root_pi / sigma
+    rhs = field_ref[0] * positions[2:3] - table(shift_ref)
+    blank = jnp.zeros((2, atoms), jnp.float32)
+    rows = [positions[0:1], blank, rhs, diag, sigma, positions[2:3], positions[1:2]]
+    block = jnp.concatenate(
+        [jnp.concatenate(rows, axis=0), jnp.zeros((8, chans - atoms), jnp.float32)], axis=1
+    )
+    block = pltpu.roll(block, 0, 1, stride=atoms, stride_axis=0)
+    row_ref[...] = jnp.sum(block, axis=0, keepdims=True)
+    lanes = local_ref.shape[0] // atoms
+    slots = chans // lanes
+    send = send_ref[...]
+    own = send < atoms
+    slot = jnp.where(own, -1, (send - atoms) ^ (space_ref[0] * slots))
+    local = jnp.where(own, send, -1)
+
+    def chosen(ref, index):
+        hit = lax.broadcasted_iota(jnp.int32, ref.shape, 0) == index
+        ref[...] = jnp.where(hit, 1.0, 0.0).astype(ref.dtype)
+
+    chosen(slot_ref, slot)
+    chosen(local_ref, local)
+    chosen(hit_ref, recv_ref[...])
+    turned_ref[...] = project_ref[...].astype(jnp.float32).T.astype(jnp.bfloat16)
 
 
 def node_kernel(
@@ -300,54 +343,42 @@
     near_ref,
     side_ref,
     far_ref,
-    send_ref,
-    recv_ref,
     filter_ref,
     unit_ref,
-    base_ref,
-    project_ref,
+    row_ref,
+    slot_ref,
+    local_ref,
+    hit_ref,
+    turned_ref,
     update_ref,
     out_ref,
     features_ref,
     block_ref,
 ):
     atoms, chans = features_ref.shape
-    edges = send_ref.shape[1]
     space = space_ref[0]
     packed = [ref[...].astype(jnp.float32) for ref in (own_ref, near_ref, side_ref, far_ref)]
     lanes = len(packed)
     slots = chans // lanes
     group = jnp.concatenate([value[:atoms] for value in packed], axis=0).astype(jnp.bfloat16)
     picks = jnp.zeros((8, chans), jnp.float32)
-    line = lax.broadcasted_iota(jnp.int32, (packed[0].shape[0] - atoms, chans), 0)
+    line = lax.broadcasted_iota(jnp.int32, (8, chans), 0)
     for place, value in enumerate(packed):
-        mine = jnp.sum(jnp.where(line == space, value[atoms:], 0.0), axis=0, keepdims=True)
-        mine = jnp.broadcast_to(mine, (8, chans))
+        mine = jnp.where(line == space, value[atoms : atoms + 8], 0.0)
         picks = picks + (pltpu.roll(mine, place * slots, 1) if place else mine)
     slot_owner = lax.broadcasted_iota(jnp.int32, (1, chans), 1) // slots * atoms
-    chosen = slot_owner + picks[0:1].astype(jnp.int32)
-    members = lanes * atoms
+    chosen = slot_owner + jnp.sum(picks, axis=0, keepdims=True).astype(jnp.int32)
     fill = jnp.where(
-        lax.broadcasted_iota(jnp.int32, (members, chans), 0) == chosen, 1.0, 0.0
+        lax.broadcasted_iota(jnp.int32, (lanes * atoms, chans), 0) == chosen, 1.0, 0.0
     ).astype(jnp.bfloat16)
-    send = send_ref[...]
-    own = send < atoms
-    slot = jnp.where(own, -1, (send - atoms) ^ (space * slots))
-    from_slot = jnp.where(
-        lax.broadcasted_iota(jnp.int32, (chans, edges), 0) == slot, 1.0, 0.0
-    ).astype(jnp.bfloat16)
-    from_own = jnp.where(
-        lax.broadcasted_iota(jnp.int32, (members, edges), 0) == jnp.where(own, send, -1), 1.0, 0.0
-    )
-    sender = jnp.dot(fill, from_slot, preferred_element_type=jnp.float32) + from_own
-    projected = jnp.dot(group, project_ref[...], preferred_element_type=jnp.float32)
-    picked = over_first(projected.astype(jnp.bfloat16), sender.astype(jnp.bfloat16))
+    sender = jnp.dot(fill, slot_ref[...], preferred_element_type=jnp.float32) + local_ref[...]
+    projected = over_last(turned_ref[...], group).astype(jnp.bfloat16)
+    picked = jnp.dot(projected, sender.astype(jnp.bfloat16), preferred_element_type=jnp.float32)
     scalar = picked[:chans] * filter_ref[:chans, :]
     carried = picked[chans:] * filter_ref[chans:, :]
     parts = [scalar] + [unit_ref[axis : axis + 1, :] * carried for axis in range(3)]
     message = jnp.concatenate([part.astype(jnp.bfloat16) for part in parts], axis=0)
-    hit = lax.broadcasted_iota(jnp.int32, (atoms, edges), 0) == recv_ref[...]
-    summed = over_last(jnp.where(hit, 1.0, 0.0).astype(jnp.bfloat16), message) * message_scale
+    summed = over_last(hit_ref[...], message) * message_scale
     square = jnp.zeros((atoms, chans), jnp.float32)
     for component in range(1, 4):
         part = summed[:, component * chans : (component + 1) * chans]
@@ -355,23 +386,22 @@
     invariant = jnp.concatenate([summed[:, :chans], square], axis=1).astype(jnp.bfloat16)
     hidden = silu(jnp.dot(invariant, update_ref[...], preferred_element_type=jnp.float32))
     features_ref[...] = (packed[0][:atoms] + hidden).astype(jnp.bfloat16)
-    readout = jnp.broadcast_to(out_ref[...], (8, chans))
-    chi = over_last(readout, hidden, lax.Precision.HIGHEST)[0:1] + base_ref[6:7, :]
-    rhs = base_ref[5:6, :] - chi
-    wide = jnp.zeros((1, chans - atoms), jnp.float32)
-    rows = [base_ref[0:1, :], jnp.zeros((2, atoms), jnp.float32), rhs]
-    rows = rows + [base_ref[place : place + 1, :] for place in range(4, 0, -1)]
-    block = jnp.concatenate(
-        [jnp.concatenate(rows, axis=0), jnp.broadcast_to(wide, (8, chans - atoms))], axis=1
-    )
-    block = pltpu.roll(block, 0, 1, stride=atoms, stride_axis=0)
-    row = jnp.sum(block, axis=0, keepdims=True)
+    chi = jnp.sum(hidden * out_ref[...], axis=1, keepdims=True)
+    lane = lax.broadcasted_iota(jnp.int32, (atoms, chans), 1)
+    atom = lax.broadcasted_iota(jnp.int32, (atoms, chans), 0)
+    place = lane == atom + rhs_segment * atoms
+    row = row_ref[...] - jnp.sum(jnp.where(place, chi, 0.0), axis=0, keepdims=True)
     block_ref[...] = jnp.broadcast_to(row[None], block_ref.shape)
 
 
+def reciprocal(value):
+    rough = pl.reciprocal(value, approx=True)
+    return rough * (2.0 - value * rough)
+
+
 def smeared(scaled):
-    decay = jnp.exp(-(scaled * scaled))
-    turn = 1.0 / (1.0 + 0.3275911 * scaled)
+    decay = jnp.exp2(scaled * scaled * -math.log2(math.e))
+    turn = reciprocal(1.0 + 0.3275911 * scaled)
     series = 1.061405429 * turn - 1.453152027
     series = series * turn + 1.421413741
     series = series * turn - 0.284496736
@@ -379,7 +409,9 @@
     return 1.0 - series * turn * decay, decay
 
 
-def charge_kernel(place_ref, field_ref, all_ref, charges_ref, forces_ref, virial_ref, matrix_ref):
+def charge_kernel(
+    place_ref, field_ref, all_ref, charges_ref, forces_ref, virial_ref, matrix_ref, side_ref
+):
     blocks, _, lanes = all_ref.shape
     own = charges_ref.shape[1]
     count = blocks * own
@@ -397,31 +429,58 @@
     everyone = jnp.concatenate(tiles, axis=1)
     everyone = pltpu.roll(everyone, lax.rem(count - place_ref[0] * own, count), 1)
     columns = everyone.T
-    spread_row = everyone[3:4] * everyone[3:4]
-    rhs = everyone[5:6]
-    diag = everyone[4:5]
+    diag, rhs = everyone[4:5], everyone[5:6]
     rows = own
-
-    def pairs(start):
+    spread_row = 2.0 * everyone[3:4] * everyone[3:4]
+    tiles = count // lanes
+    lane = lax.broadcasted_iota(jnp.int32, (rows, lanes), 1)
+    line = lax.broadcasted_iota(jnp.int32, (rows, lanes), 0)
+
+    def part(row, tile):
+        return row[:, tile * lanes : (tile + 1) * lanes]
+
+    def spread(column):
+        return jnp.broadcast_to(column, (rows, lanes))
+
+    above = [jnp.zeros((rows, lanes), jnp.float32) for _ in range(tiles)]
+    kept = []
+    for start in range(0, count, rows):
+        first = start // lanes
         column = columns[start : start + rows]
-        delta = [column[:, axis : axis + 1] - everyone[axis : axis + 1] for axis in range(3)]
-        squared = delta[0] * delta[0] + delta[1] * delta[1] + delta[2] * delta[2]
-        same = lax.broadcasted_iota(jnp.int32, (rows, count), 1) == (
-            lax.broadcasted_iota(jnp.int32, (rows, count), 0) + start
-        )
-        squared = jnp.where(same, 1.0, squared)
-        inverse = lax.rsqrt(squared)
-        spread = column[:, 3:4] * column[:, 3:4] + spread_row
-        scale = lax.rsqrt(2.0 * spread)
-        smear, decay = smeared(squared * inverse * scale)
-        return delta, same, inverse, scale, jnp.where(same, 0.0, smear * inverse), decay
-
-    image = jnp.zeros((rows, count), jnp.float32)
-    for start in range(0, count, rows):
-        kernel = pairs(start)[4]
-        matrix_ref[start : start + rows, :] = kernel
-        image = image + kernel * columns[start : start + rows, 5:6]
-    image = diag * rhs + jnp.sum(image, axis=0, keepdims=True)
+        place = [spread(column[:, axis : axis + 1]) for axis in range(3)]
+        wide = spread(2.0 * column[:, 3:4] * column[:, 3:4])
+        value = spread(column[:, 5:6])
+        below = jnp.zeros((rows, lanes), jnp.float32)
+        for tile in range(first, tiles):
+            delta = [place[axis] - part(everyone[axis : axis + 1], tile) for axis in range(3)]
+            squared = delta[0] * delta[0] + delta[1] * delta[1] + delta[2] * delta[2]
+            if tile == first:
+                same = lane == line + (start - first * lanes)
+                squared = jnp.where(same, 1.0, squared)
+            inverse = lax.rsqrt(squared)
+            scale = lax.rsqrt(wide + part(spread_row, tile))
+            smear, decay = smeared(squared * inverse * scale)
+            kernel = smear * inverse
+            if start == 0:
+                slope = (two_over_root_pi * scale * decay - kernel) * inverse * inverse
+                slope = jnp.where(same, 0.0, slope) if tile == first else slope
+                kept.append((delta, slope))
+            if tile == first:
+                kernel = jnp.where(same, 0.0, kernel)
+            else:
+                below = below + kernel * part(rhs, tile)
+            above[tile] = above[tile] + kernel * value
+            matrix_ref[start : start + rows, tile * lanes : (tile + 1) * lanes] = kernel
+        if first + 1 < tiles:
+            side_ref[start : start + rows, :] = below
+    image = []
+    for tile in range(tiles):
+        value = jnp.sum(above[tile], axis=0, keepdims=True)
+        if tile + 1 < tiles:
+            below = side_ref[tile * lanes : (tile + 1) * lanes, :].T
+            value = value + jnp.sum(below, axis=0, keepdims=True)
+        image.append(value)
+    image = diag * rhs + jnp.concatenate(image, axis=1)
 
     def total(value):
         return jnp.sum(value, axis=1, keepdims=True)
@@ -429,27 +488,38 @@
     norm = total(rhs * rhs)
     alpha = norm / total(rhs * image)
     residual = rhs - alpha * image
-    charges = alpha * rhs
     fresh = total(residual * residual)
     direction = residual + fresh / norm * rhs
     across = jnp.broadcast_to(direction, (8, count)).T
-    image = jnp.zeros((rows, count), jnp.float32)
+    onto = [jnp.zeros((rows, lanes), jnp.float32) for _ in range(tiles)]
+    above = [jnp.zeros((rows, lanes), jnp.float32) for _ in range(tiles)]
     for start in range(0, count, rows):
-        image = image + matrix_ref[start : start + rows, :] * across[start : start + rows, 0:1]
-    image = diag * direction + jnp.sum(image, axis=0, keepdims=True)
-    charges = charges + fresh / total(direction * image) * direction
-
-    delta, same, inverse, scale, kernel, decay = pairs(0)
-    slope = two_over_root_pi * scale * decay * inverse - kernel * inverse
-    weight = jnp.where(same, 0.0, charges * slope * inverse)
-    pulled = [weight * delta[axis] for axis in range(3)]
-    sums = [total(value) for value in pulled]
-    for left, right in ((0, 0), (1, 1), (2, 2), (0, 1), (0, 2), (1, 2)):
-        sums.append(total(pulled[left] * delta[right]))
-    lane = lax.broadcasted_iota(jnp.int32, (rows, 128), 1)
-    table = jnp.zeros((rows, 128), jnp.float32)
+        first = start // lanes
+        value = spread(across[start : start + rows, 0:1])
+        for tile in range(first, tiles):
+            sums = onto if tile == first else above
+            kernel = matrix_ref[start : start + rows, tile * lanes : (tile + 1) * lanes]
+            sums[tile] = sums[tile] + kernel * value
+    curved = jnp.zeros((rows, lanes), jnp.float32)
+    for tile in range(tiles):
+        curved = curved + (onto[tile] + 2.0 * above[tile]) * part(direction, tile)
+    curved = jnp.sum(curved, axis=0, keepdims=True)
+    for tile in range(tiles):
+        curved = curved + part(diag * direction * direction, tile)
+    charges = alpha * rhs + fresh / total(curved) * direction
+
+    sums = [jnp.zeros((rows, lanes), jnp.float32) for _ in range(9)]
+    for tile, (delta, slope) in enumerate(kept):
+        weight = part(charges, tile) * slope
+        pulled = [weight * delta[axis] for axis in range(3)]
+        terms = pulled + [
+            pulled[left] * delta[right]
+            for left, right in ((0, 0), (1, 1), (2, 2), (0, 1), (0, 2), (1, 2))
+        ]
+        sums = [old + term for old, term in zip(sums, terms)]
+    table = jnp.zeros((rows, lanes), jnp.float32)
     for place, value in enumerate(sums):
-        table = jnp.where(lane == place, value, table)
+        table = jnp.where(lane == place, total(value), table)
     table = table.T
     mine = charges[:, :own]
     charges_ref[...] = mine
@@ -476,10 +546,6 @@
         compiler_params=pltpu.CompilerParams(vmem_limit_bytes=32 * 1024 * 1024),
         cost_estimate=pl.CostEstimate(flops=flops, bytes_accessed=1 << 20, transcendentals=0),
     )(*arguments)
-
-
-def shape_of(value):
-    return (value.shape, value.dtype)
 
 
 def exchanged(block, axis, step):
@@ -508,36 +574,41 @@
     atoms, chans = features.shape
     edges = edge_recv.shape[0]
     rows, lanes = lax.axis_size("row"), lax.axis_size("space")
-    (packed,) = kernel_call(
+    rest = (edge_vec, w_rad1, w_rad2, species[None], hardness[None], width[None])
+    rest = rest + (chi_shift[None], positions, edge_send[None], edge_recv[None], w_msg)
+    rest = rest + (w_up, w_out[None])
+    packed, *rest = kernel_call(
         pack_kernel,
-        [((atoms + 16, chans), jnp.bfloat16)],
-        (features, ghost_list),
-        far=2,
-        scratch=[pltpu.VMEM(*shape_of(ghost_list)), pltpu.SemaphoreType.DMA((2,))],
+        [((atoms + 16, chans), jnp.bfloat16)] + [(value.shape, value.dtype) for value in rest],
+        (features, ghost_list) + rest,
+        far=2 + len(rest),
+        scratch=[
+            pltpu.VMEM(ghost_list.shape, ghost_list.dtype),
+            pltpu.SemaphoreType.DMA((2 + len(rest),)),
+        ],
     )
     others = [exchanged(packed, "space", step) for step in range(1, lanes)]
-    own = (edge_vec, w_rad1, w_rad2, species[None], hardness[None], width[None])
-    own = own + (chi_shift[None], positions)
-    kept = (edge_send[None], edge_recv[None], w_msg, w_up, w_out[None])
-    filters, units, base, *kept = kernel_call(
+    space = lax.axis_index("space").astype(jnp.int32)
+    parts = kernel_call(
         edge_kernel,
-        [((2 * chans, edges), jnp.float32), ((8, edges), jnp.float32), ((8, atoms), jnp.float32)]
-        + [shape_of(value) for value in kept],
-        (field,) + own + kept,
-        scalars=1,
-        far=len(own + kept),
-        scratch=[pltpu.VMEM(*shape_of(value)) for value in own]
-        + [pltpu.SemaphoreType.DMA((len(own + kept),))],
+        [
+            ((2 * chans, edges), jnp.float32),
+            ((8, edges), jnp.float32),
+            ((1, chans), jnp.float32),
+            ((chans, edges), jnp.bfloat16),
+            ((lanes * atoms, edges), jnp.float32),
+            ((atoms, edges), jnp.bfloat16),
+            ((2 * chans, chans), jnp.bfloat16),
+        ],
+        (field, space.reshape(1), *rest[:-2]),
+        scalars=2,
         flops=1 << 28,
     )
-    send, receive, project, update, readout = kept
-    space = lax.axis_index("space").astype(jnp.int32)
     devices = rows * lanes
     new_features, block = kernel_call(
         node_kernel,
         [((atoms, chans), jnp.bfloat16), ((devices, 1, chans), jnp.float32)],
-        (space.reshape(1), packed, *others, send, receive)
-        + (filters, units, base, project, update, readout),
+        (space.reshape(1), packed, *others, *parts, *rest[-2:]),
         scalars=1,
         flops=1 << 28,
     )
@@ -549,7 +620,10 @@
         [((count, atoms), jnp.float32) for count in (1, 3, 6)],
         (place.reshape(1), field, block),
         scalars=2,
-        scratch=[pltpu.VMEM((everybody, everybody), jnp.float32)],
+        scratch=[
+            pltpu.VMEM((everybody, everybody), jnp.float32),
+            pltpu.VMEM((everybody, chans), jnp.float32),
+        ],
         flops=1 << 28,
     )
     return (new_features, charges[0], forces, virial)

time: 25 us -> 24.6 us (0.984)
  waiting for transfers between devices: 7.84 us -> 8.99 us
  Pallas kernels: 6.97 us -> 5.98 us
  starting transfers between devices: 8.56 us -> 8.1 us
    ppermute x3, waiting for transfers between devices: 0.69 us -> 1.85 us  [exchanged(): lax.ppermute(block, axis, [(place, place ^ step) for place in range(size)])]
    pallas_call x4, Pallas kernels: 6.97 us -> 5.98 us  [kernel_call(): pl.pallas_call(kernel, out_shape=shapes, in_specs=[pl.BlockSpec(memory_sp...]
    all_to_all x1, starting transfers between devices: 5.41 us -> 4.92 us  [few_shards(): block = lax.all_to_all(block, everywhere, 0, 0, tiled=True)]
  transfers between devices with their start and end apart: 4 -> 4, of which waited for: 2 -> 3; matrix products, arithmetic and copies ran while one was open for 0% -> 0% of each run, Pallas kernels for 7% -> 2%
where the time goes in v7:
time: 24.6 us; the launch traced here: 24.4 us
  waiting for transfers between devices  8.99 us (37%)
  starting transfers between devices  8.1 us (33%)
  Pallas kernels  5.98 us (24%)
  between operations  1.33 us (5%)
    all_to_all x1, waiting for transfers between devices, few_shards(): block = lax.all_to_all(block, everywhere, 0, 0, tiled=True)  7.14 us
    pallas_call x4, Pallas kernels, kernel_call(): pl.pallas_call(kernel, out_shape=shapes, in_specs=[pl.BlockSpec(memory_sp...  5.98 us
    all_to_all x1, starting transfers between devices, few_shards(): block = lax.all_to_all(block, everywhere, 0, 0, tiled=True)  4.92 us
    ppermute x3, starting transfers between devices, exchanged(): lax.ppermute(block, axis, [(place, place ^ step) for place in range(size)])  3.18 us
    ppermute x3, waiting for transfers between devices, exchanged(): lax.ppermute(block, axis, [(place, place ^ step) for place in range(size)])  1.85 us
  transfers between devices with their start and end apart: 4, of which 3 were waited for; matrix products, arithmetic and copies ran while one was open for 0% of the time, Pallas kernels for 2%

profile of v7, /device:TPU:0, one launch (start us, length us, event | category | flops | bytes accessed | tf_op | source)
XLA Modules:
  0.0 24.4 jit_solution(12832075617666806134)
XLA Ops:
  0.6 1.2 %shard_map.183 = (bf16[32,128]{1,0:T(8,128)(2,1)S(1)}, f32[3,512]{1,0:T(4,128)S(1)}, f32[8,128]{1,0:T(8,128)S(1)}, bf16[128,256]{1,0:T(8,128)(2,1)S(1)}, s32[1,1...) custom-call(bf16[16,128]{1,0:T(8,128)(2,1)} %refs_0_.1, ...), custom_call_target="tpu_custom_call" | custom-call | bytes 1048576 | tf_op jit(solution)/shard_map/pallas_call | solution.py:540
  1.8 0.5 %collective-permute-start = (bf16[32,128]{1,0:T(8,128)(2,1)S(1)}, bf16[32,128]{1,0:T(8,128)(2,1)S(1)}, u32[]{:S(2)}, u32[]{:S(2)}) collective-permute-start(bf16[32,128]{1,0:T(8,128)(2,1)S(1)} %get-tuple-element.30.own_ref), channel_id=1, source_target_pairs={{0,1},{1,0},{2,3},{3,2},{4,5},{5,4},{6,7},{7,6},{8,9},{9,8},{10,11... | collective-permute-start | bytes 24584 | tf_op jit(solution)/shard_map/ppermute | solution.py:553
  2.3 2.6 %collective-permute-start.1 = (bf16[32,128]{1,0:T(8,128)(2,1)S(1)}, bf16[32,128]{1,0:T(8,128)(2,1)S(1)}, u32[]{:S(2)}, u32[]{:S(2)}) collective-permute-start(bf16[32,128]{1,0:T(8,128)(2,1)S(1)} %get-tuple-element.30.own_ref), channel_id=1, source_target_pairs={{0,2},{1,3},{2,0},{3,1},{4,6},{5,7},{6,4},{7,5},{8,10},{9,11},{10,... | collective-permute-start | bytes 24584 | tf_op jit(solution)/shard_map/ppermute | solution.py:553
  4.9 0.1 collective-permute-start.2
  5.7 0.5 %shard_map.184 = (f32[256,512]{1,0:T(8,128)S(1)}, f32[8,512]{1,0:T(8,128)S(1)}, f32[1,128]{1,0:T(1,128)S(1)}, bf16[128,512]{1,0:T(8,128)(2,1)S(1)}, f32[64,512]{...) custom-call(f32[1]{0:T(128)S(6)} %copy.20.field_ref, s32[1]{0:T(128)} %bitcast.space_ref, ...), custom_call_target="tpu_custom_call" | custom-call | flops 268435456 | bytes 1048576 | tf_op jit(solution)/shard_map/pallas_call | solution.py:540
  6.2 0.0 collective-permute-done.near_ref
  6.2 0.4 %collective-permute-done.1.side_ref = bf16[32,128]{1,0:T(8,128)(2,1)S(1)} collective-permute-done((bf16[32,128]{1,0:T(8,128)(2,1)S(1)}, bf16[32,128]{1,0:T(8,128)(2,1)S(1)}, u32[]{:S(2)}, u32[]{:S(2)}) %collective-permute-start.1) | collective-permute-done | bytes 8224 | tf_op jit(solution)/shard_map/ppermute | solution.py:553
  6.6 1.4 %collective-permute-done.2.far_ref = bf16[32,128]{1,0:T(8,128)(2,1)S(1)} collective-permute-done((bf16[32,128]{1,0:T(8,128)(2,1)S(1)}, bf16[32,128]{1,0:T(8,128)(2,1)S(1)}, u32[]{:S(2)}, u32[]{:S(2)}) %collective-permute-start.2) | collective-permute-done | bytes 8224 | tf_op jit(solution)/shard_map/ppermute | solution.py:553
  8.0 1.5 %shard_map.185 = (bf16[16,128]{1,0:T(8,128)(2,1)}, f32[32,1,128]{2,1,0:T(1,128)}) custom-call(s32[1]{0:T(128)} %bitcast.space_ref, bf16[32,128]{1,0:T(8,128)(2,1)S(1)} %get-tuple-element.30.own_ref, bf16[32,128]{1,0:T(8,128)(2,1)S(1)} %collective-permute-done.near_ref, bf16[32,128]{1,0:T(8,128)(2,1)S(1)} %collective-permute-done.1.side_ref, ...), custom_call_target="tpu_custom_call" | custom-call | flops 268435456 | bytes 1048576 | tf_op jit(solution)/shard_map/pallas_call | solution.py:540
  9.5 4.9 %all-to-all-start = ((f32[32,1,128]{2,1,0:T(1,128)}), f32[32,1,128]{2,1,0:T(1,128)S(1)}, u32[]{:S(2)}, u32[]{:S(2)}) async-start(f32[32,1,128]{2,1,0:T(1,128)} %get-tuple-element.52), calls=%async_computation | async-start | bytes 32768 | tf_op jit(solution)/shard_map/all_to_all | solution.py:615
  14.4 7.1 %all-to-all-done.all_ref = f32[32,1,128]{2,1,0:T(1,128)S(1)} async-done(((f32[32,1,128]{2,1,0:T(1,128)}), f32[32,1,128]{2,1,0:T(1,128)S(1)}, u32[]{:S(2)}, u32[]{:S(2)}) %all-to-all-start) | async-done | bytes 16416 | tf_op jit(solution)/shard_map/all_to_all | solution.py:615
  21.6 2.8 %shard_map.186 = (f32[1,16]{1,0:T(1,128)}, f32[3,16]{1,0:T(4,128)}, f32[6,16]{1,0:T(8,128)}) custom-call(s32[1]{0:T(128)} %bitcast.8.place_ref, f32[1]{0:T(128)S(6)} %copy.20.field_ref, f32[32,1,128]{2,1,0:T(1,128)S(1)} %all-to-all-done.all_ref), custom_call_target="tpu_custom_call" | custom-call | flops 268435456 | bytes 1048576 | tf_op jit(solution)/shard_map/pallas_call | solution.py:540
Async XLA Ops:
  1.8 4.3 %collective-permute-start = (bf16[32,128]{1,0:T(8,128)(2,1)S(1)}, bf16[32,128]{1,0:T(8,128)(2,1)S(1)}, u32[]{:S(2)}, u32[]{:S(2)}) collective-permute-start(bf16[32,128]{1,0:T(8,128)(2,1)S(1)} %get-tuple-element.30.own_ref), channel_id=1, source_target_pairs={{0,1},{1,0},{2,3},{3,2},{4,5},{5,4},{6,7},{7,6},{8,9},{9,8},{10,11... | collective-permute-start | bytes 24584 | tf_op jit(solution)/shard_map/ppermute | solution.py:553
  2.3 4.2 %collective-permute-start.1 = (bf16[32,128]{1,0:T(8,128)(2,1)S(1)}, bf16[32,128]{1,0:T(8,128)(2,1)S(1)}, u32[]{:S(2)}, u32[]{:S(2)}) collective-permute-start(bf16[32,128]{1,0:T(8,128)(2,1)S(1)} %get-tuple-element.30.own_ref), channel_id=1, source_target_pairs={{0,2},{1,3},{2,0},{3,1},{4,6},{5,7},{6,4},{7,5},{8,10},{9,11},{10,... | collective-permute-start | bytes 24584 | tf_op jit(solution)/shard_map/ppermute | solution.py:553
  4.9 3.1 %collective-permute-start.2 = (bf16[32,128]{1,0:T(8,128)(2,1)S(1)}, bf16[32,128]{1,0:T(8,128)(2,1)S(1)}, u32[]{:S(2)}, u32[]{:S(2)}) collective-permute-start(bf16[32,128]{1,0:T(8,128)(2,1)S(1)} %get-tuple-element.30.own_ref), channel_id=1, source_target_pairs={{0,3},{1,2},{2,1},{3,0},{4,7},{5,6},{6,5},{7,4},{8,11},{9,10},{10,... | collective-permute-start | bytes 24584 | tf_op jit(solution)/shard_map/ppermute | solution.py:553
  9.5 12.1 %all-to-all-start = ((f32[32,1,128]{2,1,0:T(1,128)}), f32[32,1,128]{2,1,0:T(1,128)S(1)}, u32[]{:S(2)}, u32[]{:S(2)}) async-start(f32[32,1,128]{2,1,0:T(1,128)} %get-tuple-element.52), calls=%async_computation | async-start | bytes 32768 | tf_op jit(solution)/shard_map/all_to_all | solution.py:615

commit v8 on v7

--- a/solution.py
+++ b/solution.py
@@ -612,8 +612,9 @@
         scalars=1,
         flops=1 << 28,
     )
-    block = lax.all_to_all(block, everywhere, 0, 0, tiled=True)
-    place = lax.axis_index("row").astype(jnp.int32) * lanes + space
+    order = [list(range(devices - 1, -1, -1))]
+    block = lax.all_to_all(block, everywhere, 0, 0, axis_index_groups=order, tiled=True)
+    place = devices - 1 - (lax.axis_index("row").astype(jnp.int32) * lanes + space)
     everybody = rows * lanes * atoms
     charges, forces, virial = kernel_call(
         charge_kernel,

time: 24.6 us -> 24.6 us (level)
  no operation moved by 1% of the time
where the time goes in v8:
time: 24.6 us; the launch traced here: 24.4 us
  waiting for transfers between devices  8.96 us (36%)
  starting transfers between devices  8.1 us (33%)
  Pallas kernels  5.98 us (24%)
  between operations  1.33 us (5%)
    all_to_all x1, waiting for transfers between devices, few_shards(): lax.all_to_all(block, everywhere, 0, 0, axis_index_groups=order, tiled=True)  7.11 us
    pallas_call x4, Pallas kernels, kernel_call(): pl.pallas_call(kernel, out_shape=shapes, in_specs=[pl.BlockSpec(memory_sp...  5.98 us
    all_to_all x1, starting transfers between devices, few_shards(): lax.all_to_all(block, everywhere, 0, 0, axis_index_groups=order, tiled=True)  4.92 us
    ppermute x3, starting transfers between devices, exchanged(): lax.ppermute(block, axis, [(place, place ^ step) for place in range(size)])  3.18 us
    ppermute x3, waiting for transfers between devices, exchanged(): lax.ppermute(block, axis, [(place, place ^ step) for place in range(size)])  1.85 us
  transfers between devices with their start and end apart: 4, of which 3 were waited for; matrix products, arithmetic and copies ran while one was open for 0% of the time, Pallas kernels for 2%

profile of v8, /device:TPU:0, one launch (start us, length us, event | category | flops | bytes accessed | tf_op | source)
XLA Modules:
  0.0 24.4 jit_solution(2625059834695173158)
XLA Ops:
  0.6 1.2 %shard_map.183 = (bf16[32,128]{1,0:T(8,128)(2,1)S(1)}, f32[3,512]{1,0:T(4,128)S(1)}, f32[8,128]{1,0:T(8,128)S(1)}, bf16[128,256]{1,0:T(8,128)(2,1)S(1)}, s32[1,1...) custom-call(bf16[16,128]{1,0:T(8,128)(2,1)} %refs_0_.1, ...), custom_call_target="tpu_custom_call" | custom-call | bytes 1048576 | tf_op jit(solution)/shard_map/pallas_call | solution.py:540
  1.8 0.5 %collective-permute-start = (bf16[32,128]{1,0:T(8,128)(2,1)S(1)}, bf16[32,128]{1,0:T(8,128)(2,1)S(1)}, u32[]{:S(2)}, u32[]{:S(2)}) collective-permute-start(bf16[32,128]{1,0:T(8,128)(2,1)S(1)} %get-tuple-element.30.own_ref), channel_id=1, source_target_pairs={{0,1},{1,0},{2,3},{3,2},{4,5},{5,4},{6,7},{7,6},{8,9},{9,8},{10,11... | collective-permute-start | bytes 24584 | tf_op jit(solution)/shard_map/ppermute | solution.py:553
  2.3 2.6 %collective-permute-start.1 = (bf16[32,128]{1,0:T(8,128)(2,1)S(1)}, bf16[32,128]{1,0:T(8,128)(2,1)S(1)}, u32[]{:S(2)}, u32[]{:S(2)}) collective-permute-start(bf16[32,128]{1,0:T(8,128)(2,1)S(1)} %get-tuple-element.30.own_ref), channel_id=1, source_target_pairs={{0,2},{1,3},{2,0},{3,1},{4,6},{5,7},{6,4},{7,5},{8,10},{9,11},{10,... | collective-permute-start | bytes 24584 | tf_op jit(solution)/shard_map/ppermute | solution.py:553
  4.9 0.1 collective-permute-start.2
  5.7 0.5 %shard_map.184 = (f32[256,512]{1,0:T(8,128)S(1)}, f32[8,512]{1,0:T(8,128)S(1)}, f32[1,128]{1,0:T(1,128)S(1)}, bf16[128,512]{1,0:T(8,128)(2,1)S(1)}, f32[64,512]{...) custom-call(f32[1]{0:T(128)S(6)} %copy.20.field_ref, s32[1]{0:T(128)} %bitcast.space_ref, ...), custom_call_target="tpu_custom_call" | custom-call | flops 268435456 | bytes 1048576 | tf_op jit(solution)/shard_map/pallas_call | solution.py:540
  6.2 0.0 collective-permute-done.near_ref
  6.2 0.4 %collective-permute-done.1.side_ref = bf16[32,128]{1,0:T(8,128)(2,1)S(1)} collective-permute-done((bf16[32,128]{1,0:T(8,128)(2,1)S(1)}, bf16[32,128]{1,0:T(8,128)(2,1)S(1)}, u32[]{:S(2)}, u32[]{:S(2)}) %collective-permute-start.1) | collective-permute-done | bytes 8224 | tf_op jit(solution)/shard_map/ppermute | solution.py:553
  6.6 1.4 %collective-permute-done.2.far_ref = bf16[32,128]{1,0:T(8,128)(2,1)S(1)} collective-permute-done((bf16[32,128]{1,0:T(8,128)(2,1)S(1)}, bf16[32,128]{1,0:T(8,128)(2,1)S(1)}, u32[]{:S(2)}, u32[]{:S(2)}) %collective-permute-start.2) | collective-permute-done | bytes 8224 | tf_op jit(solution)/shard_map/ppermute | solution.py:553
  8.0 1.5 %shard_map.185 = (bf16[16,128]{1,0:T(8,128)(2,1)}, f32[32,1,128]{2,1,0:T(1,128)}) custom-call(s32[1]{0:T(128)} %bitcast.space_ref, bf16[32,128]{1,0:T(8,128)(2,1)S(1)} %get-tuple-element.30.own_ref, bf16[32,128]{1,0:T(8,128)(2,1)S(1)} %collective-permute-done.near_ref, bf16[32,128]{1,0:T(8,128)(2,1)S(1)} %collective-permute-done.1.side_ref, ...), custom_call_target="tpu_custom_call" | custom-call | flops 268435456 | bytes 1048576 | tf_op jit(solution)/shard_map/pallas_call | solution.py:540
  9.5 4.9 %all-to-all-start = ((f32[32,1,128]{2,1,0:T(1,128)}), f32[32,1,128]{2,1,0:T(1,128)S(1)}, u32[]{:S(2)}, u32[]{:S(2)}) async-start(f32[32,1,128]{2,1,0:T(1,128)} %get-tuple-element.52), calls=%async_computation | async-start | bytes 32768 | tf_op jit(solution)/shard_map/all_to_all | solution.py:616
  14.4 7.1 %all-to-all-done.all_ref = f32[32,1,128]{2,1,0:T(1,128)S(1)} async-done(((f32[32,1,128]{2,1,0:T(1,128)}), f32[32,1,128]{2,1,0:T(1,128)S(1)}, u32[]{:S(2)}, u32[]{:S(2)}) %all-to-all-start) | async-done | bytes 16416 | tf_op jit(solution)/shard_map/all_to_all | solution.py:616
  21.6 2.8 %shard_map.186 = (f32[1,16]{1,0:T(1,128)}, f32[3,16]{1,0:T(4,128)}, f32[6,16]{1,0:T(8,128)}) custom-call(s32[1]{0:T(128)} %bitcast.8.place_ref, f32[1]{0:T(128)S(6)} %copy.20.field_ref, f32[32,1,128]{2,1,0:T(1,128)S(1)} %all-to-all-done.all_ref), custom_call_target="tpu_custom_call" | custom-call | flops 268435456 | bytes 1048576 | tf_op jit(solution)/shard_map/pallas_call | solution.py:540
Async XLA Ops:
  1.8 4.3 %collective-permute-start = (bf16[32,128]{1,0:T(8,128)(2,1)S(1)}, bf16[32,128]{1,0:T(8,128)(2,1)S(1)}, u32[]{:S(2)}, u32[]{:S(2)}) collective-permute-start(bf16[32,128]{1,0:T(8,128)(2,1)S(1)} %get-tuple-element.30.own_ref), channel_id=1, source_target_pairs={{0,1},{1,0},{2,3},{3,2},{4,5},{5,4},{6,7},{7,6},{8,9},{9,8},{10,11... | collective-permute-start | bytes 24584 | tf_op jit(solution)/shard_map/ppermute | solution.py:553
  2.3 4.2 %collective-permute-start.1 = (bf16[32,128]{1,0:T(8,128)(2,1)S(1)}, bf16[32,128]{1,0:T(8,128)(2,1)S(1)}, u32[]{:S(2)}, u32[]{:S(2)}) collective-permute-start(bf16[32,128]{1,0:T(8,128)(2,1)S(1)} %get-tuple-element.30.own_ref), channel_id=1, source_target_pairs={{0,2},{1,3},{2,0},{3,1},{4,6},{5,7},{6,4},{7,5},{8,10},{9,11},{10,... | collective-permute-start | bytes 24584 | tf_op jit(solution)/shard_map/ppermute | solution.py:553
  4.9 3.1 %collective-permute-start.2 = (bf16[32,128]{1,0:T(8,128)(2,1)S(1)}, bf16[32,128]{1,0:T(8,128)(2,1)S(1)}, u32[]{:S(2)}, u32[]{:S(2)}) collective-permute-start(bf16[32,128]{1,0:T(8,128)(2,1)S(1)} %get-tuple-element.30.own_ref), channel_id=1, source_target_pairs={{0,3},{1,2},{2,1},{3,0},{4,7},{5,6},{6,5},{7,4},{8,11},{9,10},{10,... | collective-permute-start | bytes 24584 | tf_op jit(solution)/shard_map/ppermute | solution.py:553
  9.5 12.0 %all-to-all-start = ((f32[32,1,128]{2,1,0:T(1,128)}), f32[32,1,128]{2,1,0:T(1,128)S(1)}, u32[]{:S(2)}, u32[]{:S(2)}) async-start(f32[32,1,128]{2,1,0:T(1,128)} %get-tuple-element.52), calls=%async_computation | async-start | bytes 32768 | tf_op jit(solution)/shard_map/all_to_all | solution.py:616

commit v9 on v7

--- a/solution.py
+++ b/solution.py
@@ -257,6 +257,25 @@
     vec_ref,
     first_ref,
     second_ref,
+    species_far,
+    hardness_far,
+    width_far,
+    shift_far,
+    positions_far,
+    send_far,
+    recv_far,
+    project_far,
+    update_far,
+    out_far,
+    filter_ref,
+    unit_ref,
+    row_ref,
+    slot_ref,
+    local_ref,
+    hit_ref,
+    turned_ref,
+    upward_ref,
+    read_ref,
     species_ref,
     hardness_ref,
     width_ref,
@@ -265,14 +284,15 @@
     send_ref,
     recv_ref,
     project_ref,
-    filter_ref,
-    unit_ref,
-    row_ref,
-    slot_ref,
-    local_ref,
-    hit_ref,
-    turned_ref,
+    update_ref,
+    out_ref,
+    semaphores,
 ):
+    far = (send_far, recv_far, project_far, update_far, species_far, hardness_far)
+    far = far + (width_far, shift_far, positions_far, out_far)
+    near = (send_ref, recv_ref, project_ref, update_ref, species_ref, hardness_ref)
+    near = near + (width_ref, shift_ref, positions_ref, out_ref)
+    copies = fetched(list(zip(far, near)), semaphores)
     edges = vec_ref.shape[1]
     orders = first_ref.shape[0]
     vec = vec_ref[...]
@@ -299,6 +319,8 @@
     )
     radial = silu_half(mixed).astype(jnp.bfloat16)
     filter_ref[...] = over_first(second_ref[...], radial)
+    for copy in copies:
+        copy.wait()
     species = species_ref[...]
 
     def table(ref):
@@ -335,6 +357,8 @@
     chosen(local_ref, local)
     chosen(hit_ref, recv_ref[...])
     turned_ref[...] = project_ref[...].astype(jnp.float32).T.astype(jnp.bfloat16)
+    upward_ref[...] = update_ref[...].astype(jnp.float32).T.astype(jnp.bfloat16)
+    read_ref[...] = jnp.broadcast_to(out_ref[...], (atoms, chans)).T
 
 
 def node_kernel(
@@ -350,8 +374,8 @@
     local_ref,
     hit_ref,
     turned_ref,
-    update_ref,
-    out_ref,
+    upward_ref,
+    read_ref,
     features_ref,
     block_ref,
 ):
@@ -378,20 +402,18 @@
     carried = picked[chans:] * filter_ref[chans:, :]
     parts = [scalar] + [unit_ref[axis : axis + 1, :] * carried for axis in range(3)]
     message = jnp.concatenate([part.astype(jnp.bfloat16) for part in parts], axis=0)
-    summed = over_last(hit_ref[...], message) * message_scale
-    square = jnp.zeros((atoms, chans), jnp.float32)
+    summed = over_last(message, hit_ref[...]) * message_scale
+    square = jnp.zeros((chans, atoms), jnp.float32)
     for component in range(1, 4):
-        part = summed[:, component * chans : (component + 1) * chans]
+        part = summed[component * chans : (component + 1) * chans]
         square = square + part * part
-    invariant = jnp.concatenate([summed[:, :chans], square], axis=1).astype(jnp.bfloat16)
-    hidden = silu(jnp.dot(invariant, update_ref[...], preferred_element_type=jnp.float32))
-    features_ref[...] = (packed[0][:atoms] + hidden).astype(jnp.bfloat16)
-    chi = jnp.sum(hidden * out_ref[...], axis=1, keepdims=True)
-    lane = lax.broadcasted_iota(jnp.int32, (atoms, chans), 1)
-    atom = lax.broadcasted_iota(jnp.int32, (atoms, chans), 0)
-    place = lane == atom + rhs_segment * atoms
-    row = row_ref[...] - jnp.sum(jnp.where(place, chi, 0.0), axis=0, keepdims=True)
+    invariant = jnp.concatenate([summed[:chans], square], axis=0).astype(jnp.bfloat16)
+    hidden = silu(jnp.dot(upward_ref[...], invariant, preferred_element_type=jnp.float32))
+    chi = jnp.sum(hidden * read_ref[...], axis=0, keepdims=True)
+    chi = jnp.concatenate([chi, jnp.zeros((1, chans - atoms), jnp.float32)], axis=1)
+    row = row_ref[...] - pltpu.roll(chi, rhs_segment * atoms, 1)
     block_ref[...] = jnp.broadcast_to(row[None], block_ref.shape)
+    features_ref[...] = (packed[0][:atoms] + hidden.T).astype(jnp.bfloat16)
 
 
 def reciprocal(value):
@@ -410,8 +432,19 @@
 
 
 def charge_kernel(
-    place_ref, field_ref, all_ref, charges_ref, forces_ref, virial_ref, matrix_ref, side_ref
+    place_ref,
+    field_ref,
+    all_ref,
+    ready_ref,
+    charges_ref,
+    forces_ref,
+    virial_ref,
+    features_ref,
+    matrix_ref,
+    side_ref,
+    value_ref,
 ):
+    features_ref[...] = ready_ref[...]
     blocks, _, lanes = all_ref.shape
     own = charges_ref.shape[1]
     count = blocks * own
@@ -421,13 +454,12 @@
     for first in range(0, blocks, fit):
         tile = jnp.zeros((8, lanes), jnp.float32)
         for place in range(fit):
-            row = jnp.broadcast_to(all_ref[first + place], (8, lanes))
-            row = pltpu.roll(row, 0, 1, stride=own, stride_axis=0)
+            row = all_ref[lax.rem(place_ref[0] + first + place, blocks)]
+            row = pltpu.roll(jnp.broadcast_to(row, (8, lanes)), 0, 1, stride=own, stride_axis=0)
             row = pltpu.roll(row, place * own, 1) if place else row
             tile = jnp.where(segment == place, row, tile)
         tiles.append(tile)
     everyone = jnp.concatenate(tiles, axis=1)
-    everyone = pltpu.roll(everyone, lax.rem(count - place_ref[0] * own, count), 1)
     columns = everyone.T
     diag, rhs = everyone[4:5], everyone[5:6]
     rows = own
@@ -450,6 +482,7 @@
         place = [spread(column[:, axis : axis + 1]) for axis in range(3)]
         wide = spread(2.0 * column[:, 3:4] * column[:, 3:4])
         value = spread(column[:, 5:6])
+        value_ref[start : start + rows, :] = value
         below = jnp.zeros((rows, lanes), jnp.float32)
         for tile in range(first, tiles):
             delta = [place[axis] - part(everyone[axis : axis + 1], tile) for axis in range(3)]
@@ -481,6 +514,7 @@
             value = value + jnp.sum(below, axis=0, keepdims=True)
         image.append(value)
     image = diag * rhs + jnp.concatenate(image, axis=1)
+    across = jnp.broadcast_to(image, (8, count)).T
 
     def total(value):
         return jnp.sum(value, axis=1, keepdims=True)
@@ -489,13 +523,14 @@
     alpha = norm / total(rhs * image)
     residual = rhs - alpha * image
     fresh = total(residual * residual)
-    direction = residual + fresh / norm * rhs
-    across = jnp.broadcast_to(direction, (8, count)).T
+    again = fresh / norm
+    direction = residual + again * rhs
     onto = [jnp.zeros((rows, lanes), jnp.float32) for _ in range(tiles)]
     above = [jnp.zeros((rows, lanes), jnp.float32) for _ in range(tiles)]
     for start in range(0, count, rows):
         first = start // lanes
-        value = spread(across[start : start + rows, 0:1])
+        value = (1.0 + again) * value_ref[start : start + rows, :]
+        value = value - alpha * spread(across[start : start + rows, 0:1])
         for tile in range(first, tiles):
             sums = onto if tile == first else above
             kernel = matrix_ref[start : start + rows, tile * lanes : (tile + 1) * lanes]
@@ -529,9 +564,9 @@
     virial_ref[...] = 0.5 * mine * table[3:9]
 
 
-def kernel_call(kernel, shapes, arguments, scalars=0, far=0, scratch=(), flops=0):
+def kernel_call(kernel, shapes, arguments, scalars=0, near=0, far=0, scratch=(), flops=0):
     shapes = tuple(jax.ShapeDtypeStruct(shape, kind) for shape, kind in shapes)
-    spaces = [pltpu.SMEM] * scalars + [pltpu.HBM] * far
+    spaces = [pltpu.SMEM] * scalars + [pltpu.VMEM] * near + [pltpu.HBM] * far
     spaces = spaces + [pltpu.VMEM] * (len(arguments) - len(spaces))
     arguments = [
         pltpu.with_memory_space_constraint(value, space) if space is pltpu.HBM else value
@@ -574,21 +609,21 @@
     atoms, chans = features.shape
     edges = edge_recv.shape[0]
     rows, lanes = lax.axis_size("row"), lax.axis_size("space")
-    rest = (edge_vec, w_rad1, w_rad2, species[None], hardness[None], width[None])
-    rest = rest + (chi_shift[None], positions, edge_send[None], edge_recv[None], w_msg)
-    rest = rest + (w_up, w_out[None])
-    packed, *rest = kernel_call(
+    first = (edge_vec, w_rad1, w_rad2)
+    packed, *first = kernel_call(
         pack_kernel,
-        [((atoms + 16, chans), jnp.bfloat16)] + [(value.shape, value.dtype) for value in rest],
-        (features, ghost_list) + rest,
-        far=2 + len(rest),
+        [((atoms + 16, chans), jnp.bfloat16)] + [(value.shape, value.dtype) for value in first],
+        (features, ghost_list) + first,
+        far=2 + len(first),
         scratch=[
             pltpu.VMEM(ghost_list.shape, ghost_list.dtype),
-            pltpu.SemaphoreType.DMA((2 + len(rest),)),
+            pltpu.SemaphoreType.DMA((2 + len(first),)),
         ],
     )
     others = [exchanged(packed, "space", step) for step in range(1, lanes)]
     space = lax.axis_index("space").astype(jnp.int32)
+    rest = (species[None], hardness[None], width[None], chi_shift[None], positions)
+    rest = rest + (edge_send[None], edge_recv[None], w_msg, w_up, w_out[None])
     parts = kernel_call(
         edge_kernel,
         [
@@ -599,29 +634,37 @@
             ((lanes * atoms, edges), jnp.float32),
             ((atoms, edges), jnp.bfloat16),
             ((2 * chans, chans), jnp.bfloat16),
+            ((chans, 2 * chans), jnp.bfloat16),
+            ((chans, atoms), jnp.float32),
         ],
-        (field, space.reshape(1), *rest[:-2]),
+        (field, space.reshape(1), *first, *rest),
         scalars=2,
+        near=len(first),
+        far=len(rest),
+        scratch=[pltpu.VMEM(value.shape, value.dtype) for value in rest]
+        + [pltpu.SemaphoreType.DMA((len(rest),))],
         flops=1 << 28,
     )
     devices = rows * lanes
-    new_features, block = kernel_call(
+    ready, block = kernel_call(
         node_kernel,
         [((atoms, chans), jnp.bfloat16), ((devices, 1, chans), jnp.float32)],
-        (space.reshape(1), packed, *others, *parts, *rest[-2:]),
+        (space.reshape(1), packed, *others, *parts),
         scalars=1,
         flops=1 << 28,
     )
     block = lax.all_to_all(block, everywhere, 0, 0, tiled=True)
     place = lax.axis_index("row").astype(jnp.int32) * lanes + space
     everybody = rows * lanes * atoms
-    charges, forces, virial = kernel_call(
+    charges, forces, virial, new_features = kernel_call(
         charge_kernel,
-        [((count, atoms), jnp.float32) for count in (1, 3, 6)],
-        (place.reshape(1), field, block),
+        [((count, atoms), jnp.float32) for count in (1, 3, 6)]
+        + [((atoms, chans), jnp.bfloat16)],
+        (place.reshape(1), field, block, ready),
         scalars=2,
         scratch=[
             pltpu.VMEM((everybody, everybody), jnp.float32),
+            pltpu.VMEM((everybody, chans), jnp.float32),
             pltpu.VMEM((everybody, chans), jnp.float32),
         ],
         flops=1 << 28,

time: 24.6 us -> 24.3 us (0.988)
  waiting for transfers between devices: 8.99 us -> 8.16 us
  Pallas kernels: 5.98 us -> 6.35 us
    ppermute x3, waiting for transfers between devices: 1.85 us -> 1.02 us  [exchanged(): lax.ppermute(block, axis, [(place, place ^ step) for place in range(size)])]
    pallas_call x4, Pallas kernels: 5.98 us -> 6.35 us  [kernel_call(): pl.pallas_call(kernel, out_shape=shapes, in_specs=[pl.BlockSpec(memory_sp...]
  transfers between devices with their start and end apart: 4 -> 4, of which waited for: 3 -> 2; matrix products, arithmetic and copies ran while one was open for 0% -> 0% of each run, Pallas kernels for 2% -> 5%
where the time goes in v9:
time: 24.3 us; the launch traced here: 24.1 us
  starting transfers between devices  8.22 us (34%)
  waiting for transfers between devices  8.16 us (34%)
  Pallas kernels  6.35 us (26%)
  between operations  1.33 us (5%)
    all_to_all x1, waiting for transfers between devices, few_shards(): block = lax.all_to_all(block, everywhere, 0, 0, tiled=True)  7.14 us
    pallas_call x4, Pallas kernels, kernel_call(): pl.pallas_call(kernel, out_shape=shapes, in_specs=[pl.BlockSpec(memory_sp...  6.35 us
    all_to_all x1, starting transfers between devices, few_shards(): block = lax.all_to_all(block, everywhere, 0, 0, tiled=True)  5.04 us
    ppermute x3, starting transfers between devices, exchanged(): lax.ppermute(block, axis, [(place, place ^ step) for place in range(size)])  3.18 us
    ppermute x3, waiting for transfers between devices, exchanged(): lax.ppermute(block, axis, [(place, place ^ step) for place in range(size)])  1.02 us
  transfers between devices with their start and end apart: 4, of which 2 were waited for; matrix products, arithmetic and copies ran while one was open for 0% of the time, Pallas kernels for 5%

profile of v9, /device:TPU:0, one launch (start us, length us, event | category | flops | bytes accessed | tf_op | source)
XLA Modules:
  0.0 24.1 jit_solution(7895335429745599675)
XLA Ops:
  0.6 0.9 %shard_map.183 = (bf16[32,128]{1,0:T(8,128)(2,1)S(1)}, f32[3,512]{1,0:T(4,128)S(1)}, f32[8,128]{1,0:T(8,128)S(1)}, bf16[128,256]{1,0:T(8,128)(2,1)S(1)}) custom-call(bf16[16,128]{1,0:T(8,128)(2,1)} %refs_0_.1, s32[1,4,32]{2,1,0:T(4,128)} %refs_1_.1, f32[3,512]{1,0:T(4,128)} %refs_2_.1, f32[8,128]{1,0:T(8,128)} %refs_3_.1, bf16[128,256]{1,0:T(8,128)(2,1)} %refs_4_.1), custom_call_target="tpu_custom_call" | custom-call | bytes 1048576 | tf_op jit(solution)/shard_map/pallas_call | solution.py:575
  1.6 0.5 %collective-permute-start = (bf16[32,128]{1,0:T(8,128)(2,1)S(1)}, bf16[32,128]{1,0:T(8,128)(2,1)S(1)}, u32[]{:S(2)}, u32[]{:S(2)}) collective-permute-start(bf16[32,128]{1,0:T(8,128)(2,1)S(1)} %get-tuple-element.23.own_ref), channel_id=1, source_target_pairs={{0,1},{1,0},{2,3},{3,2},{4,5},{5,4},{6,7},{7,6},{8,9},{9,8},{10,11... | collective-permute-start | bytes 24584 | tf_op jit(solution)/shard_map/ppermute | solution.py:588
  2.1 2.6 %collective-permute-start.1 = (bf16[32,128]{1,0:T(8,128)(2,1)S(1)}, bf16[32,128]{1,0:T(8,128)(2,1)S(1)}, u32[]{:S(2)}, u32[]{:S(2)}) collective-permute-start(bf16[32,128]{1,0:T(8,128)(2,1)S(1)} %get-tuple-element.23.own_ref), channel_id=1, source_target_pairs={{0,2},{1,3},{2,0},{3,1},{4,6},{5,7},{6,4},{7,5},{8,10},{9,11},{10,... | collective-permute-start | bytes 24584 | tf_op jit(solution)/shard_map/ppermute | solution.py:588
  4.7 0.1 collective-permute-start.2
  5.4 1.3 %shard_map.184 = (f32[256,512]{1,0:T(8,128)S(1)}, f32[8,512]{1,0:T(8,128)S(1)}, f32[1,128]{1,0:T(1,128)S(1)}, bf16[128,512]{1,0:T(8,128)(2,1)S(1)}, f32[64,512]{...) custom-call(f32[1]{0:T(128)S(6)} %copy.20.field_ref, ...), custom_call_target="tpu_custom_call" | custom-call | flops 268435456 | bytes 1048576 | tf_op jit(solution)/shard_map/pallas_call | solution.py:575
  6.7 0.0 collective-permute-done.near_ref
  6.8 0.0 collective-permute-done.1.side_ref
  6.8 1.0 %collective-permute-done.2.far_ref = bf16[32,128]{1,0:T(8,128)(2,1)S(1)} collective-permute-done((bf16[32,128]{1,0:T(8,128)(2,1)S(1)}, bf16[32,128]{1,0:T(8,128)(2,1)S(1)}, u32[]{:S(2)}, u32[]{:S(2)}) %collective-permute-start.2) | collective-permute-done | bytes 8224 | tf_op jit(solution)/shard_map/ppermute | solution.py:588
  7.8 1.6 %shard_map.185 = (bf16[16,128]{1,0:T(8,128)(2,1)S(1)}, f32[32,1,128]{2,1,0:T(1,128)}) custom-call(s32[1]{0:T(128)} %bitcast.1.space_ref, bf16[32,128]{1,0:T(8,128)(2,1)S(1)} %get-tuple-element.23.own_ref, bf16[32,128]{1,0:T(8,128)(2,1)S(1)} %collective-permute-done.near_ref, bf16[32,128]{1,0:T(8,128)(2,1)S(1)} %collective-permute-done.1.side_ref, ...), custom_call_target="tpu_custom_call" | custom-call | flops 268435456 | bytes 1048576 | tf_op jit(solution)/shard_map/pallas_call | solution.py:575
  9.3 5.0 %all-to-all-start = ((f32[32,1,128]{2,1,0:T(1,128)}), f32[32,1,128]{2,1,0:T(1,128)S(1)}, u32[]{:S(2)}, u32[]{:S(2)}) async-start(f32[32,1,128]{2,1,0:T(1,128)} %get-tuple-element.36), calls=%async_computation | async-start | bytes 32768 | tf_op jit(solution)/shard_map/all_to_all | solution.py:656
  14.4 7.1 %all-to-all-done.all_ref = f32[32,1,128]{2,1,0:T(1,128)S(1)} async-done(((f32[32,1,128]{2,1,0:T(1,128)}), f32[32,1,128]{2,1,0:T(1,128)S(1)}, u32[]{:S(2)}, u32[]{:S(2)}) %all-to-all-start) | async-done | bytes 16416 | tf_op jit(solution)/shard_map/all_to_all | solution.py:656
  21.5 2.5 %shard_map.186 = (f32[1,16]{1,0:T(1,128)}, f32[3,16]{1,0:T(4,128)}, f32[6,16]{1,0:T(8,128)}, bf16[16,128]{1,0:T(8,128)(2,1)}) custom-call(s32[1]{0:T(128)} %bitcast.place_ref, f32[1]{0:T(128)S(6)} %copy.20.field_ref, f32[32,1,128]{2,1,0:T(1,128)S(1)} %all-to-all-done.all_ref, bf16[16,128]{1,0:T(8,128)(2,1)S(1)} %get-tuple-element.37.ready_ref), custom_call_target="tpu_custom_call" | custom-call | flops 268435456 | bytes 1048576 | tf_op jit(solution)/shard_map/pallas_call | solution.py:575
Async XLA Ops:
  1.6 5.2 %collective-permute-start = (bf16[32,128]{1,0:T(8,128)(2,1)S(1)}, bf16[32,128]{1,0:T(8,128)(2,1)S(1)}, u32[]{:S(2)}, u32[]{:S(2)}) collective-permute-start(bf16[32,128]{1,0:T(8,128)(2,1)S(1)} %get-tuple-element.23.own_ref), channel_id=1, source_target_pairs={{0,1},{1,0},{2,3},{3,2},{4,5},{5,4},{6,7},{7,6},{8,9},{9,8},{10,11... | collective-permute-start | bytes 24584 | tf_op jit(solution)/shard_map/ppermute | solution.py:588
  2.1 4.6 %collective-permute-start.1 = (bf16[32,128]{1,0:T(8,128)(2,1)S(1)}, bf16[32,128]{1,0:T(8,128)(2,1)S(1)}, u32[]{:S(2)}, u32[]{:S(2)}) collective-permute-start(bf16[32,128]{1,0:T(8,128)(2,1)S(1)} %get-tuple-element.23.own_ref), channel_id=1, source_target_pairs={{0,2},{1,3},{2,0},{3,1},{4,6},{5,7},{6,4},{7,5},{8,10},{9,11},{10,... | collective-permute-start | bytes 24584 | tf_op jit(solution)/shard_map/ppermute | solution.py:588
  4.7 3.1 %collective-permute-start.2 = (bf16[32,128]{1,0:T(8,128)(2,1)S(1)}, bf16[32,128]{1,0:T(8,128)(2,1)S(1)}, u32[]{:S(2)}, u32[]{:S(2)}) collective-permute-start(bf16[32,128]{1,0:T(8,128)(2,1)S(1)} %get-tuple-element.23.own_ref), channel_id=1, source_target_pairs={{0,3},{1,2},{2,1},{3,0},{4,7},{5,6},{6,5},{7,4},{8,11},{9,10},{10,... | collective-permute-start | bytes 24584 | tf_op jit(solution)/shard_map/ppermute | solution.py:588
  9.3 12.2 %all-to-all-start = ((f32[32,1,128]{2,1,0:T(1,128)}), f32[32,1,128]{2,1,0:T(1,128)S(1)}, u32[]{:S(2)}, u32[]{:S(2)}) async-start(f32[32,1,128]{2,1,0:T(1,128)} %get-tuple-element.36), calls=%async_computation | async-start | bytes 32768 | tf_op jit(solution)/shard_map/all_to_all | solution.py:656

commit v10 on v9

--- a/solution.py
+++ b/solution.py
@@ -234,65 +234,38 @@
 rhs_segment = 3
 
 
-def pack_kernel(*refs):
-    count = (len(refs) - 3) // 2
-    features_ref, lists_ref, packed_ref = refs[0], refs[1], refs[count + 1]
-    held_ref, semaphores = refs[-2:]
+def pack_kernel(space_ref, features_ref, lists_ref, packed_ref, held_ref, semaphores):
     atoms, chans = features_ref.shape
-    pairs = [(lists_ref, held_ref), (features_ref, packed_ref.at[pl.ds(0, atoms)])]
-    copies = fetched(pairs + list(zip(refs[2 : count + 1], refs[count + 2 : -2])), semaphores)
+    copies = fetched(
+        [(lists_ref, held_ref), (features_ref, packed_ref.at[pl.ds(0, atoms)])], semaphores
+    )
     copies[0].wait()
-    lists = held_ref[0].astype(jnp.float32)
-    rows, width = lists.shape
-    lists = jnp.concatenate([lists, jnp.zeros((rows, chans - width), jnp.float32)], axis=1)
-    blank = jnp.zeros((packed_ref.shape[0] - atoms - rows, chans), jnp.float32)
-    packed_ref[atoms:, :] = jnp.concatenate([lists, blank], axis=0).astype(jnp.bfloat16)
-    for copy in copies[1:]:
-        copy.wait()
+    _, lanes, width = held_ref.shape
+    rows = []
+    for place in range(lanes):
+        row = held_ref[0, pl.ds(space_ref[0] ^ place, 1), :].astype(jnp.float32) + place * atoms
+        parts = [jnp.zeros((1, width), jnp.float32)] * lanes
+        parts[place] = row
+        rows.append(jnp.concatenate(parts, axis=1))
+    rows.append(jnp.zeros((packed_ref.shape[0] - atoms - lanes, chans), jnp.float32))
+    packed_ref[atoms:, :] = jnp.concatenate(rows, axis=0).astype(jnp.bfloat16)
+    copies[1].wait()
 
 
 def edge_kernel(
     field_ref,
     space_ref,
-    vec_ref,
-    first_ref,
-    second_ref,
-    species_far,
-    hardness_far,
-    width_far,
-    shift_far,
-    positions_far,
-    send_far,
-    recv_far,
-    project_far,
-    update_far,
-    out_far,
-    filter_ref,
-    unit_ref,
-    row_ref,
-    slot_ref,
-    local_ref,
-    hit_ref,
-    turned_ref,
-    upward_ref,
-    read_ref,
-    species_ref,
-    hardness_ref,
-    width_ref,
-    shift_ref,
-    positions_ref,
-    send_ref,
-    recv_ref,
-    project_ref,
-    update_ref,
-    out_ref,
-    semaphores,
+    *refs,
 ):
-    far = (send_far, recv_far, project_far, update_far, species_far, hardness_far)
-    far = far + (width_far, shift_far, positions_far, out_far)
-    near = (send_ref, recv_ref, project_ref, update_ref, species_ref, hardness_ref)
-    near = near + (width_ref, shift_ref, positions_ref, out_ref)
+    count = (len(refs) - 10) // 2
+    far, near, semaphores = refs[:count], refs[count + 9 : -1], refs[-1]
+    filter_ref, unit_ref, row_ref, slot_ref, local_ref, hit_ref = refs[count : count + 6]
+    turned_ref, upward_ref, read_ref = refs[count + 6 : count + 9]
+    vec_ref, first_ref, second_ref, send_ref, recv_ref, project_ref, update_ref = near[:7]
+    species_ref, hardness_ref, width_ref, shift_ref, positions_ref, out_ref = near[7:]
     copies = fetched(list(zip(far, near)), semaphores)
+    for copy in copies[:3]:
+        copy.wait()
     edges = vec_ref.shape[1]
     orders = first_ref.shape[0]
     vec = vec_ref[...]
@@ -319,7 +292,7 @@
     )
     radial = silu_half(mixed).astype(jnp.bfloat16)
     filter_ref[...] = over_first(second_ref[...], radial)
-    for copy in copies:
+    for copy in copies[3:]:
         copy.wait()
     species = species_ref[...]
 
@@ -362,7 +335,6 @@
 
 
 def node_kernel(
-    space_ref,
     own_ref,
     near_ref,
     side_ref,
@@ -376,24 +348,21 @@
     turned_ref,
     upward_ref,
     read_ref,
-    features_ref,
+    hidden_ref,
     block_ref,
 ):
-    atoms, chans = features_ref.shape
-    space = space_ref[0]
-    packed = [ref[...].astype(jnp.float32) for ref in (own_ref, near_ref, side_ref, far_ref)]
-    lanes = len(packed)
-    slots = chans // lanes
-    group = jnp.concatenate([value[:atoms] for value in packed], axis=0).astype(jnp.bfloat16)
-    picks = jnp.zeros((8, chans), jnp.float32)
-    line = lax.broadcasted_iota(jnp.int32, (8, chans), 0)
-    for place, value in enumerate(packed):
-        mine = jnp.where(line == space, value[atoms : atoms + 8], 0.0)
-        picks = picks + (pltpu.roll(mine, place * slots, 1) if place else mine)
-    slot_owner = lax.broadcasted_iota(jnp.int32, (1, chans), 1) // slots * atoms
-    chosen = slot_owner + jnp.sum(picks, axis=0, keepdims=True).astype(jnp.int32)
+    chans, atoms = hidden_ref.shape
+    packed = (own_ref, near_ref, side_ref, far_ref)
+    group = jnp.concatenate([ref[:atoms, :] for ref in packed], axis=0)
+    chosen = jnp.zeros((1, chans), jnp.float32)
+    for place, ref in enumerate(packed):
+        tail = ref[atoms:, :].astype(jnp.float32)
+        chosen = chosen + tail[place : place + 1]
     fill = jnp.where(
-        lax.broadcasted_iota(jnp.int32, (lanes * atoms, chans), 0) == chosen, 1.0, 0.0
+        lax.broadcasted_iota(jnp.int32, (len(packed) * atoms, chans), 0)
+        == chosen.astype(jnp.int32),
+        1.0,
+        0.0,
     ).astype(jnp.bfloat16)
     sender = jnp.dot(fill, slot_ref[...], preferred_element_type=jnp.float32) + local_ref[...]
     projected = over_last(turned_ref[...], group).astype(jnp.bfloat16)
@@ -413,7 +382,13 @@
     chi = jnp.concatenate([chi, jnp.zeros((1, chans - atoms), jnp.float32)], axis=1)
     row = row_ref[...] - pltpu.roll(chi, rhs_segment * atoms, 1)
     block_ref[...] = jnp.broadcast_to(row[None], block_ref.shape)
-    features_ref[...] = (packed[0][:atoms] + hidden.T).astype(jnp.bfloat16)
+    hidden_ref[...] = hidden
+
+
+def feature_kernel(packed_ref, hidden_ref, features_ref):
+    atoms = features_ref.shape[0]
+    old = packed_ref[...].astype(jnp.float32)[:atoms]
+    features_ref[...] = (old + hidden_ref[...].T).astype(jnp.bfloat16)
 
 
 def reciprocal(value):
@@ -435,16 +410,13 @@
     place_ref,
     field_ref,
     all_ref,
-    ready_ref,
     charges_ref,
     forces_ref,
     virial_ref,
-    features_ref,
     matrix_ref,
     side_ref,
     value_ref,
 ):
-    features_ref[...] = ready_ref[...]
     blocks, _, lanes = all_ref.shape
     own = charges_ref.shape[1]
     count = blocks * own
@@ -564,9 +536,9 @@
     virial_ref[...] = 0.5 * mine * table[3:9]
 
 
-def kernel_call(kernel, shapes, arguments, scalars=0, near=0, far=0, scratch=(), flops=0):
+def kernel_call(kernel, shapes, arguments, scalars=0, far=0, scratch=(), flops=0):
     shapes = tuple(jax.ShapeDtypeStruct(shape, kind) for shape, kind in shapes)
-    spaces = [pltpu.SMEM] * scalars + [pltpu.VMEM] * near + [pltpu.HBM] * far
+    spaces = [pltpu.SMEM] * scalars + [pltpu.HBM] * far
     spaces = spaces + [pltpu.VMEM] * (len(arguments) - len(spaces))
     arguments = [
         pltpu.with_memory_space_constraint(value, space) if space is pltpu.HBM else value
@@ -609,21 +581,22 @@
     atoms, chans = features.shape
     edges = edge_recv.shape[0]
     rows, lanes = lax.axis_size("row"), lax.axis_size("space")
-    first = (edge_vec, w_rad1, w_rad2)
-    packed, *first = kernel_call(
+    space = lax.axis_index("space").astype(jnp.int32)
+    (packed,) = kernel_call(
         pack_kernel,
-        [((atoms + 16, chans), jnp.bfloat16)] + [(value.shape, value.dtype) for value in first],
-        (features, ghost_list) + first,
-        far=2 + len(first),
+        [((atoms + 16, chans), jnp.bfloat16)],
+        (space.reshape(1), features, ghost_list),
+        scalars=1,
+        far=2,
         scratch=[
             pltpu.VMEM(ghost_list.shape, ghost_list.dtype),
-            pltpu.SemaphoreType.DMA((2 + len(first),)),
+            pltpu.SemaphoreType.DMA((2,)),
         ],
     )
     others = [exchanged(packed, "space", step) for step in range(1, lanes)]
-    space = lax.axis_index("space").astype(jnp.int32)
-    rest = (species[None], hardness[None], width[None], chi_shift[None], positions)
-    rest = rest + (edge_send[None], edge_recv[None], w_msg, w_up, w_out[None])
+    rest = (edge_vec, w_rad1, w_rad2, edge_send[None], edge_recv[None], w_msg, w_up)
+    rest = rest + (species[None], hardness[None], width[None], chi_shift[None], positions)
+    rest = rest + (w_out[None],)
     parts = kernel_call(
         edge_kernel,
         [
@@ -637,30 +610,30 @@
             ((chans, 2 * chans), jnp.bfloat16),
             ((chans, atoms), jnp.float32),
         ],
-        (field, space.reshape(1), *first, *rest),
+        (field, space.reshape(1), *rest),
         scalars=2,
-        near=len(first),
         far=len(rest),
         scratch=[pltpu.VMEM(value.shape, value.dtype) for value in rest]
         + [pltpu.SemaphoreType.DMA((len(rest),))],
         flops=1 << 28,
     )
     devices = rows * lanes
-    ready, block = kernel_call(
+    hidden, block = kernel_call(
         node_kernel,
-        [((atoms, chans), jnp.bfloat16), ((devices, 1, chans), jnp.float32)],
-        (space.reshape(1), packed, *others, *parts),
-        scalars=1,
+        [((chans, atoms), jnp.float32), ((devices, 1, chans), jnp.float32)],
+        (packed, *others, *parts),
         flops=1 << 28,
+    )
+    (new_features,) = kernel_call(
+        feature_kernel, [((atoms, chans), jnp.bfloat16)], (packed, hidden), flops=1 << 20
     )
     block = lax.all_to_all(block, everywhere, 0, 0, tiled=True)
     place = lax.axis_index("row").astype(jnp.int32) * lanes + space
     everybody = rows * lanes * atoms
-    charges, forces, virial, new_features = kernel_call(
+    charges, forces, virial = kernel_call(
         charge_kernel,
-        [((count, atoms), jnp.float32) for count in (1, 3, 6)]
-        + [((atoms, chans), jnp.bfloat16)],
-        (place.reshape(1), field, block, ready),
+        [((count, atoms), jnp.float32) for count in (1, 3, 6)],
+        (place.reshape(1), field, block),
         scalars=2,
         scratch=[
             pltpu.VMEM((everybody, everybody), jnp.float32),

time: 24.3 us -> 24.5 us (level)
  waiting for transfers between devices: 8.16 us -> 7.08 us
  Pallas kernels: 6.35 us -> 7.15 us
  starting transfers between devices: 8.22 us -> 8.64 us
    pallas_call x4 -> x5, Pallas kernels: 6.35 us -> 7.15 us  [kernel_call(): pl.pallas_call(kernel, out_shape=shapes, in_specs=[pl.BlockSpec(memory_sp...]
    all_to_all x1, waiting for transfers between devices: 7.14 us -> 6.47 us  [few_shards(): block = lax.all_to_all(block, everywhere, 0, 0, tiled=True)]
    all_to_all x1, starting transfers between devices: 5.04 us -> 5.49 us  [few_shards(): block = lax.all_to_all(block, everywhere, 0, 0, tiled=True)]
    ppermute x3, waiting for transfers between devices: 1.02 us -> 0.61 us  [exchanged(): lax.ppermute(block, axis, [(place, place ^ step) for place in range(size)])]
  transfers between devices with their start and end apart: 4 -> 4, of which waited for: 2 -> 2; matrix products, arithmetic and copies ran while one was open for 0% -> 0% of each run, Pallas kernels for 5% -> 10%
where the time goes in v10:
time: 24.5 us; the launch traced here: 24.2 us
  starting transfers between devices  8.64 us (35%)
  Pallas kernels  7.15 us (29%)
  waiting for transfers between devices  7.08 us (29%)
  between operations  1.33 us (5%)
    pallas_call x5, Pallas kernels, kernel_call(): pl.pallas_call(kernel, out_shape=shapes, in_specs=[pl.BlockSpec(memory_sp...  7.15 us
    all_to_all x1, waiting for transfers between devices, few_shards(): block = lax.all_to_all(block, everywhere, 0, 0, tiled=True)  6.47 us
    all_to_all x1, starting transfers between devices, few_shards(): block = lax.all_to_all(block, everywhere, 0, 0, tiled=True)  5.49 us
    ppermute x3, starting transfers between devices, exchanged(): lax.ppermute(block, axis, [(place, place ^ step) for place in range(size)])  3.15 us
    ppermute x3, waiting for transfers between devices, exchanged(): lax.ppermute(block, axis, [(place, place ^ step) for place in range(size)])  0.61 us
  transfers between devices with their start and end apart: 4, of which 2 were waited for; matrix products, arithmetic and copies ran while one was open for 0% of the time, Pallas kernels for 10%

profile of v10, /device:TPU:0, one launch (start us, length us, event | category | flops | bytes accessed | tf_op | source)
XLA Modules:
  0.0 24.2 jit_solution(2534782103327338798)
XLA Ops:
  0.6 0.8 %shard_map.183.own_ref.packed_ref = bf16[32,128]{1,0:T(8,128)(2,1)S(1)} custom-call(s32[1]{0:T(128)} %bitcast.space_ref, bf16[16,128]{1,0:T(8,128)(2,1)} %features_ref.1, s32[1,4,32]{2,1,0:T(4,128)} %lists_ref.1), custom_call_target="tpu_custom_call" | custom-call | bytes 1048576 | tf_op jit(solution)/shard_map/pallas_call | solution.py:547
  1.4 2.5 %collective-permute-start.2 = (bf16[32,128]{1,0:T(8,128)(2,1)S(1)}, bf16[32,128]{1,0:T(8,128)(2,1)S(1)}, u32[]{:S(2)}, u32[]{:S(2)}) collective-permute-start(bf16[32,128]{1,0:T(8,128)(2,1)S(1)} %shard_map.183.own_ref.packed_ref), channel_id=1, source_target_pairs={{0,3},{1,2},{2,1},{3,0},{4,7},{5,6},{6,5},{7,4},{8,11},{9,10},{10,... | collective-permute-start | bytes 24584 | tf_op jit(solution)/shard_map/ppermute | solution.py:560
  3.9 0.6 %collective-permute-start.1 = (bf16[32,128]{1,0:T(8,128)(2,1)S(1)}, bf16[32,128]{1,0:T(8,128)(2,1)S(1)}, u32[]{:S(2)}, u32[]{:S(2)}) collective-permute-start(bf16[32,128]{1,0:T(8,128)(2,1)S(1)} %shard_map.183.own_ref.packed_ref), channel_id=1, source_target_pairs={{0,2},{1,3},{2,0},{3,1},{4,6},{5,7},{6,4},{7,5},{8,10},{9,11},{10,... | collective-permute-start | bytes 24584 | tf_op jit(solution)/shard_map/ppermute | solution.py:560
  4.5 0.0 collective-permute-start
  5.2 1.7 %shard_map.184 = (f32[256,512]{1,0:T(8,128)S(1)}, f32[8,512]{1,0:T(8,128)S(1)}, f32[1,128]{1,0:T(1,128)S(1)}, bf16[128,512]{1,0:T(8,128)(2,1)S(1)}, f32[64,512]{...) custom-call(f32[1]{0:T(128)S(6)} %copy.20.field_ref, ...), custom_call_target="tpu_custom_call" | custom-call | flops 268435456 | bytes 1048576 | tf_op jit(solution)/shard_map/pallas_call | solution.py:547
  6.9 0.0 collective-permute-done.2.far_ref
  6.9 0.6 %collective-permute-done.1.side_ref = bf16[32,128]{1,0:T(8,128)(2,1)S(1)} collective-permute-done((bf16[32,128]{1,0:T(8,128)(2,1)S(1)}, bf16[32,128]{1,0:T(8,128)(2,1)S(1)}, u32[]{:S(2)}, u32[]{:S(2)}) %collective-permute-start.1) | collective-permute-done | bytes 8224 | tf_op jit(solution)/shard_map/ppermute | solution.py:560
  7.5 0.0 collective-permute-done.near_ref
  7.5 1.5 %shard_map.185 = (f32[128,16]{1,0:T(8,128)S(1)}, f32[32,1,128]{2,1,0:T(1,128)}) custom-call(bf16[32,128]{1,0:T(8,128)(2,1)S(1)} %shard_map.183.own_ref.packed_ref, bf16[32,128]{1,0:T(8,128)(2,1)S(1)} %collective-permute-done.near_ref, bf16[32,128]{1,0:T(8,128)(2,1)S(1)} %collective-permute-done.1.side_ref, ...), custom_call_target="tpu_custom_call" | custom-call | flops 268435456 | bytes 1048576 | tf_op jit(solution)/shard_map/pallas_call | solution.py:547
  9.0 5.5 %all-to-all-start = ((f32[32,1,128]{2,1,0:T(1,128)}), f32[32,1,128]{2,1,0:T(1,128)S(1)}, u32[]{:S(2)}, u32[]{:S(2)}) async-start(f32[32,1,128]{2,1,0:T(1,128)} %get-tuple-element.28), calls=%async_computation | async-start | bytes 32768 | tf_op jit(solution)/shard_map/all_to_all | solution.py:630
  14.5 0.7 %shard_map.186 = bf16[16,128]{1,0:T(8,128)(2,1)} custom-call(bf16[32,128]{1,0:T(8,128)(2,1)S(1)} %shard_map.183.own_ref.packed_ref, f32[128,16]{1,0:T(8,128)S(1)} %get-tuple-element.27.hidden_ref), custom_call_target="tpu_custom_call" | custom-call | flops 1048576 | bytes 1048576 | tf_op jit(solution)/shard_map/pallas_call | solution.py:547
  15.2 6.5 %all-to-all-done.all_ref = f32[32,1,128]{2,1,0:T(1,128)S(1)} async-done(((f32[32,1,128]{2,1,0:T(1,128)}), f32[32,1,128]{2,1,0:T(1,128)S(1)}, u32[]{:S(2)}, u32[]{:S(2)}) %all-to-all-start) | async-done | bytes 16416 | tf_op jit(solution)/shard_map/all_to_all | solution.py:630
  21.7 2.5 %shard_map.187 = (f32[1,16]{1,0:T(1,128)}, f32[3,16]{1,0:T(4,128)}, f32[6,16]{1,0:T(8,128)}) custom-call(s32[1]{0:T(128)} %bitcast.8.place_ref, f32[1]{0:T(128)S(6)} %copy.20.field_ref, f32[32,1,128]{2,1,0:T(1,128)S(1)} %all-to-all-done.all_ref), custom_call_target="tpu_custom_call" | custom-call | flops 268435456 | bytes 1048576 | tf_op jit(solution)/shard_map/pallas_call | solution.py:547
Async XLA Ops:
  1.4 5.5 %collective-permute-start.2 = (bf16[32,128]{1,0:T(8,128)(2,1)S(1)}, bf16[32,128]{1,0:T(8,128)(2,1)S(1)}, u32[]{:S(2)}, u32[]{:S(2)}) collective-permute-start(bf16[32,128]{1,0:T(8,128)(2,1)S(1)} %shard_map.183.own_ref.packed_ref), channel_id=1, source_target_pairs={{0,3},{1,2},{2,1},{3,0},{4,7},{5,6},{6,5},{7,4},{8,11},{9,10},{10,... | collective-permute-start | bytes 24584 | tf_op jit(solution)/shard_map/ppermute | solution.py:560
  3.9 3.7 %collective-permute-start.1 = (bf16[32,128]{1,0:T(8,128)(2,1)S(1)}, bf16[32,128]{1,0:T(8,128)(2,1)S(1)}, u32[]{:S(2)}, u32[]{:S(2)}) collective-permute-start(bf16[32,128]{1,0:T(8,128)(2,1)S(1)} %shard_map.183.own_ref.packed_ref), channel_id=1, source_target_pairs={{0,2},{1,3},{2,0},{3,1},{4,6},{5,7},{6,4},{7,5},{8,10},{9,11},{10,... | collective-permute-start | bytes 24584 | tf_op jit(solution)/shard_map/ppermute | solution.py:560
  4.5 3.0 %collective-permute-start = (bf16[32,128]{1,0:T(8,128)(2,1)S(1)}, bf16[32,128]{1,0:T(8,128)(2,1)S(1)}, u32[]{:S(2)}, u32[]{:S(2)}) collective-permute-start(bf16[32,128]{1,0:T(8,128)(2,1)S(1)} %shard_map.183.own_ref.packed_ref), channel_id=1, source_target_pairs={{0,1},{1,0},{2,3},{3,2},{4,5},{5,4},{6,7},{7,6},{8,9},{9,8},{10,11... | collective-permute-start | bytes 24584 | tf_op jit(solution)/shard_map/ppermute | solution.py:560
  9.0 12.6 %all-to-all-start = ((f32[32,1,128]{2,1,0:T(1,128)}), f32[32,1,128]{2,1,0:T(1,128)S(1)}, u32[]{:S(2)}, u32[]{:S(2)}) async-start(f32[32,1,128]{2,1,0:T(1,128)} %get-tuple-element.28), calls=%async_computation | async-start | bytes 32768 | tf_op jit(solution)/shard_map/all_to_all | solution.py:630

commit v11 on v10

--- a/solution.py
+++ b/solution.py
@@ -231,7 +231,7 @@
     return copies
 
 
-rhs_segment = 3
+chi_segment = 3
 
 
 def pack_kernel(space_ref, features_ref, lists_ref, packed_ref, held_ref, semaphores):
@@ -253,7 +253,6 @@
 
 
 def edge_kernel(
-    field_ref,
     space_ref,
     *refs,
 ):
@@ -307,9 +306,8 @@
     atoms = species.shape[1]
     chans = row_ref.shape[1]
     diag = table(hardness_ref) + inverse_root_pi / sigma
-    rhs = field_ref[0] * positions[2:3] - table(shift_ref)
     blank = jnp.zeros((2, atoms), jnp.float32)
-    rows = [positions[0:1], blank, rhs, diag, sigma, positions[2:3], positions[1:2]]
+    rows = [positions[0:1], blank, -table(shift_ref), diag, sigma, positions[2:3], positions[1:2]]
     block = jnp.concatenate(
         [jnp.concatenate(rows, axis=0), jnp.zeros((8, chans - atoms), jnp.float32)], axis=1
     )
@@ -380,7 +378,7 @@
     hidden = silu(jnp.dot(upward_ref[...], invariant, preferred_element_type=jnp.float32))
     chi = jnp.sum(hidden * read_ref[...], axis=0, keepdims=True)
     chi = jnp.concatenate([chi, jnp.zeros((1, chans - atoms), jnp.float32)], axis=1)
-    row = row_ref[...] - pltpu.roll(chi, rhs_segment * atoms, 1)
+    row = row_ref[...] - pltpu.roll(chi, chi_segment * atoms, 1)
     block_ref[...] = jnp.broadcast_to(row[None], block_ref.shape)
     hidden_ref[...] = hidden
 
@@ -432,6 +430,8 @@
             tile = jnp.where(segment == place, row, tile)
         tiles.append(tile)
     everyone = jnp.concatenate(tiles, axis=1)
+    last = lax.broadcasted_iota(jnp.int32, everyone.shape, 0) == 5
+    everyone = everyone + jnp.where(last, field_ref[0] * everyone[2:3], 0.0)
     columns = everyone.T
     diag, rhs = everyone[4:5], everyone[5:6]
     rows = own
@@ -610,8 +610,8 @@
             ((chans, 2 * chans), jnp.bfloat16),
             ((chans, atoms), jnp.float32),
         ],
-        (field, space.reshape(1), *rest),
-        scalars=2,
+        (space.reshape(1), *rest),
+        scalars=1,
         far=len(rest),
         scratch=[pltpu.VMEM(value.shape, value.dtype) for value in rest]
         + [pltpu.SemaphoreType.DMA((len(rest),))],

time: 24.5 us -> 24 us (0.980)
  starting transfers between devices: 8.64 us -> 8.13 us
    ppermute x3, waiting for transfers between devices: 0.61 us -> 1.28 us  [exchanged(): lax.ppermute(block, axis, [(place, place ^ step) for place in range(size)])]
    all_to_all x1, waiting for transfers between devices: 6.47 us -> 5.83 us  [few_shards(): block = lax.all_to_all(block, everywhere, 0, 0, tiled=True)]
    all_to_all x1, starting transfers between devices: 5.49 us -> 4.98 us  [few_shards(): block = lax.all_to_all(block, everywhere, 0, 0, tiled=True)]
where the time goes in v11:
time: 24 us; the launch traced here: 23.7 us
  starting transfers between devices  8.13 us (34%)
  Pallas kernels  7.14 us (30%)
  waiting for transfers between devices  7.11 us (30%)
  between operations  1.33 us (6%)
    pallas_call x5, Pallas kernels, kernel_call(): pl.pallas_call(kernel, out_shape=shapes, in_specs=[pl.BlockSpec(memory_sp...  7.14 us
    all_to_all x1, waiting for transfers between devices, few_shards(): block = lax.all_to_all(block, everywhere, 0, 0, tiled=True)  5.83 us
    all_to_all x1, starting transfers between devices, few_shards(): block = lax.all_to_all(block, everywhere, 0, 0, tiled=True)  4.98 us
    ppermute x3, starting transfers between devices, exchanged(): lax.ppermute(block, axis, [(place, place ^ step) for place in range(size)])  3.15 us
    ppermute x3, waiting for transfers between devices, exchanged(): lax.ppermute(block, axis, [(place, place ^ step) for place in range(size)])  1.28 us
  transfers between devices with their start and end apart: 4, of which 2 were waited for; matrix products, arithmetic and copies ran while one was open for 0% of the time, Pallas kernels for 10%

profile of v11, /device:TPU:0, one launch (start us, length us, event | category | flops | bytes accessed | tf_op | source)
XLA Modules:
  0.0 23.7 jit_solution(19592237761902119)
XLA Ops:
  0.6 0.8 %shard_map.183.own_ref.packed_ref = bf16[32,128]{1,0:T(8,128)(2,1)S(1)} custom-call(s32[1]{0:T(128)} %bitcast.space_ref, bf16[16,128]{1,0:T(8,128)(2,1)} %features_ref.1, s32[1,4,32]{2,1,0:T(4,128)} %lists_ref.1), custom_call_target="tpu_custom_call" | custom-call | bytes 1048576 | tf_op jit(solution)/shard_map/pallas_call | solution.py:547
  1.4 2.5 %collective-permute-start.2 = (bf16[32,128]{1,0:T(8,128)(2,1)S(1)}, bf16[32,128]{1,0:T(8,128)(2,1)S(1)}, u32[]{:S(2)}, u32[]{:S(2)}) collective-permute-start(bf16[32,128]{1,0:T(8,128)(2,1)S(1)} %shard_map.183.own_ref.packed_ref), channel_id=1, source_target_pairs={{0,3},{1,2},{2,1},{3,0},{4,7},{5,6},{6,5},{7,4},{8,11},{9,10},{10,... | collective-permute-start | bytes 24584 | tf_op jit(solution)/shard_map/ppermute | solution.py:560
  3.9 0.6 %collective-permute-start.1 = (bf16[32,128]{1,0:T(8,128)(2,1)S(1)}, bf16[32,128]{1,0:T(8,128)(2,1)S(1)}, u32[]{:S(2)}, u32[]{:S(2)}) collective-permute-start(bf16[32,128]{1,0:T(8,128)(2,1)S(1)} %shard_map.183.own_ref.packed_ref), channel_id=1, source_target_pairs={{0,2},{1,3},{2,0},{3,1},{4,6},{5,7},{6,4},{7,5},{8,10},{9,11},{10,... | collective-permute-start | bytes 24584 | tf_op jit(solution)/shard_map/ppermute | solution.py:560
  4.5 0.0 collective-permute-start
  4.6 1.7 %shard_map.184 = (f32[256,512]{1,0:T(8,128)S(1)}, f32[8,512]{1,0:T(8,128)S(1)}, f32[1,128]{1,0:T(1,128)S(1)}, bf16[128,512]{1,0:T(8,128)(2,1)S(1)}, f32[64,512]{...) custom-call(s32[1]{0:T(128)} %bitcast.space_ref, ...), custom_call_target="tpu_custom_call" | custom-call | flops 268435456 | bytes 1048576 | tf_op jit(solution)/shard_map/pallas_call | solution.py:547
  6.3 0.0 collective-permute-done.2.far_ref
  6.3 1.3 %collective-permute-done.1.side_ref = bf16[32,128]{1,0:T(8,128)(2,1)S(1)} collective-permute-done((bf16[32,128]{1,0:T(8,128)(2,1)S(1)}, bf16[32,128]{1,0:T(8,128)(2,1)S(1)}, u32[]{:S(2)}, u32[]{:S(2)}) %collective-permute-start.1) | collective-permute-done | bytes 8224 | tf_op jit(solution)/shard_map/ppermute | solution.py:560
  7.5 0.0 collective-permute-done.near_ref
  7.5 1.5 %shard_map.185 = (f32[128,16]{1,0:T(8,128)S(1)}, f32[32,1,128]{2,1,0:T(1,128)}) custom-call(bf16[32,128]{1,0:T(8,128)(2,1)S(1)} %shard_map.183.own_ref.packed_ref, bf16[32,128]{1,0:T(8,128)(2,1)S(1)} %collective-permute-done.near_ref, bf16[32,128]{1,0:T(8,128)(2,1)S(1)} %collective-permute-done.1.side_ref, ...), custom_call_target="tpu_custom_call" | custom-call | flops 268435456 | bytes 1048576 | tf_op jit(solution)/shard_map/pallas_call | solution.py:547
  9.0 5.0 %all-to-all-start = ((f32[32,1,128]{2,1,0:T(1,128)}), f32[32,1,128]{2,1,0:T(1,128)S(1)}, u32[]{:S(2)}, u32[]{:S(2)}) async-start(f32[32,1,128]{2,1,0:T(1,128)} %get-tuple-element.28), calls=%async_computation | async-start | bytes 32768 | tf_op jit(solution)/shard_map/all_to_all | solution.py:630
  14.7 0.7 %shard_map.186 = bf16[16,128]{1,0:T(8,128)(2,1)} custom-call(bf16[32,128]{1,0:T(8,128)(2,1)S(1)} %shard_map.183.own_ref.packed_ref, f32[128,16]{1,0:T(8,128)S(1)} %get-tuple-element.27.hidden_ref), custom_call_target="tpu_custom_call" | custom-call | flops 1048576 | bytes 1048576 | tf_op jit(solution)/shard_map/pallas_call | solution.py:547
  15.4 5.8 %all-to-all-done.all_ref = f32[32,1,128]{2,1,0:T(1,128)S(1)} async-done(((f32[32,1,128]{2,1,0:T(1,128)}), f32[32,1,128]{2,1,0:T(1,128)S(1)}, u32[]{:S(2)}, u32[]{:S(2)}) %all-to-all-start) | async-done | bytes 16416 | tf_op jit(solution)/shard_map/all_to_all | solution.py:630
  21.2 2.5 %shard_map.187 = (f32[1,16]{1,0:T(1,128)}, f32[3,16]{1,0:T(4,128)}, f32[6,16]{1,0:T(8,128)}) custom-call(s32[1]{0:T(128)} %bitcast.8.place_ref, f32[1]{0:T(128)S(6)} %copy.20.field_ref, f32[32,1,128]{2,1,0:T(1,128)S(1)} %all-to-all-done.all_ref), custom_call_target="tpu_custom_call" | custom-call | flops 268435456 | bytes 1048576 | tf_op jit(solution)/shard_map/pallas_call | solution.py:547
Async XLA Ops:
  1.4 4.8 %collective-permute-start.2 = (bf16[32,128]{1,0:T(8,128)(2,1)S(1)}, bf16[32,128]{1,0:T(8,128)(2,1)S(1)}, u32[]{:S(2)}, u32[]{:S(2)}) collective-permute-start(bf16[32,128]{1,0:T(8,128)(2,1)S(1)} %shard_map.183.own_ref.packed_ref), channel_id=1, source_target_pairs={{0,3},{1,2},{2,1},{3,0},{4,7},{5,6},{6,5},{7,4},{8,11},{9,10},{10,... | collective-permute-start | bytes 24584 | tf_op jit(solution)/shard_map/ppermute | solution.py:560
  3.9 3.7 %collective-permute-start.1 = (bf16[32,128]{1,0:T(8,128)(2,1)S(1)}, bf16[32,128]{1,0:T(8,128)(2,1)S(1)}, u32[]{:S(2)}, u32[]{:S(2)}) collective-permute-start(bf16[32,128]{1,0:T(8,128)(2,1)S(1)} %shard_map.183.own_ref.packed_ref), channel_id=1, source_target_pairs={{0,2},{1,3},{2,0},{3,1},{4,6},{5,7},{6,4},{7,5},{8,10},{9,11},{10,... | collective-permute-start | bytes 24584 | tf_op jit(solution)/shard_map/ppermute | solution.py:560
  4.5 3.0 %collective-permute-start = (bf16[32,128]{1,0:T(8,128)(2,1)S(1)}, bf16[32,128]{1,0:T(8,128)(2,1)S(1)}, u32[]{:S(2)}, u32[]{:S(2)}) collective-permute-start(bf16[32,128]{1,0:T(8,128)(2,1)S(1)} %shard_map.183.own_ref.packed_ref), channel_id=1, source_target_pairs={{0,1},{1,0},{2,3},{3,2},{4,5},{5,4},{6,7},{7,6},{8,9},{9,8},{10,11... | collective-permute-start | bytes 24584 | tf_op jit(solution)/shard_map/ppermute | solution.py:560
  9.0 12.1 %all-to-all-start = ((f32[32,1,128]{2,1,0:T(1,128)}), f32[32,1,128]{2,1,0:T(1,128)S(1)}, u32[]{:S(2)}, u32[]{:S(2)}) async-start(f32[32,1,128]{2,1,0:T(1,128)} %get-tuple-element.28), calls=%async_computation | async-start | bytes 32768 | tf_op jit(solution)/shard_map/all_to_all | solution.py:630

commit v12 on v11

--- a/solution.py
+++ b/solution.py
@@ -537,7 +537,9 @@
 
 
 def kernel_call(kernel, shapes, arguments, scalars=0, far=0, scratch=(), flops=0):
-    shapes = tuple(jax.ShapeDtypeStruct(shape, kind) for shape, kind in shapes)
+    shapes = tuple(
+        jax.ShapeDtypeStruct(*shape) if isinstance(shape, tuple) else shape for shape in shapes
+    )
     spaces = [pltpu.SMEM] * scalars + [pltpu.HBM] * far
     spaces = spaces + [pltpu.VMEM] * (len(arguments) - len(spaces))
     arguments = [
@@ -620,7 +622,7 @@
     devices = rows * lanes
     hidden, block = kernel_call(
         node_kernel,
-        [((chans, atoms), jnp.float32), ((devices, 1, chans), jnp.float32)],
+        [((chans, atoms), jnp.float32), pltpu.VMEM((devices, 1, chans), jnp.float32)],
         (packed, *others, *parts),
         flops=1 << 28,
     )

time: 24 us -> 24 us (level)
  no operation moved by 1% of the time
where the time goes in v12:
time: 24 us; the launch traced here: 23.7 us
  starting transfers between devices  8.13 us (34%)
  Pallas kernels  7.14 us (30%)
  waiting for transfers between devices  7.11 us (30%)
  between operations  1.33 us (6%)
    pallas_call x5, Pallas kernels, kernel_call(): pl.pallas_call(kernel, out_shape=shapes, in_specs=[pl.BlockSpec(memory_sp...  7.14 us
    all_to_all x1, waiting for transfers between devices, few_shards(): block = lax.all_to_all(block, everywhere, 0, 0, tiled=True)  5.83 us
    all_to_all x1, starting transfers between devices, few_shards(): block = lax.all_to_all(block, everywhere, 0, 0, tiled=True)  4.98 us
    ppermute x3, starting transfers between devices, exchanged(): lax.ppermute(block, axis, [(place, place ^ step) for place in range(size)])  3.15 us
    ppermute x3, waiting for transfers between devices, exchanged(): lax.ppermute(block, axis, [(place, place ^ step) for place in range(size)])  1.28 us
  transfers between devices with their start and end apart: 4, of which 2 were waited for; matrix products, arithmetic and copies ran while one was open for 0% of the time, Pallas kernels for 10%

profile of v12, /device:TPU:0, one launch (start us, length us, event | category | flops | bytes accessed | tf_op | source)
XLA Modules:
  0.0 23.7 jit_solution(19592237761902119)
XLA Ops:
  0.6 0.8 %shard_map.183.own_ref.packed_ref = bf16[32,128]{1,0:T(8,128)(2,1)S(1)} custom-call(s32[1]{0:T(128)} %bitcast.space_ref, bf16[16,128]{1,0:T(8,128)(2,1)} %features_ref.1, s32[1,4,32]{2,1,0:T(4,128)} %lists_ref.1), custom_call_target="tpu_custom_call" | custom-call | bytes 1048576 | tf_op jit(solution)/shard_map/pallas_call | solution.py:549
  1.4 2.5 %collective-permute-start.2 = (bf16[32,128]{1,0:T(8,128)(2,1)S(1)}, bf16[32,128]{1,0:T(8,128)(2,1)S(1)}, u32[]{:S(2)}, u32[]{:S(2)}) collective-permute-start(bf16[32,128]{1,0:T(8,128)(2,1)S(1)} %shard_map.183.own_ref.packed_ref), channel_id=1, source_target_pairs={{0,3},{1,2},{2,1},{3,0},{4,7},{5,6},{6,5},{7,4},{8,11},{9,10},{10,... | collective-permute-start | bytes 24584 | tf_op jit(solution)/shard_map/ppermute | solution.py:562
  3.9 0.6 %collective-permute-start.1 = (bf16[32,128]{1,0:T(8,128)(2,1)S(1)}, bf16[32,128]{1,0:T(8,128)(2,1)S(1)}, u32[]{:S(2)}, u32[]{:S(2)}) collective-permute-start(bf16[32,128]{1,0:T(8,128)(2,1)S(1)} %shard_map.183.own_ref.packed_ref), channel_id=1, source_target_pairs={{0,2},{1,3},{2,0},{3,1},{4,6},{5,7},{6,4},{7,5},{8,10},{9,11},{10,... | collective-permute-start | bytes 24584 | tf_op jit(solution)/shard_map/ppermute | solution.py:562
  4.5 0.0 collective-permute-start
  4.6 1.7 %shard_map.184 = (f32[256,512]{1,0:T(8,128)S(1)}, f32[8,512]{1,0:T(8,128)S(1)}, f32[1,128]{1,0:T(1,128)S(1)}, bf16[128,512]{1,0:T(8,128)(2,1)S(1)}, f32[64,512]{...) custom-call(s32[1]{0:T(128)} %bitcast.space_ref, ...), custom_call_target="tpu_custom_call" | custom-call | flops 268435456 | bytes 1048576 | tf_op jit(solution)/shard_map/pallas_call | solution.py:549
  6.3 0.0 collective-permute-done.2.far_ref
  6.3 1.3 %collective-permute-done.1.side_ref = bf16[32,128]{1,0:T(8,128)(2,1)S(1)} collective-permute-done((bf16[32,128]{1,0:T(8,128)(2,1)S(1)}, bf16[32,128]{1,0:T(8,128)(2,1)S(1)}, u32[]{:S(2)}, u32[]{:S(2)}) %collective-permute-start.1) | collective-permute-done | bytes 8224 | tf_op jit(solution)/shard_map/ppermute | solution.py:562
  7.5 0.0 collective-permute-done.near_ref
  7.5 1.5 %shard_map.185 = (f32[128,16]{1,0:T(8,128)S(1)}, f32[32,1,128]{2,1,0:T(1,128)}) custom-call(bf16[32,128]{1,0:T(8,128)(2,1)S(1)} %shard_map.183.own_ref.packed_ref, bf16[32,128]{1,0:T(8,128)(2,1)S(1)} %collective-permute-done.near_ref, bf16[32,128]{1,0:T(8,128)(2,1)S(1)} %collective-permute-done.1.side_ref, ...), custom_call_target="tpu_custom_call" | custom-call | flops 268435456 | bytes 1048576 | tf_op jit(solution)/shard_map/pallas_call | solution.py:549
  9.0 5.0 %all-to-all-start = ((f32[32,1,128]{2,1,0:T(1,128)}), f32[32,1,128]{2,1,0:T(1,128)S(1)}, u32[]{:S(2)}, u32[]{:S(2)}) async-start(f32[32,1,128]{2,1,0:T(1,128)} %get-tuple-element.28), calls=%async_computation | async-start | bytes 32768 | tf_op jit(solution)/shard_map/all_to_all | solution.py:632
  14.7 0.7 %shard_map.186 = bf16[16,128]{1,0:T(8,128)(2,1)} custom-call(bf16[32,128]{1,0:T(8,128)(2,1)S(1)} %shard_map.183.own_ref.packed_ref, f32[128,16]{1,0:T(8,128)S(1)} %get-tuple-element.27.hidden_ref), custom_call_target="tpu_custom_call" | custom-call | flops 1048576 | bytes 1048576 | tf_op jit(solution)/shard_map/pallas_call | solution.py:549
  15.4 5.8 %all-to-all-done.all_ref = f32[32,1,128]{2,1,0:T(1,128)S(1)} async-done(((f32[32,1,128]{2,1,0:T(1,128)}), f32[32,1,128]{2,1,0:T(1,128)S(1)}, u32[]{:S(2)}, u32[]{:S(2)}) %all-to-all-start) | async-done | bytes 16416 | tf_op jit(solution)/shard_map/all_to_all | solution.py:632
  21.2 2.5 %shard_map.187 = (f32[1,16]{1,0:T(1,128)}, f32[3,16]{1,0:T(4,128)}, f32[6,16]{1,0:T(8,128)}) custom-call(s32[1]{0:T(128)} %bitcast.8.place_ref, f32[1]{0:T(128)S(6)} %copy.20.field_ref, f32[32,1,128]{2,1,0:T(1,128)S(1)} %all-to-all-done.all_ref), custom_call_target="tpu_custom_call" | custom-call | flops 268435456 | bytes 1048576 | tf_op jit(solution)/shard_map/pallas_call | solution.py:549
Async XLA Ops:
  1.4 4.8 %collective-permute-start.2 = (bf16[32,128]{1,0:T(8,128)(2,1)S(1)}, bf16[32,128]{1,0:T(8,128)(2,1)S(1)}, u32[]{:S(2)}, u32[]{:S(2)}) collective-permute-start(bf16[32,128]{1,0:T(8,128)(2,1)S(1)} %shard_map.183.own_ref.packed_ref), channel_id=1, source_target_pairs={{0,3},{1,2},{2,1},{3,0},{4,7},{5,6},{6,5},{7,4},{8,11},{9,10},{10,... | collective-permute-start | bytes 24584 | tf_op jit(solution)/shard_map/ppermute | solution.py:562
  3.9 3.7 %collective-permute-start.1 = (bf16[32,128]{1,0:T(8,128)(2,1)S(1)}, bf16[32,128]{1,0:T(8,128)(2,1)S(1)}, u32[]{:S(2)}, u32[]{:S(2)}) collective-permute-start(bf16[32,128]{1,0:T(8,128)(2,1)S(1)} %shard_map.183.own_ref.packed_ref), channel_id=1, source_target_pairs={{0,2},{1,3},{2,0},{3,1},{4,6},{5,7},{6,4},{7,5},{8,10},{9,11},{10,... | collective-permute-start | bytes 24584 | tf_op jit(solution)/shard_map/ppermute | solution.py:562
  4.5 3.0 %collective-permute-start = (bf16[32,128]{1,0:T(8,128)(2,1)S(1)}, bf16[32,128]{1,0:T(8,128)(2,1)S(1)}, u32[]{:S(2)}, u32[]{:S(2)}) collective-permute-start(bf16[32,128]{1,0:T(8,128)(2,1)S(1)} %shard_map.183.own_ref.packed_ref), channel_id=1, source_target_pairs={{0,1},{1,0},{2,3},{3,2},{4,5},{5,4},{6,7},{7,6},{8,9},{9,8},{10,11... | collective-permute-start | bytes 24584 | tf_op jit(solution)/shard_map/ppermute | solution.py:562
  9.0 12.1 %all-to-all-start = ((f32[32,1,128]{2,1,0:T(1,128)}), f32[32,1,128]{2,1,0:T(1,128)S(1)}, u32[]{:S(2)}, u32[]{:S(2)}) async-start(f32[32,1,128]{2,1,0:T(1,128)} %get-tuple-element.28), calls=%async_computation | async-start | bytes 32768 | tf_op jit(solution)/shard_map/all_to_all | solution.py:632

commit v13 on v11

--- a/solution.py
+++ b/solution.py
@@ -424,7 +424,7 @@
     for first in range(0, blocks, fit):
         tile = jnp.zeros((8, lanes), jnp.float32)
         for place in range(fit):
-            row = all_ref[lax.rem(place_ref[0] + first + place, blocks)]
+            row = all_ref[(place_ref[0] + first + place) & (blocks - 1)]
             row = pltpu.roll(jnp.broadcast_to(row, (8, lanes)), 0, 1, stride=own, stride_axis=0)
             row = pltpu.roll(row, place * own, 1) if place else row
             tile = jnp.where(segment == place, row, tile)
@@ -434,7 +434,7 @@
     everyone = everyone + jnp.where(last, field_ref[0] * everyone[2:3], 0.0)
     columns = everyone.T
     diag, rhs = everyone[4:5], everyone[5:6]
-    rows = own
+    rows = 8
     spread_row = 2.0 * everyone[3:4] * everyone[3:4]
     tiles = count // lanes
     lane = lax.broadcasted_iota(jnp.int32, (rows, lanes), 1)
@@ -450,6 +450,8 @@
     kept = []
     for start in range(0, count, rows):
         first = start // lanes
+        if start < own:
+            kept.append([])
         column = columns[start : start + rows]
         place = [spread(column[:, axis : axis + 1]) for axis in range(3)]
         wide = spread(2.0 * column[:, 3:4] * column[:, 3:4])
@@ -466,10 +468,10 @@
             scale = lax.rsqrt(wide + part(spread_row, tile))
             smear, decay = smeared(squared * inverse * scale)
             kernel = smear * inverse
-            if start == 0:
+            if start < own:
                 slope = (two_over_root_pi * scale * decay - kernel) * inverse * inverse
                 slope = jnp.where(same, 0.0, slope) if tile == first else slope
-                kept.append((delta, slope))
+                kept[-1].append((delta, slope))
             if tile == first:
                 kernel = jnp.where(same, 0.0, kernel)
             else:
@@ -515,18 +517,22 @@
         curved = curved + part(diag * direction * direction, tile)
     charges = alpha * rhs + fresh / total(curved) * direction
 
-    sums = [jnp.zeros((rows, lanes), jnp.float32) for _ in range(9)]
-    for tile, (delta, slope) in enumerate(kept):
-        weight = part(charges, tile) * slope
-        pulled = [weight * delta[axis] for axis in range(3)]
-        terms = pulled + [
-            pulled[left] * delta[right]
-            for left, right in ((0, 0), (1, 1), (2, 2), (0, 1), (0, 2), (1, 2))
-        ]
-        sums = [old + term for old, term in zip(sums, terms)]
-    table = jnp.zeros((rows, lanes), jnp.float32)
-    for place, value in enumerate(sums):
-        table = jnp.where(lane == place, total(value), table)
+    tables = []
+    for chunk in kept:
+        sums = [jnp.zeros((rows, lanes), jnp.float32) for _ in range(9)]
+        for tile, (delta, slope) in enumerate(chunk):
+            weight = part(charges, tile) * slope
+            pulled = [weight * delta[axis] for axis in range(3)]
+            terms = pulled + [
+                pulled[left] * delta[right]
+                for left, right in ((0, 0), (1, 1), (2, 2), (0, 1), (0, 2), (1, 2))
+            ]
+            sums = [old + term for old, term in zip(sums, terms)]
+        table = jnp.zeros((rows, lanes), jnp.float32)
+        for place, value in enumerate(sums):
+            table = jnp.where(lane == place, total(value), table)
+        tables.append(table)
+    table = jnp.concatenate(tables, axis=0)
     table = table.T
     mine = charges[:, :own]
     charges_ref[...] = mine

time: 24 us -> 24.2 us (level)
  Pallas kernels: 7.14 us -> 7.4 us
    pallas_call x5, Pallas kernels: 7.14 us -> 7.4 us  [kernel_call(): pl.pallas_call(kernel, out_shape=shapes, in_specs=[pl.BlockSpec(memory_sp...]
where the time goes in v13:
time: 24.2 us; the launch traced here: 24 us
  starting transfers between devices  8.13 us (34%)
  Pallas kernels  7.4 us (31%)
  waiting for transfers between devices  7.11 us (29%)
  between operations  1.33 us (5%)
    pallas_call x5, Pallas kernels, kernel_call(): pl.pallas_call(kernel, out_shape=shapes, in_specs=[pl.BlockSpec(memory_sp...  7.4 us
    all_to_all x1, waiting for transfers between devices, few_shards(): block = lax.all_to_all(block, everywhere, 0, 0, tiled=True)  5.83 us
    all_to_all x1, starting transfers between devices, few_shards(): block = lax.all_to_all(block, everywhere, 0, 0, tiled=True)  4.98 us
    ppermute x3, starting transfers between devices, exchanged(): lax.ppermute(block, axis, [(place, place ^ step) for place in range(size)])  3.15 us
    ppermute x3, waiting for transfers between devices, exchanged(): lax.ppermute(block, axis, [(place, place ^ step) for place in range(size)])  1.28 us
  transfers between devices with their start and end apart: 4, of which 2 were waited for; matrix products, arithmetic and copies ran while one was open for 0% of the time, Pallas kernels for 10%

profile of v13, /device:TPU:0, one launch (start us, length us, event | category | flops | bytes accessed | tf_op | source)
XLA Modules:
  0.0 24.0 jit_solution(9235658422941059449)
XLA Ops:
  0.6 0.8 %shard_map.183.own_ref.packed_ref = bf16[32,128]{1,0:T(8,128)(2,1)S(1)} custom-call(s32[1]{0:T(128)} %bitcast.space_ref, bf16[16,128]{1,0:T(8,128)(2,1)} %features_ref.1, s32[1,4,32]{2,1,0:T(4,128)} %lists_ref.1), custom_call_target="tpu_custom_call" | custom-call | bytes 1048576 | tf_op jit(solution)/shard_map/pallas_call | solution.py:553
  1.4 2.5 %collective-permute-start.2 = (bf16[32,128]{1,0:T(8,128)(2,1)S(1)}, bf16[32,128]{1,0:T(8,128)(2,1)S(1)}, u32[]{:S(2)}, u32[]{:S(2)}) collective-permute-start(bf16[32,128]{1,0:T(8,128)(2,1)S(1)} %shard_map.183.own_ref.packed_ref), channel_id=1, source_target_pairs={{0,3},{1,2},{2,1},{3,0},{4,7},{5,6},{6,5},{7,4},{8,11},{9,10},{10,... | collective-permute-start | bytes 24584 | tf_op jit(solution)/shard_map/ppermute | solution.py:566
  3.9 0.6 %collective-permute-start.1 = (bf16[32,128]{1,0:T(8,128)(2,1)S(1)}, bf16[32,128]{1,0:T(8,128)(2,1)S(1)}, u32[]{:S(2)}, u32[]{:S(2)}) collective-permute-start(bf16[32,128]{1,0:T(8,128)(2,1)S(1)} %shard_map.183.own_ref.packed_ref), channel_id=1, source_target_pairs={{0,2},{1,3},{2,0},{3,1},{4,6},{5,7},{6,4},{7,5},{8,10},{9,11},{10,... | collective-permute-start | bytes 24584 | tf_op jit(solution)/shard_map/ppermute | solution.py:566
  4.5 0.0 collective-permute-start
  4.6 1.7 %shard_map.184 = (f32[256,512]{1,0:T(8,128)S(1)}, f32[8,512]{1,0:T(8,128)S(1)}, f32[1,128]{1,0:T(1,128)S(1)}, bf16[128,512]{1,0:T(8,128)(2,1)S(1)}, f32[64,512]{...) custom-call(s32[1]{0:T(128)} %bitcast.space_ref, ...), custom_call_target="tpu_custom_call" | custom-call | flops 268435456 | bytes 1048576 | tf_op jit(solution)/shard_map/pallas_call | solution.py:553
  6.3 0.0 collective-permute-done.2.far_ref
  6.3 1.3 %collective-permute-done.1.side_ref = bf16[32,128]{1,0:T(8,128)(2,1)S(1)} collective-permute-done((bf16[32,128]{1,0:T(8,128)(2,1)S(1)}, bf16[32,128]{1,0:T(8,128)(2,1)S(1)}, u32[]{:S(2)}, u32[]{:S(2)}) %collective-permute-start.1) | collective-permute-done | bytes 8224 | tf_op jit(solution)/shard_map/ppermute | solution.py:566
  7.5 0.0 collective-permute-done.near_ref
  7.5 1.5 %shard_map.185 = (f32[128,16]{1,0:T(8,128)S(1)}, f32[32,1,128]{2,1,0:T(1,128)}) custom-call(bf16[32,128]{1,0:T(8,128)(2,1)S(1)} %shard_map.183.own_ref.packed_ref, bf16[32,128]{1,0:T(8,128)(2,1)S(1)} %collective-permute-done.near_ref, bf16[32,128]{1,0:T(8,128)(2,1)S(1)} %collective-permute-done.1.side_ref, ...), custom_call_target="tpu_custom_call" | custom-call | flops 268435456 | bytes 1048576 | tf_op jit(solution)/shard_map/pallas_call | solution.py:553
  9.0 5.0 %all-to-all-start = ((f32[32,1,128]{2,1,0:T(1,128)}), f32[32,1,128]{2,1,0:T(1,128)S(1)}, u32[]{:S(2)}, u32[]{:S(2)}) async-start(f32[32,1,128]{2,1,0:T(1,128)} %get-tuple-element.28), calls=%async_computation | async-start | bytes 32768 | tf_op jit(solution)/shard_map/all_to_all | solution.py:636
  14.7 0.7 %shard_map.186 = bf16[16,128]{1,0:T(8,128)(2,1)} custom-call(bf16[32,128]{1,0:T(8,128)(2,1)S(1)} %shard_map.183.own_ref.packed_ref, f32[128,16]{1,0:T(8,128)S(1)} %get-tuple-element.27.hidden_ref), custom_call_target="tpu_custom_call" | custom-call | flops 1048576 | bytes 1048576 | tf_op jit(solution)/shard_map/pallas_call | solution.py:553
  15.4 5.8 %all-to-all-done.all_ref = f32[32,1,128]{2,1,0:T(1,128)S(1)} async-done(((f32[32,1,128]{2,1,0:T(1,128)}), f32[32,1,128]{2,1,0:T(1,128)S(1)}, u32[]{:S(2)}, u32[]{:S(2)}) %all-to-all-start) | async-done | bytes 16416 | tf_op jit(solution)/shard_map/all_to_all | solution.py:636
  21.2 2.8 %shard_map.187 = (f32[1,16]{1,0:T(1,128)}, f32[3,16]{1,0:T(4,128)}, f32[6,16]{1,0:T(8,128)}) custom-call(s32[1]{0:T(128)} %bitcast.8.place_ref, f32[1]{0:T(128)S(6)} %copy.20.field_ref, f32[32,1,128]{2,1,0:T(1,128)S(1)} %all-to-all-done.all_ref), custom_call_target="tpu_custom_call" | custom-call | flops 268435456 | bytes 1048576 | tf_op jit(solution)/shard_map/pallas_call | solution.py:553
Async XLA Ops:
  1.4 4.8 %collective-permute-start.2 = (bf16[32,128]{1,0:T(8,128)(2,1)S(1)}, bf16[32,128]{1,0:T(8,128)(2,1)S(1)}, u32[]{:S(2)}, u32[]{:S(2)}) collective-permute-start(bf16[32,128]{1,0:T(8,128)(2,1)S(1)} %shard_map.183.own_ref.packed_ref), channel_id=1, source_target_pairs={{0,3},{1,2},{2,1},{3,0},{4,7},{5,6},{6,5},{7,4},{8,11},{9,10},{10,... | collective-permute-start | bytes 24584 | tf_op jit(solution)/shard_map/ppermute | solution.py:566
  3.9 3.7 %collective-permute-start.1 = (bf16[32,128]{1,0:T(8,128)(2,1)S(1)}, bf16[32,128]{1,0:T(8,128)(2,1)S(1)}, u32[]{:S(2)}, u32[]{:S(2)}) collective-permute-start(bf16[32,128]{1,0:T(8,128)(2,1)S(1)} %shard_map.183.own_ref.packed_ref), channel_id=1, source_target_pairs={{0,2},{1,3},{2,0},{3,1},{4,6},{5,7},{6,4},{7,5},{8,10},{9,11},{10,... | collective-permute-start | bytes 24584 | tf_op jit(solution)/shard_map/ppermute | solution.py:566
  4.5 3.0 %collective-permute-start = (bf16[32,128]{1,0:T(8,128)(2,1)S(1)}, bf16[32,128]{1,0:T(8,128)(2,1)S(1)}, u32[]{:S(2)}, u32[]{:S(2)}) collective-permute-start(bf16[32,128]{1,0:T(8,128)(2,1)S(1)} %shard_map.183.own_ref.packed_ref), channel_id=1, source_target_pairs={{0,1},{1,0},{2,3},{3,2},{4,5},{5,4},{6,7},{7,6},{8,9},{9,8},{10,11... | collective-permute-start | bytes 24584 | tf_op jit(solution)/shard_map/ppermute | solution.py:566
  9.0 12.1 %all-to-all-start = ((f32[32,1,128]{2,1,0:T(1,128)}), f32[32,1,128]{2,1,0:T(1,128)S(1)}, u32[]{:S(2)}, u32[]{:S(2)}) async-start(f32[32,1,128]{2,1,0:T(1,128)} %get-tuple-element.28), calls=%async_computation | async-start | bytes 32768 | tf_op jit(solution)/shard_map/all_to_all | solution.py:636

commit v14 on v11

--- a/solution.py
+++ b/solution.py
@@ -424,7 +424,7 @@
     for first in range(0, blocks, fit):
         tile = jnp.zeros((8, lanes), jnp.float32)
         for place in range(fit):
-            row = all_ref[lax.rem(place_ref[0] + first + place, blocks)]
+            row = all_ref[(place_ref[0] + first + place) & (blocks - 1)]
             row = pltpu.roll(jnp.broadcast_to(row, (8, lanes)), 0, 1, stride=own, stride_axis=0)
             row = pltpu.roll(row, place * own, 1) if place else row
             tile = jnp.where(segment == place, row, tile)
@@ -434,36 +434,46 @@
     everyone = everyone + jnp.where(last, field_ref[0] * everyone[2:3], 0.0)
     columns = everyone.T
     diag, rhs = everyone[4:5], everyone[5:6]
-    rows = own
     spread_row = 2.0 * everyone[3:4] * everyone[3:4]
     tiles = count // lanes
-    lane = lax.broadcasted_iota(jnp.int32, (rows, lanes), 1)
-    line = lax.broadcasted_iota(jnp.int32, (rows, lanes), 0)
+    depth = own // 8
+    shape = (depth, 8, lanes)
+    lane = lax.broadcasted_iota(jnp.int32, shape, 2)
+    line = lax.broadcasted_iota(jnp.int32, shape, 0) * 8 + lax.broadcasted_iota(jnp.int32, shape, 1)
 
     def part(row, tile):
         return row[:, tile * lanes : (tile + 1) * lanes]
 
-    def spread(column):
-        return jnp.broadcast_to(column, (rows, lanes))
-
-    above = [jnp.zeros((rows, lanes), jnp.float32) for _ in range(tiles)]
+    def down(row):
+        return [jnp.broadcast_to(part(row, tile), (8, lanes))[None] for tile in range(tiles)]
+
+    def along(column):
+        return jnp.broadcast_to(column, (own, lanes)).reshape(shape)
+
+    def total(value):
+        return jnp.sum(value, axis=1, keepdims=True)
+
+    axes = [down(everyone[axis : axis + 1]) for axis in range(3)]
+    wide_row, rhs_row = down(spread_row), down(rhs)
+
+    above = [jnp.zeros((8, lanes), jnp.float32) for _ in range(tiles)]
     kept = []
-    for start in range(0, count, rows):
+    for start in range(0, count, own):
         first = start // lanes
-        column = columns[start : start + rows]
-        place = [spread(column[:, axis : axis + 1]) for axis in range(3)]
-        wide = spread(2.0 * column[:, 3:4] * column[:, 3:4])
-        value = spread(column[:, 5:6])
-        value_ref[start : start + rows, :] = value
-        below = jnp.zeros((rows, lanes), jnp.float32)
+        column = columns[start : start + own]
+        place = [along(column[:, axis : axis + 1]) for axis in range(3)]
+        wide = along(2.0 * column[:, 3:4] * column[:, 3:4])
+        value = along(column[:, 5:6])
+        value_ref[start : start + own, :] = value.reshape(own, lanes)
+        below = jnp.zeros(shape, jnp.float32)
         for tile in range(first, tiles):
-            delta = [place[axis] - part(everyone[axis : axis + 1], tile) for axis in range(3)]
+            delta = [place[axis] - axes[axis][tile] for axis in range(3)]
             squared = delta[0] * delta[0] + delta[1] * delta[1] + delta[2] * delta[2]
             if tile == first:
                 same = lane == line + (start - first * lanes)
                 squared = jnp.where(same, 1.0, squared)
             inverse = lax.rsqrt(squared)
-            scale = lax.rsqrt(wide + part(spread_row, tile))
+            scale = lax.rsqrt(wide + wide_row[tile])
             smear, decay = smeared(squared * inverse * scale)
             kernel = smear * inverse
             if start == 0:
@@ -473,11 +483,13 @@
             if tile == first:
                 kernel = jnp.where(same, 0.0, kernel)
             else:
-                below = below + kernel * part(rhs, tile)
-            above[tile] = above[tile] + kernel * value
-            matrix_ref[start : start + rows, tile * lanes : (tile + 1) * lanes] = kernel
+                below = below + kernel * rhs_row[tile]
+            above[tile] = above[tile] + jnp.sum(kernel * value, axis=0)
+            matrix_ref[start : start + own, tile * lanes : (tile + 1) * lanes] = kernel.reshape(
+                own, lanes
+            )
         if first + 1 < tiles:
-            side_ref[start : start + rows, :] = below
+            side_ref[start : start + own, :] = below.reshape(own, lanes)
     image = []
     for tile in range(tiles):
         value = jnp.sum(above[tile], axis=0, keepdims=True)
@@ -487,27 +499,24 @@
         image.append(value)
     image = diag * rhs + jnp.concatenate(image, axis=1)
     across = jnp.broadcast_to(image, (8, count)).T
-
-    def total(value):
-        return jnp.sum(value, axis=1, keepdims=True)
-
     norm = total(rhs * rhs)
     alpha = norm / total(rhs * image)
     residual = rhs - alpha * image
     fresh = total(residual * residual)
     again = fresh / norm
     direction = residual + again * rhs
-    onto = [jnp.zeros((rows, lanes), jnp.float32) for _ in range(tiles)]
-    above = [jnp.zeros((rows, lanes), jnp.float32) for _ in range(tiles)]
-    for start in range(0, count, rows):
+    onto = [jnp.zeros((8, lanes), jnp.float32) for _ in range(tiles)]
+    above = [jnp.zeros((8, lanes), jnp.float32) for _ in range(tiles)]
+    for start in range(0, count, own):
         first = start // lanes
-        value = (1.0 + again) * value_ref[start : start + rows, :]
-        value = value - alpha * spread(across[start : start + rows, 0:1])
+        value = (1.0 + again) * value_ref[start : start + own, :]
+        value = value - alpha * jnp.broadcast_to(across[start : start + own, 0:1], (own, lanes))
+        value = value.reshape(shape)
         for tile in range(first, tiles):
             sums = onto if tile == first else above
-            kernel = matrix_ref[start : start + rows, tile * lanes : (tile + 1) * lanes]
-            sums[tile] = sums[tile] + kernel * value
-    curved = jnp.zeros((rows, lanes), jnp.float32)
+            kernel = matrix_ref[start : start + own, tile * lanes : (tile + 1) * lanes]
+            sums[tile] = sums[tile] + jnp.sum(kernel.reshape(shape) * value, axis=0)
+    curved = jnp.zeros((8, lanes), jnp.float32)
     for tile in range(tiles):
         curved = curved + (onto[tile] + 2.0 * above[tile]) * part(direction, tile)
     curved = jnp.sum(curved, axis=0, keepdims=True)
@@ -515,18 +524,20 @@
         curved = curved + part(diag * direction * direction, tile)
     charges = alpha * rhs + fresh / total(curved) * direction
 
-    sums = [jnp.zeros((rows, lanes), jnp.float32) for _ in range(9)]
+    sums = [jnp.zeros(shape, jnp.float32) for _ in range(9)]
+    charge_row = down(charges)
     for tile, (delta, slope) in enumerate(kept):
-        weight = part(charges, tile) * slope
+        weight = charge_row[tile] * slope
         pulled = [weight * delta[axis] for axis in range(3)]
         terms = pulled + [
             pulled[left] * delta[right]
             for left, right in ((0, 0), (1, 1), (2, 2), (0, 1), (0, 2), (1, 2))
         ]
         sums = [old + term for old, term in zip(sums, terms)]
-    table = jnp.zeros((rows, lanes), jnp.float32)
+    table = jnp.zeros((own, lanes), jnp.float32)
+    lane = lane.reshape(own, lanes)
     for place, value in enumerate(sums):
-        table = jnp.where(lane == place, total(value), table)
+        table = jnp.where(lane == place, total(value.reshape(own, lanes)), table)
     table = table.T
     mine = charges[:, :own]
     charges_ref[...] = mine

time: 24 us -> 24 us (level)
  no operation moved by 1% of the time
where the time goes in v14:
time: 24 us; the launch traced here: 23.7 us
  starting transfers between devices  8.13 us (34%)
  Pallas kernels  7.13 us (30%)
  waiting for transfers between devices  7.11 us (30%)
  between operations  1.33 us (6%)
    pallas_call x5, Pallas kernels, kernel_call(): pl.pallas_call(kernel, out_shape=shapes, in_specs=[pl.BlockSpec(memory_sp...  7.13 us
    all_to_all x1, waiting for transfers between devices, few_shards(): block = lax.all_to_all(block, everywhere, 0, 0, tiled=True)  5.83 us
    all_to_all x1, starting transfers between devices, few_shards(): block = lax.all_to_all(block, everywhere, 0, 0, tiled=True)  4.98 us
    ppermute x3, starting transfers between devices, exchanged(): lax.ppermute(block, axis, [(place, place ^ step) for place in range(size)])  3.15 us
    ppermute x3, waiting for transfers between devices, exchanged(): lax.ppermute(block, axis, [(place, place ^ step) for place in range(size)])  1.28 us
  transfers between devices with their start and end apart: 4, of which 2 were waited for; matrix products, arithmetic and copies ran while one was open for 0% of the time, Pallas kernels for 10%

profile of v14, /device:TPU:0, one launch (start us, length us, event | category | flops | bytes accessed | tf_op | source)
XLA Modules:
  0.0 23.7 jit_solution(15378462056789914740)
XLA Ops:
  0.6 0.8 %shard_map.183.own_ref.packed_ref = bf16[32,128]{1,0:T(8,128)(2,1)S(1)} custom-call(s32[1]{0:T(128)} %bitcast.space_ref, bf16[16,128]{1,0:T(8,128)(2,1)} %features_ref.1, s32[1,4,32]{2,1,0:T(4,128)} %lists_ref.1), custom_call_target="tpu_custom_call" | custom-call | bytes 1048576 | tf_op jit(solution)/shard_map/pallas_call | solution.py:558
  1.4 2.5 %collective-permute-start.2 = (bf16[32,128]{1,0:T(8,128)(2,1)S(1)}, bf16[32,128]{1,0:T(8,128)(2,1)S(1)}, u32[]{:S(2)}, u32[]{:S(2)}) collective-permute-start(bf16[32,128]{1,0:T(8,128)(2,1)S(1)} %shard_map.183.own_ref.packed_ref), channel_id=1, source_target_pairs={{0,3},{1,2},{2,1},{3,0},{4,7},{5,6},{6,5},{7,4},{8,11},{9,10},{10,... | collective-permute-start | bytes 24584 | tf_op jit(solution)/shard_map/ppermute | solution.py:571
  3.9 0.6 %collective-permute-start.1 = (bf16[32,128]{1,0:T(8,128)(2,1)S(1)}, bf16[32,128]{1,0:T(8,128)(2,1)S(1)}, u32[]{:S(2)}, u32[]{:S(2)}) collective-permute-start(bf16[32,128]{1,0:T(8,128)(2,1)S(1)} %shard_map.183.own_ref.packed_ref), channel_id=1, source_target_pairs={{0,2},{1,3},{2,0},{3,1},{4,6},{5,7},{6,4},{7,5},{8,10},{9,11},{10,... | collective-permute-start | bytes 24584 | tf_op jit(solution)/shard_map/ppermute | solution.py:571
  4.5 0.0 collective-permute-start
  4.6 1.7 %shard_map.184 = (f32[256,512]{1,0:T(8,128)S(1)}, f32[8,512]{1,0:T(8,128)S(1)}, f32[1,128]{1,0:T(1,128)S(1)}, bf16[128,512]{1,0:T(8,128)(2,1)S(1)}, f32[64,512]{...) custom-call(s32[1]{0:T(128)} %bitcast.space_ref, ...), custom_call_target="tpu_custom_call" | custom-call | flops 268435456 | bytes 1048576 | tf_op jit(solution)/shard_map/pallas_call | solution.py:558
  6.3 0.0 collective-permute-done.2.far_ref
  6.3 1.3 %collective-permute-done.1.side_ref = bf16[32,128]{1,0:T(8,128)(2,1)S(1)} collective-permute-done((bf16[32,128]{1,0:T(8,128)(2,1)S(1)}, bf16[32,128]{1,0:T(8,128)(2,1)S(1)}, u32[]{:S(2)}, u32[]{:S(2)}) %collective-permute-start.1) | collective-permute-done | bytes 8224 | tf_op jit(solution)/shard_map/ppermute | solution.py:571
  7.5 0.0 collective-permute-done.near_ref
  7.5 1.5 %shard_map.185 = (f32[128,16]{1,0:T(8,128)S(1)}, f32[32,1,128]{2,1,0:T(1,128)}) custom-call(bf16[32,128]{1,0:T(8,128)(2,1)S(1)} %shard_map.183.own_ref.packed_ref, bf16[32,128]{1,0:T(8,128)(2,1)S(1)} %collective-permute-done.near_ref, bf16[32,128]{1,0:T(8,128)(2,1)S(1)} %collective-permute-done.1.side_ref, ...), custom_call_target="tpu_custom_call" | custom-call | flops 268435456 | bytes 1048576 | tf_op jit(solution)/shard_map/pallas_call | solution.py:558
  9.0 5.0 %all-to-all-start = ((f32[32,1,128]{2,1,0:T(1,128)}), f32[32,1,128]{2,1,0:T(1,128)S(1)}, u32[]{:S(2)}, u32[]{:S(2)}) async-start(f32[32,1,128]{2,1,0:T(1,128)} %get-tuple-element.28), calls=%async_computation | async-start | bytes 32768 | tf_op jit(solution)/shard_map/all_to_all | solution.py:641
  14.7 0.7 %shard_map.186 = bf16[16,128]{1,0:T(8,128)(2,1)} custom-call(bf16[32,128]{1,0:T(8,128)(2,1)S(1)} %shard_map.183.own_ref.packed_ref, f32[128,16]{1,0:T(8,128)S(1)} %get-tuple-element.27.hidden_ref), custom_call_target="tpu_custom_call" | custom-call | flops 1048576 | bytes 1048576 | tf_op jit(solution)/shard_map/pallas_call | solution.py:558
  15.4 5.8 %all-to-all-done.all_ref = f32[32,1,128]{2,1,0:T(1,128)S(1)} async-done(((f32[32,1,128]{2,1,0:T(1,128)}), f32[32,1,128]{2,1,0:T(1,128)S(1)}, u32[]{:S(2)}, u32[]{:S(2)}) %all-to-all-start) | async-done | bytes 16416 | tf_op jit(solution)/shard_map/all_to_all | solution.py:641
  21.2 2.5 %shard_map.187 = (f32[1,16]{1,0:T(1,128)}, f32[3,16]{1,0:T(4,128)}, f32[6,16]{1,0:T(8,128)}) custom-call(s32[1]{0:T(128)} %bitcast.8.place_ref, f32[1]{0:T(128)S(6)} %copy.20.field_ref, f32[32,1,128]{2,1,0:T(1,128)S(1)} %all-to-all-done.all_ref), custom_call_target="tpu_custom_call" | custom-call | flops 268435456 | bytes 1048576 | tf_op jit(solution)/shard_map/pallas_call | solution.py:558
Async XLA Ops:
  1.4 4.8 %collective-permute-start.2 = (bf16[32,128]{1,0:T(8,128)(2,1)S(1)}, bf16[32,128]{1,0:T(8,128)(2,1)S(1)}, u32[]{:S(2)}, u32[]{:S(2)}) collective-permute-start(bf16[32,128]{1,0:T(8,128)(2,1)S(1)} %shard_map.183.own_ref.packed_ref), channel_id=1, source_target_pairs={{0,3},{1,2},{2,1},{3,0},{4,7},{5,6},{6,5},{7,4},{8,11},{9,10},{10,... | collective-permute-start | bytes 24584 | tf_op jit(solution)/shard_map/ppermute | solution.py:571
  3.9 3.7 %collective-permute-start.1 = (bf16[32,128]{1,0:T(8,128)(2,1)S(1)}, bf16[32,128]{1,0:T(8,128)(2,1)S(1)}, u32[]{:S(2)}, u32[]{:S(2)}) collective-permute-start(bf16[32,128]{1,0:T(8,128)(2,1)S(1)} %shard_map.183.own_ref.packed_ref), channel_id=1, source_target_pairs={{0,2},{1,3},{2,0},{3,1},{4,6},{5,7},{6,4},{7,5},{8,10},{9,11},{10,... | collective-permute-start | bytes 24584 | tf_op jit(solution)/shard_map/ppermute | solution.py:571
  4.5 3.0 %collective-permute-start = (bf16[32,128]{1,0:T(8,128)(2,1)S(1)}, bf16[32,128]{1,0:T(8,128)(2,1)S(1)}, u32[]{:S(2)}, u32[]{:S(2)}) collective-permute-start(bf16[32,128]{1,0:T(8,128)(2,1)S(1)} %shard_map.183.own_ref.packed_ref), channel_id=1, source_target_pairs={{0,1},{1,0},{2,3},{3,2},{4,5},{5,4},{6,7},{7,6},{8,9},{9,8},{10,11... | collective-permute-start | bytes 24584 | tf_op jit(solution)/shard_map/ppermute | solution.py:571
  9.0 12.1 %all-to-all-start = ((f32[32,1,128]{2,1,0:T(1,128)}), f32[32,1,128]{2,1,0:T(1,128)S(1)}, u32[]{:S(2)}, u32[]{:S(2)}) async-start(f32[32,1,128]{2,1,0:T(1,128)} %get-tuple-element.28), calls=%async_computation | async-start | bytes 32768 | tf_op jit(solution)/shard_map/all_to_all | solution.py:641

commit v15 on v14

--- a/solution.py
+++ b/solution.py
@@ -436,8 +436,8 @@
     diag, rhs = everyone[4:5], everyone[5:6]
     spread_row = 2.0 * everyone[3:4] * everyone[3:4]
     tiles = count // lanes
-    depth = own // 8
-    shape = (depth, 8, lanes)
+    rows = 32
+    shape = (rows // 8, 8, lanes)
     lane = lax.broadcasted_iota(jnp.int32, shape, 2)
     line = lax.broadcasted_iota(jnp.int32, shape, 0) * 8 + lax.broadcasted_iota(jnp.int32, shape, 1)
 
@@ -448,7 +448,7 @@
         return [jnp.broadcast_to(part(row, tile), (8, lanes))[None] for tile in range(tiles)]
 
     def along(column):
-        return jnp.broadcast_to(column, (own, lanes)).reshape(shape)
+        return jnp.broadcast_to(column, (rows, lanes)).reshape(shape)
 
     def total(value):
         return jnp.sum(value, axis=1, keepdims=True)
@@ -458,13 +458,13 @@
 
     above = [jnp.zeros((8, lanes), jnp.float32) for _ in range(tiles)]
     kept = []
-    for start in range(0, count, own):
+    for start in range(0, count, rows):
         first = start // lanes
-        column = columns[start : start + own]
+        column = columns[start : start + rows]
         place = [along(column[:, axis : axis + 1]) for axis in range(3)]
         wide = along(2.0 * column[:, 3:4] * column[:, 3:4])
         value = along(column[:, 5:6])
-        value_ref[start : start + own, :] = value.reshape(own, lanes)
+        value_ref[start : start + rows, :] = value.reshape(rows, lanes)
         below = jnp.zeros(shape, jnp.float32)
         for tile in range(first, tiles):
             delta = [place[axis] - axes[axis][tile] for axis in range(3)]
@@ -479,17 +479,17 @@
             if start == 0:
                 slope = (two_over_root_pi * scale * decay - kernel) * inverse * inverse
                 slope = jnp.where(same, 0.0, slope) if tile == first else slope
-                kept.append((delta, slope))
+                kept.append(([value[: own // 8] for value in delta], slope[: own // 8]))
             if tile == first:
                 kernel = jnp.where(same, 0.0, kernel)
             else:
                 below = below + kernel * rhs_row[tile]
             above[tile] = above[tile] + jnp.sum(kernel * value, axis=0)
-            matrix_ref[start : start + own, tile * lanes : (tile + 1) * lanes] = kernel.reshape(
-                own, lanes
+            matrix_ref[start : start + rows, tile * lanes : (tile + 1) * lanes] = kernel.reshape(
+                rows, lanes
             )
         if first + 1 < tiles:
-            side_ref[start : start + own, :] = below.reshape(own, lanes)
+            side_ref[start : start + rows, :] = below.reshape(rows, lanes)
     image = []
     for tile in range(tiles):
         value = jnp.sum(above[tile], axis=0, keepdims=True)
@@ -507,14 +507,14 @@
     direction = residual + again * rhs
     onto = [jnp.zeros((8, lanes), jnp.float32) for _ in range(tiles)]
     above = [jnp.zeros((8, lanes), jnp.float32) for _ in range(tiles)]
-    for start in range(0, count, own):
+    for start in range(0, count, rows):
         first = start // lanes
-        value = (1.0 + again) * value_ref[start : start + own, :]
-        value = value - alpha * jnp.broadcast_to(across[start : start + own, 0:1], (own, lanes))
+        value = (1.0 + again) * value_ref[start : start + rows, :]
+        value = value - alpha * jnp.broadcast_to(across[start : start + rows, 0:1], (rows, lanes))
         value = value.reshape(shape)
         for tile in range(first, tiles):
             sums = onto if tile == first else above
-            kernel = matrix_ref[start : start + own, tile * lanes : (tile + 1) * lanes]
+            kernel = matrix_ref[start : start + rows, tile * lanes : (tile + 1) * lanes]
             sums[tile] = sums[tile] + jnp.sum(kernel.reshape(shape) * value, axis=0)
     curved = jnp.zeros((8, lanes), jnp.float32)
     for tile in range(tiles):
@@ -524,7 +524,7 @@
         curved = curved + part(diag * direction * direction, tile)
     charges = alpha * rhs + fresh / total(curved) * direction
 
-    sums = [jnp.zeros(shape, jnp.float32) for _ in range(9)]
+    sums = [jnp.zeros((own // 8, 8, lanes), jnp.float32) for _ in range(9)]
     charge_row = down(charges)
     for tile, (delta, slope) in enumerate(kept):
         weight = charge_row[tile] * slope
@@ -535,7 +535,7 @@
         ]
         sums = [old + term for old, term in zip(sums, terms)]
     table = jnp.zeros((own, lanes), jnp.float32)
-    lane = lane.reshape(own, lanes)
+    lane = lax.broadcasted_iota(jnp.int32, (own, lanes), 1)
     for place, value in enumerate(sums):
         table = jnp.where(lane == place, total(value.reshape(own, lanes)), table)
     table = table.T

time: 24 us -> 24.3 us (1.012)
  Pallas kernels: 7.13 us -> 7.44 us
    pallas_call x5, Pallas kernels: 7.13 us -> 7.44 us  [kernel_call(): pl.pallas_call(kernel, out_shape=shapes, in_specs=[pl.BlockSpec(memory_sp...]
where the time goes in v15:
time: 24.3 us; the launch traced here: 24 us
  starting transfers between devices  8.13 us (33%)
  Pallas kernels  7.44 us (31%)
  waiting for transfers between devices  7.11 us (29%)
  between operations  1.33 us (5%)
    pallas_call x5, Pallas kernels, kernel_call(): pl.pallas_call(kernel, out_shape=shapes, in_specs=[pl.BlockSpec(memory_sp...  7.44 us
    all_to_all x1, waiting for transfers between devices, few_shards(): block = lax.all_to_all(block, everywhere, 0, 0, tiled=True)  5.83 us
    all_to_all x1, starting transfers between devices, few_shards(): block = lax.all_to_all(block, everywhere, 0, 0, tiled=True)  4.98 us
    ppermute x3, starting transfers between devices, exchanged(): lax.ppermute(block, axis, [(place, place ^ step) for place in range(size)])  3.15 us
    ppermute x3, waiting for transfers between devices, exchanged(): lax.ppermute(block, axis, [(place, place ^ step) for place in range(size)])  1.28 us
  transfers between devices with their start and end apart: 4, of which 2 were waited for; matrix products, arithmetic and copies ran while one was open for 0% of the time, Pallas kernels for 10%

profile of v15, /device:TPU:0, one launch (start us, length us, event | category | flops | bytes accessed | tf_op | source)
XLA Modules:
  0.0 24.0 jit_solution(16121827022095515085)
XLA Ops:
  0.6 0.8 %shard_map.183.own_ref.packed_ref = bf16[32,128]{1,0:T(8,128)(2,1)S(1)} custom-call(s32[1]{0:T(128)} %bitcast.space_ref, bf16[16,128]{1,0:T(8,128)(2,1)} %features_ref.1, s32[1,4,32]{2,1,0:T(4,128)} %lists_ref.1), custom_call_target="tpu_custom_call" | custom-call | bytes 1048576 | tf_op jit(solution)/shard_map/pallas_call | solution.py:558
  1.4 2.5 %collective-permute-start.2 = (bf16[32,128]{1,0:T(8,128)(2,1)S(1)}, bf16[32,128]{1,0:T(8,128)(2,1)S(1)}, u32[]{:S(2)}, u32[]{:S(2)}) collective-permute-start(bf16[32,128]{1,0:T(8,128)(2,1)S(1)} %shard_map.183.own_ref.packed_ref), channel_id=1, source_target_pairs={{0,3},{1,2},{2,1},{3,0},{4,7},{5,6},{6,5},{7,4},{8,11},{9,10},{10,... | collective-permute-start | bytes 24584 | tf_op jit(solution)/shard_map/ppermute | solution.py:571
  3.9 0.6 %collective-permute-start.1 = (bf16[32,128]{1,0:T(8,128)(2,1)S(1)}, bf16[32,128]{1,0:T(8,128)(2,1)S(1)}, u32[]{:S(2)}, u32[]{:S(2)}) collective-permute-start(bf16[32,128]{1,0:T(8,128)(2,1)S(1)} %shard_map.183.own_ref.packed_ref), channel_id=1, source_target_pairs={{0,2},{1,3},{2,0},{3,1},{4,6},{5,7},{6,4},{7,5},{8,10},{9,11},{10,... | collective-permute-start | bytes 24584 | tf_op jit(solution)/shard_map/ppermute | solution.py:571
  4.5 0.0 collective-permute-start
  4.6 1.7 %shard_map.184 = (f32[256,512]{1,0:T(8,128)S(1)}, f32[8,512]{1,0:T(8,128)S(1)}, f32[1,128]{1,0:T(1,128)S(1)}, bf16[128,512]{1,0:T(8,128)(2,1)S(1)}, f32[64,512]{...) custom-call(s32[1]{0:T(128)} %bitcast.space_ref, ...), custom_call_target="tpu_custom_call" | custom-call | flops 268435456 | bytes 1048576 | tf_op jit(solution)/shard_map/pallas_call | solution.py:558
  6.3 0.0 collective-permute-done.2.far_ref
  6.3 1.3 %collective-permute-done.1.side_ref = bf16[32,128]{1,0:T(8,128)(2,1)S(1)} collective-permute-done((bf16[32,128]{1,0:T(8,128)(2,1)S(1)}, bf16[32,128]{1,0:T(8,128)(2,1)S(1)}, u32[]{:S(2)}, u32[]{:S(2)}) %collective-permute-start.1) | collective-permute-done | bytes 8224 | tf_op jit(solution)/shard_map/ppermute | solution.py:571
  7.5 0.0 collective-permute-done.near_ref
  7.5 1.5 %shard_map.185 = (f32[128,16]{1,0:T(8,128)S(1)}, f32[32,1,128]{2,1,0:T(1,128)}) custom-call(bf16[32,128]{1,0:T(8,128)(2,1)S(1)} %shard_map.183.own_ref.packed_ref, bf16[32,128]{1,0:T(8,128)(2,1)S(1)} %collective-permute-done.near_ref, bf16[32,128]{1,0:T(8,128)(2,1)S(1)} %collective-permute-done.1.side_ref, ...), custom_call_target="tpu_custom_call" | custom-call | flops 268435456 | bytes 1048576 | tf_op jit(solution)/shard_map/pallas_call | solution.py:558
  9.0 5.0 %all-to-all-start = ((f32[32,1,128]{2,1,0:T(1,128)}), f32[32,1,128]{2,1,0:T(1,128)S(1)}, u32[]{:S(2)}, u32[]{:S(2)}) async-start(f32[32,1,128]{2,1,0:T(1,128)} %get-tuple-element.28), calls=%async_computation | async-start | bytes 32768 | tf_op jit(solution)/shard_map/all_to_all | solution.py:641
  14.7 0.7 %shard_map.186 = bf16[16,128]{1,0:T(8,128)(2,1)} custom-call(bf16[32,128]{1,0:T(8,128)(2,1)S(1)} %shard_map.183.own_ref.packed_ref, f32[128,16]{1,0:T(8,128)S(1)} %get-tuple-element.27.hidden_ref), custom_call_target="tpu_custom_call" | custom-call | flops 1048576 | bytes 1048576 | tf_op jit(solution)/shard_map/pallas_call | solution.py:558
  15.4 5.8 %all-to-all-done.all_ref = f32[32,1,128]{2,1,0:T(1,128)S(1)} async-done(((f32[32,1,128]{2,1,0:T(1,128)}), f32[32,1,128]{2,1,0:T(1,128)S(1)}, u32[]{:S(2)}, u32[]{:S(2)}) %all-to-all-start) | async-done | bytes 16416 | tf_op jit(solution)/shard_map/all_to_all | solution.py:641
  21.2 2.8 %shard_map.187 = (f32[1,16]{1,0:T(1,128)}, f32[3,16]{1,0:T(4,128)}, f32[6,16]{1,0:T(8,128)}) custom-call(s32[1]{0:T(128)} %bitcast.8.place_ref, f32[1]{0:T(128)S(6)} %copy.20.field_ref, f32[32,1,128]{2,1,0:T(1,128)S(1)} %all-to-all-done.all_ref), custom_call_target="tpu_custom_call" | custom-call | flops 268435456 | bytes 1048576 | tf_op jit(solution)/shard_map/pallas_call | solution.py:558
Async XLA Ops:
  1.4 4.8 %collective-permute-start.2 = (bf16[32,128]{1,0:T(8,128)(2,1)S(1)}, bf16[32,128]{1,0:T(8,128)(2,1)S(1)}, u32[]{:S(2)}, u32[]{:S(2)}) collective-permute-start(bf16[32,128]{1,0:T(8,128)(2,1)S(1)} %shard_map.183.own_ref.packed_ref), channel_id=1, source_target_pairs={{0,3},{1,2},{2,1},{3,0},{4,7},{5,6},{6,5},{7,4},{8,11},{9,10},{10,... | collective-permute-start | bytes 24584 | tf_op jit(solution)/shard_map/ppermute | solution.py:571
  3.9 3.7 %collective-permute-start.1 = (bf16[32,128]{1,0:T(8,128)(2,1)S(1)}, bf16[32,128]{1,0:T(8,128)(2,1)S(1)}, u32[]{:S(2)}, u32[]{:S(2)}) collective-permute-start(bf16[32,128]{1,0:T(8,128)(2,1)S(1)} %shard_map.183.own_ref.packed_ref), channel_id=1, source_target_pairs={{0,2},{1,3},{2,0},{3,1},{4,6},{5,7},{6,4},{7,5},{8,10},{9,11},{10,... | collective-permute-start | bytes 24584 | tf_op jit(solution)/shard_map/ppermute | solution.py:571
  4.5 3.0 %collective-permute-start = (bf16[32,128]{1,0:T(8,128)(2,1)S(1)}, bf16[32,128]{1,0:T(8,128)(2,1)S(1)}, u32[]{:S(2)}, u32[]{:S(2)}) collective-permute-start(bf16[32,128]{1,0:T(8,128)(2,1)S(1)} %shard_map.183.own_ref.packed_ref), channel_id=1, source_target_pairs={{0,1},{1,0},{2,3},{3,2},{4,5},{5,4},{6,7},{7,6},{8,9},{9,8},{10,11... | collective-permute-start | bytes 24584 | tf_op jit(solution)/shard_map/ppermute | solution.py:571
  9.0 12.1 %all-to-all-start = ((f32[32,1,128]{2,1,0:T(1,128)}), f32[32,1,128]{2,1,0:T(1,128)S(1)}, u32[]{:S(2)}, u32[]{:S(2)}) async-start(f32[32,1,128]{2,1,0:T(1,128)} %get-tuple-element.28), calls=%async_computation | async-start | bytes 32768 | tf_op jit(solution)/shard_map/all_to_all | solution.py:641

commit v16 on v15

--- a/solution.py
+++ b/solution.py
@@ -444,8 +444,8 @@
     def part(row, tile):
         return row[:, tile * lanes : (tile + 1) * lanes]
 
-    def down(row):
-        return [jnp.broadcast_to(part(row, tile), (8, lanes))[None] for tile in range(tiles)]
+    def down(row, tile):
+        return jnp.broadcast_to(part(row, tile), (8, lanes))[None]
 
     def along(column):
         return jnp.broadcast_to(column, (rows, lanes)).reshape(shape)
@@ -453,50 +453,56 @@
     def total(value):
         return jnp.sum(value, axis=1, keepdims=True)
 
-    axes = [down(everyone[axis : axis + 1]) for axis in range(3)]
-    wide_row, rhs_row = down(spread_row), down(rhs)
-
-    above = [jnp.zeros((8, lanes), jnp.float32) for _ in range(tiles)]
-    kept = []
-    for start in range(0, count, rows):
-        first = start // lanes
-        column = columns[start : start + rows]
-        place = [along(column[:, axis : axis + 1]) for axis in range(3)]
-        wide = along(2.0 * column[:, 3:4] * column[:, 3:4])
-        value = along(column[:, 5:6])
-        value_ref[start : start + rows, :] = value.reshape(rows, lanes)
-        below = jnp.zeros(shape, jnp.float32)
-        for tile in range(first, tiles):
-            delta = [place[axis] - axes[axis][tile] for axis in range(3)]
+    def held(ref, start):
+        return ref[start : start + rows, :].reshape(shape)
+
+    def hold(ref, start, value):
+        ref[start : start + rows, :] = value.reshape(rows, lanes)
+
+    kept, image, summed = [], [], []
+    for tile in range(tiles):
+        axes = [down(everyone[axis : axis + 1], tile) for axis in range(3)]
+        wide_row, rhs_row = down(spread_row, tile), down(rhs, tile)
+        above = jnp.zeros((8, lanes), jnp.float32)
+        for start in range(0, (tile + 1) * lanes, rows):
+            onto = start >= tile * lanes
+            if onto:
+                column = columns[start : start + rows]
+                values = [along(column[:, axis : axis + 1]) for axis in range(3)]
+                values.append(along(2.0 * column[:, 3:4] * column[:, 3:4]))
+                values.append(along(column[:, 5:6]))
+                for place, value in enumerate(values):
+                    hold(value_ref.at[place], start, value)
+            else:
+                values = [held(value_ref.at[place], start) for place in range(5)]
+            delta = [values[axis] - axes[axis] for axis in range(3)]
             squared = delta[0] * delta[0] + delta[1] * delta[1] + delta[2] * delta[2]
-            if tile == first:
-                same = lane == line + (start - first * lanes)
+            if onto:
+                same = lane == line + (start - tile * lanes)
                 squared = jnp.where(same, 1.0, squared)
             inverse = lax.rsqrt(squared)
-            scale = lax.rsqrt(wide + wide_row[tile])
+            scale = lax.rsqrt(values[3] + wide_row)
             smear, decay = smeared(squared * inverse * scale)
             kernel = smear * inverse
             if start == 0:
-                slope = (two_over_root_pi * scale * decay - kernel) * inverse * inverse
-                slope = jnp.where(same, 0.0, slope) if tile == first else slope
-                kept.append(([value[: own // 8] for value in delta], slope[: own // 8]))
-            if tile == first:
+                few = own // 8
+                slope = two_over_root_pi * scale[:few] * decay[:few] - kernel[:few]
+                slope = slope * inverse[:few] * inverse[:few]
+                slope = jnp.where(same[:few], 0.0, slope) if onto else slope
+                kept.append(([value[:few] for value in delta], slope))
+            if onto:
                 kernel = jnp.where(same, 0.0, kernel)
             else:
-                below = below + kernel * rhs_row[tile]
-            above[tile] = above[tile] + jnp.sum(kernel * value, axis=0)
-            matrix_ref[start : start + rows, tile * lanes : (tile + 1) * lanes] = kernel.reshape(
-                rows, lanes
-            )
-        if first + 1 < tiles:
-            side_ref[start : start + rows, :] = below.reshape(rows, lanes)
-    image = []
-    for tile in range(tiles):
-        value = jnp.sum(above[tile], axis=0, keepdims=True)
-        if tile + 1 < tiles:
-            below = side_ref[tile * lanes : (tile + 1) * lanes, :].T
-            value = value + jnp.sum(below, axis=0, keepdims=True)
-        image.append(value)
+                below = kernel * rhs_row
+                if start // lanes + 1 < tile:
+                    below = below + held(side_ref, start)
+                hold(side_ref, start, below)
+            above = above + jnp.sum(kernel * values[4], axis=0)
+            hold(matrix_ref.at[tile], start, kernel)
+        image.append(jnp.sum(above, axis=0, keepdims=True))
+    for tile in range(tiles - 1):
+        below = side_ref[tile * lanes : (tile + 1) * lanes, :].T
+        image[tile] = image[tile] + jnp.sum(below, axis=0, keepdims=True)
     image = diag * rhs + jnp.concatenate(image, axis=1)
     across = jnp.broadcast_to(image, (8, count)).T
     norm = total(rhs * rhs)
@@ -505,29 +511,28 @@
     fresh = total(residual * residual)
     again = fresh / norm
     direction = residual + again * rhs
-    onto = [jnp.zeros((8, lanes), jnp.float32) for _ in range(tiles)]
-    above = [jnp.zeros((8, lanes), jnp.float32) for _ in range(tiles)]
-    for start in range(0, count, rows):
-        first = start // lanes
-        value = (1.0 + again) * value_ref[start : start + rows, :]
-        value = value - alpha * jnp.broadcast_to(across[start : start + rows, 0:1], (rows, lanes))
-        value = value.reshape(shape)
-        for tile in range(first, tiles):
-            sums = onto if tile == first else above
-            kernel = matrix_ref[start : start + rows, tile * lanes : (tile + 1) * lanes]
-            sums[tile] = sums[tile] + jnp.sum(kernel.reshape(shape) * value, axis=0)
     curved = jnp.zeros((8, lanes), jnp.float32)
     for tile in range(tiles):
-        curved = curved + (onto[tile] + 2.0 * above[tile]) * part(direction, tile)
+        sums = [jnp.zeros((8, lanes), jnp.float32) for _ in range(2)]
+        for start in range(0, (tile + 1) * lanes, rows):
+            onto = start >= tile * lanes
+            if onto:
+                value = (1.0 + again) * held(value_ref.at[4], start)
+                value = value - alpha * along(across[start : start + rows, 0:1])
+                hold(value_ref.at[0], start, value)
+            else:
+                value = held(value_ref.at[0], start)
+            add = jnp.sum(held(matrix_ref.at[tile], start) * value, axis=0)
+            sums[onto] = sums[onto] + add
+        curved = curved + (2.0 * sums[0] + sums[1]) * part(direction, tile)
     curved = jnp.sum(curved, axis=0, keepdims=True)
     for tile in range(tiles):
         curved = curved + part(diag * direction * direction, tile)
     charges = alpha * rhs + fresh / total(curved) * direction
 
     sums = [jnp.zeros((own // 8, 8, lanes), jnp.float32) for _ in range(9)]
-    charge_row = down(charges)
     for tile, (delta, slope) in enumerate(kept):
-        weight = charge_row[tile] * slope
+        weight = down(charges, tile) * slope
         pulled = [weight * delta[axis] for axis in range(3)]
         terms = pulled + [
             pulled[left] * delta[right]
@@ -647,9 +652,9 @@
         (place.reshape(1), field, block),
         scalars=2,
         scratch=[
-            pltpu.VMEM((everybody, everybody), jnp.float32),
+            pltpu.VMEM((everybody // chans, everybody, chans), jnp.float32),
             pltpu.VMEM((everybody, chans), jnp.float32),
-            pltpu.VMEM((everybody, chans), jnp.float32),
+            pltpu.VMEM((5, everybody, chans), jnp.float32),
         ],
         flops=1 << 28,
     )

time: 24.3 us -> 24.3 us (level)
  no operation moved by 1% of the time
where the time goes in v16:
time: 24.3 us; the launch traced here: 24 us
  starting transfers between devices  8.13 us (33%)
  Pallas kernels  7.44 us (31%)
  waiting for transfers between devices  7.11 us (29%)
  between operations  1.33 us (5%)
    pallas_call x5, Pallas kernels, kernel_call(): pl.pallas_call(kernel, out_shape=shapes, in_specs=[pl.BlockSpec(memory_sp...  7.44 us
    all_to_all x1, waiting for transfers between devices, few_shards(): block = lax.all_to_all(block, everywhere, 0, 0, tiled=True)  5.83 us
    all_to_all x1, starting transfers between devices, few_shards(): block = lax.all_to_all(block, everywhere, 0, 0, tiled=True)  4.98 us
    ppermute x3, starting transfers between devices, exchanged(): lax.ppermute(block, axis, [(place, place ^ step) for place in range(size)])  3.15 us
    ppermute x3, waiting for transfers between devices, exchanged(): lax.ppermute(block, axis, [(place, place ^ step) for place in range(size)])  1.28 us
  transfers between devices with their start and end apart: 4, of which 2 were waited for; matrix products, arithmetic and copies ran while one was open for 0% of the time, Pallas kernels for 10%

profile of v16, /device:TPU:0, one launch (start us, length us, event | category | flops | bytes accessed | tf_op | source)
XLA Modules:
  0.0 24.0 jit_solution(13129238133016603523)
XLA Ops:
  0.6 0.8 %shard_map.183.own_ref.packed_ref = bf16[32,128]{1,0:T(8,128)(2,1)S(1)} custom-call(s32[1]{0:T(128)} %bitcast.space_ref, bf16[16,128]{1,0:T(8,128)(2,1)} %features_ref.1, s32[1,4,32]{2,1,0:T(4,128)} %lists_ref.1), custom_call_target="tpu_custom_call" | custom-call | bytes 1048576 | tf_op jit(solution)/shard_map/pallas_call | solution.py:563
  1.4 2.5 %collective-permute-start.2 = (bf16[32,128]{1,0:T(8,128)(2,1)S(1)}, bf16[32,128]{1,0:T(8,128)(2,1)S(1)}, u32[]{:S(2)}, u32[]{:S(2)}) collective-permute-start(bf16[32,128]{1,0:T(8,128)(2,1)S(1)} %shard_map.183.own_ref.packed_ref), channel_id=1, source_target_pairs={{0,3},{1,2},{2,1},{3,0},{4,7},{5,6},{6,5},{7,4},{8,11},{9,10},{10,... | collective-permute-start | bytes 24584 | tf_op jit(solution)/shard_map/ppermute | solution.py:576
  3.9 0.6 %collective-permute-start.1 = (bf16[32,128]{1,0:T(8,128)(2,1)S(1)}, bf16[32,128]{1,0:T(8,128)(2,1)S(1)}, u32[]{:S(2)}, u32[]{:S(2)}) collective-permute-start(bf16[32,128]{1,0:T(8,128)(2,1)S(1)} %shard_map.183.own_ref.packed_ref), channel_id=1, source_target_pairs={{0,2},{1,3},{2,0},{3,1},{4,6},{5,7},{6,4},{7,5},{8,10},{9,11},{10,... | collective-permute-start | bytes 24584 | tf_op jit(solution)/shard_map/ppermute | solution.py:576
  4.5 0.0 collective-permute-start
  4.6 1.7 %shard_map.184 = (f32[256,512]{1,0:T(8,128)S(1)}, f32[8,512]{1,0:T(8,128)S(1)}, f32[1,128]{1,0:T(1,128)S(1)}, bf16[128,512]{1,0:T(8,128)(2,1)S(1)}, f32[64,512]{...) custom-call(s32[1]{0:T(128)} %bitcast.space_ref, ...), custom_call_target="tpu_custom_call" | custom-call | flops 268435456 | bytes 1048576 | tf_op jit(solution)/shard_map/pallas_call | solution.py:563
  6.3 0.0 collective-permute-done.2.far_ref
  6.3 1.3 %collective-permute-done.1.side_ref = bf16[32,128]{1,0:T(8,128)(2,1)S(1)} collective-permute-done((bf16[32,128]{1,0:T(8,128)(2,1)S(1)}, bf16[32,128]{1,0:T(8,128)(2,1)S(1)}, u32[]{:S(2)}, u32[]{:S(2)}) %collective-permute-start.1) | collective-permute-done | bytes 8224 | tf_op jit(solution)/shard_map/ppermute | solution.py:576
  7.5 0.0 collective-permute-done.near_ref
  7.5 1.5 %shard_map.185 = (f32[128,16]{1,0:T(8,128)S(1)}, f32[32,1,128]{2,1,0:T(1,128)}) custom-call(bf16[32,128]{1,0:T(8,128)(2,1)S(1)} %shard_map.183.own_ref.packed_ref, bf16[32,128]{1,0:T(8,128)(2,1)S(1)} %collective-permute-done.near_ref, bf16[32,128]{1,0:T(8,128)(2,1)S(1)} %collective-permute-done.1.side_ref, ...), custom_call_target="tpu_custom_call" | custom-call | flops 268435456 | bytes 1048576 | tf_op jit(solution)/shard_map/pallas_call | solution.py:563
  9.0 5.0 %all-to-all-start = ((f32[32,1,128]{2,1,0:T(1,128)}), f32[32,1,128]{2,1,0:T(1,128)S(1)}, u32[]{:S(2)}, u32[]{:S(2)}) async-start(f32[32,1,128]{2,1,0:T(1,128)} %get-tuple-element.28), calls=%async_computation | async-start | bytes 32768 | tf_op jit(solution)/shard_map/all_to_all | solution.py:646
  14.7 0.7 %shard_map.186 = bf16[16,128]{1,0:T(8,128)(2,1)} custom-call(bf16[32,128]{1,0:T(8,128)(2,1)S(1)} %shard_map.183.own_ref.packed_ref, f32[128,16]{1,0:T(8,128)S(1)} %get-tuple-element.27.hidden_ref), custom_call_target="tpu_custom_call" | custom-call | flops 1048576 | bytes 1048576 | tf_op jit(solution)/shard_map/pallas_call | solution.py:563
  15.4 5.8 %all-to-all-done.all_ref = f32[32,1,128]{2,1,0:T(1,128)S(1)} async-done(((f32[32,1,128]{2,1,0:T(1,128)}), f32[32,1,128]{2,1,0:T(1,128)S(1)}, u32[]{:S(2)}, u32[]{:S(2)}) %all-to-all-start) | async-done | bytes 16416 | tf_op jit(solution)/shard_map/all_to_all | solution.py:646
  21.2 2.8 %shard_map.187 = (f32[1,16]{1,0:T(1,128)}, f32[3,16]{1,0:T(4,128)}, f32[6,16]{1,0:T(8,128)}) custom-call(s32[1]{0:T(128)} %bitcast.8.place_ref, f32[1]{0:T(128)S(6)} %copy.20.field_ref, f32[32,1,128]{2,1,0:T(1,128)S(1)} %all-to-all-done.all_ref), custom_call_target="tpu_custom_call" | custom-call | flops 268435456 | bytes 1048576 | tf_op jit(solution)/shard_map/pallas_call | solution.py:563
Async XLA Ops:
  1.4 4.8 %collective-permute-start.2 = (bf16[32,128]{1,0:T(8,128)(2,1)S(1)}, bf16[32,128]{1,0:T(8,128)(2,1)S(1)}, u32[]{:S(2)}, u32[]{:S(2)}) collective-permute-start(bf16[32,128]{1,0:T(8,128)(2,1)S(1)} %shard_map.183.own_ref.packed_ref), channel_id=1, source_target_pairs={{0,3},{1,2},{2,1},{3,0},{4,7},{5,6},{6,5},{7,4},{8,11},{9,10},{10,... | collective-permute-start | bytes 24584 | tf_op jit(solution)/shard_map/ppermute | solution.py:576
  3.9 3.7 %collective-permute-start.1 = (bf16[32,128]{1,0:T(8,128)(2,1)S(1)}, bf16[32,128]{1,0:T(8,128)(2,1)S(1)}, u32[]{:S(2)}, u32[]{:S(2)}) collective-permute-start(bf16[32,128]{1,0:T(8,128)(2,1)S(1)} %shard_map.183.own_ref.packed_ref), channel_id=1, source_target_pairs={{0,2},{1,3},{2,0},{3,1},{4,6},{5,7},{6,4},{7,5},{8,10},{9,11},{10,... | collective-permute-start | bytes 24584 | tf_op jit(solution)/shard_map/ppermute | solution.py:576
  4.5 3.0 %collective-permute-start = (bf16[32,128]{1,0:T(8,128)(2,1)S(1)}, bf16[32,128]{1,0:T(8,128)(2,1)S(1)}, u32[]{:S(2)}, u32[]{:S(2)}) collective-permute-start(bf16[32,128]{1,0:T(8,128)(2,1)S(1)} %shard_map.183.own_ref.packed_ref), channel_id=1, source_target_pairs={{0,1},{1,0},{2,3},{3,2},{4,5},{5,4},{6,7},{7,6},{8,9},{9,8},{10,11... | collective-permute-start | bytes 24584 | tf_op jit(solution)/shard_map/ppermute | solution.py:576
  9.0 12.1 %all-to-all-start = ((f32[32,1,128]{2,1,0:T(1,128)}), f32[32,1,128]{2,1,0:T(1,128)S(1)}, u32[]{:S(2)}, u32[]{:S(2)}) async-start(f32[32,1,128]{2,1,0:T(1,128)} %get-tuple-element.28), calls=%async_computation | async-start | bytes 32768 | tf_op jit(solution)/shard_map/all_to_all | solution.py:646

commit v17 on v11

--- a/solution.py
+++ b/solution.py
@@ -256,15 +256,13 @@
     space_ref,
     *refs,
 ):
-    count = (len(refs) - 10) // 2
-    far, near, semaphores = refs[:count], refs[count + 9 : -1], refs[-1]
-    filter_ref, unit_ref, row_ref, slot_ref, local_ref, hit_ref = refs[count : count + 6]
-    turned_ref, upward_ref, read_ref = refs[count + 6 : count + 9]
-    vec_ref, first_ref, second_ref, send_ref, recv_ref, project_ref, update_ref = near[:7]
-    species_ref, hardness_ref, width_ref, shift_ref, positions_ref, out_ref = near[7:]
+    count = (len(refs) - 12) // 2
+    far, near, semaphores = refs[:count], refs[count + 11 : -1], refs[-1]
+    vec_ref, first_ref, filter_ref, unit_ref, row_ref, slot_ref = refs[count : count + 6]
+    local_ref, hit_ref, turned_ref, upward_ref, read_ref = refs[count + 6 : count + 11]
+    second_ref, send_ref, recv_ref, project_ref, update_ref = near[:5]
+    species_ref, hardness_ref, width_ref, shift_ref, positions_ref, out_ref = near[5:]
     copies = fetched(list(zip(far, near)), semaphores)
-    for copy in copies[:3]:
-        copy.wait()
     edges = vec_ref.shape[1]
     orders = first_ref.shape[0]
     vec = vec_ref[...]
@@ -290,8 +288,9 @@
         jnp.concatenate([b1, b2, b1, b2, b3, b1], axis=0).astype(jnp.bfloat16),
     )
     radial = silu_half(mixed).astype(jnp.bfloat16)
+    copies[0].wait()
     filter_ref[...] = over_first(second_ref[...], radial)
-    for copy in copies[3:]:
+    for copy in copies[1:]:
         copy.wait()
     species = species_ref[...]
 
@@ -424,7 +423,7 @@
     for first in range(0, blocks, fit):
         tile = jnp.zeros((8, lanes), jnp.float32)
         for place in range(fit):
-            row = all_ref[lax.rem(place_ref[0] + first + place, blocks)]
+            row = all_ref[(place_ref[0] + first + place) & (blocks - 1)]
             row = pltpu.roll(jnp.broadcast_to(row, (8, lanes)), 0, 1, stride=own, stride_axis=0)
             row = pltpu.roll(row, place * own, 1) if place else row
             tile = jnp.where(segment == place, row, tile)
@@ -593,8 +592,9 @@
             pltpu.SemaphoreType.DMA((2,)),
         ],
     )
-    others = [exchanged(packed, "space", step) for step in range(1, lanes)]
-    rest = (edge_vec, w_rad1, w_rad2, edge_send[None], edge_recv[None], w_msg, w_up)
+    near, far, side = [exchanged(packed, "space", step) for step in (1, 3, 2)]
+    others = (near, side, far)
+    rest = (w_rad2, edge_send[None], edge_recv[None], w_msg, w_up)
     rest = rest + (species[None], hardness[None], width[None], chi_shift[None], positions)
     rest = rest + (w_out[None],)
     parts = kernel_call(
@@ -610,7 +610,7 @@
             ((chans, 2 * chans), jnp.bfloat16),
             ((chans, atoms), jnp.float32),
         ],
-        (space.reshape(1), *rest),
+        (space.reshape(1), *rest, edge_vec, w_rad1),
         scalars=1,
         far=len(rest),
         scratch=[pltpu.VMEM(value.shape, value.dtype) for value in rest]

time: 24 us -> 24.3 us (1.012)
  local copies, waits for them, and re-layouts: 0 us -> 0.69 us
  waiting for transfers between devices: 7.11 us -> 6.62 us
  starting transfers between devices: 8.13 us -> 8.43 us
    unnamed x0 -> x4, local copies, waits for them, and re-layouts: none -> 0.69 us
    ppermute x3, waiting for transfers between devices: 1.28 us -> 0.8 us  [exchanged(): lax.ppermute(block, axis, [(place, place ^ step) for place in range(size)])]
    all_to_all x1, starting transfers between devices: 4.98 us -> 5.28 us  [few_shards(): block = lax.all_to_all(block, everywhere, 0, 0, tiled=True)]
  transfers between devices with their start and end apart: 4 -> 4, of which waited for: 2 -> 2; matrix products, arithmetic and copies ran while one was open for 0% -> 0% of each run, Pallas kernels for 10% -> 9%
where the time goes in v17:
time: 24.3 us; the launch traced here: 24 us
  starting transfers between devices  8.43 us (35%)
  Pallas kernels  6.94 us (29%)
  waiting for transfers between devices  6.62 us (27%)
  between operations  1.34 us (6%)
  local copies, waits for them, and re-layouts  0.69 us (3%)
    pallas_call x5, Pallas kernels, kernel_call(): pl.pallas_call(kernel, out_shape=shapes, in_specs=[pl.BlockSpec(memory_sp...  6.94 us
    all_to_all x1, waiting for transfers between devices, few_shards(): block = lax.all_to_all(block, everywhere, 0, 0, tiled=True)  5.82 us
    all_to_all x1, starting transfers between devices, few_shards(): block = lax.all_to_all(block, everywhere, 0, 0, tiled=True)  5.28 us
    ppermute x3, starting transfers between devices, exchanged(): lax.ppermute(block, axis, [(place, place ^ step) for place in range(size)])  3.15 us
    ppermute x3, waiting for transfers between devices, exchanged(): lax.ppermute(block, axis, [(place, place ^ step) for place in range(size)])  0.8 us
    unnamed x4, local copies, waits for them, and re-layouts  0.69 us
  transfers between devices with their start and end apart: 4, of which 2 were waited for; matrix products, arithmetic and copies ran while one was open for 0% of the time, Pallas kernels for 9%

profile of v17, /device:TPU:0, one launch (start us, length us, event | category | flops | bytes accessed | tf_op | source)
XLA Modules:
  0.0 24.0 jit_solution(17963610403092777559)
XLA Ops:
  0.6 0.8 %shard_map.183.own_ref.packed_ref = bf16[32,128]{1,0:T(8,128)(2,1)S(1)} custom-call(s32[1]{0:T(128)} %bitcast.space_ref, bf16[16,128]{1,0:T(8,128)(2,1)} %features_ref.1, s32[1,4,32]{2,1,0:T(4,128)} %lists_ref.1), custom_call_target="tpu_custom_call" | custom-call | bytes 1048576 | tf_op jit(solution)/shard_map/pallas_call | solution.py:546
  1.4 0.0 copy-start
  1.4 2.5 %collective-permute-start.2 = (bf16[32,128]{1,0:T(8,128)(2,1)S(1)}, bf16[32,128]{1,0:T(8,128)(2,1)S(1)}, u32[]{:S(2)}, u32[]{:S(2)}) collective-permute-start(bf16[32,128]{1,0:T(8,128)(2,1)S(1)} %shard_map.183.own_ref.packed_ref), channel_id=1, source_target_pairs={{0,3},{1,2},{2,1},{3,0},{4,7},{5,6},{6,5},{7,4},{8,11},{9,10},{10,... | collective-permute-start | bytes 24584 | tf_op jit(solution)/shard_map/ppermute | solution.py:559
  3.9 0.6 %collective-permute-start.1 = (bf16[32,128]{1,0:T(8,128)(2,1)S(1)}, bf16[32,128]{1,0:T(8,128)(2,1)S(1)}, u32[]{:S(2)}, u32[]{:S(2)}) collective-permute-start(bf16[32,128]{1,0:T(8,128)(2,1)S(1)} %shard_map.183.own_ref.packed_ref), channel_id=1, source_target_pairs={{0,2},{1,3},{2,0},{3,1},{4,6},{5,7},{6,4},{7,5},{8,10},{9,11},{10,... | collective-permute-start | bytes 24584 | tf_op jit(solution)/shard_map/ppermute | solution.py:559
  4.5 0.0 collective-permute-start
  4.6 0.0 copy-start.1
  4.6 0.0 copy-done
  4.6 0.7 %copy-done.1 = f32[8,128]{1,0:T(8,128)S(1)} copy-done((f32[8,128]{1,0:T(8,128)S(1)}, f32[8,128]{1,0:T(8,128)}, u32[]{:S(2)}) %copy-start.1) | copy-done | bytes 4120
  5.3 1.5 %shard_map.184 = (f32[256,512]{1,0:T(8,128)S(1)}, f32[8,512]{1,0:T(8,128)S(1)}, f32[1,128]{1,0:T(1,128)S(1)}, bf16[128,512]{1,0:T(8,128)(2,1)S(1)}, f32[64,512]{...) custom-call(s32[1]{0:T(128)} %bitcast.space_ref, ...), custom_call_target="tpu_custom_call" | custom-call | flops 268435456 | bytes 1048576 | tf_op jit(solution)/shard_map/pallas_call | solution.py:546
  6.8 0.0 collective-permute-done.2.far_ref
  6.8 0.8 %collective-permute-done.1.side_ref = bf16[32,128]{1,0:T(8,128)(2,1)S(1)} collective-permute-done((bf16[32,128]{1,0:T(8,128)(2,1)S(1)}, bf16[32,128]{1,0:T(8,128)(2,1)S(1)}, u32[]{:S(2)}, u32[]{:S(2)}) %collective-permute-start.1) | collective-permute-done | bytes 8224 | tf_op jit(solution)/shard_map/ppermute | solution.py:559
  7.6 0.0 collective-permute-done.near_ref
  7.6 1.5 %shard_map.185 = (f32[128,16]{1,0:T(8,128)S(1)}, f32[32,1,128]{2,1,0:T(1,128)}) custom-call(bf16[32,128]{1,0:T(8,128)(2,1)S(1)} %shard_map.183.own_ref.packed_ref, bf16[32,128]{1,0:T(8,128)(2,1)S(1)} %collective-permute-done.near_ref, bf16[32,128]{1,0:T(8,128)(2,1)S(1)} %collective-permute-done.1.side_ref, ...), custom_call_target="tpu_custom_call" | custom-call | flops 268435456 | bytes 1048576 | tf_op jit(solution)/shard_map/pallas_call | solution.py:546
  9.1 5.3 %all-to-all-start = ((f32[32,1,128]{2,1,0:T(1,128)}), f32[32,1,128]{2,1,0:T(1,128)S(1)}, u32[]{:S(2)}, u32[]{:S(2)}) async-start(f32[32,1,128]{2,1,0:T(1,128)} %get-tuple-element.28), calls=%async_computation | async-start | bytes 32768 | tf_op jit(solution)/shard_map/all_to_all | solution.py:630
  15.0 0.7 %shard_map.186 = bf16[16,128]{1,0:T(8,128)(2,1)} custom-call(bf16[32,128]{1,0:T(8,128)(2,1)S(1)} %shard_map.183.own_ref.packed_ref, f32[128,16]{1,0:T(8,128)S(1)} %get-tuple-element.27.hidden_ref), custom_call_target="tpu_custom_call" | custom-call | flops 1048576 | bytes 1048576 | tf_op jit(solution)/shard_map/pallas_call | solution.py:546
  15.7 5.8 %all-to-all-done.all_ref = f32[32,1,128]{2,1,0:T(1,128)S(1)} async-done(((f32[32,1,128]{2,1,0:T(1,128)}), f32[32,1,128]{2,1,0:T(1,128)S(1)}, u32[]{:S(2)}, u32[]{:S(2)}) %all-to-all-start) | async-done | bytes 16416 | tf_op jit(solution)/shard_map/all_to_all | solution.py:630
  21.5 2.5 %shard_map.187 = (f32[1,16]{1,0:T(1,128)}, f32[3,16]{1,0:T(4,128)}, f32[6,16]{1,0:T(8,128)}) custom-call(s32[1]{0:T(128)} %bitcast.8.place_ref, f32[1]{0:T(128)S(6)} %copy.20.field_ref, f32[32,1,128]{2,1,0:T(1,128)S(1)} %all-to-all-done.all_ref), custom_call_target="tpu_custom_call" | custom-call | flops 268435456 | bytes 1048576 | tf_op jit(solution)/shard_map/pallas_call | solution.py:546
Async XLA Ops:
  1.4 3.2 %copy-start = (f32[3,512]{1,0:T(4,128)S(1)}, f32[3,512]{1,0:T(4,128)}, u32[]{:S(2)}) copy-start(f32[3,512]{1,0:T(4,128)} %refs_11_.1) | copy-start | bytes 18436
  1.4 5.3 %collective-permute-start.2 = (bf16[32,128]{1,0:T(8,128)(2,1)S(1)}, bf16[32,128]{1,0:T(8,128)(2,1)S(1)}, u32[]{:S(2)}, u32[]{:S(2)}) collective-permute-start(bf16[32,128]{1,0:T(8,128)(2,1)S(1)} %shard_map.183.own_ref.packed_ref), channel_id=1, source_target_pairs={{0,3},{1,2},{2,1},{3,0},{4,7},{5,6},{6,5},{7,4},{8,11},{9,10},{10,... | collective-permute-start | bytes 24584 | tf_op jit(solution)/shard_map/ppermute | solution.py:559
  3.9 3.7 %collective-permute-start.1 = (bf16[32,128]{1,0:T(8,128)(2,1)S(1)}, bf16[32,128]{1,0:T(8,128)(2,1)S(1)}, u32[]{:S(2)}, u32[]{:S(2)}) collective-permute-start(bf16[32,128]{1,0:T(8,128)(2,1)S(1)} %shard_map.183.own_ref.packed_ref), channel_id=1, source_target_pairs={{0,2},{1,3},{2,0},{3,1},{4,6},{5,7},{6,4},{7,5},{8,10},{9,11},{10,... | collective-permute-start | bytes 24584 | tf_op jit(solution)/shard_map/ppermute | solution.py:559
  4.5 3.0 %collective-permute-start = (bf16[32,128]{1,0:T(8,128)(2,1)S(1)}, bf16[32,128]{1,0:T(8,128)(2,1)S(1)}, u32[]{:S(2)}, u32[]{:S(2)}) collective-permute-start(bf16[32,128]{1,0:T(8,128)(2,1)S(1)} %shard_map.183.own_ref.packed_ref), channel_id=1, source_target_pairs={{0,1},{1,0},{2,3},{3,2},{4,5},{5,4},{6,7},{7,6},{8,9},{9,8},{10,11... | collective-permute-start | bytes 24584 | tf_op jit(solution)/shard_map/ppermute | solution.py:559
  4.6 0.7 %copy-start.1 = (f32[8,128]{1,0:T(8,128)S(1)}, f32[8,128]{1,0:T(8,128)}, u32[]{:S(2)}) copy-start(f32[8,128]{1,0:T(8,128)} %refs_12_.1) | copy-start | bytes 12292
  9.1 12.4 %all-to-all-start = ((f32[32,1,128]{2,1,0:T(1,128)}), f32[32,1,128]{2,1,0:T(1,128)S(1)}, u32[]{:S(2)}, u32[]{:S(2)}) async-start(f32[32,1,128]{2,1,0:T(1,128)} %get-tuple-element.28), calls=%async_computation | async-start | bytes 32768 | tf_op jit(solution)/shard_map/all_to_all | solution.py:630

commit v18 on v17

--- a/solution.py
+++ b/solution.py
@@ -256,15 +256,16 @@
     space_ref,
     *refs,
 ):
-    count = (len(refs) - 12) // 2
-    far, near, semaphores = refs[:count], refs[count + 11 : -1], refs[-1]
-    vec_ref, first_ref, filter_ref, unit_ref, row_ref, slot_ref = refs[count : count + 6]
-    local_ref, hit_ref, turned_ref, upward_ref, read_ref = refs[count + 6 : count + 11]
-    second_ref, send_ref, recv_ref, project_ref, update_ref = near[:5]
-    species_ref, hardness_ref, width_ref, shift_ref, positions_ref, out_ref = near[5:]
+    count = (len(refs) - 11) // 2
+    far, near, semaphores = refs[:count], refs[count + 10 : -1], refs[-1]
+    vec_ref, filter_ref, unit_ref, row_ref, slot_ref = refs[count : count + 5]
+    local_ref, hit_ref, turned_ref, upward_ref, read_ref = refs[count + 5 : count + 10]
+    first_ref, second_ref, send_ref, recv_ref, project_ref, update_ref = near[:6]
+    out_ref, species_ref, hardness_ref, width_ref, shift_ref, positions_ref = near[6:]
     copies = fetched(list(zip(far, near)), semaphores)
     edges = vec_ref.shape[1]
     orders = first_ref.shape[0]
+    atoms, chans = hit_ref.shape[0], row_ref.shape[1]
     vec = vec_ref[...]
     east, north, up = vec[0:1], vec[1:2], vec[2:3]
     squared = east * east + north * north + up * up
@@ -282,15 +283,36 @@
         series = series * (part * part) + coefficient
     basis = series * part * (sign * envelope)
     b1, b2, b3 = split3(basis)
+    copies[0].wait()
     w1, w2, w3 = split3(first_ref[...])
     mixed = over_first(
         jnp.concatenate([w1, w1, w2, w2, w1, w3], axis=0).astype(jnp.bfloat16),
         jnp.concatenate([b1, b2, b1, b2, b3, b1], axis=0).astype(jnp.bfloat16),
     )
     radial = silu_half(mixed).astype(jnp.bfloat16)
-    copies[0].wait()
+    copies[1].wait()
     filter_ref[...] = over_first(second_ref[...], radial)
-    for copy in copies[1:]:
+    lanes = local_ref.shape[0] // atoms
+    slots = chans // lanes
+
+    def chosen(ref, index):
+        hit = lax.broadcasted_iota(jnp.int32, ref.shape, 0) == index
+        ref[...] = jnp.where(hit, 1.0, 0.0).astype(ref.dtype)
+
+    copies[2].wait()
+    send = send_ref[...]
+    own = send < atoms
+    chosen(slot_ref, jnp.where(own, -1, (send - atoms) ^ (space_ref[0] * slots)))
+    chosen(local_ref, jnp.where(own, send, -1))
+    copies[3].wait()
+    chosen(hit_ref, recv_ref[...])
+    copies[4].wait()
+    turned_ref[...] = project_ref[...].astype(jnp.float32).T.astype(jnp.bfloat16)
+    copies[5].wait()
+    upward_ref[...] = update_ref[...].astype(jnp.float32).T.astype(jnp.bfloat16)
+    copies[6].wait()
+    read_ref[...] = jnp.broadcast_to(out_ref[...], (atoms, chans)).T
+    for copy in copies[7:]:
         copy.wait()
     species = species_ref[...]
 
@@ -302,8 +324,6 @@
 
     positions = positions_ref[...]
     sigma = table(width_ref)
-    atoms = species.shape[1]
-    chans = row_ref.shape[1]
     diag = table(hardness_ref) + inverse_root_pi / sigma
     blank = jnp.zeros((2, atoms), jnp.float32)
     rows = [positions[0:1], blank, -table(shift_ref), diag, sigma, positions[2:3], positions[1:2]]
@@ -312,30 +332,13 @@
     )
     block = pltpu.roll(block, 0, 1, stride=atoms, stride_axis=0)
     row_ref[...] = jnp.sum(block, axis=0, keepdims=True)
-    lanes = local_ref.shape[0] // atoms
-    slots = chans // lanes
-    send = send_ref[...]
-    own = send < atoms
-    slot = jnp.where(own, -1, (send - atoms) ^ (space_ref[0] * slots))
-    local = jnp.where(own, send, -1)
-
-    def chosen(ref, index):
-        hit = lax.broadcasted_iota(jnp.int32, ref.shape, 0) == index
-        ref[...] = jnp.where(hit, 1.0, 0.0).astype(ref.dtype)
-
-    chosen(slot_ref, slot)
-    chosen(local_ref, local)
-    chosen(hit_ref, recv_ref[...])
-    turned_ref[...] = project_ref[...].astype(jnp.float32).T.astype(jnp.bfloat16)
-    upward_ref[...] = update_ref[...].astype(jnp.float32).T.astype(jnp.bfloat16)
-    read_ref[...] = jnp.broadcast_to(out_ref[...], (atoms, chans)).T
 
 
 def node_kernel(
     own_ref,
     near_ref,
+    far_ref,
     side_ref,
-    far_ref,
     filter_ref,
     unit_ref,
     row_ref,
@@ -593,10 +596,8 @@
         ],
     )
     near, far, side = [exchanged(packed, "space", step) for step in (1, 3, 2)]
-    others = (near, side, far)
-    rest = (w_rad2, edge_send[None], edge_recv[None], w_msg, w_up)
+    rest = (w_rad1, w_rad2, edge_send[None], edge_recv[None], w_msg, w_up, w_out[None])
     rest = rest + (species[None], hardness[None], width[None], chi_shift[None], positions)
-    rest = rest + (w_out[None],)
     parts = kernel_call(
         edge_kernel,
         [
@@ -610,7 +611,7 @@
             ((chans, 2 * chans), jnp.bfloat16),
             ((chans, atoms), jnp.float32),
         ],
-        (space.reshape(1), *rest, edge_vec, w_rad1),
+        (space.reshape(1), *rest, edge_vec),
         scalars=1,
         far=len(rest),
         scratch=[pltpu.VMEM(value.shape, value.dtype) for value in rest]
@@ -621,7 +622,7 @@
     hidden, block = kernel_call(
         node_kernel,
         [((chans, atoms), jnp.float32), ((devices, 1, chans), jnp.float32)],
-        (packed, *others, *parts),
+        (packed, near, far, side, *parts),
         flops=1 << 28,
     )
     (new_features,) = kernel_call(

time: 24.3 us -> 24.2 us (level)
  local copies, waits for them, and re-layouts: 0.69 us -> 0.01 us
  Pallas kernels: 6.94 us -> 7.25 us
  waiting for transfers between devices: 6.62 us -> 6.89 us
    unnamed x4 -> x2, local copies, waits for them, and re-layouts: 0.69 us -> 0.01 us
    pallas_call x5, Pallas kernels: 6.94 us -> 7.25 us  [kernel_call(): pl.pallas_call(kernel, out_shape=shapes, in_specs=[pl.BlockSpec(memory_sp...]
    ppermute x3, waiting for transfers between devices: 0.8 us -> 1.06 us  [exchanged(): lax.ppermute(block, axis, [(place, place ^ step) for place in range(size)])]
  transfers between devices with their start and end apart: 4 -> 4, of which waited for: 2 -> 2; matrix products, arithmetic and copies ran while one was open for 0% -> 0% of each run, Pallas kernels for 9% -> 10%
where the time goes in v18:
time: 24.2 us; the launch traced here: 24 us
  starting transfers between devices  8.47 us (35%)
  Pallas kernels  7.25 us (30%)
  waiting for transfers between devices  6.89 us (28%)
  between operations  1.34 us (6%)
    pallas_call x5, Pallas kernels, kernel_call(): pl.pallas_call(kernel, out_shape=shapes, in_specs=[pl.BlockSpec(memory_sp...  7.25 us
    all_to_all x1, waiting for transfers between devices, few_shards(): block = lax.all_to_all(block, everywhere, 0, 0, tiled=True)  5.82 us
    all_to_all x1, starting transfers between devices, few_shards(): block = lax.all_to_all(block, everywhere, 0, 0, tiled=True)  5.24 us
    ppermute x3, starting transfers between devices, exchanged(): lax.ppermute(block, axis, [(place, place ^ step) for place in range(size)])  3.23 us
    ppermute x3, waiting for transfers between devices, exchanged(): lax.ppermute(block, axis, [(place, place ^ step) for place in range(size)])  1.06 us
  transfers between devices with their start and end apart: 4, of which 2 were waited for; matrix products, arithmetic and copies ran while one was open for 0% of the time, Pallas kernels for 10%

profile of v18, /device:TPU:0, one launch (start us, length us, event | category | flops | bytes accessed | tf_op | source)
XLA Modules:
  0.0 24.0 jit_solution(7142068242377215306)
XLA Ops:
  0.6 0.8 %shard_map.183.own_ref.packed_ref = bf16[32,128]{1,0:T(8,128)(2,1)S(1)} custom-call(s32[1]{0:T(128)} %bitcast.space_ref, bf16[16,128]{1,0:T(8,128)(2,1)} %features_ref.1, s32[1,4,32]{2,1,0:T(4,128)} %lists_ref.1), custom_call_target="tpu_custom_call" | custom-call | bytes 1048576 | tf_op jit(solution)/shard_map/pallas_call | solution.py:549
  1.4 0.0 copy-start
  1.4 3.0 %collective-permute-start.2 = (bf16[32,128]{1,0:T(8,128)(2,1)S(1)}, bf16[32,128]{1,0:T(8,128)(2,1)S(1)}, u32[]{:S(2)}, u32[]{:S(2)}) collective-permute-start(bf16[32,128]{1,0:T(8,128)(2,1)S(1)} %shard_map.183.own_ref.packed_ref), channel_id=1, source_target_pairs={{0,2},{1,3},{2,0},{3,1},{4,6},{5,7},{6,4},{7,5},{8,10},{9,11},{10,... | collective-permute-start | bytes 24584 | tf_op jit(solution)/shard_map/ppermute | solution.py:562
  4.5 0.0 collective-permute-start.1
  4.5 0.2 collective-permute-start
  4.7 0.0 copy-done
  4.7 1.8 %shard_map.184 = (f32[256,512]{1,0:T(8,128)S(1)}, f32[8,512]{1,0:T(8,128)S(1)}, f32[1,128]{1,0:T(1,128)S(1)}, bf16[128,512]{1,0:T(8,128)(2,1)S(1)}, f32[64,512]{...) custom-call(s32[1]{0:T(128)} %bitcast.space_ref, ...), custom_call_target="tpu_custom_call" | custom-call | flops 268435456 | bytes 1048576 | tf_op jit(solution)/shard_map/pallas_call | solution.py:549
  6.5 0.0 collective-permute-done.2.side_ref
  6.5 1.1 %collective-permute-done.1.far_ref = bf16[32,128]{1,0:T(8,128)(2,1)S(1)} collective-permute-done((bf16[32,128]{1,0:T(8,128)(2,1)S(1)}, bf16[32,128]{1,0:T(8,128)(2,1)S(1)}, u32[]{:S(2)}, u32[]{:S(2)}) %collective-permute-start.1) | collective-permute-done | bytes 8224 | tf_op jit(solution)/shard_map/ppermute | solution.py:562
  7.5 0.0 collective-permute-done.near_ref
  7.5 1.5 %shard_map.185 = (f32[128,16]{1,0:T(8,128)S(1)}, f32[32,1,128]{2,1,0:T(1,128)}) custom-call(bf16[32,128]{1,0:T(8,128)(2,1)S(1)} %shard_map.183.own_ref.packed_ref, bf16[32,128]{1,0:T(8,128)(2,1)S(1)} %collective-permute-done.near_ref, bf16[32,128]{1,0:T(8,128)(2,1)S(1)} %collective-permute-done.1.far_ref, ...), custom_call_target="tpu_custom_call" | custom-call | flops 268435456 | bytes 1048576 | tf_op jit(solution)/shard_map/pallas_call | solution.py:549
  9.0 5.2 %all-to-all-start = ((f32[32,1,128]{2,1,0:T(1,128)}), f32[32,1,128]{2,1,0:T(1,128)S(1)}, u32[]{:S(2)}, u32[]{:S(2)}) async-start(f32[32,1,128]{2,1,0:T(1,128)} %get-tuple-element.28), calls=%async_computation | async-start | bytes 32768 | tf_op jit(solution)/shard_map/all_to_all | solution.py:631
  14.9 0.7 %shard_map.186 = bf16[16,128]{1,0:T(8,128)(2,1)} custom-call(bf16[32,128]{1,0:T(8,128)(2,1)S(1)} %shard_map.183.own_ref.packed_ref, f32[128,16]{1,0:T(8,128)S(1)} %get-tuple-element.27.hidden_ref), custom_call_target="tpu_custom_call" | custom-call | flops 1048576 | bytes 1048576 | tf_op jit(solution)/shard_map/pallas_call | solution.py:549
  15.6 5.8 %all-to-all-done.all_ref = f32[32,1,128]{2,1,0:T(1,128)S(1)} async-done(((f32[32,1,128]{2,1,0:T(1,128)}), f32[32,1,128]{2,1,0:T(1,128)S(1)}, u32[]{:S(2)}, u32[]{:S(2)}) %all-to-all-start) | async-done | bytes 16416 | tf_op jit(solution)/shard_map/all_to_all | solution.py:631
  21.4 2.5 %shard_map.187 = (f32[1,16]{1,0:T(1,128)}, f32[3,16]{1,0:T(4,128)}, f32[6,16]{1,0:T(8,128)}) custom-call(s32[1]{0:T(128)} %bitcast.8.place_ref, f32[1]{0:T(128)S(6)} %copy.20.field_ref, f32[32,1,128]{2,1,0:T(1,128)S(1)} %all-to-all-done.all_ref), custom_call_target="tpu_custom_call" | custom-call | flops 268435456 | bytes 1048576 | tf_op jit(solution)/shard_map/pallas_call | solution.py:549
Async XLA Ops:
  1.4 3.2 %copy-start = (f32[3,512]{1,0:T(4,128)S(1)}, f32[3,512]{1,0:T(4,128)}, u32[]{:S(2)}) copy-start(f32[3,512]{1,0:T(4,128)} %refs_12_.1) | copy-start | bytes 18436
  1.4 5.0 %collective-permute-start.2 = (bf16[32,128]{1,0:T(8,128)(2,1)S(1)}, bf16[32,128]{1,0:T(8,128)(2,1)S(1)}, u32[]{:S(2)}, u32[]{:S(2)}) collective-permute-start(bf16[32,128]{1,0:T(8,128)(2,1)S(1)} %shard_map.183.own_ref.packed_ref), channel_id=1, source_target_pairs={{0,2},{1,3},{2,0},{3,1},{4,6},{5,7},{6,4},{7,5},{8,10},{9,11},{10,... | collective-permute-start | bytes 24584 | tf_op jit(solution)/shard_map/ppermute | solution.py:562
  4.5 3.1 %collective-permute-start.1 = (bf16[32,128]{1,0:T(8,128)(2,1)S(1)}, bf16[32,128]{1,0:T(8,128)(2,1)S(1)}, u32[]{:S(2)}, u32[]{:S(2)}) collective-permute-start(bf16[32,128]{1,0:T(8,128)(2,1)S(1)} %shard_map.183.own_ref.packed_ref), channel_id=1, source_target_pairs={{0,3},{1,2},{2,1},{3,0},{4,7},{5,6},{6,5},{7,4},{8,11},{9,10},{10,... | collective-permute-start | bytes 24584 | tf_op jit(solution)/shard_map/ppermute | solution.py:562
  4.5 3.1 %collective-permute-start = (bf16[32,128]{1,0:T(8,128)(2,1)S(1)}, bf16[32,128]{1,0:T(8,128)(2,1)S(1)}, u32[]{:S(2)}, u32[]{:S(2)}) collective-permute-start(bf16[32,128]{1,0:T(8,128)(2,1)S(1)} %shard_map.183.own_ref.packed_ref), channel_id=1, source_target_pairs={{0,1},{1,0},{2,3},{3,2},{4,5},{5,4},{6,7},{7,6},{8,9},{9,8},{10,11... | collective-permute-start | bytes 24584 | tf_op jit(solution)/shard_map/ppermute | solution.py:562
  9.0 12.4 %all-to-all-start = ((f32[32,1,128]{2,1,0:T(1,128)}), f32[32,1,128]{2,1,0:T(1,128)S(1)}, u32[]{:S(2)}, u32[]{:S(2)}) async-start(f32[32,1,128]{2,1,0:T(1,128)} %get-tuple-element.28), calls=%async_computation | async-start | bytes 32768 | tf_op jit(solution)/shard_map/all_to_all | solution.py:631

commit v19 on v14

--- a/solution.py
+++ b/solution.py
@@ -1,3 +1,4 @@
+import functools
 import math
 
 import jax
@@ -252,21 +253,17 @@
     copies[1].wait()
 
 
-def edge_kernel(
-    space_ref,
-    *refs,
-):
+def edge_kernel(lanes, space_ref, *refs):
     count = (len(refs) - 10) // 2
     far, near, semaphores = refs[:count], refs[count + 9 : -1], refs[-1]
-    filter_ref, unit_ref, row_ref, slot_ref, local_ref, hit_ref = refs[count : count + 6]
-    turned_ref, upward_ref, read_ref = refs[count + 6 : count + 9]
-    vec_ref, first_ref, second_ref, send_ref, recv_ref, project_ref, update_ref = near[:7]
-    species_ref, hardness_ref, width_ref, shift_ref, positions_ref, out_ref = near[7:]
+    vec_ref, filter_ref, unit_ref, row_ref, slot_ref = refs[count : count + 5]
+    hit_ref, turned_ref, upward_ref, read_ref = refs[count + 5 : count + 9]
+    first_ref, second_ref, send_ref, recv_ref, project_ref, update_ref = near[:6]
+    out_ref, species_ref, hardness_ref, width_ref, shift_ref, positions_ref = near[6:]
     copies = fetched(list(zip(far, near)), semaphores)
-    for copy in copies[:3]:
-        copy.wait()
     edges = vec_ref.shape[1]
     orders = first_ref.shape[0]
+    atoms, chans = hit_ref.shape[0], row_ref.shape[1]
     vec = vec_ref[...]
     east, north, up = vec[0:1], vec[1:2], vec[2:3]
     squared = east * east + north * north + up * up
@@ -284,6 +281,8 @@
         series = series * (part * part) + coefficient
     basis = series * part * (sign * envelope)
     b1, b2, b3 = split3(basis)
+    for copy in copies[:2]:
+        copy.wait()
     w1, w2, w3 = split3(first_ref[...])
     mixed = over_first(
         jnp.concatenate([w1, w1, w2, w2, w1, w3], axis=0).astype(jnp.bfloat16),
@@ -291,8 +290,22 @@
     )
     radial = silu_half(mixed).astype(jnp.bfloat16)
     filter_ref[...] = over_first(second_ref[...], radial)
-    for copy in copies[3:]:
+    for copy in copies[2:]:
         copy.wait()
+    slots = slot_ref.shape[0] - atoms
+    width = slots // lanes
+
+    def chosen(ref, index, value):
+        hit = lax.broadcasted_iota(jnp.int32, ref.shape, 0) == index
+        ref[...] = jnp.where(hit, value, 0.0).astype(ref.dtype)
+
+    send = send_ref[...]
+    ghost = (send - atoms) ^ (space_ref[0] * width)
+    chosen(slot_ref, jnp.where(send < atoms, send + slots, ghost), 1.0)
+    chosen(hit_ref, recv_ref[...], message_scale)
+    turned_ref[...] = project_ref[...].astype(jnp.float32).T.astype(jnp.bfloat16)
+    upward_ref[...] = update_ref[...].astype(jnp.float32).T.astype(jnp.bfloat16)
+    read_ref[...] = jnp.broadcast_to(out_ref[...], (atoms, chans)).T
     species = species_ref[...]
 
     def table(ref):
@@ -303,8 +316,6 @@
 
     positions = positions_ref[...]
     sigma = table(width_ref)
-    atoms = species.shape[1]
-    chans = row_ref.shape[1]
     diag = table(hardness_ref) + inverse_root_pi / sigma
     blank = jnp.zeros((2, atoms), jnp.float32)
     rows = [positions[0:1], blank, -table(shift_ref), diag, sigma, positions[2:3], positions[1:2]]
@@ -313,35 +324,17 @@
     )
     block = pltpu.roll(block, 0, 1, stride=atoms, stride_axis=0)
     row_ref[...] = jnp.sum(block, axis=0, keepdims=True)
-    lanes = local_ref.shape[0] // atoms
-    slots = chans // lanes
-    send = send_ref[...]
-    own = send < atoms
-    slot = jnp.where(own, -1, (send - atoms) ^ (space_ref[0] * slots))
-    local = jnp.where(own, send, -1)
-
-    def chosen(ref, index):
-        hit = lax.broadcasted_iota(jnp.int32, ref.shape, 0) == index
-        ref[...] = jnp.where(hit, 1.0, 0.0).astype(ref.dtype)
-
-    chosen(slot_ref, slot)
-    chosen(local_ref, local)
-    chosen(hit_ref, recv_ref[...])
-    turned_ref[...] = project_ref[...].astype(jnp.float32).T.astype(jnp.bfloat16)
-    upward_ref[...] = update_ref[...].astype(jnp.float32).T.astype(jnp.bfloat16)
-    read_ref[...] = jnp.broadcast_to(out_ref[...], (atoms, chans)).T
 
 
 def node_kernel(
     own_ref,
     near_ref,
+    far_ref,
     side_ref,
-    far_ref,
     filter_ref,
     unit_ref,
     row_ref,
     slot_ref,
-    local_ref,
     hit_ref,
     turned_ref,
     upward_ref,
@@ -356,20 +349,20 @@
     for place, ref in enumerate(packed):
         tail = ref[atoms:, :].astype(jnp.float32)
         chosen = chosen + tail[place : place + 1]
-    fill = jnp.where(
-        lax.broadcasted_iota(jnp.int32, (len(packed) * atoms, chans), 0)
-        == chosen.astype(jnp.int32),
-        1.0,
-        0.0,
-    ).astype(jnp.bfloat16)
-    sender = jnp.dot(fill, slot_ref[...], preferred_element_type=jnp.float32) + local_ref[...]
+    member = lax.broadcasted_iota(jnp.int32, (len(packed) * atoms, chans), 0)
+    fill = jnp.where(member == chosen.astype(jnp.int32), 1.0, 0.0)
+    lane = lax.broadcasted_iota(jnp.int32, (len(packed) * atoms, atoms), 1)
+    fill = jnp.concatenate([fill, jnp.where(member[:, :atoms] == lane, 1.0, 0.0)], axis=1)
+    sender = jnp.dot(
+        fill.astype(jnp.bfloat16), slot_ref[...], preferred_element_type=jnp.float32
+    )
     projected = over_last(turned_ref[...], group).astype(jnp.bfloat16)
     picked = jnp.dot(projected, sender.astype(jnp.bfloat16), preferred_element_type=jnp.float32)
     scalar = picked[:chans] * filter_ref[:chans, :]
     carried = picked[chans:] * filter_ref[chans:, :]
     parts = [scalar] + [unit_ref[axis : axis + 1, :] * carried for axis in range(3)]
     message = jnp.concatenate([part.astype(jnp.bfloat16) for part in parts], axis=0)
-    summed = over_last(message, hit_ref[...]) * message_scale
+    summed = over_last(message, hit_ref[...])
     square = jnp.zeros((chans, atoms), jnp.float32)
     for component in range(1, 4):
         part = summed[component * chans : (component + 1) * chans]
@@ -604,24 +597,22 @@
             pltpu.SemaphoreType.DMA((2,)),
         ],
     )
-    others = [exchanged(packed, "space", step) for step in range(1, lanes)]
-    rest = (edge_vec, w_rad1, w_rad2, edge_send[None], edge_recv[None], w_msg, w_up)
+    near, far, side = [exchanged(packed, "space", step) for step in (1, 3, 2)]
+    rest = (w_rad1, w_rad2, edge_send[None], edge_recv[None], w_msg, w_up, w_out[None])
     rest = rest + (species[None], hardness[None], width[None], chi_shift[None], positions)
-    rest = rest + (w_out[None],)
     parts = kernel_call(
-        edge_kernel,
+        functools.partial(edge_kernel, lanes),
         [
             ((2 * chans, edges), jnp.float32),
             ((8, edges), jnp.float32),
             ((1, chans), jnp.float32),
-            ((chans, edges), jnp.bfloat16),
-            ((lanes * atoms, edges), jnp.float32),
+            ((chans + atoms, edges), jnp.bfloat16),
             ((atoms, edges), jnp.bfloat16),
             ((2 * chans, chans), jnp.bfloat16),
             ((chans, 2 * chans), jnp.bfloat16),
             ((chans, atoms), jnp.float32),
         ],
-        (space.reshape(1), *rest),
+        (space.reshape(1), *rest, edge_vec),
         scalars=1,
         far=len(rest),
         scratch=[pltpu.VMEM(value.shape, value.dtype) for value in rest]
@@ -632,7 +623,7 @@
     hidden, block = kernel_call(
         node_kernel,
         [((chans, atoms), jnp.float32), ((devices, 1, chans), jnp.float32)],
-        (packed, *others, *parts),
+        (packed, near, far, side, *parts),
         flops=1 << 28,
     )
     (new_features,) = kernel_call(

time: 24 us -> 24 us (level)
  no operation moved by 1% of the time
where the time goes in v19:
time: 24 us; the launch traced here: 23.8 us
  starting transfers between devices  8.33 us (35%)
  Pallas kernels  7.11 us (30%)
  waiting for transfers between devices  7.03 us (29%)
  between operations  1.34 us (6%)
    pallas_call x5, Pallas kernels, kernel_call(): pl.pallas_call(kernel, out_shape=shapes, in_specs=[pl.BlockSpec(memory_sp...  7.11 us
    all_to_all x1, waiting for transfers between devices, few_shards(): block = lax.all_to_all(block, everywhere, 0, 0, tiled=True)  5.82 us
    all_to_all x1, starting transfers between devices, few_shards(): block = lax.all_to_all(block, everywhere, 0, 0, tiled=True)  5.1 us
    ppermute x3, starting transfers between devices, exchanged(): lax.ppermute(block, axis, [(place, place ^ step) for place in range(size)])  3.23 us
    ppermute x3, waiting for transfers between devices, exchanged(): lax.ppermute(block, axis, [(place, place ^ step) for place in range(size)])  1.21 us
  transfers between devices with their start and end apart: 4, of which 2 were waited for; matrix products, arithmetic and copies ran while one was open for 0% of the time, Pallas kernels for 10%

profile of v19, /device:TPU:0, one launch (start us, length us, event | category | flops | bytes accessed | tf_op | source)
XLA Modules:
  0.0 23.8 jit_solution(12318303059393243994)
XLA Ops:
  0.6 0.8 %shard_map.183.own_ref.packed_ref = bf16[32,128]{1,0:T(8,128)(2,1)S(1)} custom-call(s32[1]{0:T(128)} %bitcast.space_ref, bf16[16,128]{1,0:T(8,128)(2,1)} %features_ref.1, s32[1,4,32]{2,1,0:T(4,128)} %lists_ref.1), custom_call_target="tpu_custom_call" | custom-call | bytes 1048576 | tf_op jit(solution)/shard_map/pallas_call | solution.py:551
  1.4 0.0 copy-start
  1.4 3.0 %collective-permute-start.2 = (bf16[32,128]{1,0:T(8,128)(2,1)S(1)}, bf16[32,128]{1,0:T(8,128)(2,1)S(1)}, u32[]{:S(2)}, u32[]{:S(2)}) collective-permute-start(bf16[32,128]{1,0:T(8,128)(2,1)S(1)} %shard_map.183.own_ref.packed_ref), channel_id=1, source_target_pairs={{0,2},{1,3},{2,0},{3,1},{4,6},{5,7},{6,4},{7,5},{8,10},{9,11},{10,... | collective-permute-start | bytes 24584 | tf_op jit(solution)/shard_map/ppermute | solution.py:564
  4.5 0.0 collective-permute-start.1
  4.5 0.2 collective-permute-start
  4.7 0.0 copy-done
  4.7 1.7 %shard_map.184 = (f32[256,512]{1,0:T(8,128)S(1)}, f32[8,512]{1,0:T(8,128)S(1)}, f32[1,128]{1,0:T(1,128)S(1)}, bf16[144,512]{1,0:T(8,128)(2,1)S(1)}, bf16[16,512]...) custom-call(s32[1]{0:T(128)} %bitcast.space_ref, ...), custom_call_target="tpu_custom_call" | custom-call | flops 268435456 | bytes 1048576 | tf_op jit(solution)/shard_map/pallas_call | solution.py:551
  6.3 0.0 collective-permute-done.2.side_ref
  6.3 1.2 %collective-permute-done.1.far_ref = bf16[32,128]{1,0:T(8,128)(2,1)S(1)} collective-permute-done((bf16[32,128]{1,0:T(8,128)(2,1)S(1)}, bf16[32,128]{1,0:T(8,128)(2,1)S(1)}, u32[]{:S(2)}, u32[]{:S(2)}) %collective-permute-start.1) | collective-permute-done | bytes 8224 | tf_op jit(solution)/shard_map/ppermute | solution.py:564
  7.5 0.0 collective-permute-done.near_ref
  7.5 1.5 %shard_map.185 = (f32[128,16]{1,0:T(8,128)S(1)}, f32[32,1,128]{2,1,0:T(1,128)}) custom-call(bf16[32,128]{1,0:T(8,128)(2,1)S(1)} %shard_map.183.own_ref.packed_ref, bf16[32,128]{1,0:T(8,128)(2,1)S(1)} %collective-permute-done.near_ref, bf16[32,128]{1,0:T(8,128)(2,1)S(1)} %collective-permute-done.1.far_ref, ...), custom_call_target="tpu_custom_call" | custom-call | flops 268435456 | bytes 1048576 | tf_op jit(solution)/shard_map/pallas_call | solution.py:551
  9.0 5.1 %all-to-all-start = ((f32[32,1,128]{2,1,0:T(1,128)}), f32[32,1,128]{2,1,0:T(1,128)S(1)}, u32[]{:S(2)}, u32[]{:S(2)}) async-start(f32[32,1,128]{2,1,0:T(1,128)} %get-tuple-element.26), calls=%async_computation | async-start | bytes 32768 | tf_op jit(solution)/shard_map/all_to_all | solution.py:632
  14.8 0.7 %shard_map.186 = bf16[16,128]{1,0:T(8,128)(2,1)} custom-call(bf16[32,128]{1,0:T(8,128)(2,1)S(1)} %shard_map.183.own_ref.packed_ref, f32[128,16]{1,0:T(8,128)S(1)} %get-tuple-element.25.hidden_ref), custom_call_target="tpu_custom_call" | custom-call | flops 1048576 | bytes 1048576 | tf_op jit(solution)/shard_map/pallas_call | solution.py:551
  15.5 5.8 %all-to-all-done.all_ref = f32[32,1,128]{2,1,0:T(1,128)S(1)} async-done(((f32[32,1,128]{2,1,0:T(1,128)}), f32[32,1,128]{2,1,0:T(1,128)S(1)}, u32[]{:S(2)}, u32[]{:S(2)}) %all-to-all-start) | async-done | bytes 16416 | tf_op jit(solution)/shard_map/all_to_all | solution.py:632
  21.3 2.5 %shard_map.187 = (f32[1,16]{1,0:T(1,128)}, f32[3,16]{1,0:T(4,128)}, f32[6,16]{1,0:T(8,128)}) custom-call(s32[1]{0:T(128)} %bitcast.8.place_ref, f32[1]{0:T(128)S(6)} %copy.20.field_ref, f32[32,1,128]{2,1,0:T(1,128)S(1)} %all-to-all-done.all_ref), custom_call_target="tpu_custom_call" | custom-call | flops 268435456 | bytes 1048576 | tf_op jit(solution)/shard_map/pallas_call | solution.py:551
Async XLA Ops:
  1.4 3.2 %copy-start = (f32[3,512]{1,0:T(4,128)S(1)}, f32[3,512]{1,0:T(4,128)}, u32[]{:S(2)}) copy-start(f32[3,512]{1,0:T(4,128)} %refs_12_.1) | copy-start | bytes 18436
  1.4 4.9 %collective-permute-start.2 = (bf16[32,128]{1,0:T(8,128)(2,1)S(1)}, bf16[32,128]{1,0:T(8,128)(2,1)S(1)}, u32[]{:S(2)}, u32[]{:S(2)}) collective-permute-start(bf16[32,128]{1,0:T(8,128)(2,1)S(1)} %shard_map.183.own_ref.packed_ref), channel_id=1, source_target_pairs={{0,2},{1,3},{2,0},{3,1},{4,6},{5,7},{6,4},{7,5},{8,10},{9,11},{10,... | collective-permute-start | bytes 24584 | tf_op jit(solution)/shard_map/ppermute | solution.py:564
  4.5 3.1 %collective-permute-start.1 = (bf16[32,128]{1,0:T(8,128)(2,1)S(1)}, bf16[32,128]{1,0:T(8,128)(2,1)S(1)}, u32[]{:S(2)}, u32[]{:S(2)}) collective-permute-start(bf16[32,128]{1,0:T(8,128)(2,1)S(1)} %shard_map.183.own_ref.packed_ref), channel_id=1, source_target_pairs={{0,3},{1,2},{2,1},{3,0},{4,7},{5,6},{6,5},{7,4},{8,11},{9,10},{10,... | collective-permute-start | bytes 24584 | tf_op jit(solution)/shard_map/ppermute | solution.py:564
  4.5 3.1 %collective-permute-start = (bf16[32,128]{1,0:T(8,128)(2,1)S(1)}, bf16[32,128]{1,0:T(8,128)(2,1)S(1)}, u32[]{:S(2)}, u32[]{:S(2)}) collective-permute-start(bf16[32,128]{1,0:T(8,128)(2,1)S(1)} %shard_map.183.own_ref.packed_ref), channel_id=1, source_target_pairs={{0,1},{1,0},{2,3},{3,2},{4,5},{5,4},{6,7},{7,6},{8,9},{9,8},{10,11... | collective-permute-start | bytes 24584 | tf_op jit(solution)/shard_map/ppermute | solution.py:564
  9.0 12.3 %all-to-all-start = ((f32[32,1,128]{2,1,0:T(1,128)}), f32[32,1,128]{2,1,0:T(1,128)S(1)}, u32[]{:S(2)}, u32[]{:S(2)}) async-start(f32[32,1,128]{2,1,0:T(1,128)} %get-tuple-element.26), calls=%async_computation | async-start | bytes 32768 | tf_op jit(solution)/shard_map/all_to_all | solution.py:632

commit v20 on v14

--- a/solution.py
+++ b/solution.py
@@ -414,6 +414,7 @@
     matrix_ref,
     side_ref,
     value_ref,
+    kept_ref,
 ):
     blocks, _, lanes = all_ref.shape
     own = charges_ref.shape[1]
@@ -457,7 +458,6 @@
     wide_row, rhs_row = down(spread_row), down(rhs)
 
     above = [jnp.zeros((8, lanes), jnp.float32) for _ in range(tiles)]
-    kept = []
     for start in range(0, count, own):
         first = start // lanes
         column = columns[start : start + own]
@@ -479,7 +479,8 @@
             if start == 0:
                 slope = (two_over_root_pi * scale * decay - kernel) * inverse * inverse
                 slope = jnp.where(same, 0.0, slope) if tile == first else slope
-                kept.append((delta, slope))
+                for which, kind in enumerate(delta + [slope]):
+                    kept_ref[which, :, tile * lanes : (tile + 1) * lanes] = kind.reshape(own, lanes)
             if tile == first:
                 kernel = jnp.where(same, 0.0, kernel)
             else:
@@ -500,10 +501,10 @@
     image = diag * rhs + jnp.concatenate(image, axis=1)
     across = jnp.broadcast_to(image, (8, count)).T
     norm = total(rhs * rhs)
-    alpha = norm / total(rhs * image)
+    alpha = norm * reciprocal(total(rhs * image))
     residual = rhs - alpha * image
     fresh = total(residual * residual)
-    again = fresh / norm
+    again = fresh * reciprocal(norm)
     direction = residual + again * rhs
     onto = [jnp.zeros((8, lanes), jnp.float32) for _ in range(tiles)]
     above = [jnp.zeros((8, lanes), jnp.float32) for _ in range(tiles)]
@@ -522,11 +523,15 @@
     curved = jnp.sum(curved, axis=0, keepdims=True)
     for tile in range(tiles):
         curved = curved + part(diag * direction * direction, tile)
-    charges = alpha * rhs + fresh / total(curved) * direction
+    charges = alpha * rhs + fresh * reciprocal(total(curved)) * direction
 
     sums = [jnp.zeros(shape, jnp.float32) for _ in range(9)]
     charge_row = down(charges)
-    for tile, (delta, slope) in enumerate(kept):
+    for tile in range(tiles):
+        *delta, slope = [
+            kept_ref[which, :, tile * lanes : (tile + 1) * lanes].reshape(shape)
+            for which in range(4)
+        ]
         weight = charge_row[tile] * slope
         pulled = [weight * delta[axis] for axis in range(3)]
         terms = pulled + [
@@ -650,6 +655,7 @@
             pltpu.VMEM((everybody, everybody), jnp.float32),
             pltpu.VMEM((everybody, chans), jnp.float32),
             pltpu.VMEM((everybody, chans), jnp.float32),
+            pltpu.VMEM((4, atoms, everybody), jnp.float32),
         ],
         flops=1 << 28,
     )

time: 24 us -> 23.9 us (level)
  no operation moved by 1% of the time
where the time goes in v20:
time: 23.9 us; the launch traced here: 23.7 us
  starting transfers between devices  8.13 us (34%)
  waiting for transfers between devices  7.11 us (30%)
  Pallas kernels  7.1 us (30%)
  between operations  1.33 us (6%)
    pallas_call x5, Pallas kernels, kernel_call(): pl.pallas_call(kernel, out_shape=shapes, in_specs=[pl.BlockSpec(memory_sp...  7.1 us
    all_to_all x1, waiting for transfers between devices, few_shards(): block = lax.all_to_all(block, everywhere, 0, 0, tiled=True)  5.83 us
    all_to_all x1, starting transfers between devices, few_shards(): block = lax.all_to_all(block, everywhere, 0, 0, tiled=True)  4.98 us
    ppermute x3, starting transfers between devices, exchanged(): lax.ppermute(block, axis, [(place, place ^ step) for place in range(size)])  3.15 us
    ppermute x3, waiting for transfers between devices, exchanged(): lax.ppermute(block, axis, [(place, place ^ step) for place in range(size)])  1.28 us
  transfers between devices with their start and end apart: 4, of which 2 were waited for; matrix products, arithmetic and copies ran while one was open for 0% of the time, Pallas kernels for 10%

profile of v20, /device:TPU:0, one launch (start us, length us, event | category | flops | bytes accessed | tf_op | source)
XLA Modules:
  0.0 23.7 jit_solution(4992650930916157319)
XLA Ops:
  0.6 0.8 %shard_map.183.own_ref.packed_ref = bf16[32,128]{1,0:T(8,128)(2,1)S(1)} custom-call(s32[1]{0:T(128)} %bitcast.space_ref, bf16[16,128]{1,0:T(8,128)(2,1)} %features_ref.1, s32[1,4,32]{2,1,0:T(4,128)} %lists_ref.1), custom_call_target="tpu_custom_call" | custom-call | bytes 1048576 | tf_op jit(solution)/shard_map/pallas_call | solution.py:563
  1.4 2.5 %collective-permute-start.2 = (bf16[32,128]{1,0:T(8,128)(2,1)S(1)}, bf16[32,128]{1,0:T(8,128)(2,1)S(1)}, u32[]{:S(2)}, u32[]{:S(2)}) collective-permute-start(bf16[32,128]{1,0:T(8,128)(2,1)S(1)} %shard_map.183.own_ref.packed_ref), channel_id=1, source_target_pairs={{0,3},{1,2},{2,1},{3,0},{4,7},{5,6},{6,5},{7,4},{8,11},{9,10},{10,... | collective-permute-start | bytes 24584 | tf_op jit(solution)/shard_map/ppermute | solution.py:576
  3.9 0.6 %collective-permute-start.1 = (bf16[32,128]{1,0:T(8,128)(2,1)S(1)}, bf16[32,128]{1,0:T(8,128)(2,1)S(1)}, u32[]{:S(2)}, u32[]{:S(2)}) collective-permute-start(bf16[32,128]{1,0:T(8,128)(2,1)S(1)} %shard_map.183.own_ref.packed_ref), channel_id=1, source_target_pairs={{0,2},{1,3},{2,0},{3,1},{4,6},{5,7},{6,4},{7,5},{8,10},{9,11},{10,... | collective-permute-start | bytes 24584 | tf_op jit(solution)/shard_map/ppermute | solution.py:576
  4.5 0.0 collective-permute-start
  4.6 1.7 %shard_map.184 = (f32[256,512]{1,0:T(8,128)S(1)}, f32[8,512]{1,0:T(8,128)S(1)}, f32[1,128]{1,0:T(1,128)S(1)}, bf16[128,512]{1,0:T(8,128)(2,1)S(1)}, f32[64,512]{...) custom-call(s32[1]{0:T(128)} %bitcast.space_ref, ...), custom_call_target="tpu_custom_call" | custom-call | flops 268435456 | bytes 1048576 | tf_op jit(solution)/shard_map/pallas_call | solution.py:563
  6.3 0.0 collective-permute-done.2.far_ref
  6.3 1.3 %collective-permute-done.1.side_ref = bf16[32,128]{1,0:T(8,128)(2,1)S(1)} collective-permute-done((bf16[32,128]{1,0:T(8,128)(2,1)S(1)}, bf16[32,128]{1,0:T(8,128)(2,1)S(1)}, u32[]{:S(2)}, u32[]{:S(2)}) %collective-permute-start.1) | collective-permute-done | bytes 8224 | tf_op jit(solution)/shard_map/ppermute | solution.py:576
  7.5 0.0 collective-permute-done.near_ref
  7.5 1.5 %shard_map.185 = (f32[128,16]{1,0:T(8,128)S(1)}, f32[32,1,128]{2,1,0:T(1,128)}) custom-call(bf16[32,128]{1,0:T(8,128)(2,1)S(1)} %shard_map.183.own_ref.packed_ref, bf16[32,128]{1,0:T(8,128)(2,1)S(1)} %collective-permute-done.near_ref, bf16[32,128]{1,0:T(8,128)(2,1)S(1)} %collective-permute-done.1.side_ref, ...), custom_call_target="tpu_custom_call" | custom-call | flops 268435456 | bytes 1048576 | tf_op jit(solution)/shard_map/pallas_call | solution.py:563
  9.0 5.0 %all-to-all-start = ((f32[32,1,128]{2,1,0:T(1,128)}), f32[32,1,128]{2,1,0:T(1,128)S(1)}, u32[]{:S(2)}, u32[]{:S(2)}) async-start(f32[32,1,128]{2,1,0:T(1,128)} %get-tuple-element.28), calls=%async_computation | async-start | bytes 32768 | tf_op jit(solution)/shard_map/all_to_all | solution.py:646
  14.7 0.7 %shard_map.186 = bf16[16,128]{1,0:T(8,128)(2,1)} custom-call(bf16[32,128]{1,0:T(8,128)(2,1)S(1)} %shard_map.183.own_ref.packed_ref, f32[128,16]{1,0:T(8,128)S(1)} %get-tuple-element.27.hidden_ref), custom_call_target="tpu_custom_call" | custom-call | flops 1048576 | bytes 1048576 | tf_op jit(solution)/shard_map/pallas_call | solution.py:563
  15.4 5.8 %all-to-all-done.all_ref = f32[32,1,128]{2,1,0:T(1,128)S(1)} async-done(((f32[32,1,128]{2,1,0:T(1,128)}), f32[32,1,128]{2,1,0:T(1,128)S(1)}, u32[]{:S(2)}, u32[]{:S(2)}) %all-to-all-start) | async-done | bytes 16416 | tf_op jit(solution)/shard_map/all_to_all | solution.py:646
  21.2 2.5 %shard_map.187 = (f32[1,16]{1,0:T(1,128)}, f32[3,16]{1,0:T(4,128)}, f32[6,16]{1,0:T(8,128)}) custom-call(s32[1]{0:T(128)} %bitcast.8.place_ref, f32[1]{0:T(128)S(6)} %copy.20.field_ref, f32[32,1,128]{2,1,0:T(1,128)S(1)} %all-to-all-done.all_ref), custom_call_target="tpu_custom_call" | custom-call | flops 268435456 | bytes 1048576 | tf_op jit(solution)/shard_map/pallas_call | solution.py:563
Async XLA Ops:
  1.4 4.8 %collective-permute-start.2 = (bf16[32,128]{1,0:T(8,128)(2,1)S(1)}, bf16[32,128]{1,0:T(8,128)(2,1)S(1)}, u32[]{:S(2)}, u32[]{:S(2)}) collective-permute-start(bf16[32,128]{1,0:T(8,128)(2,1)S(1)} %shard_map.183.own_ref.packed_ref), channel_id=1, source_target_pairs={{0,3},{1,2},{2,1},{3,0},{4,7},{5,6},{6,5},{7,4},{8,11},{9,10},{10,... | collective-permute-start | bytes 24584 | tf_op jit(solution)/shard_map/ppermute | solution.py:576
  3.9 3.7 %collective-permute-start.1 = (bf16[32,128]{1,0:T(8,128)(2,1)S(1)}, bf16[32,128]{1,0:T(8,128)(2,1)S(1)}, u32[]{:S(2)}, u32[]{:S(2)}) collective-permute-start(bf16[32,128]{1,0:T(8,128)(2,1)S(1)} %shard_map.183.own_ref.packed_ref), channel_id=1, source_target_pairs={{0,2},{1,3},{2,0},{3,1},{4,6},{5,7},{6,4},{7,5},{8,10},{9,11},{10,... | collective-permute-start | bytes 24584 | tf_op jit(solution)/shard_map/ppermute | solution.py:576
  4.5 3.0 %collective-permute-start = (bf16[32,128]{1,0:T(8,128)(2,1)S(1)}, bf16[32,128]{1,0:T(8,128)(2,1)S(1)}, u32[]{:S(2)}, u32[]{:S(2)}) collective-permute-start(bf16[32,128]{1,0:T(8,128)(2,1)S(1)} %shard_map.183.own_ref.packed_ref), channel_id=1, source_target_pairs={{0,1},{1,0},{2,3},{3,2},{4,5},{5,4},{6,7},{7,6},{8,9},{9,8},{10,11... | collective-permute-start | bytes 24584 | tf_op jit(solution)/shard_map/ppermute | solution.py:576
  9.0 12.1 %all-to-all-start = ((f32[32,1,128]{2,1,0:T(1,128)}), f32[32,1,128]{2,1,0:T(1,128)S(1)}, u32[]{:S(2)}, u32[]{:S(2)}) async-start(f32[32,1,128]{2,1,0:T(1,128)} %get-tuple-element.28), calls=%async_computation | async-start | bytes 32768 | tf_op jit(solution)/shard_map/all_to_all | solution.py:646

commit v21 on v20

--- a/solution.py
+++ b/solution.py
@@ -256,13 +256,13 @@
     space_ref,
     *refs,
 ):
-    count = (len(refs) - 10) // 2
+    count = (len(refs) - 8) // 2
     far, near, semaphores = refs[:count], refs[count + 9 : -1], refs[-1]
     filter_ref, unit_ref, row_ref, slot_ref, local_ref, hit_ref = refs[count : count + 6]
-    turned_ref, upward_ref, read_ref = refs[count + 6 : count + 9]
-    vec_ref, first_ref, second_ref, send_ref, recv_ref, project_ref, update_ref = near[:7]
-    species_ref, hardness_ref, width_ref, shift_ref, positions_ref, out_ref = near[7:]
-    copies = fetched(list(zip(far, near)), semaphores)
+    turned_ref, update_ref, out_ref = refs[count + 6 : count + 9]
+    vec_ref, first_ref, second_ref, send_ref, recv_ref, project_ref = near[:6]
+    species_ref, hardness_ref, width_ref, shift_ref, positions_ref = near[6:]
+    copies = fetched(list(zip(far, near + (update_ref, out_ref))), semaphores)
     for copy in copies[:3]:
         copy.wait()
     edges = vec_ref.shape[1]
@@ -328,8 +328,6 @@
     chosen(local_ref, local)
     chosen(hit_ref, recv_ref[...])
     turned_ref[...] = project_ref[...].astype(jnp.float32).T.astype(jnp.bfloat16)
-    upward_ref[...] = update_ref[...].astype(jnp.float32).T.astype(jnp.bfloat16)
-    read_ref[...] = jnp.broadcast_to(out_ref[...], (atoms, chans)).T
 
 
 def node_kernel(
@@ -344,12 +342,12 @@
     local_ref,
     hit_ref,
     turned_ref,
-    upward_ref,
-    read_ref,
+    update_ref,
+    out_ref,
     hidden_ref,
     block_ref,
 ):
-    chans, atoms = hidden_ref.shape
+    atoms, chans = hidden_ref.shape
     packed = (own_ref, near_ref, side_ref, far_ref)
     group = jnp.concatenate([ref[:atoms, :] for ref in packed], axis=0)
     chosen = jnp.zeros((1, chans), jnp.float32)
@@ -369,16 +367,18 @@
     carried = picked[chans:] * filter_ref[chans:, :]
     parts = [scalar] + [unit_ref[axis : axis + 1, :] * carried for axis in range(3)]
     message = jnp.concatenate([part.astype(jnp.bfloat16) for part in parts], axis=0)
-    summed = over_last(message, hit_ref[...]) * message_scale
-    square = jnp.zeros((chans, atoms), jnp.float32)
+    summed = over_last(hit_ref[...], message) * message_scale
+    square = jnp.zeros((atoms, chans), jnp.float32)
     for component in range(1, 4):
-        part = summed[component * chans : (component + 1) * chans]
+        part = summed[:, component * chans : (component + 1) * chans]
         square = square + part * part
-    invariant = jnp.concatenate([summed[:chans], square], axis=0).astype(jnp.bfloat16)
-    hidden = silu(jnp.dot(upward_ref[...], invariant, preferred_element_type=jnp.float32))
-    chi = jnp.sum(hidden * read_ref[...], axis=0, keepdims=True)
-    chi = jnp.concatenate([chi, jnp.zeros((1, chans - atoms), jnp.float32)], axis=1)
-    row = row_ref[...] - pltpu.roll(chi, chi_segment * atoms, 1)
+    invariant = jnp.concatenate([summed[:, :chans], square], axis=1).astype(jnp.bfloat16)
+    hidden = silu(jnp.dot(invariant, update_ref[...], preferred_element_type=jnp.float32))
+    chi = jnp.sum(hidden * out_ref[...], axis=1, keepdims=True)
+    lane = lax.broadcasted_iota(jnp.int32, (atoms, chans), 1)
+    atom = lax.broadcasted_iota(jnp.int32, (atoms, chans), 0)
+    chi = jnp.where(lane == atom + chi_segment * atoms, chi, 0.0)
+    row = row_ref[...] - jnp.sum(chi, axis=0, keepdims=True)
     block_ref[...] = jnp.broadcast_to(row[None], block_ref.shape)
     hidden_ref[...] = hidden
 
@@ -386,7 +386,7 @@
 def feature_kernel(packed_ref, hidden_ref, features_ref):
     atoms = features_ref.shape[0]
     old = packed_ref[...].astype(jnp.float32)[:atoms]
-    features_ref[...] = (old + hidden_ref[...].T).astype(jnp.bfloat16)
+    features_ref[...] = (old + hidden_ref[...]).astype(jnp.bfloat16)
 
 
 def reciprocal(value):
@@ -610,9 +610,9 @@
         ],
     )
     others = [exchanged(packed, "space", step) for step in range(1, lanes)]
-    rest = (edge_vec, w_rad1, w_rad2, edge_send[None], edge_recv[None], w_msg, w_up)
+    rest = (edge_vec, w_rad1, w_rad2, edge_send[None], edge_recv[None], w_msg)
     rest = rest + (species[None], hardness[None], width[None], chi_shift[None], positions)
-    rest = rest + (w_out[None],)
+    kept = (w_up, w_out[None])
     parts = kernel_call(
         edge_kernel,
         [
@@ -623,20 +623,20 @@
             ((lanes * atoms, edges), jnp.float32),
             ((atoms, edges), jnp.bfloat16),
             ((2 * chans, chans), jnp.bfloat16),
-            ((chans, 2 * chans), jnp.bfloat16),
-            ((chans, atoms), jnp.float32),
+            (w_up.shape, w_up.dtype),
+            ((1, chans), jnp.float32),
         ],
-        (space.reshape(1), *rest),
+        (space.reshape(1), *rest, *kept),
         scalars=1,
-        far=len(rest),
+        far=len(rest + kept),
         scratch=[pltpu.VMEM(value.shape, value.dtype) for value in rest]
-        + [pltpu.SemaphoreType.DMA((len(rest),))],
+        + [pltpu.SemaphoreType.DMA((len(rest + kept),))],
         flops=1 << 28,
     )
     devices = rows * lanes
     hidden, block = kernel_call(
         node_kernel,
-        [((chans, atoms), jnp.float32), ((devices, 1, chans), jnp.float32)],
+        [((atoms, chans), jnp.float32), ((devices, 1, chans), jnp.float32)],
         (packed, *others, *parts),
         flops=1 << 28,
     )

time: 23.9 us -> 23.8 us (level)
  transfers between devices with their start and end apart: 4 -> 4, of which waited for: 2 -> 2; matrix products, arithmetic and copies ran while one was open for 0% -> 0% of each run, Pallas kernels for 10% -> 9%
where the time goes in v21:
time: 23.8 us; the launch traced here: 23.6 us
  starting transfers between devices  8.12 us (34%)
  waiting for transfers between devices  7.26 us (31%)
  Pallas kernels  6.88 us (29%)
  between operations  1.33 us (6%)
    pallas_call x5, Pallas kernels, kernel_call(): pl.pallas_call(kernel, out_shape=shapes, in_specs=[pl.BlockSpec(memory_sp...  6.88 us
    all_to_all x1, waiting for transfers between devices, few_shards(): block = lax.all_to_all(block, everywhere, 0, 0, tiled=True)  5.9 us
    all_to_all x1, starting transfers between devices, few_shards(): block = lax.all_to_all(block, everywhere, 0, 0, tiled=True)  4.97 us
    ppermute x3, starting transfers between devices, exchanged(): lax.ppermute(block, axis, [(place, place ^ step) for place in range(size)])  3.15 us
    ppermute x3, waiting for transfers between devices, exchanged(): lax.ppermute(block, axis, [(place, place ^ step) for place in range(size)])  1.36 us
  transfers between devices with their start and end apart: 4, of which 2 were waited for; matrix products, arithmetic and copies ran while one was open for 0% of the time, Pallas kernels for 9%

profile of v21, /device:TPU:0, one launch (start us, length us, event | category | flops | bytes accessed | tf_op | source)
XLA Modules:
  0.0 23.6 jit_solution(2462813886104154382)
XLA Ops:
  0.6 0.8 %shard_map.183.own_ref.packed_ref = bf16[32,128]{1,0:T(8,128)(2,1)S(1)} custom-call(s32[1]{0:T(128)} %bitcast.space_ref, bf16[16,128]{1,0:T(8,128)(2,1)} %features_ref.1, s32[1,4,32]{2,1,0:T(4,128)} %lists_ref.1), custom_call_target="tpu_custom_call" | custom-call | bytes 1048576 | tf_op jit(solution)/shard_map/pallas_call | solution.py:563
  1.4 2.5 %collective-permute-start.2 = (bf16[32,128]{1,0:T(8,128)(2,1)S(1)}, bf16[32,128]{1,0:T(8,128)(2,1)S(1)}, u32[]{:S(2)}, u32[]{:S(2)}) collective-permute-start(bf16[32,128]{1,0:T(8,128)(2,1)S(1)} %shard_map.183.own_ref.packed_ref), channel_id=1, source_target_pairs={{0,3},{1,2},{2,1},{3,0},{4,7},{5,6},{6,5},{7,4},{8,11},{9,10},{10,... | collective-permute-start | bytes 24584 | tf_op jit(solution)/shard_map/ppermute | solution.py:576
  3.9 0.6 %collective-permute-start.1 = (bf16[32,128]{1,0:T(8,128)(2,1)S(1)}, bf16[32,128]{1,0:T(8,128)(2,1)S(1)}, u32[]{:S(2)}, u32[]{:S(2)}) collective-permute-start(bf16[32,128]{1,0:T(8,128)(2,1)S(1)} %shard_map.183.own_ref.packed_ref), channel_id=1, source_target_pairs={{0,2},{1,3},{2,0},{3,1},{4,6},{5,7},{6,4},{7,5},{8,10},{9,11},{10,... | collective-permute-start | bytes 24584 | tf_op jit(solution)/shard_map/ppermute | solution.py:576
  4.5 0.0 collective-permute-start
  4.6 1.6 %shard_map.184 = (f32[256,512]{1,0:T(8,128)S(1)}, f32[8,512]{1,0:T(8,128)S(1)}, f32[1,128]{1,0:T(1,128)S(1)}, bf16[128,512]{1,0:T(8,128)(2,1)S(1)}, f32[64,512]{...) custom-call(s32[1]{0:T(128)} %bitcast.space_ref, ...), custom_call_target="tpu_custom_call" | custom-call | flops 268435456 | bytes 1048576 | tf_op jit(solution)/shard_map/pallas_call | solution.py:563
  6.2 0.0 collective-permute-done.2.far_ref
  6.2 1.4 %collective-permute-done.1.side_ref = bf16[32,128]{1,0:T(8,128)(2,1)S(1)} collective-permute-done((bf16[32,128]{1,0:T(8,128)(2,1)S(1)}, bf16[32,128]{1,0:T(8,128)(2,1)S(1)}, u32[]{:S(2)}, u32[]{:S(2)}) %collective-permute-start.1) | collective-permute-done | bytes 8224 | tf_op jit(solution)/shard_map/ppermute | solution.py:576
  7.5 0.0 collective-permute-done.near_ref
  7.5 1.4 %shard_map.185 = (f32[16,128]{1,0:T(8,128)S(1)}, f32[32,1,128]{2,1,0:T(1,128)}) custom-call(bf16[32,128]{1,0:T(8,128)(2,1)S(1)} %shard_map.183.own_ref.packed_ref, bf16[32,128]{1,0:T(8,128)(2,1)S(1)} %collective-permute-done.near_ref, bf16[32,128]{1,0:T(8,128)(2,1)S(1)} %collective-permute-done.1.side_ref, ...), custom_call_target="tpu_custom_call" | custom-call | flops 268435456 | bytes 1048576 | tf_op jit(solution)/shard_map/pallas_call | solution.py:563
  9.0 5.0 %all-to-all-start = ((f32[32,1,128]{2,1,0:T(1,128)}), f32[32,1,128]{2,1,0:T(1,128)S(1)}, u32[]{:S(2)}, u32[]{:S(2)}) async-start(f32[32,1,128]{2,1,0:T(1,128)} %get-tuple-element.28), calls=%async_computation | async-start | bytes 32768 | tf_op jit(solution)/shard_map/all_to_all | solution.py:646
  14.6 0.6 %shard_map.186 = bf16[16,128]{1,0:T(8,128)(2,1)} custom-call(bf16[32,128]{1,0:T(8,128)(2,1)S(1)} %shard_map.183.own_ref.packed_ref, f32[16,128]{1,0:T(8,128)S(1)} %get-tuple-element.27.hidden_ref), custom_call_target="tpu_custom_call" | custom-call | flops 1048576 | bytes 1048576 | tf_op jit(solution)/shard_map/pallas_call | solution.py:563
  15.2 5.9 %all-to-all-done.all_ref = f32[32,1,128]{2,1,0:T(1,128)S(1)} async-done(((f32[32,1,128]{2,1,0:T(1,128)}), f32[32,1,128]{2,1,0:T(1,128)S(1)}, u32[]{:S(2)}, u32[]{:S(2)}) %all-to-all-start) | async-done | bytes 16416 | tf_op jit(solution)/shard_map/all_to_all | solution.py:646
  21.1 2.5 %shard_map.187 = (f32[1,16]{1,0:T(1,128)}, f32[3,16]{1,0:T(4,128)}, f32[6,16]{1,0:T(8,128)}) custom-call(s32[1]{0:T(128)} %bitcast.8.place_ref, f32[1]{0:T(128)S(6)} %copy.20.field_ref, f32[32,1,128]{2,1,0:T(1,128)S(1)} %all-to-all-done.all_ref), custom_call_target="tpu_custom_call" | custom-call | flops 268435456 | bytes 1048576 | tf_op jit(solution)/shard_map/pallas_call | solution.py:563
Async XLA Ops:
  1.4 4.8 %collective-permute-start.2 = (bf16[32,128]{1,0:T(8,128)(2,1)S(1)}, bf16[32,128]{1,0:T(8,128)(2,1)S(1)}, u32[]{:S(2)}, u32[]{:S(2)}) collective-permute-start(bf16[32,128]{1,0:T(8,128)(2,1)S(1)} %shard_map.183.own_ref.packed_ref), channel_id=1, source_target_pairs={{0,3},{1,2},{2,1},{3,0},{4,7},{5,6},{6,5},{7,4},{8,11},{9,10},{10,... | collective-permute-start | bytes 24584 | tf_op jit(solution)/shard_map/ppermute | solution.py:576
  3.9 3.7 %collective-permute-start.1 = (bf16[32,128]{1,0:T(8,128)(2,1)S(1)}, bf16[32,128]{1,0:T(8,128)(2,1)S(1)}, u32[]{:S(2)}, u32[]{:S(2)}) collective-permute-start(bf16[32,128]{1,0:T(8,128)(2,1)S(1)} %shard_map.183.own_ref.packed_ref), channel_id=1, source_target_pairs={{0,2},{1,3},{2,0},{3,1},{4,6},{5,7},{6,4},{7,5},{8,10},{9,11},{10,... | collective-permute-start | bytes 24584 | tf_op jit(solution)/shard_map/ppermute | solution.py:576
  4.5 3.0 %collective-permute-start = (bf16[32,128]{1,0:T(8,128)(2,1)S(1)}, bf16[32,128]{1,0:T(8,128)(2,1)S(1)}, u32[]{:S(2)}, u32[]{:S(2)}) collective-permute-start(bf16[32,128]{1,0:T(8,128)(2,1)S(1)} %shard_map.183.own_ref.packed_ref), channel_id=1, source_target_pairs={{0,1},{1,0},{2,3},{3,2},{4,5},{5,4},{6,7},{7,6},{8,9},{9,8},{10,11... | collective-permute-start | bytes 24584 | tf_op jit(solution)/shard_map/ppermute | solution.py:576
  9.0 12.1 %all-to-all-start = ((f32[32,1,128]{2,1,0:T(1,128)}), f32[32,1,128]{2,1,0:T(1,128)S(1)}, u32[]{:S(2)}, u32[]{:S(2)}) async-start(f32[32,1,128]{2,1,0:T(1,128)} %get-tuple-element.28), calls=%async_computation | async-start | bytes 32768 | tf_op jit(solution)/shard_map/all_to_all | solution.py:646

commit v22 on v21

--- a/solution.py
+++ b/solution.py
@@ -1,3 +1,4 @@
+import functools
 import math
 
 import jax
@@ -252,14 +253,11 @@
     copies[1].wait()
 
 
-def edge_kernel(
-    space_ref,
-    *refs,
-):
-    count = (len(refs) - 8) // 2
-    far, near, semaphores = refs[:count], refs[count + 9 : -1], refs[-1]
-    filter_ref, unit_ref, row_ref, slot_ref, local_ref, hit_ref = refs[count : count + 6]
-    turned_ref, update_ref, out_ref = refs[count + 6 : count + 9]
+def edge_kernel(lanes, space_ref, *refs):
+    count = (len(refs) - 7) // 2
+    far, near, semaphores = refs[:count], refs[count + 8 : -1], refs[-1]
+    filter_ref, unit_ref, row_ref, slot_ref, hit_ref = refs[count : count + 5]
+    turned_ref, update_ref, out_ref = refs[count + 5 : count + 8]
     vec_ref, first_ref, second_ref, send_ref, recv_ref, project_ref = near[:6]
     species_ref, hardness_ref, width_ref, shift_ref, positions_ref = near[6:]
     copies = fetched(list(zip(far, near + (update_ref, out_ref))), semaphores)
@@ -313,20 +311,17 @@
     )
     block = pltpu.roll(block, 0, 1, stride=atoms, stride_axis=0)
     row_ref[...] = jnp.sum(block, axis=0, keepdims=True)
-    lanes = local_ref.shape[0] // atoms
-    slots = chans // lanes
+    slots = slot_ref.shape[0] - atoms
+    width = slots // lanes
     send = send_ref[...]
-    own = send < atoms
-    slot = jnp.where(own, -1, (send - atoms) ^ (space_ref[0] * slots))
-    local = jnp.where(own, send, -1)
-
-    def chosen(ref, index):
+    ghost = (send - atoms) ^ (space_ref[0] * width)
+
+    def chosen(ref, index, value):
         hit = lax.broadcasted_iota(jnp.int32, ref.shape, 0) == index
-        ref[...] = jnp.where(hit, 1.0, 0.0).astype(ref.dtype)
-
-    chosen(slot_ref, slot)
-    chosen(local_ref, local)
-    chosen(hit_ref, recv_ref[...])
+        ref[...] = jnp.where(hit, value, 0.0).astype(ref.dtype)
+
+    chosen(slot_ref, jnp.where(send < atoms, send + slots, ghost), 1.0)
+    chosen(hit_ref, recv_ref[...], message_scale)
     turned_ref[...] = project_ref[...].astype(jnp.float32).T.astype(jnp.bfloat16)
 
 
@@ -339,7 +334,6 @@
     unit_ref,
     row_ref,
     slot_ref,
-    local_ref,
     hit_ref,
     turned_ref,
     update_ref,
@@ -354,20 +348,20 @@
     for place, ref in enumerate(packed):
         tail = ref[atoms:, :].astype(jnp.float32)
         chosen = chosen + tail[place : place + 1]
-    fill = jnp.where(
-        lax.broadcasted_iota(jnp.int32, (len(packed) * atoms, chans), 0)
-        == chosen.astype(jnp.int32),
-        1.0,
-        0.0,
-    ).astype(jnp.bfloat16)
-    sender = jnp.dot(fill, slot_ref[...], preferred_element_type=jnp.float32) + local_ref[...]
+    member = lax.broadcasted_iota(jnp.int32, (len(packed) * atoms, chans), 0)
+    fill = jnp.where(member == chosen.astype(jnp.int32), 1.0, 0.0)
+    lane = lax.broadcasted_iota(jnp.int32, (len(packed) * atoms, atoms), 1)
+    fill = jnp.concatenate([fill, jnp.where(member[:, :atoms] == lane, 1.0, 0.0)], axis=1)
+    sender = jnp.dot(
+        fill.astype(jnp.bfloat16), slot_ref[...], preferred_element_type=jnp.float32
+    )
     projected = over_last(turned_ref[...], group).astype(jnp.bfloat16)
     picked = jnp.dot(projected, sender.astype(jnp.bfloat16), preferred_element_type=jnp.float32)
     scalar = picked[:chans] * filter_ref[:chans, :]
     carried = picked[chans:] * filter_ref[chans:, :]
     parts = [scalar] + [unit_ref[axis : axis + 1, :] * carried for axis in range(3)]
     message = jnp.concatenate([part.astype(jnp.bfloat16) for part in parts], axis=0)
-    summed = over_last(hit_ref[...], message) * message_scale
+    summed = over_last(hit_ref[...], message)
     square = jnp.zeros((atoms, chans), jnp.float32)
     for component in range(1, 4):
         part = summed[:, component * chans : (component + 1) * chans]
@@ -600,7 +594,7 @@
     space = lax.axis_index("space").astype(jnp.int32)
     (packed,) = kernel_call(
         pack_kernel,
-        [((atoms + 16, chans), jnp.bfloat16)],
+        [((atoms + 8, chans), jnp.bfloat16)],
         (space.reshape(1), features, ghost_list),
         scalars=1,
         far=2,
@@ -614,13 +608,12 @@
     rest = rest + (species[None], hardness[None], width[None], chi_shift[None], positions)
     kept = (w_up, w_out[None])
     parts = kernel_call(
-        edge_kernel,
+        functools.partial(edge_kernel, lanes),
         [
             ((2 * chans, edges), jnp.float32),
             ((8, edges), jnp.float32),
             ((1, chans), jnp.float32),
-            ((chans, edges), jnp.bfloat16),
-            ((lanes * atoms, edges), jnp.float32),
+            ((chans + atoms, edges), jnp.bfloat16),
             ((atoms, edges), jnp.bfloat16),
             ((2 * chans, chans), jnp.bfloat16),
             (w_up.shape, w_up.dtype),

time: 23.8 us -> 23.8 us (level)
  no operation moved by 1% of the time
where the time goes in v22:
time: 23.8 us; the launch traced here: 23.6 us
  starting transfers between devices  8.11 us (34%)
  waiting for transfers between devices  7.23 us (30%)
  Pallas kernels  6.89 us (29%)
  between operations  1.33 us (6%)
    pallas_call x5, Pallas kernels, kernel_call(): pl.pallas_call(kernel, out_shape=shapes, in_specs=[pl.BlockSpec(memory_sp...  6.89 us
    all_to_all x1, waiting for transfers between devices, few_shards(): block = lax.all_to_all(block, everywhere, 0, 0, tiled=True)  5.9 us
    all_to_all x1, starting transfers between devices, few_shards(): block = lax.all_to_all(block, everywhere, 0, 0, tiled=True)  4.96 us
    ppermute x3, starting transfers between devices, exchanged(): lax.ppermute(block, axis, [(place, place ^ step) for place in range(size)])  3.15 us
    ppermute x3, waiting for transfers between devices, exchanged(): lax.ppermute(block, axis, [(place, place ^ step) for place in range(size)])  1.33 us
  transfers between devices with their start and end apart: 4, of which 2 were waited for; matrix products, arithmetic and copies ran while one was open for 0% of the time, Pallas kernels for 9%

profile of v22, /device:TPU:0, one launch (start us, length us, event | category | flops | bytes accessed | tf_op | source)
XLA Modules:
  0.0 23.6 jit_solution(3948994881545513834)
XLA Ops:
  0.6 0.8 %shard_map.183.own_ref.packed_ref = bf16[24,128]{1,0:T(8,128)(2,1)S(1)} custom-call(s32[1]{0:T(128)} %bitcast.space_ref, bf16[16,128]{1,0:T(8,128)(2,1)} %features_ref.1, s32[1,4,32]{2,1,0:T(4,128)} %lists_ref.1), custom_call_target="tpu_custom_call" | custom-call | bytes 1048576 | tf_op jit(solution)/shard_map/pallas_call | solution.py:557
  1.4 2.5 %collective-permute-start.2 = (bf16[24,128]{1,0:T(8,128)(2,1)S(1)}, bf16[24,128]{1,0:T(8,128)(2,1)S(1)}, u32[]{:S(2)}, u32[]{:S(2)}) collective-permute-start(bf16[24,128]{1,0:T(8,128)(2,1)S(1)} %shard_map.183.own_ref.packed_ref), channel_id=1, source_target_pairs={{0,3},{1,2},{2,1},{3,0},{4,7},{5,6},{6,5},{7,4},{8,11},{9,10},{10,... | collective-permute-start | bytes 18440 | tf_op jit(solution)/shard_map/ppermute | solution.py:570
  3.9 0.6 %collective-permute-start.1 = (bf16[24,128]{1,0:T(8,128)(2,1)S(1)}, bf16[24,128]{1,0:T(8,128)(2,1)S(1)}, u32[]{:S(2)}, u32[]{:S(2)}) collective-permute-start(bf16[24,128]{1,0:T(8,128)(2,1)S(1)} %shard_map.183.own_ref.packed_ref), channel_id=1, source_target_pairs={{0,2},{1,3},{2,0},{3,1},{4,6},{5,7},{6,4},{7,5},{8,10},{9,11},{10,... | collective-permute-start | bytes 18440 | tf_op jit(solution)/shard_map/ppermute | solution.py:570
  4.5 0.0 collective-permute-start
  4.6 1.6 %shard_map.184 = (f32[256,512]{1,0:T(8,128)S(1)}, f32[8,512]{1,0:T(8,128)S(1)}, f32[1,128]{1,0:T(1,128)S(1)}, bf16[144,512]{1,0:T(8,128)(2,1)S(1)}, bf16[16,512]...) custom-call(s32[1]{0:T(128)} %bitcast.space_ref, ...), custom_call_target="tpu_custom_call" | custom-call | flops 268435456 | bytes 1048576 | tf_op jit(solution)/shard_map/pallas_call | solution.py:557
  6.2 0.0 collective-permute-done.2.far_ref
  6.2 1.3 %collective-permute-done.1.side_ref = bf16[24,128]{1,0:T(8,128)(2,1)S(1)} collective-permute-done((bf16[24,128]{1,0:T(8,128)(2,1)S(1)}, bf16[24,128]{1,0:T(8,128)(2,1)S(1)}, u32[]{:S(2)}, u32[]{:S(2)}) %collective-permute-start.1) | collective-permute-done | bytes 6176 | tf_op jit(solution)/shard_map/ppermute | solution.py:570
  7.5 0.0 collective-permute-done.near_ref
  7.5 1.4 %shard_map.185 = (f32[16,128]{1,0:T(8,128)S(1)}, f32[32,1,128]{2,1,0:T(1,128)}) custom-call(bf16[24,128]{1,0:T(8,128)(2,1)S(1)} %shard_map.183.own_ref.packed_ref, bf16[24,128]{1,0:T(8,128)(2,1)S(1)} %collective-permute-done.near_ref, bf16[24,128]{1,0:T(8,128)(2,1)S(1)} %collective-permute-done.1.side_ref, ...), custom_call_target="tpu_custom_call" | custom-call | flops 268435456 | bytes 1048576 | tf_op jit(solution)/shard_map/pallas_call | solution.py:557
  9.0 5.0 %all-to-all-start = ((f32[32,1,128]{2,1,0:T(1,128)}), f32[32,1,128]{2,1,0:T(1,128)S(1)}, u32[]{:S(2)}, u32[]{:S(2)}) async-start(f32[32,1,128]{2,1,0:T(1,128)} %get-tuple-element.26), calls=%async_computation | async-start | bytes 32768 | tf_op jit(solution)/shard_map/all_to_all | solution.py:639
  14.6 0.6 %shard_map.186 = bf16[16,128]{1,0:T(8,128)(2,1)} custom-call(bf16[24,128]{1,0:T(8,128)(2,1)S(1)} %shard_map.183.own_ref.packed_ref, f32[16,128]{1,0:T(8,128)S(1)} %get-tuple-element.25.hidden_ref), custom_call_target="tpu_custom_call" | custom-call | flops 1048576 | bytes 1048576 | tf_op jit(solution)/shard_map/pallas_call | solution.py:557
  15.2 5.9 %all-to-all-done.all_ref = f32[32,1,128]{2,1,0:T(1,128)S(1)} async-done(((f32[32,1,128]{2,1,0:T(1,128)}), f32[32,1,128]{2,1,0:T(1,128)S(1)}, u32[]{:S(2)}, u32[]{:S(2)}) %all-to-all-start) | async-done | bytes 16416 | tf_op jit(solution)/shard_map/all_to_all | solution.py:639
  21.1 2.5 %shard_map.187 = (f32[1,16]{1,0:T(1,128)}, f32[3,16]{1,0:T(4,128)}, f32[6,16]{1,0:T(8,128)}) custom-call(s32[1]{0:T(128)} %bitcast.8.place_ref, f32[1]{0:T(128)S(6)} %copy.20.field_ref, f32[32,1,128]{2,1,0:T(1,128)S(1)} %all-to-all-done.all_ref), custom_call_target="tpu_custom_call" | custom-call | flops 268435456 | bytes 1048576 | tf_op jit(solution)/shard_map/pallas_call | solution.py:557
Async XLA Ops:
  1.4 4.8 %collective-permute-start.2 = (bf16[24,128]{1,0:T(8,128)(2,1)S(1)}, bf16[24,128]{1,0:T(8,128)(2,1)S(1)}, u32[]{:S(2)}, u32[]{:S(2)}) collective-permute-start(bf16[24,128]{1,0:T(8,128)(2,1)S(1)} %shard_map.183.own_ref.packed_ref), channel_id=1, source_target_pairs={{0,3},{1,2},{2,1},{3,0},{4,7},{5,6},{6,5},{7,4},{8,11},{9,10},{10,... | collective-permute-start | bytes 18440 | tf_op jit(solution)/shard_map/ppermute | solution.py:570
  3.9 3.6 %collective-permute-start.1 = (bf16[24,128]{1,0:T(8,128)(2,1)S(1)}, bf16[24,128]{1,0:T(8,128)(2,1)S(1)}, u32[]{:S(2)}, u32[]{:S(2)}) collective-permute-start(bf16[24,128]{1,0:T(8,128)(2,1)S(1)} %shard_map.183.own_ref.packed_ref), channel_id=1, source_target_pairs={{0,2},{1,3},{2,0},{3,1},{4,6},{5,7},{6,4},{7,5},{8,10},{9,11},{10,... | collective-permute-start | bytes 18440 | tf_op jit(solution)/shard_map/ppermute | solution.py:570
  4.5 3.0 %collective-permute-start = (bf16[24,128]{1,0:T(8,128)(2,1)S(1)}, bf16[24,128]{1,0:T(8,128)(2,1)S(1)}, u32[]{:S(2)}, u32[]{:S(2)}) collective-permute-start(bf16[24,128]{1,0:T(8,128)(2,1)S(1)} %shard_map.183.own_ref.packed_ref), channel_id=1, source_target_pairs={{0,1},{1,0},{2,3},{3,2},{4,5},{5,4},{6,7},{7,6},{8,9},{9,8},{10,11... | collective-permute-start | bytes 18440 | tf_op jit(solution)/shard_map/ppermute | solution.py:570
  9.0 12.1 %all-to-all-start = ((f32[32,1,128]{2,1,0:T(1,128)}), f32[32,1,128]{2,1,0:T(1,128)S(1)}, u32[]{:S(2)}, u32[]{:S(2)}) async-start(f32[32,1,128]{2,1,0:T(1,128)} %get-tuple-element.26), calls=%async_computation | async-start | bytes 32768 | tf_op jit(solution)/shard_map/all_to_all | solution.py:639

commit v23 on v22

--- a/solution.py
+++ b/solution.py
@@ -594,7 +594,7 @@
     space = lax.axis_index("space").astype(jnp.int32)
     (packed,) = kernel_call(
         pack_kernel,
-        [((atoms + 8, chans), jnp.bfloat16)],
+        [((atoms + 16, chans), jnp.bfloat16)],
         (space.reshape(1), features, ghost_list),
         scalars=1,
         far=2,

time: 23.8 us -> 23.8 us (level)
  no operation moved by 1% of the time
where the time goes in v23:
time: 23.8 us; the launch traced here: 23.6 us
  starting transfers between devices  8.12 us (34%)
  waiting for transfers between devices  7.25 us (30%)
  Pallas kernels  6.88 us (29%)
  between operations  1.33 us (6%)
    pallas_call x5, Pallas kernels, kernel_call(): pl.pallas_call(kernel, out_shape=shapes, in_specs=[pl.BlockSpec(memory_sp...  6.88 us
    all_to_all x1, waiting for transfers between devices, few_shards(): block = lax.all_to_all(block, everywhere, 0, 0, tiled=True)  5.9 us
    all_to_all x1, starting transfers between devices, few_shards(): block = lax.all_to_all(block, everywhere, 0, 0, tiled=True)  4.97 us
    ppermute x3, starting transfers between devices, exchanged(): lax.ppermute(block, axis, [(place, place ^ step) for place in range(size)])  3.15 us
    ppermute x3, waiting for transfers between devices, exchanged(): lax.ppermute(block, axis, [(place, place ^ step) for place in range(size)])  1.36 us
  transfers between devices with their start and end apart: 4, of which 2 were waited for; matrix products, arithmetic and copies ran while one was open for 0% of the time, Pallas kernels for 9%

profile of v23, /device:TPU:0, one launch (start us, length us, event | category | flops | bytes accessed | tf_op | source)
XLA Modules:
  0.0 23.6 jit_solution(10967163210305155958)
XLA Ops:
  0.6 0.8 %shard_map.183.own_ref.packed_ref = bf16[32,128]{1,0:T(8,128)(2,1)S(1)} custom-call(s32[1]{0:T(128)} %bitcast.space_ref, bf16[16,128]{1,0:T(8,128)(2,1)} %features_ref.1, s32[1,4,32]{2,1,0:T(4,128)} %lists_ref.1), custom_call_target="tpu_custom_call" | custom-call | bytes 1048576 | tf_op jit(solution)/shard_map/pallas_call | solution.py:557
  1.4 2.5 %collective-permute-start.2 = (bf16[32,128]{1,0:T(8,128)(2,1)S(1)}, bf16[32,128]{1,0:T(8,128)(2,1)S(1)}, u32[]{:S(2)}, u32[]{:S(2)}) collective-permute-start(bf16[32,128]{1,0:T(8,128)(2,1)S(1)} %shard_map.183.own_ref.packed_ref), channel_id=1, source_target_pairs={{0,3},{1,2},{2,1},{3,0},{4,7},{5,6},{6,5},{7,4},{8,11},{9,10},{10,... | collective-permute-start | bytes 24584 | tf_op jit(solution)/shard_map/ppermute | solution.py:570
  3.9 0.6 %collective-permute-start.1 = (bf16[32,128]{1,0:T(8,128)(2,1)S(1)}, bf16[32,128]{1,0:T(8,128)(2,1)S(1)}, u32[]{:S(2)}, u32[]{:S(2)}) collective-permute-start(bf16[32,128]{1,0:T(8,128)(2,1)S(1)} %shard_map.183.own_ref.packed_ref), channel_id=1, source_target_pairs={{0,2},{1,3},{2,0},{3,1},{4,6},{5,7},{6,4},{7,5},{8,10},{9,11},{10,... | collective-permute-start | bytes 24584 | tf_op jit(solution)/shard_map/ppermute | solution.py:570
  4.5 0.0 collective-permute-start
  4.6 1.6 %shard_map.184 = (f32[256,512]{1,0:T(8,128)S(1)}, f32[8,512]{1,0:T(8,128)S(1)}, f32[1,128]{1,0:T(1,128)S(1)}, bf16[144,512]{1,0:T(8,128)(2,1)S(1)}, bf16[16,512]...) custom-call(s32[1]{0:T(128)} %bitcast.space_ref, ...), custom_call_target="tpu_custom_call" | custom-call | flops 268435456 | bytes 1048576 | tf_op jit(solution)/shard_map/pallas_call | solution.py:557
  6.2 0.0 collective-permute-done.2.far_ref
  6.2 1.4 %collective-permute-done.1.side_ref = bf16[32,128]{1,0:T(8,128)(2,1)S(1)} collective-permute-done((bf16[32,128]{1,0:T(8,128)(2,1)S(1)}, bf16[32,128]{1,0:T(8,128)(2,1)S(1)}, u32[]{:S(2)}, u32[]{:S(2)}) %collective-permute-start.1) | collective-permute-done | bytes 8224 | tf_op jit(solution)/shard_map/ppermute | solution.py:570
  7.5 0.0 collective-permute-done.near_ref
  7.5 1.4 %shard_map.185 = (f32[16,128]{1,0:T(8,128)S(1)}, f32[32,1,128]{2,1,0:T(1,128)}) custom-call(bf16[32,128]{1,0:T(8,128)(2,1)S(1)} %shard_map.183.own_ref.packed_ref, bf16[32,128]{1,0:T(8,128)(2,1)S(1)} %collective-permute-done.near_ref, bf16[32,128]{1,0:T(8,128)(2,1)S(1)} %collective-permute-done.1.side_ref, ...), custom_call_target="tpu_custom_call" | custom-call | flops 268435456 | bytes 1048576 | tf_op jit(solution)/shard_map/pallas_call | solution.py:557
  9.0 5.0 %all-to-all-start = ((f32[32,1,128]{2,1,0:T(1,128)}), f32[32,1,128]{2,1,0:T(1,128)S(1)}, u32[]{:S(2)}, u32[]{:S(2)}) async-start(f32[32,1,128]{2,1,0:T(1,128)} %get-tuple-element.26), calls=%async_computation | async-start | bytes 32768 | tf_op jit(solution)/shard_map/all_to_all | solution.py:639
  14.6 0.6 %shard_map.186 = bf16[16,128]{1,0:T(8,128)(2,1)} custom-call(bf16[32,128]{1,0:T(8,128)(2,1)S(1)} %shard_map.183.own_ref.packed_ref, f32[16,128]{1,0:T(8,128)S(1)} %get-tuple-element.25.hidden_ref), custom_call_target="tpu_custom_call" | custom-call | flops 1048576 | bytes 1048576 | tf_op jit(solution)/shard_map/pallas_call | solution.py:557
  15.2 5.9 %all-to-all-done.all_ref = f32[32,1,128]{2,1,0:T(1,128)S(1)} async-done(((f32[32,1,128]{2,1,0:T(1,128)}), f32[32,1,128]{2,1,0:T(1,128)S(1)}, u32[]{:S(2)}, u32[]{:S(2)}) %all-to-all-start) | async-done | bytes 16416 | tf_op jit(solution)/shard_map/all_to_all | solution.py:639
  21.1 2.5 %shard_map.187 = (f32[1,16]{1,0:T(1,128)}, f32[3,16]{1,0:T(4,128)}, f32[6,16]{1,0:T(8,128)}) custom-call(s32[1]{0:T(128)} %bitcast.8.place_ref, f32[1]{0:T(128)S(6)} %copy.20.field_ref, f32[32,1,128]{2,1,0:T(1,128)S(1)} %all-to-all-done.all_ref), custom_call_target="tpu_custom_call" | custom-call | flops 268435456 | bytes 1048576 | tf_op jit(solution)/shard_map/pallas_call | solution.py:557
Async XLA Ops:
  1.4 4.8 %collective-permute-start.2 = (bf16[32,128]{1,0:T(8,128)(2,1)S(1)}, bf16[32,128]{1,0:T(8,128)(2,1)S(1)}, u32[]{:S(2)}, u32[]{:S(2)}) collective-permute-start(bf16[32,128]{1,0:T(8,128)(2,1)S(1)} %shard_map.183.own_ref.packed_ref), channel_id=1, source_target_pairs={{0,3},{1,2},{2,1},{3,0},{4,7},{5,6},{6,5},{7,4},{8,11},{9,10},{10,... | collective-permute-start | bytes 24584 | tf_op jit(solution)/shard_map/ppermute | solution.py:570
  3.9 3.7 %collective-permute-start.1 = (bf16[32,128]{1,0:T(8,128)(2,1)S(1)}, bf16[32,128]{1,0:T(8,128)(2,1)S(1)}, u32[]{:S(2)}, u32[]{:S(2)}) collective-permute-start(bf16[32,128]{1,0:T(8,128)(2,1)S(1)} %shard_map.183.own_ref.packed_ref), channel_id=1, source_target_pairs={{0,2},{1,3},{2,0},{3,1},{4,6},{5,7},{6,4},{7,5},{8,10},{9,11},{10,... | collective-permute-start | bytes 24584 | tf_op jit(solution)/shard_map/ppermute | solution.py:570
  4.5 3.0 %collective-permute-start = (bf16[32,128]{1,0:T(8,128)(2,1)S(1)}, bf16[32,128]{1,0:T(8,128)(2,1)S(1)}, u32[]{:S(2)}, u32[]{:S(2)}) collective-permute-start(bf16[32,128]{1,0:T(8,128)(2,1)S(1)} %shard_map.183.own_ref.packed_ref), channel_id=1, source_target_pairs={{0,1},{1,0},{2,3},{3,2},{4,5},{5,4},{6,7},{7,6},{8,9},{9,8},{10,11... | collective-permute-start | bytes 24584 | tf_op jit(solution)/shard_map/ppermute | solution.py:570
  9.0 12.1 %all-to-all-start = ((f32[32,1,128]{2,1,0:T(1,128)}), f32[32,1,128]{2,1,0:T(1,128)S(1)}, u32[]{:S(2)}, u32[]{:S(2)}) async-start(f32[32,1,128]{2,1,0:T(1,128)} %get-tuple-element.26), calls=%async_computation | async-start | bytes 32768 | tf_op jit(solution)/shard_map/all_to_all | solution.py:639

commit v24 on v23

--- a/solution.py
+++ b/solution.py
@@ -452,6 +452,7 @@
     wide_row, rhs_row = down(spread_row), down(rhs)
 
     above = [jnp.zeros((8, lanes), jnp.float32) for _ in range(tiles)]
+    image, across = [], []
     for start in range(0, count, own):
         first = start // lanes
         column = columns[start : start + own]
@@ -485,15 +486,15 @@
             )
         if first + 1 < tiles:
             side_ref[start : start + own, :] = below.reshape(own, lanes)
-    image = []
-    for tile in range(tiles):
-        value = jnp.sum(above[tile], axis=0, keepdims=True)
-        if tile + 1 < tiles:
-            below = side_ref[tile * lanes : (tile + 1) * lanes, :].T
-            value = value + jnp.sum(below, axis=0, keepdims=True)
-        image.append(value)
-    image = diag * rhs + jnp.concatenate(image, axis=1)
-    across = jnp.broadcast_to(image, (8, count)).T
+        if (start + own) % lanes == 0:
+            done = jnp.sum(above[first], axis=0, keepdims=True)
+            if first + 1 < tiles:
+                turned = side_ref[first * lanes : (first + 1) * lanes, :].T
+                done = done + jnp.sum(turned, axis=0, keepdims=True)
+            done = done + part(diag, first) * part(rhs, first)
+            image.append(done)
+            across.append(jnp.broadcast_to(done, (8, lanes)).T)
+    image = jnp.concatenate(image, axis=1)
     norm = total(rhs * rhs)
     alpha = norm * reciprocal(total(rhs * image))
     residual = rhs - alpha * image
@@ -505,7 +506,8 @@
     for start in range(0, count, own):
         first = start // lanes
         value = (1.0 + again) * value_ref[start : start + own, :]
-        value = value - alpha * jnp.broadcast_to(across[start : start + own, 0:1], (own, lanes))
+        column = across[first][start - first * lanes : start - first * lanes + own, 0:1]
+        value = value - alpha * jnp.broadcast_to(column, (own, lanes))
         value = value.reshape(shape)
         for tile in range(first, tiles):
             sums = onto if tile == first else above

time: 23.8 us -> 24 us (level)
  no operation moved by 1% of the time
where the time goes in v24:
time: 24 us; the launch traced here: 23.8 us
  starting transfers between devices  8.12 us (34%)
  waiting for transfers between devices  7.25 us (30%)
  Pallas kernels  7.07 us (29%)
  between operations  1.33 us (6%)
    pallas_call x5, Pallas kernels, kernel_call(): pl.pallas_call(kernel, out_shape=shapes, in_specs=[pl.BlockSpec(memory_sp...  7.07 us
    all_to_all x1, waiting for transfers between devices, few_shards(): block = lax.all_to_all(block, everywhere, 0, 0, tiled=True)  5.9 us
    all_to_all x1, starting transfers between devices, few_shards(): block = lax.all_to_all(block, everywhere, 0, 0, tiled=True)  4.97 us
    ppermute x3, starting transfers between devices, exchanged(): lax.ppermute(block, axis, [(place, place ^ step) for place in range(size)])  3.15 us
    ppermute x3, waiting for transfers between devices, exchanged(): lax.ppermute(block, axis, [(place, place ^ step) for place in range(size)])  1.36 us
  transfers between devices with their start and end apart: 4, of which 2 were waited for; matrix products, arithmetic and copies ran while one was open for 0% of the time, Pallas kernels for 9%

profile of v24, /device:TPU:0, one launch (start us, length us, event | category | flops | bytes accessed | tf_op | source)
XLA Modules:
  0.0 23.8 jit_solution(13461897825377944655)
XLA Ops:
  0.6 0.8 %shard_map.183.own_ref.packed_ref = bf16[32,128]{1,0:T(8,128)(2,1)S(1)} custom-call(s32[1]{0:T(128)} %bitcast.space_ref, bf16[16,128]{1,0:T(8,128)(2,1)} %features_ref.1, s32[1,4,32]{2,1,0:T(4,128)} %lists_ref.1), custom_call_target="tpu_custom_call" | custom-call | bytes 1048576 | tf_op jit(solution)/shard_map/pallas_call | solution.py:559
  1.4 2.5 %collective-permute-start.2 = (bf16[32,128]{1,0:T(8,128)(2,1)S(1)}, bf16[32,128]{1,0:T(8,128)(2,1)S(1)}, u32[]{:S(2)}, u32[]{:S(2)}) collective-permute-start(bf16[32,128]{1,0:T(8,128)(2,1)S(1)} %shard_map.183.own_ref.packed_ref), channel_id=1, source_target_pairs={{0,3},{1,2},{2,1},{3,0},{4,7},{5,6},{6,5},{7,4},{8,11},{9,10},{10,... | collective-permute-start | bytes 24584 | tf_op jit(solution)/shard_map/ppermute | solution.py:572
  3.9 0.6 %collective-permute-start.1 = (bf16[32,128]{1,0:T(8,128)(2,1)S(1)}, bf16[32,128]{1,0:T(8,128)(2,1)S(1)}, u32[]{:S(2)}, u32[]{:S(2)}) collective-permute-start(bf16[32,128]{1,0:T(8,128)(2,1)S(1)} %shard_map.183.own_ref.packed_ref), channel_id=1, source_target_pairs={{0,2},{1,3},{2,0},{3,1},{4,6},{5,7},{6,4},{7,5},{8,10},{9,11},{10,... | collective-permute-start | bytes 24584 | tf_op jit(solution)/shard_map/ppermute | solution.py:572
  4.5 0.0 collective-permute-start
  4.6 1.6 %shard_map.184 = (f32[256,512]{1,0:T(8,128)S(1)}, f32[8,512]{1,0:T(8,128)S(1)}, f32[1,128]{1,0:T(1,128)S(1)}, bf16[144,512]{1,0:T(8,128)(2,1)S(1)}, bf16[16,512]...) custom-call(s32[1]{0:T(128)} %bitcast.space_ref, ...), custom_call_target="tpu_custom_call" | custom-call | flops 268435456 | bytes 1048576 | tf_op jit(solution)/shard_map/pallas_call | solution.py:559
  6.2 0.0 collective-permute-done.2.far_ref
  6.2 1.4 %collective-permute-done.1.side_ref = bf16[32,128]{1,0:T(8,128)(2,1)S(1)} collective-permute-done((bf16[32,128]{1,0:T(8,128)(2,1)S(1)}, bf16[32,128]{1,0:T(8,128)(2,1)S(1)}, u32[]{:S(2)}, u32[]{:S(2)}) %collective-permute-start.1) | collective-permute-done | bytes 8224 | tf_op jit(solution)/shard_map/ppermute | solution.py:572
  7.5 0.0 collective-permute-done.near_ref
  7.5 1.4 %shard_map.185 = (f32[16,128]{1,0:T(8,128)S(1)}, f32[32,1,128]{2,1,0:T(1,128)}) custom-call(bf16[32,128]{1,0:T(8,128)(2,1)S(1)} %shard_map.183.own_ref.packed_ref, bf16[32,128]{1,0:T(8,128)(2,1)S(1)} %collective-permute-done.near_ref, bf16[32,128]{1,0:T(8,128)(2,1)S(1)} %collective-permute-done.1.side_ref, ...), custom_call_target="tpu_custom_call" | custom-call | flops 268435456 | bytes 1048576 | tf_op jit(solution)/shard_map/pallas_call | solution.py:559
  9.0 5.0 %all-to-all-start = ((f32[32,1,128]{2,1,0:T(1,128)}), f32[32,1,128]{2,1,0:T(1,128)S(1)}, u32[]{:S(2)}, u32[]{:S(2)}) async-start(f32[32,1,128]{2,1,0:T(1,128)} %get-tuple-element.26), calls=%async_computation | async-start | bytes 32768 | tf_op jit(solution)/shard_map/all_to_all | solution.py:641
  14.6 0.6 %shard_map.186 = bf16[16,128]{1,0:T(8,128)(2,1)} custom-call(bf16[32,128]{1,0:T(8,128)(2,1)S(1)} %shard_map.183.own_ref.packed_ref, f32[16,128]{1,0:T(8,128)S(1)} %get-tuple-element.25.hidden_ref), custom_call_target="tpu_custom_call" | custom-call | flops 1048576 | bytes 1048576 | tf_op jit(solution)/shard_map/pallas_call | solution.py:559
  15.2 5.9 %all-to-all-done.all_ref = f32[32,1,128]{2,1,0:T(1,128)S(1)} async-done(((f32[32,1,128]{2,1,0:T(1,128)}), f32[32,1,128]{2,1,0:T(1,128)S(1)}, u32[]{:S(2)}, u32[]{:S(2)}) %all-to-all-start) | async-done | bytes 16416 | tf_op jit(solution)/shard_map/all_to_all | solution.py:641
  21.1 2.7 %shard_map.187 = (f32[1,16]{1,0:T(1,128)}, f32[3,16]{1,0:T(4,128)}, f32[6,16]{1,0:T(8,128)}) custom-call(s32[1]{0:T(128)} %bitcast.8.place_ref, f32[1]{0:T(128)S(6)} %copy.20.field_ref, f32[32,1,128]{2,1,0:T(1,128)S(1)} %all-to-all-done.all_ref), custom_call_target="tpu_custom_call" | custom-call | flops 268435456 | bytes 1048576 | tf_op jit(solution)/shard_map/pallas_call | solution.py:559
Async XLA Ops:
  1.4 4.8 %collective-permute-start.2 = (bf16[32,128]{1,0:T(8,128)(2,1)S(1)}, bf16[32,128]{1,0:T(8,128)(2,1)S(1)}, u32[]{:S(2)}, u32[]{:S(2)}) collective-permute-start(bf16[32,128]{1,0:T(8,128)(2,1)S(1)} %shard_map.183.own_ref.packed_ref), channel_id=1, source_target_pairs={{0,3},{1,2},{2,1},{3,0},{4,7},{5,6},{6,5},{7,4},{8,11},{9,10},{10,... | collective-permute-start | bytes 24584 | tf_op jit(solution)/shard_map/ppermute | solution.py:572
  3.9 3.7 %collective-permute-start.1 = (bf16[32,128]{1,0:T(8,128)(2,1)S(1)}, bf16[32,128]{1,0:T(8,128)(2,1)S(1)}, u32[]{:S(2)}, u32[]{:S(2)}) collective-permute-start(bf16[32,128]{1,0:T(8,128)(2,1)S(1)} %shard_map.183.own_ref.packed_ref), channel_id=1, source_target_pairs={{0,2},{1,3},{2,0},{3,1},{4,6},{5,7},{6,4},{7,5},{8,10},{9,11},{10,... | collective-permute-start | bytes 24584 | tf_op jit(solution)/shard_map/ppermute | solution.py:572
  4.5 3.0 %collective-permute-start = (bf16[32,128]{1,0:T(8,128)(2,1)S(1)}, bf16[32,128]{1,0:T(8,128)(2,1)S(1)}, u32[]{:S(2)}, u32[]{:S(2)}) collective-permute-start(bf16[32,128]{1,0:T(8,128)(2,1)S(1)} %shard_map.183.own_ref.packed_ref), channel_id=1, source_target_pairs={{0,1},{1,0},{2,3},{3,2},{4,5},{5,4},{6,7},{7,6},{8,9},{9,8},{10,11... | collective-permute-start | bytes 24584 | tf_op jit(solution)/shard_map/ppermute | solution.py:572
  9.0 12.1 %all-to-all-start = ((f32[32,1,128]{2,1,0:T(1,128)}), f32[32,1,128]{2,1,0:T(1,128)S(1)}, u32[]{:S(2)}, u32[]{:S(2)}) async-start(f32[32,1,128]{2,1,0:T(1,128)} %get-tuple-element.26), calls=%async_computation | async-start | bytes 32768 | tf_op jit(solution)/shard_map/all_to_all | solution.py:641

commit v25 on v23

--- a/solution.py
+++ b/solution.py
@@ -211,8 +211,12 @@
     )
 
 
+def reciprocal(value):
+    return pl.reciprocal(value, approx=True)
+
+
 def silu(value):
-    return value / (1.0 + jnp.exp(-value))
+    return value * reciprocal(1.0 + jnp.exp(-value))
 
 
 def silu_half(value):
@@ -381,11 +385,6 @@
     atoms = features_ref.shape[0]
     old = packed_ref[...].astype(jnp.float32)[:atoms]
     features_ref[...] = (old + hidden_ref[...]).astype(jnp.bfloat16)
-
-
-def reciprocal(value):
-    rough = pl.reciprocal(value, approx=True)
-    return rough * (2.0 - value * rough)
 
 
 def smeared(scaled):

time: 23.8 us -> 23.8 us (level)
  no operation moved by 1% of the time
where the time goes in v25:
time: 23.8 us; the launch traced here: 23.6 us
  starting transfers between devices  8.12 us (34%)
  waiting for transfers between devices  7.25 us (30%)
  Pallas kernels  6.86 us (29%)
  between operations  1.33 us (6%)
    pallas_call x5, Pallas kernels, kernel_call(): pl.pallas_call(kernel, out_shape=shapes, in_specs=[pl.BlockSpec(memory_sp...  6.86 us
    all_to_all x1, waiting for transfers between devices, few_shards(): block = lax.all_to_all(block, everywhere, 0, 0, tiled=True)  5.9 us
    all_to_all x1, starting transfers between devices, few_shards(): block = lax.all_to_all(block, everywhere, 0, 0, tiled=True)  4.97 us
    ppermute x3, starting transfers between devices, exchanged(): lax.ppermute(block, axis, [(place, place ^ step) for place in range(size)])  3.15 us
    ppermute x3, waiting for transfers between devices, exchanged(): lax.ppermute(block, axis, [(place, place ^ step) for place in range(size)])  1.36 us
  transfers between devices with their start and end apart: 4, of which 2 were waited for; matrix products, arithmetic and copies ran while one was open for 0% of the time, Pallas kernels for 9%

profile of v25, /device:TPU:0, one launch (start us, length us, event | category | flops | bytes accessed | tf_op | source)
XLA Modules:
  0.0 23.6 jit_solution(7222054147201086206)
XLA Ops:
  0.6 0.8 %shard_map.183.own_ref.packed_ref = bf16[32,128]{1,0:T(8,128)(2,1)S(1)} custom-call(s32[1]{0:T(128)} %bitcast.space_ref, bf16[16,128]{1,0:T(8,128)(2,1)} %features_ref.1, s32[1,4,32]{2,1,0:T(4,128)} %lists_ref.1), custom_call_target="tpu_custom_call" | custom-call | bytes 1048576 | tf_op jit(solution)/shard_map/pallas_call | solution.py:556
  1.4 2.5 %collective-permute-start.2 = (bf16[32,128]{1,0:T(8,128)(2,1)S(1)}, bf16[32,128]{1,0:T(8,128)(2,1)S(1)}, u32[]{:S(2)}, u32[]{:S(2)}) collective-permute-start(bf16[32,128]{1,0:T(8,128)(2,1)S(1)} %shard_map.183.own_ref.packed_ref), channel_id=1, source_target_pairs={{0,3},{1,2},{2,1},{3,0},{4,7},{5,6},{6,5},{7,4},{8,11},{9,10},{10,... | collective-permute-start | bytes 24584 | tf_op jit(solution)/shard_map/ppermute | solution.py:569
  3.9 0.6 %collective-permute-start.1 = (bf16[32,128]{1,0:T(8,128)(2,1)S(1)}, bf16[32,128]{1,0:T(8,128)(2,1)S(1)}, u32[]{:S(2)}, u32[]{:S(2)}) collective-permute-start(bf16[32,128]{1,0:T(8,128)(2,1)S(1)} %shard_map.183.own_ref.packed_ref), channel_id=1, source_target_pairs={{0,2},{1,3},{2,0},{3,1},{4,6},{5,7},{6,4},{7,5},{8,10},{9,11},{10,... | collective-permute-start | bytes 24584 | tf_op jit(solution)/shard_map/ppermute | solution.py:569
  4.5 0.0 collective-permute-start
  4.6 1.6 %shard_map.184 = (f32[256,512]{1,0:T(8,128)S(1)}, f32[8,512]{1,0:T(8,128)S(1)}, f32[1,128]{1,0:T(1,128)S(1)}, bf16[144,512]{1,0:T(8,128)(2,1)S(1)}, bf16[16,512]...) custom-call(s32[1]{0:T(128)} %bitcast.space_ref, ...), custom_call_target="tpu_custom_call" | custom-call | flops 268435456 | bytes 1048576 | tf_op jit(solution)/shard_map/pallas_call | solution.py:556
  6.2 0.0 collective-permute-done.2.far_ref
  6.2 1.4 %collective-permute-done.1.side_ref = bf16[32,128]{1,0:T(8,128)(2,1)S(1)} collective-permute-done((bf16[32,128]{1,0:T(8,128)(2,1)S(1)}, bf16[32,128]{1,0:T(8,128)(2,1)S(1)}, u32[]{:S(2)}, u32[]{:S(2)}) %collective-permute-start.1) | collective-permute-done | bytes 8224 | tf_op jit(solution)/shard_map/ppermute | solution.py:569
  7.5 0.0 collective-permute-done.near_ref
  7.5 1.4 %shard_map.185 = (f32[16,128]{1,0:T(8,128)S(1)}, f32[32,1,128]{2,1,0:T(1,128)}) custom-call(bf16[32,128]{1,0:T(8,128)(2,1)S(1)} %shard_map.183.own_ref.packed_ref, bf16[32,128]{1,0:T(8,128)(2,1)S(1)} %collective-permute-done.near_ref, bf16[32,128]{1,0:T(8,128)(2,1)S(1)} %collective-permute-done.1.side_ref, ...), custom_call_target="tpu_custom_call" | custom-call | flops 268435456 | bytes 1048576 | tf_op jit(solution)/shard_map/pallas_call | solution.py:556
  9.0 5.0 %all-to-all-start = ((f32[32,1,128]{2,1,0:T(1,128)}), f32[32,1,128]{2,1,0:T(1,128)S(1)}, u32[]{:S(2)}, u32[]{:S(2)}) async-start(f32[32,1,128]{2,1,0:T(1,128)} %get-tuple-element.26), calls=%async_computation | async-start | bytes 32768 | tf_op jit(solution)/shard_map/all_to_all | solution.py:638
  14.6 0.6 %shard_map.186 = bf16[16,128]{1,0:T(8,128)(2,1)} custom-call(bf16[32,128]{1,0:T(8,128)(2,1)S(1)} %shard_map.183.own_ref.packed_ref, f32[16,128]{1,0:T(8,128)S(1)} %get-tuple-element.25.hidden_ref), custom_call_target="tpu_custom_call" | custom-call | flops 1048576 | bytes 1048576 | tf_op jit(solution)/shard_map/pallas_call | solution.py:556
  15.2 5.9 %all-to-all-done.all_ref = f32[32,1,128]{2,1,0:T(1,128)S(1)} async-done(((f32[32,1,128]{2,1,0:T(1,128)}), f32[32,1,128]{2,1,0:T(1,128)S(1)}, u32[]{:S(2)}, u32[]{:S(2)}) %all-to-all-start) | async-done | bytes 16416 | tf_op jit(solution)/shard_map/all_to_all | solution.py:638
  21.1 2.5 %shard_map.187 = (f32[1,16]{1,0:T(1,128)}, f32[3,16]{1,0:T(4,128)}, f32[6,16]{1,0:T(8,128)}) custom-call(s32[1]{0:T(128)} %bitcast.8.place_ref, f32[1]{0:T(128)S(6)} %copy.20.field_ref, f32[32,1,128]{2,1,0:T(1,128)S(1)} %all-to-all-done.all_ref), custom_call_target="tpu_custom_call" | custom-call | flops 268435456 | bytes 1048576 | tf_op jit(solution)/shard_map/pallas_call | solution.py:556
Async XLA Ops:
  1.4 4.8 %collective-permute-start.2 = (bf16[32,128]{1,0:T(8,128)(2,1)S(1)}, bf16[32,128]{1,0:T(8,128)(2,1)S(1)}, u32[]{:S(2)}, u32[]{:S(2)}) collective-permute-start(bf16[32,128]{1,0:T(8,128)(2,1)S(1)} %shard_map.183.own_ref.packed_ref), channel_id=1, source_target_pairs={{0,3},{1,2},{2,1},{3,0},{4,7},{5,6},{6,5},{7,4},{8,11},{9,10},{10,... | collective-permute-start | bytes 24584 | tf_op jit(solution)/shard_map/ppermute | solution.py:569
  3.9 3.7 %collective-permute-start.1 = (bf16[32,128]{1,0:T(8,128)(2,1)S(1)}, bf16[32,128]{1,0:T(8,128)(2,1)S(1)}, u32[]{:S(2)}, u32[]{:S(2)}) collective-permute-start(bf16[32,128]{1,0:T(8,128)(2,1)S(1)} %shard_map.183.own_ref.packed_ref), channel_id=1, source_target_pairs={{0,2},{1,3},{2,0},{3,1},{4,6},{5,7},{6,4},{7,5},{8,10},{9,11},{10,... | collective-permute-start | bytes 24584 | tf_op jit(solution)/shard_map/ppermute | solution.py:569
  4.5 3.0 %collective-permute-start = (bf16[32,128]{1,0:T(8,128)(2,1)S(1)}, bf16[32,128]{1,0:T(8,128)(2,1)S(1)}, u32[]{:S(2)}, u32[]{:S(2)}) collective-permute-start(bf16[32,128]{1,0:T(8,128)(2,1)S(1)} %shard_map.183.own_ref.packed_ref), channel_id=1, source_target_pairs={{0,1},{1,0},{2,3},{3,2},{4,5},{5,4},{6,7},{7,6},{8,9},{9,8},{10,11... | collective-permute-start | bytes 24584 | tf_op jit(solution)/shard_map/ppermute | solution.py:569
  9.0 12.1 %all-to-all-start = ((f32[32,1,128]{2,1,0:T(1,128)}), f32[32,1,128]{2,1,0:T(1,128)S(1)}, u32[]{:S(2)}, u32[]{:S(2)}) async-start(f32[32,1,128]{2,1,0:T(1,128)} %get-tuple-element.26), calls=%async_computation | async-start | bytes 32768 | tf_op jit(solution)/shard_map/all_to_all | solution.py:638

commit v26 on v25

--- a/solution.py
+++ b/solution.py
@@ -387,9 +387,12 @@
     features_ref[...] = (old + hidden_ref[...]).astype(jnp.bfloat16)
 
 
+turn_rate = 0.3275911
+
+
 def smeared(scaled):
-    decay = jnp.exp2(scaled * scaled * -math.log2(math.e))
-    turn = reciprocal(1.0 + 0.3275911 * scaled)
+    decay = jnp.exp2(scaled * scaled * (-math.log2(math.e) / turn_rate**2))
+    turn = reciprocal(1.0 + scaled)
     series = 1.061405429 * turn - 1.453152027
     series = series * turn + 1.421413741
     series = series * turn - 0.284496736
@@ -428,7 +431,8 @@
     everyone = everyone + jnp.where(last, field_ref[0] * everyone[2:3], 0.0)
     columns = everyone.T
     diag, rhs = everyone[4:5], everyone[5:6]
-    spread_row = 2.0 * everyone[3:4] * everyone[3:4]
+    twice = 2.0 / turn_rate**2
+    spread_row = twice * everyone[3:4] * everyone[3:4]
     tiles = count // lanes
     depth = own // 8
     shape = (depth, 8, lanes)
@@ -455,7 +459,7 @@
         first = start // lanes
         column = columns[start : start + own]
         place = [along(column[:, axis : axis + 1]) for axis in range(3)]
-        wide = along(2.0 * column[:, 3:4] * column[:, 3:4])
+        wide = along(twice * column[:, 3:4] * column[:, 3:4])
         value = along(column[:, 5:6])
         value_ref[start : start + own, :] = value.reshape(own, lanes)
         below = jnp.zeros(shape, jnp.float32)
@@ -470,7 +474,7 @@
             smear, decay = smeared(squared * inverse * scale)
             kernel = smear * inverse
             if start == 0:
-                slope = (two_over_root_pi * scale * decay - kernel) * inverse * inverse
+                slope = (two_over_root_pi / turn_rate * scale * decay - kernel) * inverse * inverse
                 slope = jnp.where(same, 0.0, slope) if tile == first else slope
                 for which, kind in enumerate(delta + [slope]):
                     kept_ref[which, :, tile * lanes : (tile + 1) * lanes] = kind.reshape(own, lanes)

time: 23.8 us -> 23.8 us (level)
  no operation moved by 1% of the time
where the time goes in v26:
time: 23.8 us; the launch traced here: 23.5 us
  starting transfers between devices  8.12 us (34%)
  waiting for transfers between devices  7.25 us (30%)
  Pallas kernels  6.84 us (29%)
  between operations  1.33 us (6%)
    pallas_call x5, Pallas kernels, kernel_call(): pl.pallas_call(kernel, out_shape=shapes, in_specs=[pl.BlockSpec(memory_sp...  6.84 us
    all_to_all x1, waiting for transfers between devices, few_shards(): block = lax.all_to_all(block, everywhere, 0, 0, tiled=True)  5.9 us
    all_to_all x1, starting transfers between devices, few_shards(): block = lax.all_to_all(block, everywhere, 0, 0, tiled=True)  4.97 us
    ppermute x3, starting transfers between devices, exchanged(): lax.ppermute(block, axis, [(place, place ^ step) for place in range(size)])  3.15 us
    ppermute x3, waiting for transfers between devices, exchanged(): lax.ppermute(block, axis, [(place, place ^ step) for place in range(size)])  1.36 us
  transfers between devices with their start and end apart: 4, of which 2 were waited for; matrix products, arithmetic and copies ran while one was open for 0% of the time, Pallas kernels for 9%

profile of v26, /device:TPU:0, one launch (start us, length us, event | category | flops | bytes accessed | tf_op | source)
XLA Modules:
  0.0 23.5 jit_solution(621145090562070263)
XLA Ops:
  0.6 0.8 %shard_map.183.own_ref.packed_ref = bf16[32,128]{1,0:T(8,128)(2,1)S(1)} custom-call(s32[1]{0:T(128)} %bitcast.space_ref, bf16[16,128]{1,0:T(8,128)(2,1)} %features_ref.1, s32[1,4,32]{2,1,0:T(4,128)} %lists_ref.1), custom_call_target="tpu_custom_call" | custom-call | bytes 1048576 | tf_op jit(solution)/shard_map/pallas_call | solution.py:560
  1.4 2.5 %collective-permute-start.2 = (bf16[32,128]{1,0:T(8,128)(2,1)S(1)}, bf16[32,128]{1,0:T(8,128)(2,1)S(1)}, u32[]{:S(2)}, u32[]{:S(2)}) collective-permute-start(bf16[32,128]{1,0:T(8,128)(2,1)S(1)} %shard_map.183.own_ref.packed_ref), channel_id=1, source_target_pairs={{0,3},{1,2},{2,1},{3,0},{4,7},{5,6},{6,5},{7,4},{8,11},{9,10},{10,... | collective-permute-start | bytes 24584 | tf_op jit(solution)/shard_map/ppermute | solution.py:573
  3.9 0.6 %collective-permute-start.1 = (bf16[32,128]{1,0:T(8,128)(2,1)S(1)}, bf16[32,128]{1,0:T(8,128)(2,1)S(1)}, u32[]{:S(2)}, u32[]{:S(2)}) collective-permute-start(bf16[32,128]{1,0:T(8,128)(2,1)S(1)} %shard_map.183.own_ref.packed_ref), channel_id=1, source_target_pairs={{0,2},{1,3},{2,0},{3,1},{4,6},{5,7},{6,4},{7,5},{8,10},{9,11},{10,... | collective-permute-start | bytes 24584 | tf_op jit(solution)/shard_map/ppermute | solution.py:573
  4.5 0.0 collective-permute-start
  4.6 1.6 %shard_map.184 = (f32[256,512]{1,0:T(8,128)S(1)}, f32[8,512]{1,0:T(8,128)S(1)}, f32[1,128]{1,0:T(1,128)S(1)}, bf16[144,512]{1,0:T(8,128)(2,1)S(1)}, bf16[16,512]...) custom-call(s32[1]{0:T(128)} %bitcast.space_ref, ...), custom_call_target="tpu_custom_call" | custom-call | flops 268435456 | bytes 1048576 | tf_op jit(solution)/shard_map/pallas_call | solution.py:560
  6.2 0.0 collective-permute-done.2.far_ref
  6.2 1.4 %collective-permute-done.1.side_ref = bf16[32,128]{1,0:T(8,128)(2,1)S(1)} collective-permute-done((bf16[32,128]{1,0:T(8,128)(2,1)S(1)}, bf16[32,128]{1,0:T(8,128)(2,1)S(1)}, u32[]{:S(2)}, u32[]{:S(2)}) %collective-permute-start.1) | collective-permute-done | bytes 8224 | tf_op jit(solution)/shard_map/ppermute | solution.py:573
  7.5 0.0 collective-permute-done.near_ref
  7.5 1.4 %shard_map.185 = (f32[16,128]{1,0:T(8,128)S(1)}, f32[32,1,128]{2,1,0:T(1,128)}) custom-call(bf16[32,128]{1,0:T(8,128)(2,1)S(1)} %shard_map.183.own_ref.packed_ref, bf16[32,128]{1,0:T(8,128)(2,1)S(1)} %collective-permute-done.near_ref, bf16[32,128]{1,0:T(8,128)(2,1)S(1)} %collective-permute-done.1.side_ref, ...), custom_call_target="tpu_custom_call" | custom-call | flops 268435456 | bytes 1048576 | tf_op jit(solution)/shard_map/pallas_call | solution.py:560
  9.0 5.0 %all-to-all-start = ((f32[32,1,128]{2,1,0:T(1,128)}), f32[32,1,128]{2,1,0:T(1,128)S(1)}, u32[]{:S(2)}, u32[]{:S(2)}) async-start(f32[32,1,128]{2,1,0:T(1,128)} %get-tuple-element.26), calls=%async_computation | async-start | bytes 32768 | tf_op jit(solution)/shard_map/all_to_all | solution.py:642
  14.6 0.6 %shard_map.186 = bf16[16,128]{1,0:T(8,128)(2,1)} custom-call(bf16[32,128]{1,0:T(8,128)(2,1)S(1)} %shard_map.183.own_ref.packed_ref, f32[16,128]{1,0:T(8,128)S(1)} %get-tuple-element.25.hidden_ref), custom_call_target="tpu_custom_call" | custom-call | flops 1048576 | bytes 1048576 | tf_op jit(solution)/shard_map/pallas_call | solution.py:560
  15.2 5.9 %all-to-all-done.all_ref = f32[32,1,128]{2,1,0:T(1,128)S(1)} async-done(((f32[32,1,128]{2,1,0:T(1,128)}), f32[32,1,128]{2,1,0:T(1,128)S(1)}, u32[]{:S(2)}, u32[]{:S(2)}) %all-to-all-start) | async-done | bytes 16416 | tf_op jit(solution)/shard_map/all_to_all | solution.py:642
  21.1 2.4 %shard_map.187 = (f32[1,16]{1,0:T(1,128)}, f32[3,16]{1,0:T(4,128)}, f32[6,16]{1,0:T(8,128)}) custom-call(s32[1]{0:T(128)} %bitcast.8.place_ref, f32[1]{0:T(128)S(6)} %copy.20.field_ref, f32[32,1,128]{2,1,0:T(1,128)S(1)} %all-to-all-done.all_ref), custom_call_target="tpu_custom_call" | custom-call | flops 268435456 | bytes 1048576 | tf_op jit(solution)/shard_map/pallas_call | solution.py:560
Async XLA Ops:
  1.4 4.8 %collective-permute-start.2 = (bf16[32,128]{1,0:T(8,128)(2,1)S(1)}, bf16[32,128]{1,0:T(8,128)(2,1)S(1)}, u32[]{:S(2)}, u32[]{:S(2)}) collective-permute-start(bf16[32,128]{1,0:T(8,128)(2,1)S(1)} %shard_map.183.own_ref.packed_ref), channel_id=1, source_target_pairs={{0,3},{1,2},{2,1},{3,0},{4,7},{5,6},{6,5},{7,4},{8,11},{9,10},{10,... | collective-permute-start | bytes 24584 | tf_op jit(solution)/shard_map/ppermute | solution.py:573
  3.9 3.7 %collective-permute-start.1 = (bf16[32,128]{1,0:T(8,128)(2,1)S(1)}, bf16[32,128]{1,0:T(8,128)(2,1)S(1)}, u32[]{:S(2)}, u32[]{:S(2)}) collective-permute-start(bf16[32,128]{1,0:T(8,128)(2,1)S(1)} %shard_map.183.own_ref.packed_ref), channel_id=1, source_target_pairs={{0,2},{1,3},{2,0},{3,1},{4,6},{5,7},{6,4},{7,5},{8,10},{9,11},{10,... | collective-permute-start | bytes 24584 | tf_op jit(solution)/shard_map/ppermute | solution.py:573
  4.5 3.0 %collective-permute-start = (bf16[32,128]{1,0:T(8,128)(2,1)S(1)}, bf16[32,128]{1,0:T(8,128)(2,1)S(1)}, u32[]{:S(2)}, u32[]{:S(2)}) collective-permute-start(bf16[32,128]{1,0:T(8,128)(2,1)S(1)} %shard_map.183.own_ref.packed_ref), channel_id=1, source_target_pairs={{0,1},{1,0},{2,3},{3,2},{4,5},{5,4},{6,7},{7,6},{8,9},{9,8},{10,11... | collective-permute-start | bytes 24584 | tf_op jit(solution)/shard_map/ppermute | solution.py:573
  9.0 12.1 %all-to-all-start = ((f32[32,1,128]{2,1,0:T(1,128)}), f32[32,1,128]{2,1,0:T(1,128)S(1)}, u32[]{:S(2)}, u32[]{:S(2)}) async-start(f32[32,1,128]{2,1,0:T(1,128)} %get-tuple-element.26), calls=%async_computation | async-start | bytes 32768 | tf_op jit(solution)/shard_map/all_to_all | solution.py:642

commit v27 on v26

--- a/solution.py
+++ b/solution.py
@@ -466,21 +466,18 @@
         for tile in range(first, tiles):
             delta = [place[axis] - axes[axis][tile] for axis in range(3)]
             squared = delta[0] * delta[0] + delta[1] * delta[1] + delta[2] * delta[2]
+            inverse = lax.rsqrt(squared)
             if tile == first:
                 same = lane == line + (start - first * lanes)
-                squared = jnp.where(same, 1.0, squared)
-            inverse = lax.rsqrt(squared)
+                inverse = jnp.where(same, 0.0, inverse)
             scale = lax.rsqrt(wide + wide_row[tile])
             smear, decay = smeared(squared * inverse * scale)
             kernel = smear * inverse
             if start == 0:
                 slope = (two_over_root_pi / turn_rate * scale * decay - kernel) * inverse * inverse
-                slope = jnp.where(same, 0.0, slope) if tile == first else slope
                 for which, kind in enumerate(delta + [slope]):
                     kept_ref[which, :, tile * lanes : (tile + 1) * lanes] = kind.reshape(own, lanes)
-            if tile == first:
-                kernel = jnp.where(same, 0.0, kernel)
-            else:
+            if tile > first:
                 below = below + kernel * rhs_row[tile]
             above[tile] = above[tile] + jnp.sum(kernel * value, axis=0)
             matrix_ref[start : start + own, tile * lanes : (tile + 1) * lanes] = kernel.reshape(

time: 23.8 us -> 23.8 us (level)
  no operation moved by 1% of the time
where the time goes in v27:
time: 23.8 us; the launch traced here: 23.5 us
  starting transfers between devices  8.12 us (34%)
  waiting for transfers between devices  7.25 us (30%)
  Pallas kernels  6.83 us (29%)
  between operations  1.33 us (6%)
    pallas_call x5, Pallas kernels, kernel_call(): pl.pallas_call(kernel, out_shape=shapes, in_specs=[pl.BlockSpec(memory_sp...  6.83 us
    all_to_all x1, waiting for transfers between devices, few_shards(): block = lax.all_to_all(block, everywhere, 0, 0, tiled=True)  5.9 us
    all_to_all x1, starting transfers between devices, few_shards(): block = lax.all_to_all(block, everywhere, 0, 0, tiled=True)  4.97 us
    ppermute x3, starting transfers between devices, exchanged(): lax.ppermute(block, axis, [(place, place ^ step) for place in range(size)])  3.15 us
    ppermute x3, waiting for transfers between devices, exchanged(): lax.ppermute(block, axis, [(place, place ^ step) for place in range(size)])  1.36 us
  transfers between devices with their start and end apart: 4, of which 2 were waited for; matrix products, arithmetic and copies ran while one was open for 0% of the time, Pallas kernels for 9%

profile of v27, /device:TPU:0, one launch (start us, length us, event | category | flops | bytes accessed | tf_op | source)
XLA Modules:
  0.0 23.5 jit_solution(1863776331693957444)
XLA Ops:
  0.6 0.8 %shard_map.183.own_ref.packed_ref = bf16[32,128]{1,0:T(8,128)(2,1)S(1)} custom-call(s32[1]{0:T(128)} %bitcast.space_ref, bf16[16,128]{1,0:T(8,128)(2,1)} %features_ref.1, s32[1,4,32]{2,1,0:T(4,128)} %lists_ref.1), custom_call_target="tpu_custom_call" | custom-call | bytes 1048576 | tf_op jit(solution)/shard_map/pallas_call | solution.py:557
  1.4 2.5 %collective-permute-start.2 = (bf16[32,128]{1,0:T(8,128)(2,1)S(1)}, bf16[32,128]{1,0:T(8,128)(2,1)S(1)}, u32[]{:S(2)}, u32[]{:S(2)}) collective-permute-start(bf16[32,128]{1,0:T(8,128)(2,1)S(1)} %shard_map.183.own_ref.packed_ref), channel_id=1, source_target_pairs={{0,3},{1,2},{2,1},{3,0},{4,7},{5,6},{6,5},{7,4},{8,11},{9,10},{10,... | collective-permute-start | bytes 24584 | tf_op jit(solution)/shard_map/ppermute | solution.py:570
  3.9 0.6 %collective-permute-start.1 = (bf16[32,128]{1,0:T(8,128)(2,1)S(1)}, bf16[32,128]{1,0:T(8,128)(2,1)S(1)}, u32[]{:S(2)}, u32[]{:S(2)}) collective-permute-start(bf16[32,128]{1,0:T(8,128)(2,1)S(1)} %shard_map.183.own_ref.packed_ref), channel_id=1, source_target_pairs={{0,2},{1,3},{2,0},{3,1},{4,6},{5,7},{6,4},{7,5},{8,10},{9,11},{10,... | collective-permute-start | bytes 24584 | tf_op jit(solution)/shard_map/ppermute | solution.py:570
  4.5 0.0 collective-permute-start
  4.6 1.6 %shard_map.184 = (f32[256,512]{1,0:T(8,128)S(1)}, f32[8,512]{1,0:T(8,128)S(1)}, f32[1,128]{1,0:T(1,128)S(1)}, bf16[144,512]{1,0:T(8,128)(2,1)S(1)}, bf16[16,512]...) custom-call(s32[1]{0:T(128)} %bitcast.space_ref, ...), custom_call_target="tpu_custom_call" | custom-call | flops 268435456 | bytes 1048576 | tf_op jit(solution)/shard_map/pallas_call | solution.py:557
  6.2 0.0 collective-permute-done.2.far_ref
  6.2 1.4 %collective-permute-done.1.side_ref = bf16[32,128]{1,0:T(8,128)(2,1)S(1)} collective-permute-done((bf16[32,128]{1,0:T(8,128)(2,1)S(1)}, bf16[32,128]{1,0:T(8,128)(2,1)S(1)}, u32[]{:S(2)}, u32[]{:S(2)}) %collective-permute-start.1) | collective-permute-done | bytes 8224 | tf_op jit(solution)/shard_map/ppermute | solution.py:570
  7.5 0.0 collective-permute-done.near_ref
  7.5 1.4 %shard_map.185 = (f32[16,128]{1,0:T(8,128)S(1)}, f32[32,1,128]{2,1,0:T(1,128)}) custom-call(bf16[32,128]{1,0:T(8,128)(2,1)S(1)} %shard_map.183.own_ref.packed_ref, bf16[32,128]{1,0:T(8,128)(2,1)S(1)} %collective-permute-done.near_ref, bf16[32,128]{1,0:T(8,128)(2,1)S(1)} %collective-permute-done.1.side_ref, ...), custom_call_target="tpu_custom_call" | custom-call | flops 268435456 | bytes 1048576 | tf_op jit(solution)/shard_map/pallas_call | solution.py:557
  9.0 5.0 %all-to-all-start = ((f32[32,1,128]{2,1,0:T(1,128)}), f32[32,1,128]{2,1,0:T(1,128)S(1)}, u32[]{:S(2)}, u32[]{:S(2)}) async-start(f32[32,1,128]{2,1,0:T(1,128)} %get-tuple-element.26), calls=%async_computation | async-start | bytes 32768 | tf_op jit(solution)/shard_map/all_to_all | solution.py:639
  14.6 0.6 %shard_map.186 = bf16[16,128]{1,0:T(8,128)(2,1)} custom-call(bf16[32,128]{1,0:T(8,128)(2,1)S(1)} %shard_map.183.own_ref.packed_ref, f32[16,128]{1,0:T(8,128)S(1)} %get-tuple-element.25.hidden_ref), custom_call_target="tpu_custom_call" | custom-call | flops 1048576 | bytes 1048576 | tf_op jit(solution)/shard_map/pallas_call | solution.py:557
  15.2 5.9 %all-to-all-done.all_ref = f32[32,1,128]{2,1,0:T(1,128)S(1)} async-done(((f32[32,1,128]{2,1,0:T(1,128)}), f32[32,1,128]{2,1,0:T(1,128)S(1)}, u32[]{:S(2)}, u32[]{:S(2)}) %all-to-all-start) | async-done | bytes 16416 | tf_op jit(solution)/shard_map/all_to_all | solution.py:639
  21.1 2.4 %shard_map.187 = (f32[1,16]{1,0:T(1,128)}, f32[3,16]{1,0:T(4,128)}, f32[6,16]{1,0:T(8,128)}) custom-call(s32[1]{0:T(128)} %bitcast.8.place_ref, f32[1]{0:T(128)S(6)} %copy.20.field_ref, f32[32,1,128]{2,1,0:T(1,128)S(1)} %all-to-all-done.all_ref), custom_call_target="tpu_custom_call" | custom-call | flops 268435456 | bytes 1048576 | tf_op jit(solution)/shard_map/pallas_call | solution.py:557
Async XLA Ops:
  1.4 4.8 %collective-permute-start.2 = (bf16[32,128]{1,0:T(8,128)(2,1)S(1)}, bf16[32,128]{1,0:T(8,128)(2,1)S(1)}, u32[]{:S(2)}, u32[]{:S(2)}) collective-permute-start(bf16[32,128]{1,0:T(8,128)(2,1)S(1)} %shard_map.183.own_ref.packed_ref), channel_id=1, source_target_pairs={{0,3},{1,2},{2,1},{3,0},{4,7},{5,6},{6,5},{7,4},{8,11},{9,10},{10,... | collective-permute-start | bytes 24584 | tf_op jit(solution)/shard_map/ppermute | solution.py:570
  3.9 3.7 %collective-permute-start.1 = (bf16[32,128]{1,0:T(8,128)(2,1)S(1)}, bf16[32,128]{1,0:T(8,128)(2,1)S(1)}, u32[]{:S(2)}, u32[]{:S(2)}) collective-permute-start(bf16[32,128]{1,0:T(8,128)(2,1)S(1)} %shard_map.183.own_ref.packed_ref), channel_id=1, source_target_pairs={{0,2},{1,3},{2,0},{3,1},{4,6},{5,7},{6,4},{7,5},{8,10},{9,11},{10,... | collective-permute-start | bytes 24584 | tf_op jit(solution)/shard_map/ppermute | solution.py:570
  4.5 3.0 %collective-permute-start = (bf16[32,128]{1,0:T(8,128)(2,1)S(1)}, bf16[32,128]{1,0:T(8,128)(2,1)S(1)}, u32[]{:S(2)}, u32[]{:S(2)}) collective-permute-start(bf16[32,128]{1,0:T(8,128)(2,1)S(1)} %shard_map.183.own_ref.packed_ref), channel_id=1, source_target_pairs={{0,1},{1,0},{2,3},{3,2},{4,5},{5,4},{6,7},{7,6},{8,9},{9,8},{10,11... | collective-permute-start | bytes 24584 | tf_op jit(solution)/shard_map/ppermute | solution.py:570
  9.0 12.1 %all-to-all-start = ((f32[32,1,128]{2,1,0:T(1,128)}), f32[32,1,128]{2,1,0:T(1,128)S(1)}, u32[]{:S(2)}, u32[]{:S(2)}) async-start(f32[32,1,128]{2,1,0:T(1,128)} %get-tuple-element.26), calls=%async_computation | async-start | bytes 32768 | tf_op jit(solution)/shard_map/all_to_all | solution.py:639
